TPU v7x, 32 devices: a whole 2x2x4 slice. The times are simulated.
32 devices in a mesh: wide: 8 (over y, x, core), narrow: 4 (over z).
Axes of the slice: x: 2, y: 2, z: 4, core: 2. Of those that a mesh axis runs over, the one named last changes fastest.
Arguments:
- token_ids: int32 [4096], P(('wide', 'narrow')), may hold values from 0 to 50256
- lengths: int32 [32], P(('wide', 'narrow')), may hold values from 1 to 128, as said below
- top_ids: int32 [4096, 32], P(('wide', 'narrow')), may hold values from 0 to 32767, as said below
- aux_ids: int32 [4096, 512], P(('wide', 'narrow')), may hold values from 0 to 32767, as said below
- dead_set: int32 [32768], replicated, may hold values 0 or 1
- token_table: bfloat16 [50304, 768], P('wide'), may hold values from -6 to 6
- position_table: bfloat16 [1024, 768], replicated, may hold values from -4 to 4
- ln_gains: float32 [2, 768], replicated, may hold values from 0.5 to 1.5
- frozen_bias: float32 [8448], replicated, may hold values from -1.5 to 1.5
- w_qkv: bfloat16 [768, 2304], replicated, may hold values from -0.21875 to 0.21875
- w_proj: bfloat16 [768, 768], replicated, may hold values from -0.21875 to 0.21875
- w_fc: bfloat16 [768, 3072], replicated, may hold values from -0.21875 to 0.21875
- w_out: bfloat16 [3072, 768], replicated, may hold values from -0.109375 to 0.109375
- enc_weight: float32 [768, 32768], P('narrow', 'wide'), may hold values from -0.21875 to 0.21875
- enc_bias: float32 [32768], P(('wide', 'narrow')), may hold values from -4 to 4
- dec_weight: float32 [32768, 768], P('wide', 'narrow'), may hold values from -0.375 to 0.375
- decoder_bias: float32 [768], replicated, may hold values from -4 to 4
- enc_moment: float32 [768, 32768], P('narrow', 'wide'), may hold values from -0.25 to 0.25
- dec_moment: float32 [32768, 768], P('wide', 'narrow'), may hold values from -0.109375 to 0.109375
- encb_first: float32 [32768], P(('wide', 'narrow')), may hold values from -0.01953125 to 0.01953125
- encb_second: float32 [32768], P(('wide', 'narrow')), may hold values from 1.4322917e-07 to 5.729167e-07
- decb_first: float32 [768], replicated, may hold values from -0.375 to 0.375
- decb_second: float32 [768], replicated, may hold values from 5.953836e-05 to 0.00023815344
Outputs:
- token_loss: float32 [4096], P(('wide', 'narrow'))
- enc_new: float32 [768, 32768], P('narrow', 'wide')
- enc_moment_new: float32 [768, 32768], P('narrow', 'wide')
- enc_copy: bfloat16 [768, 32768], P('narrow', 'wide')
- dec_new: float32 [32768, 768], P('wide', 'narrow')
- dec_moment_new: float32 [32768, 768], P('wide', 'narrow')
- dec_copy: bfloat16 [32768, 768], P('wide', 'narrow')
- encb_new: float32 [32768], P(('wide', 'narrow'))
- encb_first_new: float32 [32768], P(('wide', 'narrow'))
- encb_second_new: float32 [32768], P(('wide', 'narrow'))
- decb_new: float32 [768], replicated
- decb_first_new: float32 [768], replicated
- decb_second_new: float32 [768], replicated
Inputs may be any that keep to these rules, and one draw needn't show every extreme that they name: `lengths`: the last context has 128 counted tokens. Each row of top_ids and aux_ids together names 544 different latents. `aux_ids`: no aux id of a row equals a top id of that row.
All inputs are finite; a program needn't handle non-finite values.
Results may differ from a plain program's by a relative error of at most 0.014.
Values may be sent and summed in bfloat16 or wider, within the bound.
No kernel may reach another device: no remote copies, remote signals or barrier semaphores. Data moves between devices by JAX's collectives and lax.ppermute only.
A program may use at most 256 MiB of HBM per device.

v0:
```python
import math

import jax
import jax.numpy as jnp
from jax import lax
from jax.sharding import PartitionSpec as P

D = 768
HEAD_DIM = 64
L = 32768
NS_STEPS = 5
STEP = 10


HIGH_PRECISION = lax.Precision.HIGHEST
AUX_COEF = 1.0 / 32.0
EPS_NORM = 1e-05
NS_EPS = 1e-07
QA = 3.4445
QB = -4.775
QC = 2.0315
MOMENTUM = 0.95
MUON_RATE = 0.1
DECAY = 0.1
BIAS_RATE = 0.3
BETA_ONE = 0.9
BETA_TWO = 0.999
ADAM_EPS = 1e-08


def layer_norm(value, gain, shift):
    row_mean = jnp.mean(value, -1, keepdims=True)
    centred = value - row_mean
    row_var = jnp.mean(centred * centred, -1, keepdims=True)
    return centred * lax.rsqrt(row_var + EPS_NORM) * gain + shift


def frozen_block(start, ctx_length, ln_gains, frozen_bias, w_qkv, w_proj, w_fc, w_out):
    row_count, model_width = start.shape
    head_count = model_width // HEAD_DIM
    ff_width = w_fc.shape[1]
    shifts = frozen_bias[: 2 * model_width].reshape(2, model_width)
    b_qkv = frozen_bias[2 * model_width : 5 * model_width]
    b_proj = frozen_bias[5 * model_width : 6 * model_width]
    b_fc = frozen_bias[6 * model_width : 6 * model_width + ff_width]
    b_out = frozen_bias[6 * model_width + ff_width :]
    normed = layer_norm(start, ln_gains[0], shifts[0]).astype(jnp.bfloat16)
    qkv_rows = (jnp.dot(normed, w_qkv, preferred_element_type=jnp.float32) + b_qkv).astype(
        jnp.bfloat16
    )
    head_split = qkv_rows.reshape(row_count, 3, head_count, HEAD_DIM)
    scores = jnp.einsum(
        "qhd,khd->hqk", head_split[:, 0], head_split[:, 1], preferred_element_type=jnp.float32
    ) * HEAD_DIM ** (-0.5)
    positions = jnp.arange(row_count)
    allowed = (positions[None, :] <= positions[:, None]) & (positions[None, :] < ctx_length)
    attn_probs = jax.nn.softmax(jnp.where(allowed[None], scores, -1e30), axis=-1).astype(
        jnp.bfloat16
    )
    mixed = jnp.einsum(
        "hqk,khd->qhd", attn_probs, head_split[:, 2], preferred_element_type=jnp.float32
    )
    mixed = mixed.reshape(row_count, model_width).astype(jnp.bfloat16)
    hidden = start + jnp.dot(mixed, w_proj, preferred_element_type=jnp.float32) + b_proj
    normed_two = layer_norm(hidden, ln_gains[1], shifts[1]).astype(jnp.bfloat16)
    inner_acts = jax.nn.gelu(
        jnp.dot(normed_two, w_fc, preferred_element_type=jnp.float32) + b_fc, approximate=True
    ).astype(jnp.bfloat16)
    return (hidden + jnp.dot(inner_acts, w_out, preferred_element_type=jnp.float32) + b_out).astype(
        jnp.bfloat16
    )


def kind_codes(id_lists, code_row, first_col, col_count):
    row_total, pick_count = id_lists.shape
    lane_width = min(128, col_count)
    group_count = col_count // lane_width
    block_rows = math.gcd(row_total, max(1, 8192 // group_count))
    offset_ids = id_lists - first_col
    high_ids = jnp.where(offset_ids >= 0, offset_ids // lane_width, -1)
    lane_ids = offset_ids % lane_width
    group_range = jnp.arange(group_count)
    lane_range = jnp.arange(lane_width)

    def one_block(packed):
        high_part, lane_part = packed
        high_hot = jnp.where(
            high_part[:, None, :] == group_range[None, :, None], code_row[None, None, :], 0.0
        ).astype(jnp.bfloat16)
        low_hot = (lane_part[:, :, None] == lane_range[None, None, :]).astype(jnp.bfloat16)
        placed = jnp.einsum("rhk,rkl->rhl", high_hot, low_hot, preferred_element_type=jnp.float32)
        return placed.reshape(high_part.shape[0], col_count)

    blocked = (
        high_ids.reshape(row_total // block_rows, block_rows, pick_count),
        lane_ids.reshape(row_total // block_rows, block_rows, pick_count),
    )
    return lax.map(one_block, blocked).reshape(row_total, col_count)


def newton_schulz(stacked):
    current = stacked
    for ns_step in range(NS_STEPS):
        every_rows = lax.all_gather(current, "narrow", axis=1, tiled=True)
        partial_value = jnp.einsum("arl,adl->ard", current, every_rows, precision=HIGH_PRECISION)
        gram_part = lax.psum(partial_value.astype(jnp.bfloat16), "wide").astype(jnp.float32)
        gram_full = lax.all_gather(gram_part, "narrow", axis=1, tiled=True)
        if ns_step == 0:
            trace_sum = jnp.trace(gram_full, axis1=1, axis2=2)
            norm_scale = (1.0 / (jnp.sqrt(trace_sum) + NS_EPS))[:, None, None]
            current = current * norm_scale
            every_rows = every_rows * norm_scale
            gram_part = gram_part * (norm_scale * norm_scale)
            gram_full = gram_full * (norm_scale * norm_scale)
        polynomial = QB * gram_part + QC * jnp.einsum(
            "ard,ade->are", gram_part, gram_full, precision=HIGH_PRECISION
        )
        current = QA * current + jnp.einsum(
            "ard,adl->arl", polynomial, every_rows, precision=HIGH_PRECISION
        )
    return current


def adam_update(param, grad, first, second):
    first = BETA_ONE * first + (1.0 - BETA_ONE) * grad
    second = BETA_TWO * second + (1.0 - BETA_TWO) * grad * grad
    denom = jnp.sqrt(second / (1.0 - BETA_TWO**STEP)) + ADAM_EPS
    return (param - BIAS_RATE * (first / (1.0 - BETA_ONE**STEP)) / denom, first, second)


def local(
    token_ids,
    lengths,
    top_ids,
    aux_ids,
    dead_set,
    token_table,
    position_table,
    ln_gains,
    frozen_bias,
    w_qkv,
    w_proj,
    w_fc,
    w_out,
    enc_weight,
    enc_bias,
    dec_weight,
    decoder_bias,
    enc_moment,
    dec_moment,
    encb_first,
    encb_second,
    decb_first,
    decb_second,
):
    enc_rows, dec_cols, bias_copy = (
        lax.all_gather(enc_weight.astype(jnp.bfloat16), "narrow", axis=0, tiled=True),
        lax.all_gather(dec_weight.astype(jnp.bfloat16), "narrow", axis=1, tiled=True),
        lax.all_gather(enc_bias.astype(jnp.bfloat16), "narrow", axis=0, tiled=True),
    )
    row_count = token_ids.shape[0]
    model_width = token_table.shape[1]
    wide_pos = lax.axis_index("wide")
    vocab_dev = token_table.shape[0]
    every_ids = lax.all_gather(token_ids, "wide", axis=0, tiled=True)
    local_ids = every_ids - wide_pos * vocab_dev
    inside = (local_ids >= 0) & (local_ids < vocab_dev)
    looked = jnp.take(token_table, jnp.clip(local_ids, 0, vocab_dev - 1), axis=0).astype(
        jnp.float32
    )
    embedded = lax.psum_scatter(
        jnp.where(inside[:, None], looked, 0.0).astype(jnp.bfloat16),
        "wide",
        scatter_dimension=0,
        tiled=True,
    ).astype(jnp.float32)
    start = embedded + position_table[:row_count].astype(jnp.float32)
    ctx_length = lengths[0]
    inputs = frozen_block(start, ctx_length, ln_gains, frozen_bias, w_qkv, w_proj, w_fc, w_out)
    counted = (jnp.arange(row_count) < ctx_length).astype(jnp.float32)
    all_inputs = lax.all_gather(inputs, "wide", axis=0, tiled=True)
    encoder_in = (all_inputs.astype(jnp.float32) - decoder_bias).astype(jnp.bfloat16)
    pre_acts = (
        jnp.dot(encoder_in, enc_rows, preferred_element_type=jnp.float32)
        + bias_copy.astype(jnp.float32)
    ).astype(jnp.bfloat16)
    top_count = top_ids.shape[1]
    pick_total = top_count + aux_ids.shape[1]
    code_row = jnp.where(jnp.arange(pick_total) < top_count, 1.0, 2.0).astype(jnp.float32)
    zero_bf = jnp.zeros((), jnp.bfloat16)
    token_scores = lax.all_to_all(pre_acts, "wide", split_axis=0, concat_axis=1, tiled=True)
    all_latents = token_scores.shape[1]
    codes = kind_codes(jnp.concatenate([top_ids, aux_ids], 1), code_row, 0, all_latents)
    top_here = codes == 1.0
    aux_here = (codes == 2.0) & (dead_set[None, :] == 1)
    picked = jnp.where(top_here | aux_here, token_scores, zero_bf)
    kind_value = jnp.where(top_here, 1.0, jnp.where(aux_here, 2.0, 0.0)).astype(jnp.bfloat16)
    planes = jnp.stack([picked, kind_value])
    returned = lax.all_to_all(planes, "wide", split_axis=2, concat_axis=1, tiled=True)
    top_mask = returned[1] == 1.0
    aux_mask = returned[1] == 2.0
    chosen_values = returned[0]
    top_acts = jnp.where(top_mask, chosen_values, zero_bf)
    aux_acts = jnp.where(aux_mask, chosen_values, zero_bf)
    top_part = top_acts
    aux_part = aux_acts
    rebuilt_both = lax.psum_scatter(
        jnp.concatenate(
            [
                jnp.dot(top_part, dec_cols, preferred_element_type=jnp.float32),
                jnp.dot(aux_part, dec_cols, preferred_element_type=jnp.float32),
            ],
            1,
        ),
        "wide",
        scatter_dimension=0,
        tiled=True,
    )
    target = inputs.astype(jnp.float32)
    reconstructed_input = rebuilt_both[:, :model_width] + decoder_bias
    auxiliary_reconstruction = rebuilt_both[:, model_width:]
    recon_error = target - reconstructed_input
    aux_gap = auxiliary_reconstruction - recon_error
    token_loss = (
        counted
        * (jnp.sum(recon_error * recon_error, 1) + AUX_COEF * jnp.sum(aux_gap * aux_gap, 1))
        / model_width
    )
    back_recon = 2.0 / model_width * counted[:, None] * (reconstructed_input - target)
    back_aux = 2.0 * AUX_COEF / model_width * counted[:, None] * aux_gap
    back_rows = jnp.concatenate([back_recon, back_aux], 1).astype(jnp.bfloat16)
    to_latents = (((1,), (1,)), ((), ()))
    over_rows = (((0,), (0,)), ((), ()))
    shard_rows = lax.all_gather(back_rows, "wide", axis=0, tiled=True)
    top_part = top_acts
    aux_part = aux_acts
    recon_part = shard_rows[:, :model_width]
    aux_back = shard_rows[:, model_width:]
    back_top = lax.dot_general(recon_part, dec_cols, to_latents, preferred_element_type=jnp.float32)
    back_side = lax.dot_general(aux_back, dec_cols, to_latents, preferred_element_type=jnp.float32)
    latent_grad = jnp.where(top_mask, back_top, jnp.where(aux_mask, back_side, 0.0)).astype(
        jnp.bfloat16
    )
    grad_dec = lax.dot_general(top_part, recon_part, over_rows, preferred_element_type=jnp.float32)
    grad_dec = grad_dec + lax.dot_general(
        aux_part, aux_back, over_rows, preferred_element_type=jnp.float32
    )
    grad_enc = lax.dot_general(
        encoder_in, latent_grad, over_rows, preferred_element_type=jnp.float32
    )
    column_sum = jnp.sum(latent_grad, 0, dtype=jnp.float32)
    grad_enc, grad_dec, column_sum = (grad_enc, grad_dec, column_sum)
    bias_term = jnp.sum(back_rows[:, :model_width], 0, dtype=jnp.float32) - jnp.dot(
        enc_rows.astype(jnp.float32), column_sum, precision=HIGH_PRECISION
    )
    grad_decb = lax.psum(bias_term, ("wide", "narrow"))
    enc_grad, dec_grad, encb_grad = (
        lax.psum_scatter(grad_enc, "narrow", scatter_dimension=0, tiled=True),
        lax.psum_scatter(grad_dec, "narrow", scatter_dimension=1, tiled=True),
        lax.psum_scatter(column_sum, "narrow", scatter_dimension=0, tiled=True),
    )
    enc_next = MOMENTUM * enc_moment + enc_grad
    dec_next = MOMENTUM * dec_moment + dec_grad
    ortho_dirs = newton_schulz(jnp.stack([enc_next, dec_next.T]))
    step_scale = MUON_RATE * 0.2 * math.sqrt(max(D, L))
    enc_new = enc_weight * (1.0 - MUON_RATE * DECAY) - step_scale * ortho_dirs[0]
    dec_new = dec_weight * (1.0 - MUON_RATE * DECAY) - step_scale * ortho_dirs[1].T
    encb_new, encb_one, encb_two = adam_update(enc_bias, encb_grad, encb_first, encb_second)
    decb_new, decb_one, decb_two = adam_update(decoder_bias, grad_decb, decb_first, decb_second)
    return (
        token_loss,
        enc_new,
        enc_next,
        enc_new.astype(jnp.bfloat16),
        dec_new,
        dec_next,
        dec_new.astype(jnp.bfloat16),
        encb_new,
        encb_one,
        encb_two,
        decb_new,
        decb_one,
        decb_two,
    )


def solution(mesh):
    placed = (
        P(("wide", "narrow")),
        P(("wide", "narrow")),
        P(("wide", "narrow"), None),
        P(("wide", "narrow"), None),
        P(),
        P("wide", None),
        P(),
        P(),
        P(),
        P(),
        P(),
        P(),
        P(),
        P("narrow", "wide"),
        P(("wide", "narrow")),
        P("wide", "narrow"),
        P(),
        P("narrow", "wide"),
        P("wide", "narrow"),
        P(("wide", "narrow")),
        P(("wide", "narrow")),
        P(),
        P(),
    )
    return jax.shard_map(
        local,
        mesh=mesh,
        in_specs=placed,
        out_specs=(
            P(("wide", "narrow")),
            P("narrow", "wide"),
            P("narrow", "wide"),
            P("narrow", "wide"),
            P("wide", "narrow"),
            P("wide", "narrow"),
            P("wide", "narrow"),
            P(("wide", "narrow")),
            P(("wide", "narrow")),
            P(("wide", "narrow")),
            P(),
            P(),
            P(),
        ),
        check_vma=False,
    )
```

profile of v0, /device:TPU:0, one launch (start us, length us, event | category | flops | bytes accessed | tf_op | source)
XLA Modules:
  0.0 4437.5 jit_solution(7296889359834255043)
XLA Ops:
  36.8 33.4 reduce-scatter.5.cloned.1.call-done
  88.6 77.6 %while.11 = (s32[]{:T(128)}, f32[4,32,32768]{2,1,0:T(8,128)}, s32[4,32,544]{2,1,0:T(8,128)S(1)}, s32[4,32,544]{2,1,0:T(8,128)S(1)}, s32[]{:T(128)}) while((s32[]{:T(128)}, f32[4,32,32768]{2,1,0:T(8,128)}, s32[4,32,544]{2,1,0:T(8,128)S(1)}, s32[4,32,544]{2,1,0:T(8,128)S(1)}, s32[]{:T(128)}) %tuple.51), condition=%wide.region_8.9_spmd.clone, body=%wide.region_7.8_spmd.clone.sunk | while | flops 1151992960 | bytes 21392064 | solution.py:98
  190.3 39.5 all-gather.18.cloned.1.call-done
  269.3 83.0 %all-to-all-done = bf16[8,128,4096]{1,2,0:T(8,128)(2,1)} async-done(((bf16[8,128,4096]{1,2,0:T(8,128)(2,1)}), bf16[8,128,4096]{1,2,0:T(8,128)(2,1)}, u32[]{:S(2)}, u32[]{:S(2)}) %all-to-all-start) | async-done | bytes 8388640 | tf_op jit(solution)/shard_map/all_to_all | solution.py:191
  379.2 40.9 copy.71
  428.1 182.0 %all-to-all-done.1 = bf16[2,128,32768]{1,0,2:T(2,128)(2,1)} async-done(((bf16[2,128,32768]{1,0,2:T(2,128)(2,1)}), bf16[2,128,32768]{1,0,2:T(2,128)(2,1)}, u32[]{:S(2)}, u32[]{:S(2)}) %all-to-all-start.1) | async-done | bytes 16777248 | tf_op jit(solution)/shard_map/all_to_all | solution.py:199
  696.5 58.3 %reduce-scatter.7.cloned.1.call-done = f32[128,1536]{1,0:T(8,128)} async-done(((f32[1024,1536]{1,0:T(8,128)}), f32[128,1536]{1,0:T(8,128)}) %reduce-scatter.7.cloned.1.call-update) | async-done | bytes 786448 | tf_op jit(solution)/shard_map/reduce_scatter | solution.py:207
  757.5 32.4 all-gather.22.cloned.1.call-done
  855.9 188.4 %reduce-scatter.9.cloned.1.call-done = f32[192,4096]{1,0:T(8,128)} async-done(((f32[768,4096]{1,0:T(8,128)}), f32[192,4096]{1,0:T(8,128)}) %reduce-scatter.9.cloned.1.call-update) | async-done | bytes 3145744 | tf_op jit(solution)/shard_map/reduce_scatter | solution.py:258
  1047.6 212.1 %reduce-scatter.11.cloned.1.call-done = f32[4096,192]{0,1:T(8,128)} async-done(((f32[4096,768]{0,1:T(8,128)}), f32[4096,192]{0,1:T(8,128)}) %reduce-scatter.11.cloned.1.call-update) | async-done | bytes 3145744 | tf_op jit(solution)/shard_map/reduce_scatter | solution.py:259
  1267.9 425.3 %all-gather.24.cloned.1.call-done = f32[2,768,4096]{2,1,0:T(8,128)} async-done(((f32[2,192,4096]{2,1,0:T(8,128)}), f32[2,768,4096]{2,1,0:T(8,128)}) %all-gather.24.cloned.1.call-update) | async-done | bytes 25165840 | tf_op jit(solution)/shard_map/all_gather | solution.py:104
  1693.2 31.5 convolution_convert_fusion.4
  1724.9 53.2 %all-reduce.7.cloned.1.call-done = bf16[2,192,768]{2,1,0:T(8,128)(2,1)} async-done(((bf16[2,192,768]{2,1,0:T(8,128)(2,1)}), bf16[2,192,768]{2,1,0:T(8,128)(2,1)}) %all-reduce.7.cloned.1.call-update) | async-done | bytes 589840 | tf_op jit(solution)/shard_map/psum | solution.py:106
  1781.3 87.8 %all-gather.26.cloned.1.call-done = f32[2,768,768]{2,1,0:T(8,128)} async-done(((f32[2,192,768]{2,1,0:T(8,128)}), f32[2,768,768]{2,1,0:T(8,128)}) %all-gather.26.cloned.1.call-update) | async-done | bytes 4718608 | tf_op jit(solution)/shard_map/all_gather | solution.py:107
  1902.6 422.7 %all-gather.28.cloned.1.call-done = f32[2,768,4096]{2,1,0:T(8,128)} async-done(((f32[2,192,4096]{2,1,0:T(8,128)}), f32[2,768,4096]{2,1,0:T(8,128)}) %all-gather.28.cloned.1.call-update) | async-done | bytes 25165840 | tf_op jit(solution)/shard_map/all_gather | solution.py:104
  2325.4 32.1 convolution_convert_fusion.3
  2357.5 53.2 %all-reduce.9.cloned.1.call-done = bf16[2,192,768]{2,1,0:T(8,128)(2,1)} async-done(((bf16[2,192,768]{2,1,0:T(8,128)(2,1)}), bf16[2,192,768]{2,1,0:T(8,128)(2,1)}) %all-reduce.9.cloned.1.call-update) | async-done | bytes 589840 | tf_op jit(solution)/shard_map/psum | solution.py:106
  2413.0 88.8 %all-gather.30.cloned.1.call-done = f32[2,768,768]{2,1,0:T(8,128)} async-done(((f32[2,192,768]{2,1,0:T(8,128)}), f32[2,768,768]{2,1,0:T(8,128)}) %all-gather.30.cloned.1.call-update) | async-done | bytes 4718608 | tf_op jit(solution)/shard_map/all_gather | solution.py:107
  2506.7 25.2 multiply_add_fusion.3
  2532.0 422.7 %all-gather.32.cloned.1.call-done = f32[2,768,4096]{2,1,0:T(8,128)} async-done(((f32[2,192,4096]{2,1,0:T(8,128)}), f32[2,768,4096]{2,1,0:T(8,128)}) %all-gather.32.cloned.1.call-update) | async-done | bytes 25165840 | tf_op jit(solution)/shard_map/all_gather | solution.py:104
  2954.7 32.0 convolution_convert_fusion.2
  2986.8 53.2 %all-reduce.11.cloned.1.call-done = bf16[2,192,768]{2,1,0:T(8,128)(2,1)} async-done(((bf16[2,192,768]{2,1,0:T(8,128)(2,1)}), bf16[2,192,768]{2,1,0:T(8,128)(2,1)}) %all-reduce.11.cloned.1.call-update) | async-done | bytes 589840 | tf_op jit(solution)/shard_map/psum | solution.py:106
  3042.3 88.8 %all-gather.34.cloned.1.call-done = f32[2,768,768]{2,1,0:T(8,128)} async-done(((f32[2,192,768]{2,1,0:T(8,128)}), f32[2,768,768]{2,1,0:T(8,128)}) %all-gather.34.cloned.1.call-update) | async-done | bytes 4718608 | tf_op jit(solution)/shard_map/all_gather | solution.py:107
  3136.0 25.0 multiply_add_fusion.2
  3161.1 422.7 %all-gather.36.cloned.1.call-done = f32[2,768,4096]{2,1,0:T(8,128)} async-done(((f32[2,192,4096]{2,1,0:T(8,128)}), f32[2,768,4096]{2,1,0:T(8,128)}) %all-gather.36.cloned.1.call-update) | async-done | bytes 25165840 | tf_op jit(solution)/shard_map/all_gather | solution.py:104
  3583.8 32.3 convolution_convert_fusion.1
  3616.2 53.2 %all-reduce.13.cloned.1.call-done = bf16[2,192,768]{2,1,0:T(8,128)(2,1)} async-done(((bf16[2,192,768]{2,1,0:T(8,128)(2,1)}), bf16[2,192,768]{2,1,0:T(8,128)(2,1)}) %all-reduce.13.cloned.1.call-update) | async-done | bytes 589840 | tf_op jit(solution)/shard_map/psum | solution.py:106
  3671.6 88.8 %all-gather.38.cloned.1.call-done = f32[2,768,768]{2,1,0:T(8,128)} async-done(((f32[2,192,768]{2,1,0:T(8,128)}), f32[2,768,768]{2,1,0:T(8,128)}) %all-gather.38.cloned.1.call-update) | async-done | bytes 4718608 | tf_op jit(solution)/shard_map/all_gather | solution.py:107
  3790.4 422.7 %all-gather.40.cloned.1.call-done = f32[2,768,4096]{2,1,0:T(8,128)} async-done(((f32[2,192,4096]{2,1,0:T(8,128)}), f32[2,768,4096]{2,1,0:T(8,128)}) %all-gather.40.cloned.1.call-update) | async-done | bytes 25165840 | tf_op jit(solution)/shard_map/all_gather | solution.py:104
  4213.1 32.1 convolution_convert_fusion
  4245.3 53.2 %all-reduce.15.cloned.1.call-done = bf16[2,192,768]{2,1,0:T(8,128)(2,1)} async-done(((bf16[2,192,768]{2,1,0:T(8,128)(2,1)}), bf16[2,192,768]{2,1,0:T(8,128)(2,1)}) %all-reduce.15.cloned.1.call-update) | async-done | bytes 589840 | tf_op jit(solution)/shard_map/psum | solution.py:106
  4309.6 42.8 psum.47
  (250 shorter events, 561.6 us)
Async XLA Ops:
  7.2 62.9 %reduce-scatter.5.cloned.1.call-start = ((), (), s32[]{:S(2)}) async-start(), calls=%async_computation.6 | async-start | bytes 1769472 | tf_op jit(solution)/shard_map/reduce_scatter | solution.py:171
  31.3 159.0 %all-gather.16.cloned.1.call-start = ((), (), s32[]{:S(2)}) async-start(), calls=%async_computation.7 | async-start | bytes 1769472 | tf_op jit(solution)/shard_map/all_gather | solution.py:181
  86.4 143.5 %all-gather.18.cloned.1.call-start = ((), (), s32[]{:S(2)}) async-start(), calls=%async_computation.8 | async-start | bytes 7864320 | tf_op jit(solution)/shard_map/all_gather | solution.py:157
  88.6 91.0 %copy-start.21 = (s32[32768]{0:T(1024)S(1)}, s32[32768]{0:T(1024)}, u32[]{:S(2)}) copy-start(s32[32768]{0:T(1024)} %param.29) | copy-start | bytes 393220
  253.0 99.3 %all-to-all-start = ((bf16[8,128,4096]{1,2,0:T(8,128)(2,1)}), bf16[8,128,4096]{1,2,0:T(8,128)(2,1)}, u32[]{:S(2)}, u32[]{:S(2)}) async-start(bf16[8,128,4096]{1,2,0:T(8,128)(2,1)} %copy.69), calls=%async_computation.1 | async-start | bytes 16777216 | tf_op jit(solution)/shard_map/all_to_all | solution.py:191
  420.1 190.0 %all-to-all-start.1 = ((bf16[2,128,32768]{1,0,2:T(2,128)(2,1)}), bf16[2,128,32768]{1,0,2:T(2,128)(2,1)}, u32[]{:S(2)}, u32[]{:S(2)}) async-start(bf16[2,128,32768]{1,0,2:T(2,128)(2,1)} %copy.71), calls=%async_computation.2 | async-start | bytes 33554432 | tf_op jit(solution)/shard_map/all_to_all | solution.py:199
  426.2 248.6 %all-gather.20.cloned.1.call-start = ((), (), s32[]{:S(2)}) async-start(), calls=%async_computation.9 | async-start | bytes 7864320 | tf_op jit(solution)/shard_map/all_gather | solution.py:158
  427.6 327.2 %reduce-scatter.7.cloned.1.call-start = ((), (), s32[]{:S(2)}) async-start(), calls=%async_computation.10 | async-start | bytes 7077888 | tf_op jit(solution)/shard_map/reduce_scatter | solution.py:207
  696.4 93.5 %all-gather.22.cloned.1.call-start = ((), (), s32[]{:S(2)}) async-start(), calls=%async_computation.11 | async-start | bytes 3538944 | tf_op jit(solution)/shard_map/all_gather | solution.py:234
  757.5 286.8 %reduce-scatter.9.cloned.1.call-start = ((), (), s32[]{:S(2)}) async-start(), calls=%async_computation.12 | async-start | bytes 15728640 | tf_op jit(solution)/shard_map/reduce_scatter | solution.py:258
  832.3 427.4 %reduce-scatter.11.cloned.1.call-start = ((), (), s32[]{:S(2)}) async-start(), calls=%async_computation.13 | async-start | bytes 15728640 | tf_op jit(solution)/shard_map/reduce_scatter | solution.py:259
  855.9 837.4 %all-gather.24.cloned.1.call-start = ((), (), s32[]{:S(2)}) async-start(), calls=%async_computation.14 | async-start | bytes 31457280 | tf_op jit(solution)/shard_map/all_gather | solution.py:104
  1047.6 830.2 %copy-start.2 = (f32[192,4096]{1,0:T(8,128)}, f32[192,4096]{1,0:T(8,128)S(1)}, u32[]{:S(2)}) copy-start(f32[192,4096]{1,0:T(8,128)S(1)} %multiply_add_fusion.6) | copy-start | bytes 9437188
  1267.9 510.2 %all-reduce.7.cloned.1.call-start = ((), (), s32[]{:S(2)}) async-start(), calls=%async_computation.15 | async-start | bytes 1179648 | tf_op jit(solution)/shard_map/psum | solution.py:106
  1724.8 144.3 %all-gather.26.cloned.1.call-start = ((), (), s32[]{:S(2)}) async-start(), calls=%async_computation.16 | async-start | bytes 5898240 | tf_op jit(solution)/shard_map/all_gather | solution.py:107
  1780.3 545.1 %all-gather.28.cloned.1.call-start = ((), (), s32[]{:S(2)}) async-start(), calls=%async_computation.17 | async-start | bytes 31457280 | tf_op jit(solution)/shard_map/all_gather | solution.py:104
  1902.6 508.2 %all-reduce.9.cloned.1.call-start = ((), (), s32[]{:S(2)}) async-start(), calls=%async_computation.18 | async-start | bytes 1179648 | tf_op jit(solution)/shard_map/psum | solution.py:106
  2357.5 144.3 %all-gather.30.cloned.1.call-start = ((), (), s32[]{:S(2)}) async-start(), calls=%async_computation.19 | async-start | bytes 5898240 | tf_op jit(solution)/shard_map/all_gather | solution.py:107
  2412.9 541.8 %all-gather.32.cloned.1.call-start = ((), (), s32[]{:S(2)}) async-start(), calls=%async_computation.20 | async-start | bytes 31457280 | tf_op jit(solution)/shard_map/all_gather | solution.py:104
  2531.9 508.1 %all-reduce.11.cloned.1.call-start = ((), (), s32[]{:S(2)}) async-start(), calls=%async_computation.21 | async-start | bytes 1179648 | tf_op jit(solution)/shard_map/psum | solution.py:106
  2986.8 144.3 %all-gather.34.cloned.1.call-start = ((), (), s32[]{:S(2)}) async-start(), calls=%async_computation.22 | async-start | bytes 5898240 | tf_op jit(solution)/shard_map/all_gather | solution.py:107
  3042.2 541.6 %all-gather.36.cloned.1.call-start = ((), (), s32[]{:S(2)}) async-start(), calls=%async_computation.23 | async-start | bytes 31457280 | tf_op jit(solution)/shard_map/all_gather | solution.py:104
  3161.0 508.4 %all-reduce.13.cloned.1.call-start = ((), (), s32[]{:S(2)}) async-start(), calls=%async_computation.24 | async-start | bytes 1179648 | tf_op jit(solution)/shard_map/psum | solution.py:106
  3616.1 144.3 %all-gather.38.cloned.1.call-start = ((), (), s32[]{:S(2)}) async-start(), calls=%async_computation.25 | async-start | bytes 5898240 | tf_op jit(solution)/shard_map/all_gather | solution.py:107
  3671.6 541.5 %all-gather.40.cloned.1.call-start = ((), (), s32[]{:S(2)}) async-start(), calls=%async_computation.26 | async-start | bytes 31457280 | tf_op jit(solution)/shard_map/all_gather | solution.py:104
  3790.3 510.4 %copy-start.42 = (u32[32]{0:T(128)S(1)}, u32[32]{0:T(128)}, u32[]{:S(2)}) copy-start(u32[32]{0:T(128)} %constant.173) | copy-start | bytes 388
  3790.3 511.6 %copy-start.37 = (f32[128]{0:T(128)S(1)}, f32[128]{0:T(128)}, u32[]{:S(2)}) copy-start(f32[128]{0:T(128)} %get-tuple-element.97) | copy-start | bytes 1540
  3790.3 511.6 %copy-start.38 = (f32[128]{0:T(128)S(1)}, f32[128]{0:T(128)}, u32[]{:S(2)}) copy-start(f32[128]{0:T(128)} %get-tuple-element.98) | copy-start | bytes 1540
  3790.4 512.2 %copy-start.22 = (f32[4096]{0:T(1024)S(1)}, f32[4096]{0:T(1024)}, u32[]{:S(2)}) copy-start(f32[4096]{0:T(1024)} %get-tuple-element.108) | copy-start | bytes 49156
  3790.4 508.1 %all-reduce.15.cloned.1.call-start = ((), (), s32[]{:S(2)}) async-start(), calls=%async_computation.27 | async-start | bytes 1179648 | tf_op jit(solution)/shard_map/psum | solution.py:106
  4245.2 145.9 %all-gather.42.cloned.1.call-start = ((), (), s32[]{:S(2)}) async-start(), calls=%async_computation.28 | async-start | bytes 5898240 | tf_op jit(solution)/shard_map/all_gather | solution.py:107
  4300.7 90.4 %copy-start.16 = (bf16[2,192,768]{2,1,0:T(8,128)(2,1)S(1)}, bf16[2,192,768]{2,1,0:T(8,128)(2,1)}, u32[]{:S(2)}) copy-start(bf16[2,192,768]{2,1,0:T(8,128)(2,1)} %all-reduce.15.cloned.1.call-done) | copy-start | bytes 1769476
  (38 other events, 875.6 us)
Sparse Core Ops, SparseCore 0:
  31.4 38.6 reduce-scatter.4
  86.5 25.6 all-gather.15
  114.4 115.4 all-gather.17
  428.8 113.9 all-gather.19
  696.6 58.1 reduce-scatter.6
  757.6 32.2 all-gather.21
  832.4 211.8 reduce-scatter.8
  1046.8 212.8 reduce-scatter.10
  1268.0 425.2 all-gather.23
  1724.9 53.1 all-reduce.6
  1780.4 88.6 all-gather.25
  1902.7 422.6 all-gather.27
  2357.6 53.0 all-reduce.8
  2413.1 88.6 all-gather.29
  2532.1 422.6 all-gather.31
  2986.9 53.0 all-reduce.10
  3042.3 88.6 all-gather.33
  3161.1 422.6 all-gather.35
  3616.2 53.1 all-reduce.12
  3671.7 88.6 all-gather.37
  3790.4 422.6 all-gather.39
  4245.3 53.1 all-reduce.14
  4300.9 90.1 all-gather.41
where the time goes:
time: 4450 us; the launch traced here: 4440 us
  waiting for transfers between devices  3580 us (80%)
  matrix products  461 us (10%)
  local copies, waits for them, and re-layouts  175 us (4%)
  other arithmetic  102 us (2%)
  blocking collectives  88.6 us (2%)
    all_gather x5, waiting for transfers between devices, newton_schulz(): every_rows = lax.all_gather(current, 'narrow', axis=1, tiled=True)  2120 us
    all_gather x5, waiting for transfers between devices, newton_schulz(): gram_full = lax.all_gather(gram_part, 'narrow', axis=1, tiled=True)  370 us
    psum x5, waiting for transfers between devices, newton_schulz(): lax.psum(partial_value.astype(jnp.bfloat16), 'wide').astype(jnp.float32)  266 us
    reduce_scatter x1, waiting for transfers between devices, local(): lax.psum_scatter(grad_dec, 'narrow', scatter_dimension=1, tiled=True)  212 us
    reduce_scatter x1, waiting for transfers between devices, local(): lax.psum_scatter(grad_enc, 'narrow', scatter_dimension=0, tiled=True)  188 us
    all_to_all x1, waiting for transfers between devices, local(): lax.all_to_all(planes, 'wide', split_axis=2, concat_axis=1, tiled=True)  182 us
    dot_general x5, matrix products, newton_schulz(): jnp.einsum('arl,adl->ard', current, every_rows, precision=HIGH_PRECISION)  160 us
    dot_general x5, matrix products, newton_schulz(): jnp.einsum('ard,adl->arl', polynomial, every_rows, precision=HIGH_PRECISION)  125 us
  transfers between devices with their start and end apart: 25, of which 23 were waited for; matrix products, arithmetic and copies ran while one was open for 5% of the time, Pallas kernels for 0%

commit v1 on v0

--- a/solution.py
+++ b/solution.py
@@ -98,27 +98,20 @@
     return lax.map(one_block, blocked).reshape(row_total, col_count)
 
 
-def newton_schulz(stacked):
-    current = stacked
+def gram_series(gram):
+    trace_sum = jnp.trace(gram)
+    norm_scale = 1.0 / (jnp.sqrt(trace_sum) + NS_EPS)
+    gram = gram * (norm_scale * norm_scale)
+    eye = jnp.eye(gram.shape[0], dtype=jnp.float32)
+    product = None
     for ns_step in range(NS_STEPS):
-        every_rows = lax.all_gather(current, "narrow", axis=1, tiled=True)
-        partial_value = jnp.einsum("arl,adl->ard", current, every_rows, precision=HIGH_PRECISION)
-        gram_part = lax.psum(partial_value.astype(jnp.bfloat16), "wide").astype(jnp.float32)
-        gram_full = lax.all_gather(gram_part, "narrow", axis=1, tiled=True)
-        if ns_step == 0:
-            trace_sum = jnp.trace(gram_full, axis1=1, axis2=2)
-            norm_scale = (1.0 / (jnp.sqrt(trace_sum) + NS_EPS))[:, None, None]
-            current = current * norm_scale
-            every_rows = every_rows * norm_scale
-            gram_part = gram_part * (norm_scale * norm_scale)
-            gram_full = gram_full * (norm_scale * norm_scale)
-        polynomial = QB * gram_part + QC * jnp.einsum(
-            "ard,ade->are", gram_part, gram_full, precision=HIGH_PRECISION
-        )
-        current = QA * current + jnp.einsum(
-            "ard,adl->arl", polynomial, every_rows, precision=HIGH_PRECISION
-        )
-    return current
+        square = jnp.dot(gram, gram, precision=HIGH_PRECISION)
+        poly = QA * eye + QB * gram + QC * square
+        product = poly if product is None else jnp.dot(poly, product, precision=HIGH_PRECISION)
+        if ns_step < NS_STEPS - 1:
+            half = jnp.dot(gram, poly, precision=HIGH_PRECISION)
+            gram = jnp.dot(poly, half, precision=HIGH_PRECISION)
+    return product * norm_scale
 
 
 def adam_update(param, grad, first, second):
@@ -153,66 +146,78 @@
     decb_first,
     decb_second,
 ):
-    enc_rows, dec_cols, bias_copy = (
-        lax.all_gather(enc_weight.astype(jnp.bfloat16), "narrow", axis=0, tiled=True),
-        lax.all_gather(dec_weight.astype(jnp.bfloat16), "narrow", axis=1, tiled=True),
-        lax.all_gather(enc_bias.astype(jnp.bfloat16), "narrow", axis=0, tiled=True),
-    )
+    wide_count = lax.axis_size("wide")
+    narrow_count = lax.axis_size("narrow")
+    wide_pos = lax.axis_index("wide")
+    narrow_pos = lax.axis_index("narrow")
+    both = ("wide", "narrow")
     row_count = token_ids.shape[0]
     model_width = token_table.shape[1]
-    wide_pos = lax.axis_index("wide")
+    wide_latents = enc_weight.shape[1]
+    own_latents = wide_latents // narrow_count
+
+    def rows_to_latents(value):
+        return lax.all_to_all(value, "narrow", split_axis=1, concat_axis=0, tiled=True)
+
+    def cols_to_latents(value):
+        return lax.all_to_all(value, "narrow", split_axis=0, concat_axis=1, tiled=True)
+
+    enc_own = rows_to_latents(enc_weight.astype(jnp.bfloat16))
+    dec_own = cols_to_latents(dec_weight.astype(jnp.bfloat16))
+    enc_full = lax.all_gather(enc_own, "wide", axis=1, tiled=True)
+    dec_full = lax.all_gather(dec_own, "wide", axis=0, tiled=True)
+    bias_copy = lax.all_gather(enc_bias.astype(jnp.bfloat16), "wide", axis=0, tiled=True)
+    latent_count = wide_count * own_latents
+
     vocab_dev = token_table.shape[0]
     every_ids = lax.all_gather(token_ids, "wide", axis=0, tiled=True)
     local_ids = every_ids - wide_pos * vocab_dev
     inside = (local_ids >= 0) & (local_ids < vocab_dev)
-    looked = jnp.take(token_table, jnp.clip(local_ids, 0, vocab_dev - 1), axis=0).astype(
-        jnp.float32
-    )
-    embedded = lax.psum_scatter(
-        jnp.where(inside[:, None], looked, 0.0).astype(jnp.bfloat16),
-        "wide",
-        scatter_dimension=0,
-        tiled=True,
-    ).astype(jnp.float32)
+    looked = jnp.take(token_table, jnp.clip(local_ids, 0, vocab_dev - 1), axis=0)
+    looked = jnp.where(inside[:, None], looked, jnp.zeros((), jnp.bfloat16))
+    spread = lax.all_to_all(
+        looked.reshape(wide_count, row_count, model_width), "wide", 0, 0, tiled=True
+    )
+    embedded = jnp.sum(spread.astype(jnp.float32), 0)
     start = embedded + position_table[:row_count].astype(jnp.float32)
     ctx_length = lengths[0]
     inputs = frozen_block(start, ctx_length, ln_gains, frozen_bias, w_qkv, w_proj, w_fc, w_out)
     counted = (jnp.arange(row_count) < ctx_length).astype(jnp.float32)
-    all_inputs = lax.all_gather(inputs, "wide", axis=0, tiled=True)
+
+    top_count = top_ids.shape[1]
+    id_lists = lax.all_gather(
+        jnp.concatenate([top_ids, aux_ids], 1), "narrow", axis=0, tiled=True
+    )
+    within = id_lists % wide_latents
+    column = (id_lists // wide_latents) * own_latents + within % own_latents
+    column = jnp.where(within // own_latents == narrow_pos, column, -1)
+    pick_total = id_lists.shape[1]
+    code_row = jnp.where(jnp.arange(pick_total) < top_count, 1.0, 2.0).astype(jnp.float32)
+    codes = kind_codes(column, code_row, 0, latent_count)
+    dead_here = lax.dynamic_index_in_dim(
+        dead_set.reshape(wide_count, narrow_count, own_latents), narrow_pos, 1, keepdims=False
+    ).reshape(latent_count)
+    top_mask = codes == 1.0
+    aux_mask = (codes == 2.0) & (dead_here[None, :] == 1)
+
+    all_inputs = lax.all_gather(inputs, "narrow", axis=0, tiled=True)
     encoder_in = (all_inputs.astype(jnp.float32) - decoder_bias).astype(jnp.bfloat16)
     pre_acts = (
-        jnp.dot(encoder_in, enc_rows, preferred_element_type=jnp.float32)
+        jnp.dot(encoder_in, enc_full, preferred_element_type=jnp.float32)
         + bias_copy.astype(jnp.float32)
     ).astype(jnp.bfloat16)
-    top_count = top_ids.shape[1]
-    pick_total = top_count + aux_ids.shape[1]
-    code_row = jnp.where(jnp.arange(pick_total) < top_count, 1.0, 2.0).astype(jnp.float32)
     zero_bf = jnp.zeros((), jnp.bfloat16)
-    token_scores = lax.all_to_all(pre_acts, "wide", split_axis=0, concat_axis=1, tiled=True)
-    all_latents = token_scores.shape[1]
-    codes = kind_codes(jnp.concatenate([top_ids, aux_ids], 1), code_row, 0, all_latents)
-    top_here = codes == 1.0
-    aux_here = (codes == 2.0) & (dead_set[None, :] == 1)
-    picked = jnp.where(top_here | aux_here, token_scores, zero_bf)
-    kind_value = jnp.where(top_here, 1.0, jnp.where(aux_here, 2.0, 0.0)).astype(jnp.bfloat16)
-    planes = jnp.stack([picked, kind_value])
-    returned = lax.all_to_all(planes, "wide", split_axis=2, concat_axis=1, tiled=True)
-    top_mask = returned[1] == 1.0
-    aux_mask = returned[1] == 2.0
-    chosen_values = returned[0]
-    top_acts = jnp.where(top_mask, chosen_values, zero_bf)
-    aux_acts = jnp.where(aux_mask, chosen_values, zero_bf)
-    top_part = top_acts
-    aux_part = aux_acts
+    top_acts = jnp.where(top_mask, pre_acts, zero_bf)
+    aux_acts = jnp.where(aux_mask, pre_acts, zero_bf)
     rebuilt_both = lax.psum_scatter(
         jnp.concatenate(
             [
-                jnp.dot(top_part, dec_cols, preferred_element_type=jnp.float32),
-                jnp.dot(aux_part, dec_cols, preferred_element_type=jnp.float32),
+                jnp.dot(top_acts, dec_full, preferred_element_type=jnp.float32),
+                jnp.dot(aux_acts, dec_full, preferred_element_type=jnp.float32),
             ],
             1,
         ),
-        "wide",
+        "narrow",
         scatter_dimension=0,
         tiled=True,
     )
@@ -231,40 +236,82 @@
     back_rows = jnp.concatenate([back_recon, back_aux], 1).astype(jnp.bfloat16)
     to_latents = (((1,), (1,)), ((), ()))
     over_rows = (((0,), (0,)), ((), ()))
-    shard_rows = lax.all_gather(back_rows, "wide", axis=0, tiled=True)
-    top_part = top_acts
-    aux_part = aux_acts
+    shard_rows = lax.all_gather(back_rows, "narrow", axis=0, tiled=True)
     recon_part = shard_rows[:, :model_width]
     aux_back = shard_rows[:, model_width:]
-    back_top = lax.dot_general(recon_part, dec_cols, to_latents, preferred_element_type=jnp.float32)
-    back_side = lax.dot_general(aux_back, dec_cols, to_latents, preferred_element_type=jnp.float32)
+    grad_dec = lax.dot_general(top_acts, recon_part, over_rows, preferred_element_type=jnp.float32)
+    grad_dec = grad_dec + lax.dot_general(
+        aux_acts, aux_back, over_rows, preferred_element_type=jnp.float32
+    )
+    dec_grad = lax.psum_scatter(
+        grad_dec.astype(jnp.bfloat16), "wide", scatter_dimension=0, tiled=True
+    )
+    back_top = lax.dot_general(recon_part, dec_full, to_latents, preferred_element_type=jnp.float32)
+    back_side = lax.dot_general(aux_back, dec_full, to_latents, preferred_element_type=jnp.float32)
     latent_grad = jnp.where(top_mask, back_top, jnp.where(aux_mask, back_side, 0.0)).astype(
         jnp.bfloat16
     )
-    grad_dec = lax.dot_general(top_part, recon_part, over_rows, preferred_element_type=jnp.float32)
-    grad_dec = grad_dec + lax.dot_general(
-        aux_part, aux_back, over_rows, preferred_element_type=jnp.float32
-    )
     grad_enc = lax.dot_general(
         encoder_in, latent_grad, over_rows, preferred_element_type=jnp.float32
     )
+    enc_grad = lax.psum_scatter(
+        grad_enc.astype(jnp.bfloat16), "wide", scatter_dimension=1, tiled=True
+    )
     column_sum = jnp.sum(latent_grad, 0, dtype=jnp.float32)
-    grad_enc, grad_dec, column_sum = (grad_enc, grad_dec, column_sum)
+    encb_grad = lax.psum_scatter(column_sum, "wide", scatter_dimension=0, tiled=True)
     bias_term = jnp.sum(back_rows[:, :model_width], 0, dtype=jnp.float32) - jnp.dot(
-        enc_rows.astype(jnp.float32), column_sum, precision=HIGH_PRECISION
-    )
-    grad_decb = lax.psum(bias_term, ("wide", "narrow"))
-    enc_grad, dec_grad, encb_grad = (
-        lax.psum_scatter(grad_enc, "narrow", scatter_dimension=0, tiled=True),
-        lax.psum_scatter(grad_dec, "narrow", scatter_dimension=1, tiled=True),
-        lax.psum_scatter(column_sum, "narrow", scatter_dimension=0, tiled=True),
-    )
-    enc_next = MOMENTUM * enc_moment + enc_grad
-    dec_next = MOMENTUM * dec_moment + dec_grad
-    ortho_dirs = newton_schulz(jnp.stack([enc_next, dec_next.T]))
+        enc_own.astype(jnp.float32), encb_grad, precision=HIGH_PRECISION
+    )
+    grad_decb = lax.psum(bias_term, both)
+
+    def latents_to_rows(value):
+        return lax.all_to_all(
+            value.astype(jnp.bfloat16), "narrow", split_axis=0, concat_axis=1, tiled=True
+        ).astype(jnp.float32)
+
+    def latents_to_cols(value):
+        return lax.all_to_all(
+            value.astype(jnp.bfloat16), "narrow", split_axis=1, concat_axis=0, tiled=True
+        ).astype(jnp.float32)
+
+    enc_next = MOMENTUM * enc_moment + latents_to_rows(enc_grad)
+    dec_next = MOMENTUM * dec_moment + latents_to_cols(dec_grad)
+    enc_own_next = MOMENTUM * rows_to_latents(enc_moment.astype(jnp.bfloat16)).astype(
+        jnp.float32
+    ) + enc_grad.astype(jnp.float32)
+    dec_own_next = MOMENTUM * cols_to_latents(dec_moment.astype(jnp.bfloat16)).astype(
+        jnp.float32
+    ) + dec_grad.astype(jnp.float32)
+    split_next = enc_own_next.astype(jnp.bfloat16), dec_own_next.astype(jnp.bfloat16)
+    enc_gram = lax.psum(
+        lax.dot_general(
+            split_next[0], split_next[0], to_latents, preferred_element_type=jnp.float32
+        ),
+        both,
+    )
+    dec_gram = lax.psum(
+        lax.dot_general(
+            split_next[1], split_next[1], over_rows, preferred_element_type=jnp.float32
+        ),
+        both,
+    )
+    enc_ortho = latents_to_rows(
+        jnp.dot(
+            gram_series(enc_gram).astype(jnp.bfloat16),
+            split_next[0],
+            preferred_element_type=jnp.float32,
+        )
+    )
+    dec_ortho = latents_to_cols(
+        jnp.dot(
+            split_next[1],
+            gram_series(dec_gram).astype(jnp.bfloat16),
+            preferred_element_type=jnp.float32,
+        )
+    )
     step_scale = MUON_RATE * 0.2 * math.sqrt(max(D, L))
-    enc_new = enc_weight * (1.0 - MUON_RATE * DECAY) - step_scale * ortho_dirs[0]
-    dec_new = dec_weight * (1.0 - MUON_RATE * DECAY) - step_scale * ortho_dirs[1].T
+    enc_new = enc_weight * (1.0 - MUON_RATE * DECAY) - step_scale * enc_ortho
+    dec_new = dec_weight * (1.0 - MUON_RATE * DECAY) - step_scale * dec_ortho
     encb_new, encb_one, encb_two = adam_update(enc_bias, encb_grad, encb_first, encb_second)
     decb_new, decb_one, decb_two = adam_update(decoder_bias, grad_decb, decb_first, decb_second)
     return (

time: 4450 us -> 1350 us (0.30)
  waiting for transfers between devices: 3580 us -> 554 us
  local copies, waits for them, and re-layouts: 175 us -> 82.2 us
    all_gather x14 -> x4, waiting for transfers between devices: 2560 us -> 30.8 us  [the longest x1 30.8 us: local(): shard_rows = lax.all_gather(back_rows, 'narrow', axis=0, tiled=True)]
    reduce_scatter x4 -> x3, waiting for transfers between devices: 492 us -> 205 us  [the longest x1 91.3 us: local(): lax.psum_scatter(grad_dec.astype(jnp.bfloat16), 'wide', scatter_dimension...]
    psum x5 -> x1, waiting for transfers between devices: 266 us -> 141 us  [local(): lax.psum(lax.dot_general(split_next[0], split_next[0], to_latents, prefer...]
    all_to_all x2 -> x9, waiting for transfers between devices: 265 us -> 177 us  [the longest x2 84.8 us: rows_to_latents(): lax.all_to_all(value, 'narrow', split_axis=1, concat_axis=0, tiled=True)]
    dot_general x23 -> x46, matrix products: 397 us -> 352 us  [the longest x10 61.2 us: gram_series(): square = jnp.dot(gram, gram, precision=HIGH_PRECISION)]
  transfers between devices with their start and end apart: 25 -> 17, of which waited for: 23 -> 11; matrix products, arithmetic and copies ran while one was open for 5% -> 27% of each run, Pallas kernels for 0% -> 0%
where the time goes in v1:
time: 1350 us; the launch traced here: 1340 us
  waiting for transfers between devices  554 us (41%)
  matrix products  441 us (33%)
  other arithmetic  100 us (7%)
  blocking collectives  98.3 us (7%)
  local copies, waits for them, and re-layouts  82.2 us (6%)
  starting transfers between devices  42.8 us (3%)
  between operations  18.1 us (1%)
    psum x1, waiting for transfers between devices, local(): lax.psum(lax.dot_general(split_next[0], split_next[0], to_latents, prefer...  141 us
    reduce_scatter x1, waiting for transfers between devices, local(): lax.psum_scatter(grad_dec.astype(jnp.bfloat16), 'wide', scatter_dimension...  91.3 us
    all_to_all x2, waiting for transfers between devices, rows_to_latents(): lax.all_to_all(value, 'narrow', split_axis=1, concat_axis=0, tiled=True)  84.8 us
    dot_general x4, matrix products, one_block(): jnp.einsum('rhk,rkl->rhl', high_hot, low_hot, preferred_element_type=jnp....  63.4 us
    dot_general x10, matrix products, gram_series(): square = jnp.dot(gram, gram, precision=HIGH_PRECISION)  61.2 us
    reduce_scatter x1, waiting for transfers between devices, local(): lax.psum_scatter(jnp.concatenate([jnp.dot(top_acts, dec_full, preferred_e...  60.5 us
    dot_general x8, matrix products, gram_series(): jnp.dot(poly, product, precision=HIGH_PRECISION)  53 us
    reduce_scatter x1, waiting for transfers between devices, local(): lax.psum_scatter(grad_enc.astype(jnp.bfloat16), 'wide', scatter_dimension...  52.7 us
  transfers between devices with their start and end apart: 17, of which 11 were waited for; matrix products, arithmetic and copies ran while one was open for 27% of the time, Pallas kernels for 0%

profile of v1, /device:TPU:0, one launch (start us, length us, event | category | flops | bytes accessed | tf_op | source)
XLA Modules:
  0.0 1336.1 jit_solution(16690958650311301152)
XLA Ops:
  19.8 55.5 %all-to-all-done.1 = bf16[192,4,1024]{2,0,1:T(8,128)(2,1)} async-done(((bf16[192,4,1024]{2,0,1:T(8,128)(2,1)}), bf16[192,4,1024]{2,0,1:T(8,128)(2,1)}, u32[]{:S(2)}, u32[]{:S(2)}) %all-to-all-start.1) | async-done | bytes 1572896 | tf_op jit(solution)/shard_map/all_to_all | solution.py:160
  75.4 8.7 all-gather
  84.1 11.4 gather_fusion
  105.7 21.3 %all-to-all-done = bf16[8,128,768]{2,1,0:T(8,128)(2,1)} async-done(((bf16[8,128,768]{2,1,0:T(8,128)(2,1)}), bf16[8,128,768]{2,1,0:T(8,128)(2,1)}, u32[]{:S(2)}, u32[]{:S(2)}) %all-to-all-start) | async-done | bytes 1572896 | tf_op jit(solution)/shard_map/all_to_all | solution.py:178
  138.0 7.9 all_gather.25
  153.9 11.2 all-to-all-done.2
  179.8 18.8 %all_gather.23 = bf16[512,768]{1,0:T(8,128)(2,1)} all-gather(bf16[128,768]{1,0:T(8,128)(2,1)S(1)} %fusion.194), channel_id=1, replica_groups=mesh['wide'=8,'narrow'=4] {'narrow'}, dimensions={0}, use_global_device_ids=true | all-gather | bytes 983040 | tf_op jit(solution)/shard_map/all_gather | solution.py:203
  203.7 132.7 %while.11 = (s32[]{:T(128)}, f32[4,128,8192]{2,1,0:T(8,128)}, s32[4,128,544]{2,1,0:T(8,128)S(1)}, s32[4,128,544]{2,1,0:T(8,128)S(1)}, s32[]{:T(128)}) while((s32[]{:T(128)}, f32[4,128,8192]{2,1,0:T(8,128)}, s32[4,128,544]{2,1,0:T(8,128)S(1)}, s32[4,128,544]{2,1,0:T(8,128)S(1)}, s32[]{:T(128)}) %tuple.73), condition=%wide.region_8.9_spmd.clone, body=%wide.region_7.8_spmd.clone.sunk | while | flops 1158677632 | bytes 40470732 | solution.py:98
  211.5 15.9 %fusion.402 = f32[128,64,128]{2,1,0:T(8,128)} fusion(s32[128,544]{1,0:T(8,128)S(1)} %get-tuple-element.142, bf16[128,64,544]{2,1,0:T(8,128)(2,1)} %select_convert_fusion.8), kind=kOutput, calls=%fused_computation.5.clone.3 | convolution fusion | flops 1149763584 | bytes 13385728 | tf_op jit(solution)/shard_map/while/body/eval_jaxpr/rhk,rkl->rhl/dot_general | solution.py:91
  244.7 15.9 %fusion.402 = f32[128,64,128]{2,1,0:T(8,128)} fusion(s32[128,544]{1,0:T(8,128)S(1)} %get-tuple-element.142, bf16[128,64,544]{2,1,0:T(8,128)(2,1)} %select_convert_fusion.8), kind=kOutput, calls=%fused_computation.5.clone.3 | convolution fusion | flops 1149763584 | bytes 13385728 | tf_op jit(solution)/shard_map/while/body/eval_jaxpr/rhk,rkl->rhl/dot_general | solution.py:91
  277.9 15.9 %fusion.402 = f32[128,64,128]{2,1,0:T(8,128)} fusion(s32[128,544]{1,0:T(8,128)S(1)} %get-tuple-element.142, bf16[128,64,544]{2,1,0:T(8,128)(2,1)} %select_convert_fusion.8), kind=kOutput, calls=%fused_computation.5.clone.3 | convolution fusion | flops 1149763584 | bytes 13385728 | tf_op jit(solution)/shard_map/while/body/eval_jaxpr/rhk,rkl->rhl/dot_general | solution.py:91
  311.1 15.9 %fusion.402 = f32[128,64,128]{2,1,0:T(8,128)} fusion(s32[128,544]{1,0:T(8,128)S(1)} %get-tuple-element.142, bf16[128,64,544]{2,1,0:T(8,128)(2,1)} %select_convert_fusion.8), kind=kOutput, calls=%fused_computation.5.clone.3 | convolution fusion | flops 1149763584 | bytes 13385728 | tf_op jit(solution)/shard_map/while/body/eval_jaxpr/rhk,rkl->rhl/dot_general | solution.py:91
  336.4 10.7 broadcast_compare_fusion.1
  347.1 18.4 %bitcast_select_fusion = (bf16[512,8192]{1,0:T(8,128)(2,1)}, bf16[512,8192]{1,0:T(8,128)(2,1)}) fusion(pred[4,128,8192]{2,1,0:T(32,128)(4,1)} %get-tuple-element.94, pred[8192]{0:T(1024)(128)(4,1)S(1)} %bitcast.202, pred[4,128,8192]{2,1,0:T(32,128)(4,1)} %get-tuple-element.95, f32[8192]{0:T(1024)S(1)} %copy-done.31, ...), kind=kOutput, calls=%fused_computation.24 | convolution fusion | flops 6464602112 | bytes 38579200 | tf_op jit(solution)/shard_map/dot_general | solution.py:206
  365.5 12.5 fusion.319
  378.0 11.9 fusion.318
  392.2 60.5 %reduce-scatter.4.cloned.1.call-done = f32[128,1536]{1,0:T(8,128)} async-done(((f32[512,1536]{1,0:T(8,128)}), f32[128,1536]{1,0:T(8,128)}) %reduce-scatter.4.cloned.1.call-update) | async-done | bytes 786448 | tf_op jit(solution)/shard_map/reduce_scatter | solution.py:212
  461.9 30.8 %all-gather.12.cloned.1.call-done = bf16[512,1536]{1,0:T(8,128)(2,1)} async-done(((bf16[128,1536]{1,0:T(8,128)(2,1)}), bf16[512,1536]{1,0:T(8,128)(2,1)}) %all-gather.12.cloned.1.call-update) | async-done | bytes 1572880 | tf_op jit(solution)/shard_map/all_gather | solution.py:239
  492.7 13.9 %fusion.200 = bf16[512,8192]{1,0:T(8,128)(2,1)} fusion(bf16[8192,768]{0,1:T(8,128)(2,1)} %all-gather.10.cloned.1.call-done, bf16[512,1536]{1,0:T(8,128)(2,1)} %all-gather.12.cloned.1.call-done), kind=kOutput, calls=%fused_computation.250 | convolution fusion | flops 6442450944 | bytes 21757952 | tf_op jit(solution)/shard_map/dot_general | solution.py:249
  506.6 22.6 %convert_reduce_fusion = (f32[8192]{0:T(1024)}, bf16[512,8192]{1,0:T(8,128)(2,1)}) fusion(bf16[512,8192]{1,0:T(8,128)(2,1)} %fusion.200, pred[512,8192]{1,0:T(32,128)(4,1)} %bitcast_and_fusion, bf16[8192,768]{0,1:T(8,128)(2,1)} %all-gather.10.cloned.1.call-done, bf16[512,1536]{1,0:T(8,128)(2,1)S(1)} %copy-done.53, pred[4,128,8192]{2,1,0:T(32,128)(4,1)} %get-tuple-element.94), kind=kOutput, calls=%fused_computation.20 | convolution fusion | flops 6459219968 | bytes 38567936 | tf_op jit(solution)/shard_map/dot_general | solution.py:250
  529.2 13.1 convolution_convert_fusion
  542.3 19.3 %fusion.198 = f32[8192,768]{1,0:T(8,128)} fusion(bf16[512,8192]{1,0:T(8,128)(2,1)} %get-tuple-element.96, bf16[512,1536]{1,0:T(8,128)(2,1)S(1)} %copy-done.53), kind=kOutput, calls=%fused_computation.248 | convolution fusion | flops 6442450944 | bytes 34340864 | tf_op jit(solution)/shard_map/dot_general | solution.py:242
  561.6 19.4 %add_convert_fusion = bf16[8192,768]{1,0:T(8,128)(2,1)} fusion(f32[8192,768]{1,0:T(8,128)} %fusion.198, bf16[512,8192]{1,0:T(8,128)(2,1)} %get-tuple-element.97, bf16[512,1536]{1,0:T(8,128)(2,1)S(1)} %copy-done.53), kind=kOutput, calls=%fused_computation.19 | convolution fusion | flops 6455033856 | bytes 46923776 | tf_op jit(solution)/shard_map/dot_general | solution.py:243
  581.1 52.7 %reduce-scatter.6.cloned.1.call-done = bf16[768,1024]{1,0:T(8,128)(2,1)} async-done(((bf16[768,8192]{1,0:T(8,128)(2,1)}), bf16[768,1024]{1,0:T(8,128)(2,1)}) %reduce-scatter.6.cloned.1.call-update) | async-done | bytes 1572880 | tf_op jit(solution)/shard_map/reduce_scatter | solution.py:257
  638.3 91.3 %reduce-scatter.8.cloned.1.call-done = bf16[1024,768]{1,0:T(8,128)(2,1)} async-done(((bf16[8192,768]{1,0:T(8,128)(2,1)}), bf16[1024,768]{1,0:T(8,128)(2,1)}) %reduce-scatter.8.cloned.1.call-update) | async-done | bytes 1572880 | tf_op jit(solution)/shard_map/reduce_scatter | solution.py:246
  745.2 29.8 %all-to-all-done.8 = bf16[1024,4,192]{0,2,1:T(8,128)(2,1)} async-done(((bf16[1024,4,192]{0,2,1:T(8,128)(2,1)}), bf16[1024,4,192]{0,2,1:T(8,128)(2,1)}, u32[]{:S(2)}, u32[]{:S(2)}) %all-to-all-start.8) | async-done | bytes 1572896 | tf_op jit(solution)/shard_map/all_to_all | solution.py:273
  786.6 29.3 %all-to-all-done.3 = bf16[192,4,1024]{2,0,1:T(8,128)(2,1)} async-done(((bf16[192,4,1024]{2,0,1:T(8,128)(2,1)}), bf16[192,4,1024]{2,0,1:T(8,128)(2,1)}, u32[]{:S(2)}, u32[]{:S(2)}) %all-to-all-start.3) | async-done | bytes 1572896 | tf_op jit(solution)/shard_map/all_to_all | solution.py:160
  826.9 29.9 %all-to-all-done.6 = bf16[4,1024,192]{1,2,0:T(8,128)(2,1)} async-done(((bf16[4,1024,192]{1,2,0:T(8,128)(2,1)}), bf16[4,1024,192]{1,2,0:T(8,128)(2,1)}, u32[]{:S(2)}, u32[]{:S(2)}) %all-to-all-start.6) | async-done | bytes 1572896 | tf_op jit(solution)/shard_map/all_to_all | solution.py:163
  869.9 141.2 %all-reduce.4.cloned.1.call-done = (f32[768,768]{1,0:T(8,128)}, f32[768,768]{1,0:T(8,128)}) async-done(((f32[768,768]{1,0:T(8,128)}, f32[768,768]{1,0:T(8,128)}), (f32[768,768]{1,0:T(8,128)}, f32[768,768]{1,0:T(8,128)})) %all-reduce.4.cloned.1.call-update) | async-done | bytes 4718608 | tf_op jit(solution)/shard_map/psum | solution.py:286
  1170.1 8.5 fusion.61
  1248.9 22.9 %all-reduce = f32[8192]{0:T(1024)S(1)} all-reduce(f32[8192]{0:T(1024)S(1)} %copy-done.32), channel_id=5, replica_groups=mesh['wide'=8,'narrow'=4] {'wide'}, use_global_device_ids=true, to_apply=%region_19.20.clone | all-reduce | flops 8192 | bytes 65536
  1275.2 39.9 %psum.23 = f32[768]{0:T(1024)S(1)} all-reduce(f32[768]{0:T(1024)S(1)} %sub.95), channel_id=1, replica_groups=mesh['wide'=8,'narrow'=4] {'wide','narrow'}, use_global_device_ids=true, to_apply=%region_21.22 | all-reduce | flops 768 | bytes 6144 | tf_op jit(solution)/shard_map/psum | solution.py:265
  (269 shorter events, 441.0 us)
Async XLA Ops:
  7.2 158.7 %copy-start = (bf16[768,2304]{1,0:T(8,128)(2,1)S(1)}, bf16[768,2304]{1,0:T(8,128)(2,1)}, u32[]{:S(2)}) copy-start(bf16[768,2304]{1,0:T(8,128)(2,1)} %param.34) | copy-start | bytes 10616836
  10.7 64.6 %all-to-all-start.1 = ((bf16[192,4,1024]{2,0,1:T(8,128)(2,1)}), bf16[192,4,1024]{2,0,1:T(8,128)(2,1)}, u32[]{:S(2)}, u32[]{:S(2)}) async-start(bf16[192,4,1024]{2,0,1:T(8,128)(2,1)} %bitcast.186), calls=%async_computation.1 | async-start | bytes 3145728 | tf_op jit(solution)/shard_map/all_to_all | solution.py:160
  17.2 181.5 %all-gather.6.cloned.1.call-start = ((), (), s32[]{:S(2)}) async-start(), calls=%async_computation.12 | async-start | bytes 1638400 | tf_op jit(solution)/shard_map/all_gather | solution.py:188
  17.9 57.5 %copy-start.52 = (s32[128]{0:T(128)S(1)}, s32[128]{0:T(128)}, u32[]{:S(2)}) copy-start(s32[128]{0:T(128)} %param.25) | copy-start | bytes 1540
  19.8 327.3 %all-gather.8.cloned.1.call-start = ((), (), s32[]{:S(2)}) async-start(), calls=%async_computation.13 | async-start | bytes 14155776 | tf_op jit(solution)/shard_map/all_gather | solution.py:167
  98.1 29.0 %all-to-all-start = ((bf16[8,128,768]{2,1,0:T(8,128)(2,1)}), bf16[8,128,768]{2,1,0:T(8,128)(2,1)}, u32[]{:S(2)}, u32[]{:S(2)}) async-start(bf16[8,128,768]{2,1,0:T(8,128)(2,1)} %select_select_fusion), calls=%async_computation | async-start | bytes 3145728 | tf_op jit(solution)/shard_map/all_to_all | solution.py:178
  105.7 32.3 %copy-start.37 = (f32[1024]{0:T(1024)S(1)}, f32[1024]{0:T(1024)}, u32[]{:S(2)}) copy-start(f32[1024]{0:T(1024)} %param.39) | copy-start | bytes 12292
  105.7 40.8 %copy-start.41 = (f32[2,768]{1,0:T(2,128)S(1)}, f32[2,768]{1,0:T(2,128)}, u32[]{:S(2)}) copy-start(f32[2,768]{1,0:T(2,128)} %param.32) | copy-start | bytes 18436
  127.0 38.1 %all-to-all-start.2 = ((bf16[4,1024,192]{1,2,0:T(8,128)(2,1)}), bf16[4,1024,192]{1,2,0:T(8,128)(2,1)}, u32[]{:S(2)}, u32[]{:S(2)}) async-start(bf16[4,1024,192]{1,2,0:T(8,128)(2,1)} %bitcast.185), calls=%async_computation.2 | async-start | bytes 3145728 | tf_op jit(solution)/shard_map/all_to_all | solution.py:163
  131.4 234.1 %all-gather.10.cloned.1.call-start = ((), (), s32[]{:S(2)}) async-start(), calls=%async_computation.14 | async-start | bytes 14155776 | tf_op jit(solution)/shard_map/all_gather | solution.py:168
  165.1 287.6 %reduce-scatter.4.cloned.1.call-start = ((), (), s32[]{:S(2)}) async-start(), calls=%async_computation.15 | async-start | bytes 3932160 | tf_op jit(solution)/shard_map/reduce_scatter | solution.py:212
  179.8 23.1 %copy-start.28 = (bf16[128,768]{1,0:T(8,128)(2,1)}, bf16[128,768]{1,0:T(8,128)(2,1)S(1)}, u32[]{:S(2)}) copy-start(bf16[128,768]{1,0:T(8,128)(2,1)S(1)} %fusion.194) | copy-start | bytes 589828
  392.1 60.6 %copy-start.29 = (bf16[128,768]{1,0:T(8,128)(2,1)S(1)}, bf16[128,768]{1,0:T(8,128)(2,1)}, u32[]{:S(2)}) copy-start(bf16[128,768]{1,0:T(8,128)(2,1)} %copy-done.28) | copy-start | bytes 589828
  392.1 100.6 %all-gather.12.cloned.1.call-start = ((), (), s32[]{:S(2)}) async-start(), calls=%async_computation.16 | async-start | bytes 1966080 | tf_op jit(solution)/shard_map/all_gather | solution.py:239
  455.4 178.3 %reduce-scatter.6.cloned.1.call-start = ((), (), s32[]{:S(2)}) async-start(), calls=%async_computation.17 | async-start | bytes 14155776 | tf_op jit(solution)/shard_map/reduce_scatter | solution.py:257
  492.7 13.9 %copy-start.53 = (bf16[512,1536]{1,0:T(8,128)(2,1)S(1)}, bf16[512,1536]{1,0:T(8,128)(2,1)}, u32[]{:S(2)}) copy-start(bf16[512,1536]{1,0:T(8,128)(2,1)} %all-gather.12.cloned.1.call-done) | copy-start | bytes 4718596
  506.6 22.6 %copy-start.27 = (bf16[512,768]{1,0:T(8,128)(2,1)S(1)}, bf16[512,768]{1,0:T(8,128)(2,1)}, u32[]{:S(2)}) copy-start(bf16[512,768]{1,0:T(8,128)(2,1)} %all_gather.23) | copy-start | bytes 2359300
  542.3 187.4 %reduce-scatter.8.cloned.1.call-start = ((), (), s32[]{:S(2)}) async-start(), calls=%async_computation.18 | async-start | bytes 14155776 | tf_op jit(solution)/shard_map/reduce_scatter | solution.py:246
  633.7 98.5 %all-to-all-start.5 = ((bf16[4,192,1024]{2,1,0:T(8,128)(2,1)}), bf16[4,192,1024]{2,1,0:T(8,128)(2,1)S(1)}, u32[]{:S(2)}, u32[]{:S(2)}) async-start(bf16[4,192,1024]{2,1,0:T(8,128)(2,1)} %bitcast.187), calls=%async_computation.7 | async-start | bytes 3145728 | tf_op jit(solution)/shard_map/all_to_all | solution.py:268
  733.4 41.7 %all-to-all-start.8 = ((bf16[1024,4,192]{0,2,1:T(8,128)(2,1)}), bf16[1024,4,192]{0,2,1:T(8,128)(2,1)}, u32[]{:S(2)}, u32[]{:S(2)}) async-start(bf16[1024,4,192]{0,2,1:T(8,128)(2,1)} %bitcast.31), calls=%async_computation.11 | async-start | bytes 3145728 | tf_op jit(solution)/shard_map/all_to_all | solution.py:273
  775.0 40.9 %all-to-all-start.3 = ((bf16[192,4,1024]{2,0,1:T(8,128)(2,1)}), bf16[192,4,1024]{2,0,1:T(8,128)(2,1)}, u32[]{:S(2)}, u32[]{:S(2)}) async-start(bf16[192,4,1024]{2,0,1:T(8,128)(2,1)} %bitcast.167), calls=%async_computation.4 | async-start | bytes 3145728 | tf_op jit(solution)/shard_map/all_to_all | solution.py:160
  815.9 40.9 %all-to-all-start.6 = ((bf16[4,1024,192]{1,2,0:T(8,128)(2,1)}), bf16[4,1024,192]{1,2,0:T(8,128)(2,1)}, u32[]{:S(2)}, u32[]{:S(2)}) async-start(bf16[4,1024,192]{1,2,0:T(8,128)(2,1)} %bitcast.166), calls=%async_computation.8 | async-start | bytes 3145728 | tf_op jit(solution)/shard_map/all_to_all | solution.py:163
  820.3 190.9 %all-reduce.4.cloned.1.call-start = ((), (), s32[]{:S(2)}) async-start(), calls=%async_computation.19 | async-start | bytes 9437184 | tf_op jit(solution)/shard_map/psum | solution.py:286
  1165.7 77.4 %all-to-all-start.4 = ((bf16[4,192,1024]{2,1,0:T(8,128)(2,1)}), bf16[4,192,1024]{2,1,0:T(8,128)(2,1)}, u32[]{:S(2)}, u32[]{:S(2)}) async-start(bf16[4,192,1024]{2,1,0:T(8,128)(2,1)} %bitcast.197), calls=%async_computation.6 | async-start | bytes 3145728 | tf_op jit(solution)/shard_map/all_to_all | solution.py:268
  1243.1 28.7 %copy-start.38 = (f32[1024]{0:T(1024)S(1)}, f32[1024]{0:T(1024)}, u32[]{:S(2)}) copy-start(f32[1024]{0:T(1024)} %param.39) | copy-start | bytes 12292
  1243.1 28.7 %copy-start.45 = (f32[1024]{0:T(1024)S(1)}, f32[1024]{0:T(1024)}, u32[]{:S(2)}) copy-start(f32[1024]{0:T(1024)} %param.44) | copy-start | bytes 12292
  1243.1 28.7 %copy-start.46 = (f32[1024]{0:T(1024)S(1)}, f32[1024]{0:T(1024)}, u32[]{:S(2)}) copy-start(f32[1024]{0:T(1024)} %param.45) | copy-start | bytes 12292
  1243.1 32.1 %copy-start.35 = (f32[768]{0:T(1024)S(1)}, f32[768]{0:T(1024)}, u32[]{:S(2)}) copy-start(f32[768]{0:T(1024)} %get-tuple-element.80) | copy-start | bytes 9220
  1243.1 71.9 %copy-start.34 = (f32[768]{0:T(1024)S(1)}, f32[768]{0:T(1024)}, u32[]{:S(2)}) copy-start(f32[768]{0:T(1024)} %param.41) | copy-start | bytes 9220
  1243.1 71.9 %copy-start.42 = (f32[768]{0:T(1024)S(1)}, f32[768]{0:T(1024)}, u32[]{:S(2)}) copy-start(f32[768]{0:T(1024)} %param.46) | copy-start | bytes 9220
  1243.2 71.9 %copy-start.43 = (f32[768]{0:T(1024)S(1)}, f32[768]{0:T(1024)}, u32[]{:S(2)}) copy-start(f32[768]{0:T(1024)} %param.47) | copy-start | bytes 9220
  1243.2 79.0 %all-to-all-start.7 = ((bf16[1024,4,192]{0,2,1:T(8,128)(2,1)}), bf16[1024,4,192]{0,2,1:T(8,128)(2,1)}, u32[]{:S(2)}, u32[]{:S(2)}) async-start(bf16[1024,4,192]{0,2,1:T(8,128)(2,1)} %bitcast.196), calls=%async_computation.10 | async-start | bytes 3145728 | tf_op jit(solution)/shard_map/all_to_all | solution.py:273
  (40 other events, 191.1 us)
Sparse Core Ops, SparseCore 0:
  20.1 53.3 all-gather.5
  75.5 83.6 all-gather.7
  165.2 72.5 all-gather.9
  392.2 60.4 reduce-scatter.3
  455.6 37.1 all-gather.11
  542.4 91.2 reduce-scatter.5
  637.2 92.3 reduce-scatter.7
  868.2 142.9 all-reduce.3

commit v2 on v1

v2 whole, which is shorter than its diff:
```python
import math

import jax
import jax.numpy as jnp
from jax import lax
from jax.experimental import pallas as pl
from jax.experimental.pallas import tpu as pltpu
from jax.sharding import Mesh
from jax.sharding import PartitionSpec as P

D = 768
HEAD_DIM = 64
L = 32768
NS_STEPS = 5
STEP = 10


HIGH_PRECISION = lax.Precision.HIGHEST
AUX_COEF = 1.0 / 32.0
EPS_NORM = 1e-05
NS_EPS = 1e-07
QA = 3.4445
QB = -4.775
QC = 2.0315
MOMENTUM = 0.95
MUON_RATE = 0.1
DECAY = 0.1
BIAS_RATE = 0.3
BETA_ONE = 0.9
BETA_TWO = 0.999
ADAM_EPS = 1e-08


def layer_norm(value, gain, shift):
    row_mean = jnp.mean(value, -1, keepdims=True)
    centred = value - row_mean
    row_var = jnp.mean(centred * centred, -1, keepdims=True)
    return centred * lax.rsqrt(row_var + EPS_NORM) * gain + shift


def frozen_block(start, ctx_length, ln_gains, frozen_bias, w_qkv, w_proj, w_fc, w_out):
    row_count, model_width = start.shape
    head_count = model_width // HEAD_DIM
    ff_width = w_fc.shape[1]
    shifts = frozen_bias[: 2 * model_width].reshape(2, model_width)
    b_qkv = frozen_bias[2 * model_width : 5 * model_width]
    b_proj = frozen_bias[5 * model_width : 6 * model_width]
    b_fc = frozen_bias[6 * model_width : 6 * model_width + ff_width]
    b_out = frozen_bias[6 * model_width + ff_width :]
    normed = layer_norm(start, ln_gains[0], shifts[0]).astype(jnp.bfloat16)
    qkv_rows = (jnp.dot(normed, w_qkv, preferred_element_type=jnp.float32) + b_qkv).astype(
        jnp.bfloat16
    )
    head_split = qkv_rows.reshape(row_count, 3, head_count, HEAD_DIM)
    scores = jnp.einsum(
        "qhd,khd->hqk", head_split[:, 0], head_split[:, 1], preferred_element_type=jnp.float32
    ) * HEAD_DIM ** (-0.5)
    positions = jnp.arange(row_count)
    allowed = (positions[None, :] <= positions[:, None]) & (positions[None, :] < ctx_length)
    attn_probs = jax.nn.softmax(jnp.where(allowed[None], scores, -1e30), axis=-1).astype(
        jnp.bfloat16
    )
    mixed = jnp.einsum(
        "hqk,khd->qhd", attn_probs, head_split[:, 2], preferred_element_type=jnp.float32
    )
    mixed = mixed.reshape(row_count, model_width).astype(jnp.bfloat16)
    hidden = start + jnp.dot(mixed, w_proj, preferred_element_type=jnp.float32) + b_proj
    normed_two = layer_norm(hidden, ln_gains[1], shifts[1]).astype(jnp.bfloat16)
    inner_acts = jax.nn.gelu(
        jnp.dot(normed_two, w_fc, preferred_element_type=jnp.float32) + b_fc, approximate=True
    ).astype(jnp.bfloat16)
    return (hidden + jnp.dot(inner_acts, w_out, preferred_element_type=jnp.float32) + b_out).astype(
        jnp.bfloat16
    )


def split_bf(value):
    high = value.astype(jnp.bfloat16)
    return high, (value - high.astype(jnp.float32)).astype(jnp.bfloat16)


def series_kernel(
    place_ref, near_ref, far_ref, out_ref, gram, g_hi, g_lo, p_hi, p_lo, r_hi, r_lo, q_hi
):
    size = gram.shape[0]
    block = 256
    f32 = jnp.float32
    place = place_ref[0]
    chips, rows_each = near_ref.shape[:2]
    for chip in range(chips):
        for core, source in enumerate((near_ref, far_ref)):
            first = jnp.bitwise_xor(place, 2 * chip + core) * rows_each
            gram[pl.ds(pl.multiple_of(first, 8), rows_each), :] = source[chip].astype(f32)

    def dot(a, b):
        return jnp.dot(a, b, preferred_element_type=f32)

    def eye_rows(start):
        rows = lax.broadcasted_iota(jnp.int32, (block, size), 0) + start
        cols = lax.broadcasted_iota(jnp.int32, (block, size), 1)
        return (rows == cols).astype(f32)

    def row_blocks(body):
        def step(index, carry):
            body(pl.multiple_of(index * block, block))
            return carry

        lax.fori_loop(0, size // block, step, 0)

    def trace_part(index, total):
        start = pl.multiple_of(index * block, block)
        return total + jnp.sum(gram[pl.ds(start, block), :] * eye_rows(start))

    trace_sum = lax.fori_loop(0, size // block, trace_part, jnp.zeros((), f32))
    norm_scale = 1.0 / (jnp.sqrt(jnp.full((1, 1), trace_sum)) + NS_EPS)

    def store(ref_hi, ref_lo, rows, value):
        high, low = split_bf(value)
        ref_hi[rows, :] = high
        ref_lo[rows, :] = low

    def load_gram(start):
        rows = pl.ds(start, block)
        store(g_hi, g_lo, rows, gram[rows, :] * (norm_scale * norm_scale))

    row_blocks(load_gram)

    def three(a_hi, a_lo, b_hi, b_lo, rows):
        high, low = a_hi[rows, :], a_lo[rows, :]
        return dot(high, b_hi[...]) + (dot(high, b_lo[...]) + dot(low, b_hi[...]))

    def poly_rows(start):
        rows = pl.ds(start, block)
        here = g_hi[rows, :].astype(f32) + g_lo[rows, :].astype(f32)
        poly = QA * eye_rows(start) + QB * here + QC * three(g_hi, g_lo, g_hi, g_lo, rows)
        store(p_hi, p_lo, rows, poly)

    def half_rows(start):
        rows = pl.ds(start, block)
        store(r_hi, r_lo, rows, three(g_hi, g_lo, p_hi, p_lo, rows))

    def gram_rows(start):
        rows = pl.ds(start, block)
        store(g_hi, g_lo, rows, three(p_hi, p_lo, r_hi, r_lo, rows))

    def product_rows(start):
        rows = pl.ds(start, block)
        r_hi[rows, :] = dot(p_hi[rows, :], q_hi[...]).astype(jnp.bfloat16)

    def full_step(index, carry):
        row_blocks(poly_rows)
        row_blocks(half_rows)
        row_blocks(gram_rows)

        @pl.when(index == 0)
        def _():
            q_hi[...] = p_hi[...]

        @pl.when(index > 0)
        def _():
            row_blocks(product_rows)
            q_hi[...] = r_hi[...]

        return carry

    lax.fori_loop(0, NS_STEPS - 1, full_step, 0)
    row_blocks(poly_rows)

    def last_rows(start):
        rows = pl.ds(start, block)
        out_ref[rows, :] = (dot(p_hi[rows, :], q_hi[...]) * norm_scale).astype(out_ref.dtype)

    row_blocks(last_rows)


def gram_series(place, near, far):
    size = near.shape[2]
    whole = pl.BlockSpec(memory_space=pltpu.VMEM)
    return pl.pallas_call(
        series_kernel,
        out_shape=jax.ShapeDtypeStruct((size, size), jnp.bfloat16),
        in_specs=[pl.BlockSpec(memory_space=pltpu.SMEM), whole, whole],
        out_specs=whole,
        scratch_shapes=[pltpu.VMEM((size, size), jnp.float32)]
        + [pltpu.VMEM((size, size), jnp.bfloat16)] * 7,
        compiler_params=pltpu.CompilerParams(vmem_limit_bytes=40 * 2**20),
        cost_estimate=pl.CostEstimate(
            flops=43 * 2 * size**3, bytes_accessed=6 * size * size, transcendentals=0
        ),
    )(place, near, far)


def code_kernel(high_ref, low_ref, kind_ref, out_ref, stage):
    batch, groups = stage.shape[:2]
    picks = high_ref.shape[1]
    bf16, f32 = jnp.bfloat16, jnp.float32
    one, zero = jnp.ones((16, picks), bf16), jnp.zeros((16, picks), bf16)
    kinds = jnp.broadcast_to(kind_ref[...], (16, picks)).astype(bf16)
    steps = lax.broadcasted_iota(jnp.int32, (16, picks), 0).astype(f32).astype(bf16)

    def hot(row, count, value):
        row = jnp.broadcast_to(row, (16, picks)).astype(bf16)
        parts = [
            jnp.where(steps + jnp.asarray(16 * part, bf16) == row, value, zero)
            for part in range(max(1, count // 16))
        ]
        return jnp.concatenate(parts, 0).astype(jnp.float8_e4m3fn)

    def one_batch(index, carry):
        first = pl.multiple_of(index * batch, batch)
        for token in range(batch):
            row = pl.ds(first + token, 1)
            codes = lax.dot_general(
                hot(high_ref[row, :], groups, kinds),
                hot(low_ref[row, :], 128, one),
                (((1,), (1,)), ((), ())),
                preferred_element_type=f32,
            )
            stage[token] = codes[:groups]
        for group in range(groups):
            lanes = slice(group * 128, (group + 1) * 128)
            out_ref[pl.ds(first, batch), lanes] = stage[:, group, :].astype(bf16)
        return carry

    lax.fori_loop(0, high_ref.shape[0] // batch, one_batch, 0)


def kind_codes(column, code_row, latent_count):
    row_total, pick_total = column.shape
    groups = latent_count // 128
    rows = min(128, row_total)
    high = (column // 128).astype(jnp.float32)
    low = (column % 128).astype(jnp.float32)
    return pl.pallas_call(
        code_kernel,
        grid=(row_total // rows,),
        out_shape=jax.ShapeDtypeStruct((row_total, latent_count), jnp.bfloat16),
        in_specs=[
            pl.BlockSpec((rows, pick_total), lambda i: (i, 0)),
            pl.BlockSpec((rows, pick_total), lambda i: (i, 0)),
            pl.BlockSpec((1, pick_total), lambda i: (0, 0)),
        ],
        out_specs=pl.BlockSpec((rows, latent_count), lambda i: (i, 0)),
        scratch_shapes=[pltpu.VMEM((32, groups, 128), jnp.float32)],
        compiler_params=pltpu.CompilerParams(vmem_limit_bytes=40 * 2**20),
        cost_estimate=pl.CostEstimate(
            flops=40 * row_total * latent_count * 128,
            bytes_accessed=2 * row_total * latent_count,
            transcendentals=0,
        ),
    )(high, low, code_row[None, :])


def adam_update(param, grad, first, second):
    first = BETA_ONE * first + (1.0 - BETA_ONE) * grad
    second = BETA_TWO * second + (1.0 - BETA_TWO) * grad * grad
    denom = jnp.sqrt(second / (1.0 - BETA_TWO**STEP)) + ADAM_EPS
    return (param - BIAS_RATE * (first / (1.0 - BETA_ONE**STEP)) / denom, first, second)


def local(
    token_ids,
    lengths,
    top_ids,
    aux_ids,
    dead_set,
    token_table,
    position_table,
    ln_gains,
    frozen_bias,
    w_qkv,
    w_proj,
    w_fc,
    w_out,
    enc_weight,
    enc_bias,
    dec_weight,
    decoder_bias,
    enc_moment,
    dec_moment,
    encb_first,
    encb_second,
    decb_first,
    decb_second,
):
    chips = lax.axis_size("chip")
    narrow_count = lax.axis_size("narrow")
    wide_count = 2 * chips
    wide = ("chip", "core")
    chip_pos = lax.axis_index("chip")
    core_pos = lax.axis_index("core")
    wide_pos = 2 * chip_pos + core_pos
    narrow_pos = lax.axis_index("narrow")
    row_count = token_ids.shape[0]
    model_width = token_table.shape[1]
    wide_latents = enc_weight.shape[1]
    own_latents = wide_latents // narrow_count
    latent_count = chips * own_latents
    bf16, f32 = jnp.bfloat16, jnp.float32
    to_latents = (((1,), (1,)), ((), ()))
    over_rows = (((0,), (0,)), ((), ()))

    def swap(value, axis, offset):
        count = lax.axis_size(axis)
        return lax.ppermute(value, axis, [(place, place ^ offset) for place in range(count)])

    def spread(value):
        narrow_rows = jnp.concatenate(
            [value] + [swap(value, "narrow", k) for k in range(1, narrow_count)], 0
        )
        return jnp.concatenate([narrow_rows, swap(narrow_rows, "core", 1)], 0)

    def rows_to_latents(value):
        return lax.all_to_all(value, "narrow", split_axis=1, concat_axis=0, tiled=True)

    def cols_to_latents(value):
        return lax.all_to_all(value, "narrow", split_axis=0, concat_axis=1, tiled=True)

    def latents_to_rows(value):
        return lax.all_to_all(value, "narrow", split_axis=0, concat_axis=1, tiled=True)

    def latents_to_cols(value):
        return lax.all_to_all(value, "narrow", split_axis=1, concat_axis=0, tiled=True)

    vocab_dev = token_table.shape[0]
    every_ids = lax.all_gather(token_ids, wide, axis=0, tiled=True)
    pick_ids = spread(jnp.concatenate([top_ids, aux_ids], 1))
    enc_own = rows_to_latents(enc_weight.astype(bf16))
    dec_own = cols_to_latents(dec_weight.astype(bf16))
    bias_rows = jnp.concatenate(
        [enc_bias.astype(bf16)[None], jnp.zeros((15, own_latents), bf16)], 0
    )
    enc_biased = lax.all_gather(
        jnp.concatenate([enc_own, bias_rows], 0), "chip", axis=1, tiled=True
    )
    dec_full = lax.all_gather(dec_own, "chip", axis=0, tiled=True)
    enc_full = enc_biased[:model_width]
    bias_copy = enc_biased[model_width]

    local_ids = every_ids - wide_pos * vocab_dev
    inside = (local_ids >= 0) & (local_ids < vocab_dev)
    looked = jnp.take(token_table, jnp.clip(local_ids, 0, vocab_dev - 1), axis=0)
    looked = jnp.where(inside[:, None], looked, jnp.zeros((), bf16))
    pieces = lax.all_to_all(
        looked.reshape(wide_count, row_count, model_width), wide, 0, 0, tiled=True
    )
    start = jnp.sum(pieces.astype(f32), 0) + position_table[:row_count].astype(f32)
    ctx_length = lengths[0]
    inputs = frozen_block(start, ctx_length, ln_gains, frozen_bias, w_qkv, w_proj, w_fc, w_out)
    counted = (jnp.arange(row_count) < ctx_length).astype(f32)

    top_count = top_ids.shape[1]
    pick_total = pick_ids.shape[1]
    owner = pick_ids // wide_latents
    within = pick_ids % wide_latents
    column = (owner // 2) * own_latents + within % own_latents
    mine = (within // own_latents == narrow_pos) & (owner % 2 == core_pos)
    column = jnp.where(mine, column, -1)
    code_row = jnp.where(jnp.arange(pick_total) < top_count, 1.0, 2.0).astype(f32)
    codes = kind_codes(column, code_row, latent_count)
    dead_here = dead_set.reshape(chips, 2, narrow_count, own_latents)
    dead_here = lax.dynamic_slice(
        dead_here, (0, core_pos, narrow_pos, 0), (chips, 1, 1, own_latents)
    ).reshape(latent_count)
    top_mask = codes == 1.0
    aux_mask = (codes == 2.0) & (dead_here[None, :] == 1)

    all_inputs = spread(inputs)
    encoder_in = (all_inputs.astype(f32) - decoder_bias).astype(bf16)
    pre_acts = (
        jnp.dot(encoder_in, enc_full, preferred_element_type=f32) + bias_copy.astype(f32)
    ).astype(bf16)
    zero_bf = jnp.zeros((), bf16)
    top_acts = jnp.where(top_mask, pre_acts, zero_bf)
    aux_acts = jnp.where(aux_mask, pre_acts, zero_bf)
    core_rows = narrow_count * row_count

    def rebuild(acts):
        far = jnp.dot(acts[core_rows:], dec_full, preferred_element_type=f32).astype(bf16)
        near = jnp.dot(acts[:core_rows], dec_full, preferred_element_type=f32)
        total = near + swap(far, "core", 1).astype(f32)
        rounded = total.astype(bf16)
        result = total[:row_count]
        for k in range(1, narrow_count):
            part = rounded[k * row_count : (k + 1) * row_count]
            result = result + swap(part, "narrow", k).astype(f32)
        return result

    target = inputs.astype(f32)
    reconstructed_input = rebuild(top_acts) + decoder_bias
    auxiliary_reconstruction = rebuild(aux_acts)
    recon_error = target - reconstructed_input
    aux_gap = auxiliary_reconstruction - recon_error
    token_loss = (
        counted
        * (jnp.sum(recon_error * recon_error, 1) + AUX_COEF * jnp.sum(aux_gap * aux_gap, 1))
        / model_width
    )
    back_recon = 2.0 / model_width * counted[:, None] * (reconstructed_input - target)
    back_aux = 2.0 * AUX_COEF / model_width * counted[:, None] * aux_gap
    back_rows = jnp.concatenate([back_recon, back_aux], 1).astype(bf16)
    shard_rows = spread(back_rows)
    recon_part = shard_rows[:, :model_width]
    aux_back = shard_rows[:, model_width:]

    def scatter_chips(value, axis):
        def block(place):
            return lax.dynamic_slice_in_dim(value, place * own_latents, own_latents, axis)

        total = block(chip_pos).astype(f32)
        for k in range(1, chips):
            total = total + swap(block(chip_pos ^ k).astype(bf16), "chip", k).astype(f32)
        return total

    grad_dec = lax.dot_general(top_acts, recon_part, over_rows, preferred_element_type=f32)
    grad_dec = grad_dec + lax.dot_general(
        aux_acts, aux_back, over_rows, preferred_element_type=f32
    )
    dec_grad = scatter_chips(grad_dec, 0)
    back_top = lax.dot_general(recon_part, dec_full, to_latents, preferred_element_type=f32)
    back_side = lax.dot_general(aux_back, dec_full, to_latents, preferred_element_type=f32)
    latent_grad = jnp.where(top_mask, back_top, jnp.where(aux_mask, back_side, 0.0)).astype(bf16)
    grad_enc = lax.dot_general(encoder_in, latent_grad, over_rows, preferred_element_type=f32)
    own_moments = (
        rows_to_latents(enc_moment.astype(bf16)),
        cols_to_latents(dec_moment.astype(bf16)),
    )
    grad_enc, own_moments = lax.optimization_barrier((grad_enc, own_moments))
    enc_grad = scatter_chips(grad_enc, 1)
    column_sum = jnp.sum(latent_grad, 0, dtype=f32)
    encb_grad = jnp.sum(
        lax.all_to_all(column_sum.reshape(chips, own_latents), "chip", 0, 0, tiled=True), 0
    )
    bias_term = jnp.sum(back_rows[:, :model_width], 0, dtype=f32) - jnp.dot(
        enc_own.astype(f32), encb_grad, precision=HIGH_PRECISION
    )

    def sum_gram(part, extra):
        rows = model_width // wide_count
        spare = jnp.zeros((16, model_width), bf16)
        if extra is not None:
            spare = jnp.concatenate([*(half[None] for half in split_bf(extra)), spare[2:]], 0)
        chunks = jnp.concatenate(
            [
                part.reshape(wide_count, rows, model_width).astype(bf16),
                jnp.broadcast_to(spare[None], (wide_count, 16, model_width)),
            ],
            1,
        )
        chunks = lax.all_to_all(chunks, wide, 0, 0, tiled=True)
        total = jnp.sum(chunks.astype(f32), 0)
        vector = total[rows] + total[rows + 1]
        high, low = split_bf(vector)
        sent = jnp.concatenate(
            [total[:rows].astype(bf16), high[None], low[None], spare[2:]], 0
        )
        total = total[:rows]
        for k in range(1, narrow_count):
            got = swap(sent, "narrow", k).astype(f32)
            total = total + got[:rows]
            vector = vector + (got[rows] + got[rows + 1])
        near = jnp.stack([total] + [swap(total, "chip", k) for k in range(1, chips)])
        return near, swap(near, "core", 1), vector

    place = wide_pos.reshape(1)
    dec_own_next = (MOMENTUM * own_moments[1].astype(f32) + dec_grad).astype(bf16)
    dec_near, dec_far, _ = sum_gram(
        lax.dot_general(dec_own_next, dec_own_next, over_rows, preferred_element_type=f32), None
    )
    dec_rows_grad = latents_to_cols(dec_grad.astype(bf16))
    dec_factor = gram_series(place, dec_near, dec_far)
    dec_ortho = latents_to_cols(
        jnp.dot(dec_own_next, dec_factor, preferred_element_type=f32).astype(bf16)
    )
    enc_own_next = (MOMENTUM * own_moments[0].astype(f32) + enc_grad).astype(bf16)
    enc_near, enc_far, grad_decb = sum_gram(
        lax.dot_general(enc_own_next, enc_own_next, to_latents, preferred_element_type=f32),
        bias_term,
    )
    enc_rows_grad = latents_to_rows(enc_grad.astype(bf16))
    enc_factor = gram_series(place, enc_near, enc_far)
    enc_factor, enc_rows_grad, dec_rows_grad = lax.optimization_barrier(
        (enc_factor, enc_rows_grad, dec_rows_grad)
    )
    enc_ortho = latents_to_rows(
        jnp.dot(enc_factor, enc_own_next, preferred_element_type=f32).astype(bf16)
    )
    enc_next = MOMENTUM * enc_moment + enc_rows_grad.astype(f32)
    dec_next = MOMENTUM * dec_moment + dec_rows_grad.astype(f32)
    step_scale = MUON_RATE * 0.2 * math.sqrt(max(D, L))
    enc_new = enc_weight * (1.0 - MUON_RATE * DECAY) - step_scale * enc_ortho.astype(f32)
    dec_new = dec_weight * (1.0 - MUON_RATE * DECAY) - step_scale * dec_ortho.astype(f32)
    encb_new, encb_one, encb_two = adam_update(enc_bias, encb_grad, encb_first, encb_second)
    decb_new, decb_one, decb_two = adam_update(decoder_bias, grad_decb, decb_first, decb_second)
    return (
        token_loss,
        enc_new,
        enc_next,
        enc_new.astype(bf16),
        dec_new,
        dec_next,
        dec_new.astype(bf16),
        encb_new,
        encb_one,
        encb_two,
        decb_new,
        decb_one,
        decb_two,
    )


def solution(mesh):
    wide, narrow = mesh.devices.shape
    fine = Mesh(mesh.devices.reshape(wide // 2, 2, narrow), ("chip", "core", "narrow"))
    placed = (
        P(("chip", "core", "narrow")),
        P(("chip", "core", "narrow")),
        P(("chip", "core", "narrow"), None),
        P(("chip", "core", "narrow"), None),
        P(),
        P(("chip", "core"), None),
        P(),
        P(),
        P(),
        P(),
        P(),
        P(),
        P(),
        P("narrow", ("chip", "core")),
        P(("chip", "core", "narrow")),
        P(("chip", "core"), "narrow"),
        P(),
        P("narrow", ("chip", "core")),
        P(("chip", "core"), "narrow"),
        P(("chip", "core", "narrow")),
        P(("chip", "core", "narrow")),
        P(),
        P(),
    )
    return jax.shard_map(
        local,
        mesh=fine,
        in_specs=placed,
        out_specs=(
            P(("chip", "core", "narrow")),
            P("narrow", ("chip", "core")),
            P("narrow", ("chip", "core")),
            P("narrow", ("chip", "core")),
            P(("chip", "core"), "narrow"),
            P(("chip", "core"), "narrow"),
            P(("chip", "core"), "narrow"),
            P(("chip", "core", "narrow")),
            P(("chip", "core", "narrow")),
            P(("chip", "core", "narrow")),
            P(),
            P(),
            P(),
        ),
        check_vma=False,
    )
```

time: 1350 us -> 939 us (0.70)
  matrix products: 441 us -> 130 us
  waiting for transfers between devices: 554 us -> 359 us
  Pallas kernels: 0 us -> 147 us
  blocking collectives: 98.3 us -> 30.8 us
  starting transfers between devices: 42.8 us -> 107 us
  other arithmetic: 100 us -> 68.1 us
    dot_general x49 -> x13, matrix products: 402 us -> 88.3 us  [the longest x1 17.5 us: local(): jnp.dot(encoder_in, enc_full, preferred_element_type=f32)]
    reduce_scatter x3 -> x0, waiting for transfers between devices: 205 us -> none  [the longest x1 91.3 us: local(): lax.psum_scatter(grad_dec.astype(jnp.bfloat16), 'wide', scatter_dimension...]
    ppermute x0 -> x40, waiting for transfers between devices: none -> 175 us  [swap(): lax.ppermute(value, axis, [(place, place ^ offset) for place in range(cou...]
    pallas_call x0 -> x3, Pallas kernels: none -> 147 us  [the longest x2 107 us: gram_series(): pl.pallas_call(series_kernel, out_shape=jax.ShapeDtypeStruct((size, size)...]
    psum x1 -> x0, waiting for transfers between devices: 141 us -> none  [local(): lax.psum(lax.dot_general(split_next[0], split_next[0], to_latents, prefer...]
    all_to_all x5 -> x7, waiting for transfers between devices: 51.1 us -> 116 us  [the longest x2 62.6 us: latents_to_rows(): lax.all_to_all(value, 'narrow', split_axis=0, concat_axis=1, tiled=True)]
    ppermute x0 -> x40, starting transfers between devices: none -> 52.1 us  [swap(): lax.ppermute(value, axis, [(place, place ^ offset) for place in range(cou...]
    all_to_all x2, waiting for transfers between devices: 84.8 us -> 40.7 us  [rows_to_latents(): lax.all_to_all(value, 'narrow', split_axis=1, concat_axis=0, tiled=True)]
  transfers between devices with their start and end apart: 17 -> 53, of which waited for: 11 -> 24; matrix products, arithmetic and copies ran while one was open for 27% -> 24% of each run, Pallas kernels for 0% -> 16%
where the time goes in v2:
time: 939 us; the launch traced here: 929 us
  waiting for transfers between devices  359 us (38%)
  Pallas kernels  147 us (16%)
  matrix products  130 us (14%)
  starting transfers between devices  107 us (11%)
  local copies, waits for them, and re-layouts  70.2 us (7%)
  other arithmetic  68.1 us (7%)
  blocking collectives  30.8 us (3%)
  between operations  16.2 us (2%)
    ppermute x40, waiting for transfers between devices, swap(): lax.ppermute(value, axis, [(place, place ^ offset) for place in range(cou...  175 us
    pallas_call x2, Pallas kernels, gram_series(): pl.pallas_call(series_kernel, out_shape=jax.ShapeDtypeStruct((size, size)...  107 us
    all_to_all x2, waiting for transfers between devices, latents_to_rows(): lax.all_to_all(value, 'narrow', split_axis=0, concat_axis=1, tiled=True)  62.6 us
    ppermute x40, starting transfers between devices, swap(): lax.ppermute(value, axis, [(place, place ^ offset) for place in range(cou...  52.1 us
    all_to_all x1, waiting for transfers between devices, local(): lax.all_to_all(column_sum.reshape(chips, own_latents), 'chip', 0, 0, tile...  41.3 us
    all_to_all x2, waiting for transfers between devices, rows_to_latents(): lax.all_to_all(value, 'narrow', split_axis=1, concat_axis=0, tiled=True)  40.7 us
    pallas_call x1, Pallas kernels, kind_codes(): pl.pallas_call(code_kernel, grid=(row_total // rows,), out_shape=jax.Shap...  40.4 us
    all_to_all x2, waiting for transfers between devices, cols_to_latents(): lax.all_to_all(value, 'narrow', split_axis=0, concat_axis=1, tiled=True)  27.1 us
  transfers between devices with their start and end apart: 53, of which 24 were waited for; matrix products, arithmetic and copies ran while one was open for 24% of the time, Pallas kernels for 16%

profile of v2, /device:TPU:0, one launch (start us, length us, event | category | flops | bytes accessed | tf_op | source)
XLA Modules:
  0.0 929.3 jit_solution(13966532047131625963)
XLA Ops:
  17.2 36.9 %all-to-all-done.1 = bf16[192,4,1024]{2,0,1:T(8,128)(2,1)} async-done(((bf16[192,4,1024]{2,0,1:T(8,128)(2,1)}), bf16[192,4,1024]{2,0,1:T(8,128)(2,1)}, u32[]{:S(2)}, u32[]{:S(2)}) %all-to-all-start.1) | async-done | bytes 1572896 | tf_op jit(solution)/shard_map/all_to_all | solution.py:314
  57.0 8.8 all-gather
  65.8 10.9 %gather_fusion = bf16[1024,768]{1,0:T(8,128)(2,1)} fusion(bf16[6288,768]{1,0:T(8,128)(2,1)} %param.28, s32[1024]{0:T(1024)S(1)} %fusion.82), kind=kCustom, calls=%fused_computation | custom fusion | bytes 3149824 | tf_op jit(solution)/shard_map/jit(_take)/gather | solution.py:342
  103.3 8.4 all-to-all-done
  136.3 16.0 %all-to-all-done.2 = bf16[4,1024,192]{1,2,0:T(8,128)(2,1)} async-done(((bf16[4,1024,192]{1,2,0:T(8,128)(2,1)}), bf16[4,1024,192]{1,2,0:T(8,128)(2,1)}, u32[]{:S(2)}, u32[]{:S(2)}) %all-to-all-start.2) | async-done | bytes 1572896 | tf_op jit(solution)/shard_map/all_to_all | solution.py:317
  153.9 6.3 constant_dynamic-update-slice_fusion.9
  167.5 9.4 %fusion.18 = (f32[1024,544]{1,0:T(8,128)S(1)}, s32[1024,544]{1,0:T(8,128)S(1)}) fusion(s32[]{:T(128)S(6)} %axis_index.36, s32[1024,544]{1,0:T(8,128)} %constant_dynamic-update-slice_fusion, s32[]{:T(128)S(6)} %axis_index.38), kind=kLoop, calls=%fused_computation.67 | loop fusion | flops 41779200 | bytes 6684680 | tf_op jit(solution)/shard_map/convert_element_type | solution.py:233
  178.6 40.4 %shard_map.318 = bf16[1024,4096]{1,0:T(8,128)(2,1)S(1)} custom-call(f32[1024,544]{1,0:T(8,128)S(1)} %fusion.17.high_ref, f32[1024,544]{1,0:T(8,128)S(1)} %get-tuple-element.48.low_ref, f32[1,544]{1,0:T(1,128)S(1)} %compare_select_fusion.2.kind_ref), custom_call_target="tpu_custom_call" | custom-call | flops 21474836480 | bytes 8388608 | tf_op jit(solution)/shard_map/pallas_call | solution.py:234
  226.2 17.5 %compare_select_fusion = (bf16[1024,4096]{1,0:T(8,128)(2,1)}, bf16[1024,4096]{1,0:T(8,128)(2,1)}) fusion(bf16[1024,4096]{1,0:T(8,128)(2,1)} %copy-done.2, pred[4096]{0:T(1024)(128)(4,1)S(1)} %bitcast.165, f32[4096]{0:T(1024)S(1)} %bitcast.163, bf16[784,4096]{1,0:T(8,128)(2,1)} %all-gather.4.cloned.1.call-done, ...), kind=kOutput, calls=%fused_computation.8 | convolution fusion | flops 6486753280 | bytes 33053696 | tf_op jit(solution)/shard_map/dot_general | solution.py:371
  243.7 7.6 fusion.35
  285.5 10.0 %collective-permute-done.14 = bf16[128,768]{1,0:T(8,128)(2,1)S(1)} collective-permute-done((bf16[128,768]{1,0:T(8,128)(2,1)S(1)}, bf16[128,768]{1,0:T(8,128)(2,1)S(1)}, u32[]{:S(2)}, u32[]{:S(2)}) %collective-permute-start.14) | collective-permute-done | bytes 196640 | tf_op jit(solution)/shard_map/ppermute | solution.py:305
  305.3 14.0 %collective-permute-done.16 = bf16[128,1536]{1,0:T(8,128)(2,1)S(1)} collective-permute-done((bf16[128,1536]{1,0:T(8,128)(2,1)S(1)}, bf16[128,1536]{1,0:T(8,128)(2,1)S(1)}, u32[]{:S(2)}, u32[]{:S(2)}) %collective-permute-start.16) | collective-permute-done | bytes 393248 | tf_op jit(solution)/shard_map/ppermute | solution.py:305
  319.2 13.5 %collective-permute-done.17 = bf16[128,1536]{1,0:T(8,128)(2,1)S(1)} collective-permute-done((bf16[128,1536]{1,0:T(8,128)(2,1)S(1)}, bf16[128,1536]{1,0:T(8,128)(2,1)S(1)}, u32[]{:S(2)}, u32[]{:S(2)}) %collective-permute-start.17) | collective-permute-done | bytes 393248 | tf_op jit(solution)/shard_map/ppermute | solution.py:305
  335.6 9.3 %all-to-all-start.3 = ((bf16[192,4,1024]{2,0,1:T(8,128)(2,1)}), bf16[192,4,1024]{2,0,1:T(8,128)(2,1)}, u32[]{:S(2)}, u32[]{:S(2)}) async-start(bf16[192,4,1024]{2,0,1:T(8,128)(2,1)} %bitcast.134), calls=%async_computation.3 | async-start | bytes 3145728 | tf_op jit(solution)/shard_map/all_to_all | solution.py:314
  351.5 11.4 %fusion.43 = bf16[1024,4096]{1,0:T(8,128)(2,1)} fusion(bf16[4096,768]{0,1:T(8,128)(2,1)} %all-gather.6.cloned.1.call-done, bf16[1024,1536]{1,0:T(8,128)(2,1)} %constant_dynamic-update-slice_fusion.10), kind=kOutput, calls=%fused_computation.106 | convolution fusion | flops 6442450944 | bytes 16252928 | tf_op jit(solution)/shard_map/dot_general | solution.py:421
  363.0 16.6 %convert_reduce_fusion = (f32[4096]{0:T(1024)}, bf16[1024,4096]{1,0:T(8,128)(2,1)}) fusion(bf16[1024,4096]{1,0:T(8,128)(2,1)} %fusion.43, pred[4096]{0:T(1024)(128)(4,1)S(1)} %bitcast.166, bf16[1024,4096]{1,0:T(8,128)(2,1)S(1)} %bitcast.129, bf16[4096,768]{0,1:T(8,128)(2,1)} %all-gather.6.cloned.1.call-done, bf16[1024,1536]{1,0:T(8,128)(2,1)S(1)} %copy-done.31), kind=kOutput, calls=%fused_computation.2 | convolution fusion | flops 6484389888 | bytes 33050624 | tf_op jit(solution)/shard_map/dot_general | solution.py:420
  386.9 13.5 %fusion.47 = f32[768,4096]{1,0:T(8,128)} fusion(bf16[1024,4096]{1,0:T(8,128)(2,1)} %get-tuple-element.88, bf16[1024,768]{1,0:T(8,128)(2,1)} %constant_dynamic-update-slice_fusion.5, f32[768]{0:T(1024)S(1)} %copy-done.33), kind=kOutput, calls=%fused_computation.110 | convolution fusion | flops 6444810240 | bytes 22547456 | tf_op jit(solution)/shard_map/dot_general | solution.py:423
  400.4 12.7 %fusion.41 = f32[4096,768]{0,1:T(8,128)} fusion(bf16[1024,4096]{1,0:T(8,128)(2,1)} %get-tuple-element.55, bf16[1024,1536]{1,0:T(8,128)(2,1)S(1)} %copy-done.32), kind=kOutput, calls=%fused_computation.104 | convolution fusion | flops 6442450944 | bytes 22544384 | tf_op jit(solution)/shard_map/dot_general | solution.py:416
  413.1 11.1 %all-to-all-done.4 = bf16[4,1024,192]{1,2,0:T(8,128)(2,1)S(1)} async-done(((bf16[4,1024,192]{1,2,0:T(8,128)(2,1)}), bf16[4,1024,192]{1,2,0:T(8,128)(2,1)S(1)}, u32[]{:S(2)}, u32[]{:S(2)}) %all-to-all-start.4) | async-done | bytes 1572896 | tf_op jit(solution)/shard_map/all_to_all | solution.py:317
  438.2 13.5 %convolution_add_fusion = f32[4096,768]{0,1:T(8,128)S(1)} fusion(f32[4096,768]{0,1:T(8,128)} %fusion.41, bf16[1024,4096]{1,0:T(8,128)(2,1)} %get-tuple-element.54, bf16[1024,1536]{1,0:T(8,128)(2,1)} %constant_dynamic-update-slice_fusion.10), kind=kOutput, calls=%fused_computation.6 | convolution fusion | flops 6445596672 | bytes 35127296 | tf_op jit(solution)/shard_map/dot_general | solution.py:415
  462.2 41.3 %all-to-all-done.5 = f32[4,1,1024]{2,1,0:T(1,128)S(1)} async-done(((f32[4,1,1024]{2,1,0:T(1,128)}), f32[4,1,1024]{2,1,0:T(1,128)S(1)}, u32[]{:S(2)}, u32[]{:S(2)}) %all-to-all-start.5) | async-done | bytes 16416 | tf_op jit(solution)/shard_map/all_to_all | solution.py:432
  507.9 6.6 fusion.74
  520.7 14.9 %collective-permute-done.30 = bf16[1024,768]{0,1:T(8,128)(2,1)} collective-permute-done((bf16[1024,768]{0,1:T(8,128)(2,1)}, bf16[1024,768]{0,1:T(8,128)(2,1)}, u32[]{:S(2)}, u32[]{:S(2)}) %collective-permute-start.30) | collective-permute-done | bytes 1572896 | tf_op jit(solution)/shard_map/ppermute | solution.py:305
  535.7 36.0 %collective-permute-done.31 = bf16[1024,768]{0,1:T(8,128)(2,1)} collective-permute-done((bf16[1024,768]{0,1:T(8,128)(2,1)}, bf16[1024,768]{0,1:T(8,128)(2,1)}, u32[]{:S(2)}, u32[]{:S(2)}) %collective-permute-start.31) | collective-permute-done | bytes 1572896 | tf_op jit(solution)/shard_map/ppermute | solution.py:305
  583.4 22.0 %all_to_all.164 = bf16[8,112,768]{2,1,0:T(8,128)(2,1)} all-to-all(bf16[8,112,768]{2,1,0:T(8,128)(2,1)S(1)} %concatenate.58), channel_id=1, replica_groups=mesh['chip'=4,'core'=2,'narrow'=4] {'chip','core'}, dimensions={0} | all-to-all | bytes 2752512 | tf_op jit(solution)/shard_map/all_to_all | solution.py:450
  610.8 35.5 %all-to-all-done.7 = bf16[4,192,1024]{2,1,0:T(8,128)(2,1)S(1)} async-done(((bf16[4,192,1024]{2,1,0:T(8,128)(2,1)}), bf16[4,192,1024]{2,1,0:T(8,128)(2,1)S(1)}, u32[]{:S(2)}, u32[]{:S(2)}) %all-to-all-start.7) | async-done | bytes 1572896 | tf_op jit(solution)/shard_map/all_to_all | solution.py:320
  655.2 25.8 %collective-permute-done.33 = bf16[112,768]{1,0:T(8,128)(2,1)S(1)} collective-permute-done((bf16[112,768]{1,0:T(8,128)(2,1)S(1)}, bf16[112,768]{1,0:T(8,128)(2,1)S(1)}, u32[]{:S(2)}, u32[]{:S(2)}) %collective-permute-start.33) | collective-permute-done | bytes 172064 | tf_op jit(solution)/shard_map/ppermute | solution.py:305
  681.0 18.2 %collective-permute-done.34 = bf16[112,768]{1,0:T(8,128)(2,1)S(1)} collective-permute-done((bf16[112,768]{1,0:T(8,128)(2,1)S(1)}, bf16[112,768]{1,0:T(8,128)(2,1)S(1)}, u32[]{:S(2)}, u32[]{:S(2)}) %collective-permute-start.34) | collective-permute-done | bytes 172064 | tf_op jit(solution)/shard_map/ppermute | solution.py:305
  724.6 8.9 collective-permute-done.24
  752.9 52.8 %shard_map.320 = bf16[768,768]{1,0:T(8,128)(2,1)S(1)} custom-call(s32[1]{0:T(128)} %bitcast.18.place_ref, f32[4,96,768]{2,1,0:T(8,128)S(1)} %pad_maximum_fusion.3.near_ref, f32[4,96,768]{2,1,0:T(8,128)S(1)} %collective-permute-done.39.far_ref), custom_call_target="tpu_custom_call" | custom-call | flops 38956695552 | bytes 3538944 | tf_op jit(solution)/shard_map/pallas_call | solution.py:179
  814.0 54.1 %shard_map.319 = bf16[768,768]{1,0:T(8,128)(2,1)S(1)} custom-call(s32[1]{0:T(128)} %bitcast.18.place_ref, f32[4,96,768]{2,1,0:T(8,128)S(1)} %pad_maximum_fusion.2.near_ref, f32[4,96,768]{2,1,0:T(8,128)} %collective-permute-done.29.far_ref), custom_call_target="tpu_custom_call" | custom-call | flops 38956695552 | bytes 3538944 | tf_op jit(solution)/shard_map/pallas_call | solution.py:179
  888.3 27.1 %all-to-all-done.9 = bf16[4,192,1024]{2,1,0:T(8,128)(2,1)} async-done(((bf16[4,192,1024]{2,1,0:T(8,128)(2,1)}), bf16[4,192,1024]{2,1,0:T(8,128)(2,1)}, u32[]{:S(2)}, u32[]{:S(2)}) %all-to-all-start.9) | async-done | bytes 1572896 | tf_op jit(solution)/shard_map/all_to_all | solution.py:320
  (323 shorter events, 282.0 us)
Async XLA Ops:
  10.7 43.4 %all-to-all-start.1 = ((bf16[192,4,1024]{2,0,1:T(8,128)(2,1)}), bf16[192,4,1024]{2,0,1:T(8,128)(2,1)}, u32[]{:S(2)}, u32[]{:S(2)}) async-start(bf16[192,4,1024]{2,0,1:T(8,128)(2,1)} %bitcast.136), calls=%async_computation.1 | async-start | bytes 3145728 | tf_op jit(solution)/shard_map/all_to_all | solution.py:314
  17.0 208.3 %all-gather.4.cloned.1.call-start = ((), (), s32[]{:S(2)}) async-start(), calls=%async_computation.12 | async-start | bytes 8028160 | tf_op jit(solution)/shard_map/all_gather | solution.py:333
  79.3 32.4 %all-to-all-start = ((bf16[8,128,768]{2,1,0:T(8,128)(2,1)}), bf16[8,128,768]{2,1,0:T(8,128)(2,1)}, u32[]{:S(2)}, u32[]{:S(2)}) async-start(bf16[8,128,768]{2,1,0:T(8,128)(2,1)} %select_select_fusion), calls=%async_computation | async-start | bytes 3145728 | tf_op jit(solution)/shard_map/all_to_all | solution.py:344
  86.2 29.9 %collective-permute-start = (s32[128,544]{1,0:T(8,128)}, s32[128,544]{1,0:T(8,128)}, u32[]{:S(2)}, u32[]{:S(2)}) collective-permute-start(s32[128,544]{1,0:T(8,128)} %get-tuple-element.73), channel_id=1, source_target_pairs={{0,1},{1,0},{2,3},{3,2},{4,5},{5,4},{6,7},{7,6},{8,9},{9,8},{10,11... | collective-permute-start | bytes 835592 | tf_op jit(solution)/shard_map/ppermute | solution.py:305
  86.2 29.9 %collective-permute-start.1 = (s32[128,544]{1,0:T(8,128)}, s32[128,544]{1,0:T(8,128)}, u32[]{:S(2)}, u32[]{:S(2)}) collective-permute-start(s32[128,544]{1,0:T(8,128)} %get-tuple-element.73), channel_id=1, source_target_pairs={{0,2},{1,3},{2,0},{3,1},{4,6},{5,7},{6,4},{7,5},{8,10},{9,11},{10,... | collective-permute-start | bytes 835592 | tf_op jit(solution)/shard_map/ppermute | solution.py:305
  88.9 27.3 %collective-permute-start.2 = (s32[128,544]{1,0:T(8,128)}, s32[128,544]{1,0:T(8,128)}, u32[]{:S(2)}, u32[]{:S(2)}) collective-permute-start(s32[128,544]{1,0:T(8,128)} %get-tuple-element.73), channel_id=1, source_target_pairs={{0,3},{1,2},{2,1},{3,0},{4,7},{5,6},{6,5},{7,4},{8,11},{9,10},{10,... | collective-permute-start | bytes 835592 | tf_op jit(solution)/shard_map/ppermute | solution.py:305
  111.7 40.6 %all-to-all-start.2 = ((bf16[4,1024,192]{1,2,0:T(8,128)(2,1)}), bf16[4,1024,192]{1,2,0:T(8,128)(2,1)}, u32[]{:S(2)}, u32[]{:S(2)}) async-start(bf16[4,1024,192]{1,2,0:T(8,128)(2,1)} %bitcast.135), calls=%async_computation.2 | async-start | bytes 3145728 | tf_op jit(solution)/shard_map/all_to_all | solution.py:317
  116.1 127.6 %all-gather.6.cloned.1.call-start = ((), (), s32[]{:S(2)}) async-start(), calls=%async_computation.13 | async-start | bytes 7864320 | tf_op jit(solution)/shard_map/all_gather | solution.py:336
  121.3 43.4 %collective-permute-start.3 = (s32[512,544]{0,1:T(8,128)}, s32[512,544]{0,1:T(8,128)}, u32[]{:S(2)}, u32[]{:S(2)}) collective-permute-start(s32[512,544]{0,1:T(8,128)} %copy.99), channel_id=1, source_target_pairs={{0,4},{4,0},{1,5},{5,1},{2,6},{6,2},{3,7},{7,3},{8,12},{12,8},{9,1... | collective-permute-start | bytes 3342344 | tf_op jit(solution)/shard_map/ppermute | solution.py:305
  178.5 45.9 %collective-permute-start.7 = (bf16[512,768]{1,0:T(8,128)(2,1)S(1)}, bf16[512,768]{1,0:T(8,128)(2,1)S(1)}, u32[]{:S(2)}, u32[]{:S(2)}) collective-permute-start(bf16[512,768]{1,0:T(8,128)(2,1)S(1)} %pad_maximum_fusion.4), channel_id=1, source_target_pairs={{0,4},{4,0},{1,5},{5,1},{2,6},{6,2},{3,7},{7,3},{8,12},{12,8},{9,1... | collective-permute-start | bytes 2359304 | tf_op jit(solution)/shard_map/ppermute | solution.py:305
  273.9 21.6 %collective-permute-start.14 = (bf16[128,768]{1,0:T(8,128)(2,1)S(1)}, bf16[128,768]{1,0:T(8,128)(2,1)S(1)}, u32[]{:S(2)}, u32[]{:S(2)}) collective-permute-start(bf16[128,768]{1,0:T(8,128)(2,1)S(1)} %get-tuple-element.67), channel_id=1, source_target_pairs={{0,2},{1,3},{2,0},{3,1},{4,6},{5,7},{6,4},{7,5},{8,10},{9,11},{10,... | collective-permute-start | bytes 589832 | tf_op jit(solution)/shard_map/ppermute | solution.py:305
  302.9 29.8 %collective-permute-start.17 = (bf16[128,1536]{1,0:T(8,128)(2,1)S(1)}, bf16[128,1536]{1,0:T(8,128)(2,1)S(1)}, u32[]{:S(2)}, u32[]{:S(2)}) collective-permute-start(bf16[128,1536]{1,0:T(8,128)(2,1)S(1)} %get-tuple-element.69), channel_id=1, source_target_pairs={{0,2},{1,3},{2,0},{3,1},{4,6},{5,7},{6,4},{7,5},{8,10},{9,11},{10,... | collective-permute-start | bytes 1179656 | tf_op jit(solution)/shard_map/ppermute | solution.py:305
  303.5 29.2 %collective-permute-start.18 = (bf16[128,1536]{1,0:T(8,128)(2,1)S(1)}, bf16[128,1536]{1,0:T(8,128)(2,1)S(1)}, u32[]{:S(2)}, u32[]{:S(2)}) collective-permute-start(bf16[128,1536]{1,0:T(8,128)(2,1)S(1)} %get-tuple-element.69), channel_id=1, source_target_pairs={{0,3},{1,2},{2,1},{3,0},{4,7},{5,6},{6,5},{7,4},{8,11},{9,10},{10,... | collective-permute-start | bytes 1179656 | tf_op jit(solution)/shard_map/ppermute | solution.py:305
  335.6 47.8 %all-to-all-start.3 = ((bf16[192,4,1024]{2,0,1:T(8,128)(2,1)}), bf16[192,4,1024]{2,0,1:T(8,128)(2,1)}, u32[]{:S(2)}, u32[]{:S(2)}) async-start(bf16[192,4,1024]{2,0,1:T(8,128)(2,1)} %bitcast.134), calls=%async_computation.3 | async-start | bytes 3145728 | tf_op jit(solution)/shard_map/all_to_all | solution.py:314
  383.3 40.9 %all-to-all-start.4 = ((bf16[4,1024,192]{1,2,0:T(8,128)(2,1)}), bf16[4,1024,192]{1,2,0:T(8,128)(2,1)S(1)}, u32[]{:S(2)}, u32[]{:S(2)}) async-start(bf16[4,1024,192]{1,2,0:T(8,128)(2,1)} %bitcast.119), calls=%async_computation.4 | async-start | bytes 3145728 | tf_op jit(solution)/shard_map/all_to_all | solution.py:317
  430.4 75.9 %collective-permute-start.20 = (bf16[768,1024]{1,0:T(8,128)(2,1)}, bf16[768,1024]{1,0:T(8,128)(2,1)S(1)}, u32[]{:S(2)}, u32[]{:S(2)}) collective-permute-start(bf16[768,1024]{1,0:T(8,128)(2,1)} %get-tuple-element.59), channel_id=1, source_target_pairs={{0,8},{8,0},{16,24},{24,16},{1,9},{9,1},{17,25},{25,17},{2,10},{10... | collective-permute-start | bytes 4718600 | tf_op jit(solution)/shard_map/ppermute | solution.py:305
  432.1 75.9 %collective-permute-start.21 = (bf16[768,1024]{1,0:T(8,128)(2,1)}, bf16[768,1024]{1,0:T(8,128)(2,1)}, u32[]{:S(2)}, u32[]{:S(2)}) collective-permute-start(bf16[768,1024]{1,0:T(8,128)(2,1)} %get-tuple-element.61), channel_id=1, source_target_pairs={{0,16},{8,24},{16,0},{24,8},{1,17},{9,25},{17,1},{25,9},{2,18},{10... | collective-permute-start | bytes 4718600 | tf_op jit(solution)/shard_map/ppermute | solution.py:305
  433.6 74.4 %collective-permute-start.22 = (bf16[768,1024]{1,0:T(8,128)(2,1)}, bf16[768,1024]{1,0:T(8,128)(2,1)}, u32[]{:S(2)}, u32[]{:S(2)}) collective-permute-start(bf16[768,1024]{1,0:T(8,128)(2,1)} %get-tuple-element.60), channel_id=1, source_target_pairs={{0,24},{8,16},{16,8},{24,0},{1,25},{9,17},{17,9},{25,1},{2,26},{10... | collective-permute-start | bytes 4718600 | tf_op jit(solution)/shard_map/ppermute | solution.py:305
  433.9 69.6 %all-to-all-start.5 = ((f32[4,1,1024]{2,1,0:T(1,128)}), f32[4,1,1024]{2,1,0:T(1,128)S(1)}, u32[]{:S(2)}, u32[]{:S(2)}) async-start(f32[4,1,1024]{2,1,0:T(1,128)} %bitcast.24), calls=%async_computation.5 | async-start | bytes 32768 | tf_op jit(solution)/shard_map/all_to_all | solution.py:432
  458.7 77.0 %collective-permute-start.30 = (bf16[1024,768]{0,1:T(8,128)(2,1)}, bf16[1024,768]{0,1:T(8,128)(2,1)}, u32[]{:S(2)}, u32[]{:S(2)}) collective-permute-start(bf16[1024,768]{0,1:T(8,128)(2,1)} %get-tuple-element.56), channel_id=1, source_target_pairs={{0,8},{8,0},{16,24},{24,16},{1,9},{9,1},{17,25},{25,17},{2,10},{10... | collective-permute-start | bytes 4718600 | tf_op jit(solution)/shard_map/ppermute | solution.py:305
  460.7 110.9 %collective-permute-start.31 = (bf16[1024,768]{0,1:T(8,128)(2,1)}, bf16[1024,768]{0,1:T(8,128)(2,1)}, u32[]{:S(2)}, u32[]{:S(2)}) collective-permute-start(bf16[1024,768]{0,1:T(8,128)(2,1)} %get-tuple-element.58), channel_id=1, source_target_pairs={{0,16},{8,24},{16,0},{24,8},{1,17},{9,25},{17,1},{25,9},{2,18},{10... | collective-permute-start | bytes 4718600 | tf_op jit(solution)/shard_map/ppermute | solution.py:305
  506.3 65.3 %collective-permute-start.32 = (bf16[1024,768]{0,1:T(8,128)(2,1)}, bf16[1024,768]{0,1:T(8,128)(2,1)}, u32[]{:S(2)}, u32[]{:S(2)}) collective-permute-start(bf16[1024,768]{0,1:T(8,128)(2,1)} %get-tuple-element.57), channel_id=1, source_target_pairs={{0,24},{8,16},{16,8},{24,0},{1,25},{9,17},{17,9},{25,1},{2,26},{10... | collective-permute-start | bytes 4718600 | tf_op jit(solution)/shard_map/ppermute | solution.py:305
  517.2 66.3 %all-to-all-start.6 = ((bf16[8,112,768]{2,1,0:T(8,128)(2,1)}), bf16[8,112,768]{2,1,0:T(8,128)(2,1)S(1)}, u32[]{:S(2)}, u32[]{:S(2)}) async-start(bf16[8,112,768]{2,1,0:T(8,128)(2,1)} %pad_maximum_fusion.1), calls=%async_computation.6 | async-start | bytes 2752512 | tf_op jit(solution)/shard_map/all_to_all | solution.py:450
  605.4 40.9 %all-to-all-start.7 = ((bf16[4,192,1024]{2,1,0:T(8,128)(2,1)}), bf16[4,192,1024]{2,1,0:T(8,128)(2,1)S(1)}, u32[]{:S(2)}, u32[]{:S(2)}) async-start(bf16[4,192,1024]{2,1,0:T(8,128)(2,1)} %bitcast.31), calls=%async_computation.7 | async-start | bytes 3145728 | tf_op jit(solution)/shard_map/all_to_all | solution.py:320
  646.3 103.9 %all-to-all-start.8 = ((bf16[1024,4,192]{0,2,1:T(8,128)(2,1)}), bf16[1024,4,192]{0,2,1:T(8,128)(2,1)}, u32[]{:S(2)}, u32[]{:S(2)}) async-start(bf16[1024,4,192]{0,2,1:T(8,128)(2,1)} %bitcast.33), calls=%async_computation.8 | async-start | bytes 3145728 | tf_op jit(solution)/shard_map/all_to_all | solution.py:323
  650.8 30.2 %collective-permute-start.33 = (bf16[112,768]{1,0:T(8,128)(2,1)S(1)}, bf16[112,768]{1,0:T(8,128)(2,1)S(1)}, u32[]{:S(2)}, u32[]{:S(2)}) collective-permute-start(bf16[112,768]{1,0:T(8,128)(2,1)S(1)} %get-tuple-element.79), channel_id=1, source_target_pairs={{0,1},{1,0},{2,3},{3,2},{4,5},{5,4},{6,7},{7,6},{8,9},{9,8},{10,11... | collective-permute-start | bytes 516104 | tf_op jit(solution)/shard_map/ppermute | solution.py:305
  652.8 46.5 %collective-permute-start.34 = (bf16[112,768]{1,0:T(8,128)(2,1)S(1)}, bf16[112,768]{1,0:T(8,128)(2,1)S(1)}, u32[]{:S(2)}, u32[]{:S(2)}) collective-permute-start(bf16[112,768]{1,0:T(8,128)(2,1)S(1)} %get-tuple-element.79), channel_id=1, source_target_pairs={{0,2},{1,3},{2,0},{3,1},{4,6},{5,7},{6,4},{7,5},{8,10},{9,11},{10,... | collective-permute-start | bytes 516104 | tf_op jit(solution)/shard_map/ppermute | solution.py:305
  655.1 44.1 %collective-permute-start.35 = (bf16[112,768]{1,0:T(8,128)(2,1)S(1)}, bf16[112,768]{1,0:T(8,128)(2,1)S(1)}, u32[]{:S(2)}, u32[]{:S(2)}) collective-permute-start(bf16[112,768]{1,0:T(8,128)(2,1)S(1)} %get-tuple-element.79), channel_id=1, source_target_pairs={{0,3},{1,2},{2,1},{3,0},{4,7},{5,6},{6,5},{7,4},{8,11},{9,10},{10,... | collective-permute-start | bytes 516104 | tf_op jit(solution)/shard_map/ppermute | solution.py:305
  713.2 39.7 %collective-permute-start.39 = (f32[4,96,768]{2,1,0:T(8,128)S(1)}, f32[4,96,768]{2,1,0:T(8,128)S(1)}, u32[]{:S(2)}, u32[]{:S(2)}) collective-permute-start(f32[4,96,768]{2,1,0:T(8,128)S(1)} %pad_maximum_fusion.3.near_ref), channel_id=1, source_target_pairs={{0,4},{4,0},{1,5},{5,1},{2,6},{6,2},{3,7},{7,3},{8,12},{12,8},{9,1... | collective-permute-start | bytes 3538952 | tf_op jit(solution)/shard_map/ppermute | solution.py:305
  748.8 65.2 %collective-permute-start.29 = (f32[4,96,768]{2,1,0:T(8,128)S(1)}, f32[4,96,768]{2,1,0:T(8,128)}, u32[]{:S(2)}, u32[]{:S(2)}) collective-permute-start(f32[4,96,768]{2,1,0:T(8,128)S(1)} %pad_maximum_fusion.2.near_ref), channel_id=1, source_target_pairs={{0,4},{4,0},{1,5},{5,1},{2,6},{6,2},{3,7},{7,3},{8,12},{12,8},{9,1... | collective-permute-start | bytes 3538952 | tf_op jit(solution)/shard_map/ppermute | solution.py:305
  808.3 64.6 %all-to-all-start.11 = ((bf16[1024,4,192]{0,2,1:T(8,128)(2,1)}), bf16[1024,4,192]{0,2,1:T(8,128)(2,1)}, u32[]{:S(2)}, u32[]{:S(2)}) async-start(bf16[1024,4,192]{0,2,1:T(8,128)(2,1)} %bitcast.42), calls=%async_computation.11 | async-start | bytes 3145728 | tf_op jit(solution)/shard_map/all_to_all | solution.py:323
  872.9 42.5 %all-to-all-start.9 = ((bf16[4,192,1024]{2,1,0:T(8,128)(2,1)}), bf16[4,192,1024]{2,1,0:T(8,128)(2,1)}, u32[]{:S(2)}, u32[]{:S(2)}) async-start(bf16[4,192,1024]{2,1,0:T(8,128)(2,1)} %bitcast.147), calls=%async_computation.9 | async-start | bytes 3145728 | tf_op jit(solution)/shard_map/all_to_all | solution.py:320
  (76 other events, 1483.5 us)
Sparse Core Ops, SparseCore 0:
  57.1 81.1 all-gather.3
  152.4 70.0 all-gather.5

commit v3 on v2

v3 whole, which is shorter than its diff:
```python
import functools
import math

import jax
import jax.numpy as jnp
from jax import lax
from jax.experimental import pallas as pl
from jax.experimental.pallas import tpu as pltpu
from jax.sharding import Mesh
from jax.sharding import PartitionSpec as P

D = 768
HEAD_DIM = 64
L = 32768
NS_STEPS = 5
STEP = 10


HIGH_PRECISION = lax.Precision.HIGHEST
AUX_COEF = 1.0 / 32.0
EPS_NORM = 1e-05
NS_EPS = 1e-07
QA = 3.4445
QB = -4.775
QC = 2.0315
MOMENTUM = 0.95
MUON_RATE = 0.1
DECAY = 0.1
BIAS_RATE = 0.3
BETA_ONE = 0.9
BETA_TWO = 0.999
ADAM_EPS = 1e-08


def layer_norm(value, gain, shift):
    row_mean = jnp.mean(value, -1, keepdims=True)
    centred = value - row_mean
    row_var = jnp.mean(centred * centred, -1, keepdims=True)
    return centred * lax.rsqrt(row_var + EPS_NORM) * gain + shift


def frozen_block(start, ctx_length, ln_gains, frozen_bias, w_qkv, w_proj, w_fc, w_out):
    row_count, model_width = start.shape
    head_count = model_width // HEAD_DIM
    ff_width = w_fc.shape[1]
    shifts = frozen_bias[: 2 * model_width].reshape(2, model_width)
    b_qkv = frozen_bias[2 * model_width : 5 * model_width]
    b_proj = frozen_bias[5 * model_width : 6 * model_width]
    b_fc = frozen_bias[6 * model_width : 6 * model_width + ff_width]
    b_out = frozen_bias[6 * model_width + ff_width :]
    normed = layer_norm(start, ln_gains[0], shifts[0]).astype(jnp.bfloat16)
    qkv_rows = (jnp.dot(normed, w_qkv, preferred_element_type=jnp.float32) + b_qkv).astype(
        jnp.bfloat16
    )
    head_split = qkv_rows.reshape(row_count, 3, head_count, HEAD_DIM)
    scores = jnp.einsum(
        "qhd,khd->hqk", head_split[:, 0], head_split[:, 1], preferred_element_type=jnp.float32
    ) * HEAD_DIM ** (-0.5)
    positions = jnp.arange(row_count)
    allowed = (positions[None, :] <= positions[:, None]) & (positions[None, :] < ctx_length)
    attn_probs = jax.nn.softmax(jnp.where(allowed[None], scores, -1e30), axis=-1).astype(
        jnp.bfloat16
    )
    mixed = jnp.einsum(
        "hqk,khd->qhd", attn_probs, head_split[:, 2], preferred_element_type=jnp.float32
    )
    mixed = mixed.reshape(row_count, model_width).astype(jnp.bfloat16)
    hidden = start + jnp.dot(mixed, w_proj, preferred_element_type=jnp.float32) + b_proj
    normed_two = layer_norm(hidden, ln_gains[1], shifts[1]).astype(jnp.bfloat16)
    inner_acts = jax.nn.gelu(
        jnp.dot(normed_two, w_fc, preferred_element_type=jnp.float32) + b_fc, approximate=True
    ).astype(jnp.bfloat16)
    return (hidden + jnp.dot(inner_acts, w_out, preferred_element_type=jnp.float32) + b_out).astype(
        jnp.bfloat16
    )


def split_bf(value):
    high = value.astype(jnp.bfloat16)
    return high, (value - high.astype(jnp.float32)).astype(jnp.bfloat16)


def row_blocks(size, body):
    block = 256

    def step(index, carry):
        body(pl.ds(pl.multiple_of(index * block, block), block), index * block)
        return carry

    lax.fori_loop(0, size // block, step, 0)


def eye_rows(start, size):
    rows = lax.broadcasted_iota(jnp.int32, (256, size), 0) + start
    cols = lax.broadcasted_iota(jnp.int32, (256, size), 1)
    return (rows == cols).astype(jnp.float32)


def dot_f32(a, b):
    return jnp.dot(a, b, preferred_element_type=jnp.float32)


def store_split(pair, rows, value):
    pair[0][rows, :], pair[1][rows, :] = split_bf(value)


def three(left, right, rows):
    high, low = left[0][rows, :], left[1][rows, :]
    return dot_f32(high, right[0][...]) + (
        dot_f32(high, right[1][...]) + dot_f32(low, right[0][...])
    )


def series_step(gram, poly, half, out, old, new, step):
    size = gram[0].shape[0]
    last = step == NS_STEPS - 1
    exact_square = step >= 3

    def poly_rows(rows, start):
        here = gram[0][rows, :].astype(jnp.float32) + gram[1][rows, :].astype(jnp.float32)
        if exact_square:
            square = three(gram, gram, rows)
        else:
            square = dot_f32(gram[0][rows, :], gram[0][...])
        store_split(poly, rows, QA * eye_rows(start, size) + QB * here + QC * square)

    def half_rows(rows, start):
        store_split(half, rows, three(gram, poly, rows))

    def gram_rows(rows, start):
        store_split(out, rows, three(poly, half, rows))

    def product_rows(rows, start):
        new[rows, :] = dot_f32(poly[0][rows, :], old[...]).astype(jnp.bfloat16)

    row_blocks(size, poly_rows)
    if not last:
        row_blocks(size, half_rows)
        row_blocks(size, gram_rows)
    if step > 0:
        row_blocks(size, product_rows)


def first_kernel(place_ref, near_ref, far_ref, o_hi, o_lo, q_ref, total, *scratch):
    size = total.shape[0]
    chips, rows_each = near_ref.shape[:2]
    chip, core = place_ref[0], place_ref[1]
    gram, poly, half = scratch[:2], scratch[2:4], scratch[4:6]
    for offset in range(chips):
        for side, source in enumerate((near_ref, far_ref)):
            first = jnp.bitwise_xor(core, side) * (size // 2)
            first = first + jnp.bitwise_xor(chip, offset) * rows_each
            total[pl.ds(pl.multiple_of(first, 8), rows_each), :] = source[offset].astype(
                jnp.float32
            )

    def trace_part(index, value):
        start = pl.multiple_of(index * 256, 256)
        return value + jnp.sum(total[pl.ds(start, 256), :] * eye_rows(start, size))

    trace_sum = lax.fori_loop(0, size // 256, trace_part, jnp.zeros((), jnp.float32))
    scale = 1.0 / (jnp.sqrt(jnp.full((1, 1), trace_sum)) + NS_EPS)

    def load_rows(rows, start):
        store_split(gram, rows, total[rows, :] * (scale * scale))

    row_blocks(size, load_rows)
    series_step(gram, poly, half, (o_hi, o_lo), None, None, 0)

    def product_rows(rows, start):
        value = poly[0][rows, :].astype(jnp.float32) + poly[1][rows, :].astype(jnp.float32)
        q_ref[rows, :] = (value * scale).astype(jnp.bfloat16)

    row_blocks(size, product_rows)


def middle_kernel(step, g_hi, g_lo, q_ref, o_hi, o_lo, out_ref, *scratch):
    series_step(
        (g_hi, g_lo), scratch[:2], scratch[2:4], (o_hi, o_lo), q_ref, out_ref, step
    )


def last_kernel(g_hi, g_lo, q_ref, out_ref, *scratch):
    series_step((g_hi, g_lo), scratch[:2], None, None, q_ref, out_ref, NS_STEPS - 1)


def square_call(kernel, outs, scratch, passes, *operands):
    size = operands[-1].shape[-1]
    whole = pl.BlockSpec(memory_space=pltpu.VMEM)
    specs = [whole] * len(operands)
    if operands[0].ndim == 1:
        specs[0] = pl.BlockSpec(memory_space=pltpu.SMEM)
    square = jax.ShapeDtypeStruct((size, size), jnp.bfloat16)
    return pl.pallas_call(
        kernel,
        out_shape=[square] * outs,
        in_specs=specs,
        out_specs=[whole] * outs,
        scratch_shapes=[pltpu.VMEM((size, size), kind) for kind in scratch],
        compiler_params=pltpu.CompilerParams(vmem_limit_bytes=40 * 2**20),
        cost_estimate=pl.CostEstimate(
            flops=passes * 2 * size**3, bytes_accessed=12 * size * size, transcendentals=0
        ),
    )(*operands)


def series_start(place, near, far):
    bf16 = jnp.bfloat16
    return square_call(first_kernel, 3, [jnp.float32] + [bf16] * 6, 8, place, near, far)


def series_finish(state):
    bf16 = jnp.bfloat16
    for step in range(1, NS_STEPS - 1):
        kernel = functools.partial(middle_kernel, step)
        state = square_call(kernel, 3, [bf16] * 4, 8 if step < 3 else 10, *state)
    return square_call(last_kernel, 1, [bf16] * 2, 4, *state)[0]


def code_kernel(shifts, place_ref, ids_ref, dead_ref, out_ref, high, low, stage):
    wide_shift, own_shift, top_count = shifts
    batch, groups = stage.shape[:2]
    rows, picks = ids_ref.shape
    bf16, f32 = jnp.bfloat16, jnp.float32
    chip, core, narrow = place_ref[0], place_ref[1], place_ref[2]
    latent_count = dead_ref.shape[1]
    half_shift = own_shift - 1

    ids = ids_ref[...]
    owner = lax.shift_right_logical(ids, wide_shift)
    within = jnp.bitwise_and(ids, (1 << wide_shift) - 1)
    mine = (lax.shift_right_logical(within, own_shift) == narrow) & (
        jnp.bitwise_and(owner, 1) == core
    )
    inner = jnp.bitwise_and(within, (1 << own_shift) - 1)
    offset = jnp.bitwise_xor(lax.shift_right_logical(owner, 1), chip)
    column = (
        lax.shift_right_logical(inner, half_shift) * (latent_count // 2)
        + lax.shift_left(offset, half_shift)
        + jnp.bitwise_and(inner, (1 << half_shift) - 1)
    )
    high[...] = jnp.where(mine, lax.shift_right_logical(column, 7), -1).astype(f32)
    low[...] = jnp.bitwise_and(column, 127).astype(f32)

    one, zero = jnp.ones((16, picks), bf16), jnp.zeros((16, picks), bf16)
    places = lax.broadcasted_iota(jnp.int32, (16, picks), 1)
    kinds = jnp.where(places < top_count, 1.0, 2.0).astype(bf16)
    steps = lax.broadcasted_iota(jnp.int32, (16, picks), 0).astype(f32).astype(bf16)

    def hot(row, count, value):
        row = jnp.broadcast_to(row, (16, picks)).astype(bf16)
        parts = [
            jnp.where(steps + jnp.asarray(16 * part, bf16) == row, value, zero)
            for part in range(max(1, count // 16))
        ]
        return jnp.concatenate(parts, 0).astype(jnp.float8_e4m3fn)

    def one_batch(index, carry):
        first = pl.multiple_of(index * batch, batch)
        for token in range(batch):
            row = pl.ds(first + token, 1)
            codes = lax.dot_general(
                hot(high[row, :], groups, kinds),
                hot(low[row, :], 128, one),
                (((1,), (1,)), ((), ())),
                preferred_element_type=f32,
            )
            stage[token] = codes[:groups]
        for group in range(groups):
            lanes = slice(group * 128, (group + 1) * 128)
            codes = stage[:, group, :]
            live = (codes != 2.0) | (dead_ref[:, lanes] == 1)
            out_ref[pl.ds(first, batch), lanes] = jnp.where(live, codes, 0.0).astype(bf16)
        return carry

    lax.fori_loop(0, rows // batch, one_batch, 0)


def kind_codes(place, ids, dead_here, wide_latents, own_latents, top_count):
    row_total, pick_total = ids.shape
    latent_count = dead_here.shape[1]
    rows = min(128, row_total)
    shifts = (wide_latents.bit_length() - 1, own_latents.bit_length() - 1, top_count)
    return pl.pallas_call(
        functools.partial(code_kernel, shifts),
        grid=(row_total // rows,),
        out_shape=jax.ShapeDtypeStruct((row_total, latent_count), jnp.bfloat16),
        in_specs=[
            pl.BlockSpec(memory_space=pltpu.SMEM),
            pl.BlockSpec((rows, pick_total), lambda i: (i, 0)),
            pl.BlockSpec((1, latent_count), lambda i: (0, 0)),
        ],
        out_specs=pl.BlockSpec((rows, latent_count), lambda i: (i, 0)),
        scratch_shapes=[
            pltpu.VMEM((rows, pick_total), jnp.float32),
            pltpu.VMEM((rows, pick_total), jnp.float32),
            pltpu.VMEM((32, latent_count // 128, 128), jnp.float32),
        ],
        compiler_params=pltpu.CompilerParams(vmem_limit_bytes=40 * 2**20),
        cost_estimate=pl.CostEstimate(
            flops=40 * row_total * latent_count * 128,
            bytes_accessed=2 * row_total * latent_count,
            transcendentals=0,
        ),
    )(place, ids, dead_here)


def adam_update(param, grad, first, second):
    first = BETA_ONE * first + (1.0 - BETA_ONE) * grad
    second = BETA_TWO * second + (1.0 - BETA_TWO) * grad * grad
    denom = jnp.sqrt(second / (1.0 - BETA_TWO**STEP)) + ADAM_EPS
    return (param - BIAS_RATE * (first / (1.0 - BETA_ONE**STEP)) / denom, first, second)


def local(
    token_ids,
    lengths,
    top_ids,
    aux_ids,
    dead_set,
    token_table,
    position_table,
    ln_gains,
    frozen_bias,
    w_qkv,
    w_proj,
    w_fc,
    w_out,
    enc_weight,
    enc_bias,
    dec_weight,
    decoder_bias,
    enc_moment,
    dec_moment,
    encb_first,
    encb_second,
    decb_first,
    decb_second,
):
    chips = lax.axis_size("chip")
    narrow_count = lax.axis_size("narrow")
    wide_count = 2 * chips
    wide = ("chip", "core")
    chip_pos = lax.axis_index("chip")
    core_pos = lax.axis_index("core")
    wide_pos = 2 * chip_pos + core_pos
    narrow_pos = lax.axis_index("narrow")
    row_count = token_ids.shape[0]
    model_width = token_table.shape[1]
    wide_latents = enc_weight.shape[1]
    own_latents = wide_latents // narrow_count
    half_latents = own_latents // 2
    latent_count = chips * own_latents
    core_rows = narrow_count * row_count
    bf16, f32 = jnp.bfloat16, jnp.float32
    to_latents = (((1,), (1,)), ((), ()))
    over_rows = (((0,), (0,)), ((), ()))
    place = jnp.stack([chip_pos, core_pos, narrow_pos]).astype(jnp.int32)
    bits = [1 << bit for bit in range(chips.bit_length() - 1)]
    orders = (bits, bits[::-1])

    def after(value, *others):
        return lax.optimization_barrier((value, others))[0]

    def swap(value, axis, offset):
        count = lax.axis_size(axis)
        return lax.ppermute(value, axis, [(spot, spot ^ offset) for spot in range(count)])

    def spread_narrow(value):
        parts = [value] + [swap(value, "narrow", k) for k in range(1, narrow_count)]
        return jnp.concatenate(parts, 0)

    def rows_to_latents(value):
        return lax.all_to_all(value, "narrow", split_axis=1, concat_axis=0, tiled=True)

    def cols_to_latents(value):
        return lax.all_to_all(value, "narrow", split_axis=0, concat_axis=1, tiled=True)

    def latents_to_rows(value):
        return lax.all_to_all(value, "narrow", split_axis=0, concat_axis=1, tiled=True)

    def latents_to_cols(value):
        return lax.all_to_all(value, "narrow", split_axis=1, concat_axis=0, tiled=True)

    def gather_chips(own, axis):
        pieces = []
        for part, order in enumerate(orders):
            first = lax.slice_in_dim(own, part * half_latents, (part + 1) * half_latents, axis=axis)
            held = {0: first}
            for bit in order:
                offsets = sorted(held)
                sent = [held[offset] for offset in offsets]
                sent = sent[0] if len(sent) == 1 else jnp.concatenate(sent, axis)
                got = jnp.split(swap(sent, "chip", bit), len(offsets), axis)
                held.update({offset ^ bit: piece for offset, piece in zip(offsets, got)})
            pieces += [held[offset] for offset in range(chips)]
        return jnp.concatenate(pieces, axis)

    def scatter_chips(value, axis, extra=None):
        results, extras = [], []
        for part, order in enumerate(orders):
            base = part * chips * half_latents
            held, added = {}, {}
            for offset in range(chips):
                start = base + offset * half_latents
                held[offset] = lax.slice_in_dim(value, start, start + half_latents, axis=axis)
                if extra is not None:
                    added[offset] = lax.slice_in_dim(extra, start, start + half_latents, axis=0)
            for bit in reversed(order):
                keep = sorted(offset for offset in held if not offset & bit)
                sent = jnp.concatenate([held[offset | bit].astype(bf16) for offset in keep], axis)
                if extra is not None:
                    vector = jnp.concatenate([added[offset | bit] for offset in keep])
                    lines = jnp.stack(split_bf(vector))
                    lines = jnp.concatenate([lines, jnp.zeros((14, lines.shape[1]), bf16)], 0)
                    sent = jnp.concatenate([sent, lines], 0)
                got = swap(sent, "chip", bit).astype(f32)
                if extra is not None:
                    vector = got[model_width] + got[model_width + 1]
                    got = got[:model_width]
                    added = {
                        offset: added[offset] + piece
                        for offset, piece in zip(keep, jnp.split(vector, len(keep)))
                    }
                got = jnp.split(got, len(keep), axis)
                held = {offset: held[offset] + piece for offset, piece in zip(keep, got)}
            results.append(held[0])
            if extra is not None:
                extras.append(added[0])
        result = jnp.concatenate(results, axis)
        return result if extra is None else (result, jnp.concatenate(extras))

    vocab_dev = token_table.shape[0]
    every_ids = lax.all_gather(token_ids, wide, axis=0, tiled=False).reshape(wide_count, row_count)
    every_ids = jnp.concatenate(
        [
            lax.dynamic_slice_in_dim(every_ids, wide_pos ^ offset, 1, 0)
            for offset in range(wide_count)
        ],
        1,
    )[0]
    local_ids = every_ids - wide_pos * vocab_dev
    inside = (local_ids >= 0) & (local_ids < vocab_dev)
    looked = jnp.take(token_table, jnp.clip(local_ids, 0, vocab_dev - 1), axis=0)
    looked = jnp.where(inside[:, None], looked, jnp.zeros((), bf16))
    enc_own = rows_to_latents(enc_weight.astype(bf16))
    near_picks = spread_narrow(jnp.concatenate([top_ids, aux_ids], 1))
    far_picks = swap(near_picks, "core", 1)

    looked = looked.reshape(chips, 2, row_count, model_width)
    looked = looked[:, 0] + swap(looked[:, 1], "core", 1)
    embedded = looked[0].astype(f32)
    for k in range(1, chips):
        embedded = embedded + swap(looked[k], "chip", k).astype(f32)

    enc_own = after(enc_own, looked)
    dec_own = cols_to_latents(after(dec_weight, enc_own).astype(bf16))
    bias_rows = jnp.concatenate(
        [enc_bias.astype(bf16)[None], jnp.zeros((15, own_latents), bf16)], 0
    )
    enc_biased = gather_chips(jnp.concatenate([enc_own, bias_rows], 0), 1)
    enc_full = enc_biased[:model_width]
    bias_copy = enc_biased[model_width]

    dead_here = jnp.stack(
        [
            lax.dynamic_slice_in_dim(
                dead_set,
                (2 * (chip_pos ^ offset) + core_pos) * wide_latents + narrow_pos * own_latents,
                own_latents,
            )
            for offset in range(chips)
        ]
    )
    dead_here = dead_here.reshape(chips, 2, half_latents).transpose(1, 0, 2)
    dead_here = dead_here.reshape(1, latent_count)
    sizes = (wide_latents, own_latents, top_ids.shape[1])
    near_codes = kind_codes(place, near_picks, dead_here, *sizes)

    start = after(embedded, near_codes) + position_table[:row_count].astype(f32)
    ctx_length = lengths[0]
    inputs = frozen_block(start, ctx_length, ln_gains, frozen_bias, w_qkv, w_proj, w_fc, w_out)
    counted = (jnp.arange(row_count) < ctx_length).astype(f32)
    dec_full = gather_chips(after(dec_own, inputs), 0)
    far_codes = kind_codes(place, after(far_picks, inputs), dead_here, *sizes)

    near_inputs = spread_narrow(inputs)
    far_inputs = swap(near_inputs, "core", 1)
    zero_bf = jnp.zeros((), bf16)

    def encode(tokens, codes):
        encoder_in = (tokens.astype(f32) - decoder_bias).astype(bf16)
        pre_acts = (
            jnp.dot(encoder_in, enc_full, preferred_element_type=f32) + bias_copy.astype(f32)
        ).astype(bf16)
        top_acts = jnp.where(codes == 1.0, pre_acts, zero_bf)
        return encoder_in, top_acts, jnp.where(codes == 2.0, pre_acts, zero_bf)

    all_inputs = jnp.concatenate([near_inputs, far_inputs], 0)
    codes = jnp.concatenate([near_codes, far_codes], 0)
    encoder_in, top_acts, aux_acts = encode(all_inputs, codes)

    def rebuild(acts):
        far = jnp.dot(acts[core_rows:], dec_full, preferred_element_type=f32).astype(bf16)
        near = jnp.dot(acts[:core_rows], dec_full, preferred_element_type=f32)
        total = near + swap(far, "core", 1).astype(f32)
        rounded = total.astype(bf16)
        result = total[:row_count]
        for k in range(1, narrow_count):
            part = rounded[k * row_count : (k + 1) * row_count]
            result = result + swap(part, "narrow", k).astype(f32)
        return result

    target = inputs.astype(f32)
    reconstructed_input = rebuild(top_acts) + decoder_bias
    auxiliary_reconstruction = rebuild(aux_acts)
    recon_error = target - reconstructed_input
    aux_gap = auxiliary_reconstruction - recon_error
    token_loss = (
        counted
        * (jnp.sum(recon_error * recon_error, 1) + AUX_COEF * jnp.sum(aux_gap * aux_gap, 1))
        / model_width
    )
    back_recon = 2.0 / model_width * counted[:, None] * (reconstructed_input - target)
    back_aux = 2.0 * AUX_COEF / model_width * counted[:, None] * aux_gap
    back_rows = jnp.concatenate([back_recon, back_aux], 1).astype(bf16)
    near_back = spread_narrow(back_rows)
    shard_rows = jnp.concatenate([near_back, swap(near_back, "core", 1)], 0)
    recon_part = shard_rows[:, :model_width]
    aux_back = shard_rows[:, model_width:]

    grad_dec = lax.dot_general(top_acts, recon_part, over_rows, preferred_element_type=f32)
    grad_dec = grad_dec + lax.dot_general(
        aux_acts, aux_back, over_rows, preferred_element_type=f32
    )
    grad_dec, recon_part, aux_back = lax.optimization_barrier((grad_dec, recon_part, aux_back))
    dec_grad = scatter_chips(grad_dec, 0)
    back_top = lax.dot_general(recon_part, dec_full, to_latents, preferred_element_type=f32)
    back_side = lax.dot_general(aux_back, dec_full, to_latents, preferred_element_type=f32)
    latent_grad = jnp.where(codes == 1.0, back_top, jnp.where(codes == 2.0, back_side, 0.0))
    latent_grad = latent_grad.astype(bf16)
    grad_enc = lax.dot_general(encoder_in, latent_grad, over_rows, preferred_element_type=f32)
    column_sum = jnp.sum(latent_grad, 0, dtype=f32)
    enc_grad, encb_grad = scatter_chips(grad_enc, 1, column_sum)
    bias_term = jnp.sum(back_rows[:, :model_width], 0, dtype=f32) - jnp.dot(
        enc_own.astype(f32), encb_grad, precision=HIGH_PRECISION
    )
    dec_moment_own = cols_to_latents(after(dec_moment, back_rows).astype(bf16))
    enc_moment_own = rows_to_latents(after(enc_moment, dec_moment_own).astype(bf16))

    def sum_gram(part, extra):
        half = model_width // 2
        rows = half // chips
        spare = jnp.zeros((14, model_width), bf16)

        def pack(block, vector):
            lines = [line[None] for line in split_bf(vector)]
            return jnp.concatenate([block.astype(bf16), *lines, spare], 0)

        def unpack(got):
            got = got.astype(f32)
            return got[:-16], got[-16] + got[-15]

        def block_of(value, index, count):
            return lax.dynamic_slice_in_dim(value, index * count, count, 0)

        vector = extra
        got, more = unpack(swap(pack(block_of(part, 1 - core_pos, half), vector), "core", 1))
        part, vector = block_of(part, core_pos, half) + got, vector + more
        total, sent_vector = block_of(part, chip_pos, rows), vector
        for k in range(1, chips):
            sent = pack(block_of(part, chip_pos ^ k, rows), sent_vector)
            got, more = unpack(swap(sent, "chip", k))
            total, vector = total + got, vector + more
        sent = pack(total, vector)
        for k in range(1, narrow_count):
            got, more = unpack(swap(sent, "narrow", k))
            total, vector = total + got, vector + more
        near = jnp.stack([total] + [swap(total, "chip", k) for k in range(1, chips)])
        return near, swap(near, "core", 1), vector

    dec_own_next = (MOMENTUM * dec_moment_own.astype(f32) + dec_grad).astype(bf16)
    dec_near, dec_far, _ = sum_gram(
        lax.dot_general(dec_own_next, dec_own_next, over_rows, preferred_element_type=f32),
        jnp.zeros((model_width,), f32),
    )
    dec_state = series_start(place, dec_near, dec_far)
    dec_rows_grad = latents_to_cols(after(dec_grad, enc_moment_own).astype(bf16))
    enc_own_next = (MOMENTUM * enc_moment_own.astype(f32) + enc_grad).astype(bf16)
    enc_near, enc_far, grad_decb = sum_gram(
        lax.dot_general(enc_own_next, enc_own_next, to_latents, preferred_element_type=f32),
        bias_term,
    )
    dec_factor = series_finish(dec_state)
    dec_ortho = latents_to_cols(
        jnp.dot(dec_own_next, dec_factor, preferred_element_type=f32).astype(bf16)
    )
    enc_rows_grad = latents_to_rows(after(enc_grad, dec_rows_grad).astype(bf16))
    enc_state = series_start(place, after(enc_near, dec_factor, dec_rows_grad), enc_far)
    enc_factor = series_finish(enc_state)
    enc_factor = after(enc_factor, enc_rows_grad)
    enc_ortho = latents_to_rows(
        jnp.dot(enc_factor, enc_own_next, preferred_element_type=f32).astype(bf16)
    )
    enc_next = MOMENTUM * enc_moment + enc_rows_grad.astype(f32)
    dec_next = MOMENTUM * dec_moment + dec_rows_grad.astype(f32)
    step_scale = MUON_RATE * 0.2 * math.sqrt(max(D, L))
    enc_new = enc_weight * (1.0 - MUON_RATE * DECAY) - step_scale * enc_ortho.astype(f32)
    dec_new = dec_weight * (1.0 - MUON_RATE * DECAY) - step_scale * dec_ortho.astype(f32)
    encb_new, encb_one, encb_two = adam_update(enc_bias, encb_grad, encb_first, encb_second)
    decb_new, decb_one, decb_two = adam_update(decoder_bias, grad_decb, decb_first, decb_second)
    return (
        token_loss,
        enc_new,
        enc_next,
        enc_new.astype(bf16),
        dec_new,
        dec_next,
        dec_new.astype(bf16),
        encb_new,
        encb_one,
        encb_two,
        decb_new,
        decb_one,
        decb_two,
    )


def solution(mesh):
    wide, narrow = mesh.devices.shape
    fine = Mesh(mesh.devices.reshape(wide // 2, 2, narrow), ("chip", "core", "narrow"))
    placed = (
        P(("chip", "core", "narrow")),
        P(("chip", "core", "narrow")),
        P(("chip", "core", "narrow"), None),
        P(("chip", "core", "narrow"), None),
        P(),
        P(("chip", "core"), None),
        P(),
        P(),
        P(),
        P(),
        P(),
        P(),
        P(),
        P("narrow", ("chip", "core")),
        P(("chip", "core", "narrow")),
        P(("chip", "core"), "narrow"),
        P(),
        P("narrow", ("chip", "core")),
        P(("chip", "core"), "narrow"),
        P(("chip", "core", "narrow")),
        P(("chip", "core", "narrow")),
        P(),
        P(),
    )
    return jax.shard_map(
        local,
        mesh=fine,
        in_specs=placed,
        out_specs=(
            P(("chip", "core", "narrow")),
            P("narrow", ("chip", "core")),
            P("narrow", ("chip", "core")),
            P("narrow", ("chip", "core")),
            P(("chip", "core"), "narrow"),
            P(("chip", "core"), "narrow"),
            P(("chip", "core"), "narrow"),
            P(("chip", "core", "narrow")),
            P(("chip", "core", "narrow")),
            P(("chip", "core", "narrow")),
            P(),
            P(),
            P(),
        ),
        check_vma=False,
    )
```

time: 939 us -> 939 us (level)
  waiting for transfers between devices: 359 us -> 262 us
  other arithmetic: 68.1 us -> 125 us
  starting transfers between devices: 107 us -> 154 us
  local copies, waits for them, and re-layouts: 70.2 us -> 99.7 us
  blocking collectives: 30.8 us -> 9.07 us
  between operations: 16.2 us -> 3.39 us
    ppermute x40 -> x62, waiting for transfers between devices: 175 us -> 235 us  [swap(): lax.ppermute(value, axis, [(spot, spot ^ offset) for spot in range(count)])]
    all_to_all x3 -> x0, waiting for transfers between devices: 53.8 us -> none  [the longest x1 41.3 us: local(): lax.all_to_all(column_sum.reshape(chips, own_latents), 'chip', 0, 0, tile...]
    ppermute x40 -> x62, starting transfers between devices: 52.1 us -> 98.2 us  [swap(): lax.ppermute(value, axis, [(spot, spot ^ offset) for spot in range(count)])]
    all_to_all x2, waiting for transfers between devices: 40.7 us -> 0.01 us  [rows_to_latents(): lax.all_to_all(value, 'narrow', split_axis=1, concat_axis=0, tiled=True)]
    all_to_all x2, waiting for transfers between devices: 62.6 us -> 26.3 us  [latents_to_rows(): lax.all_to_all(value, 'narrow', split_axis=0, concat_axis=1, tiled=True)]
    all_to_all x2, waiting for transfers between devices: 27.1 us -> 0.01 us  [cols_to_latents(): lax.all_to_all(value, 'narrow', split_axis=0, concat_axis=1, tiled=True)]
    all_to_all x1 -> x0, blocking collectives: 22 us -> none  [sum_gram(): chunks = lax.all_to_all(chunks, wide, 0, 0, tiled=True)]
    concatenate x8 -> x20, other arithmetic: 9.91 us -> 31.3 us  [the longest x4 8.22 us: gather_chips(): sent = sent[0] if len(sent) == 1 else jnp.concatenate(sent, axis)]
  transfers between devices with their start and end apart: 53 -> 70, of which waited for: 24 -> 21; matrix products, arithmetic and copies ran while one was open for 24% -> 25% of each run, Pallas kernels for 16% -> 16%
where the time goes in v3:
time: 939 us; the launch traced here: 933 us
  waiting for transfers between devices  262 us (28%)
  starting transfers between devices  154 us (16%)
  Pallas kernels  151 us (16%)
  matrix products  130 us (14%)
  other arithmetic  125 us (13%)
  local copies, waits for them, and re-layouts  99.7 us (11%)
    ppermute x62, waiting for transfers between devices, swap(): lax.ppermute(value, axis, [(spot, spot ^ offset) for spot in range(count)])  235 us
    ppermute x62, starting transfers between devices, swap(): lax.ppermute(value, axis, [(spot, spot ^ offset) for spot in range(count)])  98.2 us
    pallas_call x10, Pallas kernels, square_call(): pl.pallas_call(kernel, out_shape=[square] * outs, in_specs=specs, out_spe...  96.6 us
    pallas_call x2, Pallas kernels, kind_codes(): pl.pallas_call(functools.partial(code_kernel, shifts), grid=(row_total //...  54 us
    unnamed x194, local copies, waits for them, and re-layouts  38.5 us
    all_to_all x2, waiting for transfers between devices, latents_to_rows(): lax.all_to_all(value, 'narrow', split_axis=0, concat_axis=1, tiled=True)  26.3 us
  transfers between devices with their start and end apart: 70, of which 21 were waited for; matrix products, arithmetic and copies ran while one was open for 25% of the time, Pallas kernels for 16%

profile of v3, /device:TPU:0, one launch (start us, length us, event | category | flops | bytes accessed | tf_op | source)
XLA Modules:
  0.0 932.6 jit_solution(9711460174592238511)
XLA Ops:
  9.7 9.1 all-gather.1
  19.0 10.6 %gather_fusion = bf16[1024,768]{1,0:T(8,128)(2,1)} fusion(bf16[6288,768]{1,0:T(8,128)(2,1)} %param.28, s32[1024]{0:T(1024)S(1)} %broadcast_clamp_fusion), kind=kCustom, calls=%fused_computation | custom fusion | bytes 3149824 | tf_op jit(solution)/shard_map/jit(_take)/gather | solution.py:444
  60.8 27.0 %shard_map.318 = bf16[512,4096]{1,0:T(8,128)(2,1)S(1)} custom-call(s32[3]{0:T(128)S(1)} %copy-done.3, s32[512,544]{1,0:T(8,128)S(1)} %copy-done.2, s32[1,4096]{1,0:T(1,128)S(1)} %reshape.311.dead_ref), custom_call_target="tpu_custom_call" | custom-call | flops 10737418240 | bytes 4194304 | tf_op jit(solution)/shard_map/pallas_call | solution.py:284
  125.3 44.5 %collective-permute-done.9 = bf16[128,768]{1,0:T(8,128)(2,1)S(1)} collective-permute-done((bf16[128,768]{1,0:T(8,128)(2,1)S(1)}, bf16[128,768]{1,0:T(8,128)(2,1)S(1)}, u32[]{:S(2)}, u32[]{:S(2)}) %collective-permute-start.9) | collective-permute-done | bytes 196640 | tf_op jit(solution)/shard_map/ppermute | solution.py:367
  183.7 27.0 %shard_map.319 = bf16[512,4096]{1,0:T(8,128)(2,1)S(1)} custom-call(s32[3]{0:T(128)S(1)} %copy-done.4, s32[512,544]{1,0:T(8,128)S(1)} %copy.99.ids_ref, s32[1,4096]{1,0:T(1,128)S(1)} %reshape.311.dead_ref), custom_call_target="tpu_custom_call" | custom-call | flops 10737418240 | bytes 4194304 | tf_op jit(solution)/shard_map/pallas_call | solution.py:284
  242.7 15.7 %broadcast_select_fusion.1 = (bf16[1024,4096]{1,0:T(8,128)(2,1)}, bf16[1024,4096]{1,0:T(8,128)(2,1)}) fusion(bf16[512,4096]{1,0:T(8,128)(2,1)} %copy-done.8, bf16[512,4096]{1,0:T(8,128)(2,1)} %copy-done.6, f32[4096]{0:T(1024)S(1)} %bitcast.228, bf16[784,4096]{1,0:T(8,128)(2,1)} %slice_dynamic-update-slice_fusion, bf16[1024,768]{1,0:T(8,128)(2,1)S(1)} %copy-done.48, ...), kind=kOutput, calls=%fused_computation.19 | convolution fusion | flops 6490947584 | bytes 33049600 | tf_op jit(solution)/shard_map/dot_general | solution.py:494
  259.4 15.5 %collective-permute-done.17 = bf16[1024,768]{0,1:T(8,128)(2,1)} collective-permute-done((bf16[1024,768]{0,1:T(8,128)(2,1)}, bf16[1024,768]{0,1:T(8,128)(2,1)}, u32[]{:S(2)}, u32[]{:S(2)}) %collective-permute-start.17) | collective-permute-done | bytes 1572896 | tf_op jit(solution)/shard_map/ppermute | solution.py:367
  318.0 11.1 %collective-permute-done.26 = bf16[128,768]{1,0:T(8,128)(2,1)S(1)} collective-permute-done((bf16[128,768]{1,0:T(8,128)(2,1)S(1)}, bf16[128,768]{1,0:T(8,128)(2,1)S(1)}, u32[]{:S(2)}, u32[]{:S(2)}) %collective-permute-start.26) | collective-permute-done | bytes 196640 | tf_op jit(solution)/shard_map/ppermute | solution.py:367
  343.7 14.5 %collective-permute-done.28 = bf16[128,1536]{1,0:T(8,128)(2,1)S(1)} collective-permute-done((bf16[128,1536]{1,0:T(8,128)(2,1)S(1)}, bf16[128,1536]{1,0:T(8,128)(2,1)S(1)}, u32[]{:S(2)}, u32[]{:S(2)}) %collective-permute-start.28) | collective-permute-done | bytes 393248 | tf_op jit(solution)/shard_map/ppermute | solution.py:367
  358.2 11.0 %collective-permute-done.29 = bf16[128,1536]{1,0:T(8,128)(2,1)S(1)} collective-permute-done((bf16[128,1536]{1,0:T(8,128)(2,1)S(1)}, bf16[128,1536]{1,0:T(8,128)(2,1)S(1)}, u32[]{:S(2)}, u32[]{:S(2)}) %collective-permute-start.29) | collective-permute-done | bytes 393248 | tf_op jit(solution)/shard_map/ppermute | solution.py:367
  372.9 13.0 %fusion.108 = f32[4096,768]{1,0:T(8,128)} fusion(bf16[1024,4096]{1,0:T(8,128)(2,1)} %get-tuple-element.132, bf16[1024,1536]{1,0:T(8,128)(2,1)S(1)} %constant_dynamic-update-slice_fusion.23), kind=kOutput, calls=%fused_computation.326 | convolution fusion | flops 6442450944 | bytes 22544384 | tf_op jit(solution)/shard_map/dot_general | solution.py:533
  387.3 16.1 %convolution_add_fusion = f32[4096,768]{1,0:T(8,128)} fusion(f32[4096,768]{1,0:T(8,128)} %fusion.108, bf16[1024,4096]{1,0:T(8,128)(2,1)} %get-tuple-element.131, bf16[1024,1536]{1,0:T(8,128)(2,1)S(1)} %constant_dynamic-update-slice_fusion.23), kind=kOutput, calls=%fused_computation.6 | convolution fusion | flops 6445596672 | bytes 35127296 | tf_op jit(solution)/shard_map/dot_general | solution.py:532
  403.3 8.9 fusion.141
  412.3 15.7 %convert_reduce_fusion = (f32[4096]{0:T(1024)S(1)}, bf16[1024,4096]{1,0:T(8,128)(2,1)}) fusion(bf16[1024,4096]{1,0:T(8,128)(2,1)} %fusion.141, bf16[1024,768]{1,0:T(8,128)(2,1)S(1)} %copy-done.50, bf16[4096,768]{0,1:T(8,128)(2,1)} %slice_dynamic-update-slice_fusion.2, bf16[512,4096]{1,0:T(8,128)(2,1)} %copy-done.8, bf16[512,4096]{1,0:T(8,128)(2,1)S(1)} %copy-done.7), kind=kOutput, calls=%fused_computation.2 | convolution fusion | flops 6488584192 | bytes 33046528 | tf_op jit(solution)/shard_map/dot_general | solution.py:538
  428.0 12.8 %fusion.140 = (bf16[768,4096]{1,0:T(8,128)(2,1)S(1)}, f32[768,4096]{1,0:T(8,128)}) fusion(bf16[1024,4096]{1,0:T(8,128)(2,1)} %get-tuple-element.203, bf16[1024,768]{1,0:T(8,128)(2,1)S(1)} %copy-done.48, f32[768]{0:T(1024)S(1)} %copy-done.62), kind=kOutput, calls=%fused_computation.350 | convolution fusion | flops 6447955968 | bytes 28838912 | tf_op jit(solution)/shard_map/dot_general | solution.py:542
  458.1 10.3 %all-to-all-start.2 = ((bf16[4,1024,192]{1,2,0:T(8,128)(2,1)}), bf16[4,1024,192]{1,2,0:T(8,128)(2,1)S(1)}, u32[]{:S(2)}, u32[]{:S(2)}) async-start(bf16[4,1024,192]{1,2,0:T(8,128)(2,1)} %bitcast.180), calls=%async_computation.2 | async-start | bytes 3145728 | tf_op jit(solution)/shard_map/all_to_all | solution.py:377
  473.8 41.2 %collective-permute-done.46 = bf16[1024,768]{1,0:T(8,128)(2,1)} collective-permute-done((bf16[1024,768]{1,0:T(8,128)(2,1)}, bf16[1024,768]{1,0:T(8,128)(2,1)}, u32[]{:S(2)}, u32[]{:S(2)}) %collective-permute-start.46) | collective-permute-done | bytes 1572896 | tf_op jit(solution)/shard_map/ppermute | solution.py:367
  534.3 10.5 %all-to-all-start.3 = ((bf16[192,4,1024]{2,0,1:T(8,128)(2,1)}), bf16[192,4,1024]{2,0,1:T(8,128)(2,1)}, u32[]{:S(2)}, u32[]{:S(2)}) async-start(bf16[192,4,1024]{2,0,1:T(8,128)(2,1)} %bitcast.179), calls=%async_computation.3 | async-start | bytes 3145728 | tf_op jit(solution)/shard_map/all_to_all | solution.py:374
  546.7 30.0 %collective-permute-done.47 = bf16[512,768]{1,0:T(8,128)(2,1)} collective-permute-done((bf16[512,768]{1,0:T(8,128)(2,1)}, bf16[512,768]{1,0:T(8,128)(2,1)}, u32[]{:S(2)}, u32[]{:S(2)}) %collective-permute-start.47) | collective-permute-done | bytes 786464 | tf_op jit(solution)/shard_map/ppermute | solution.py:367
  583.2 9.0 collective-permute-done.33
  653.7 10.4 %all-to-all-start.4 = ((bf16[1024,4,192]{0,2,1:T(8,128)(2,1)}), bf16[1024,4,192]{0,2,1:T(8,128)(2,1)}, u32[]{:S(2)}, u32[]{:S(2)}) async-start(bf16[1024,4,192]{0,2,1:T(8,128)(2,1)} %bitcast.66), calls=%async_computation.4 | async-start | bytes 3145728 | tf_op jit(solution)/shard_map/all_to_all | solution.py:383
  698.9 21.5 %collective-permute-start.54 = (bf16[112,768]{1,0:T(8,128)(2,1)S(1)}, bf16[112,768]{1,0:T(8,128)(2,1)S(1)}, u32[]{:S(2)}, u32[]{:S(2)}) collective-permute-start(bf16[112,768]{1,0:T(8,128)(2,1)S(1)} %get-tuple-element.181), channel_id=1, source_target_pairs={{0,1},{1,0},{2,3},{3,2},{4,5},{5,4},{6,7},{7,6},{8,9},{9,8},{10,11... | collective-permute-start | bytes 516104 | tf_op jit(solution)/shard_map/ppermute | solution.py:367
  744.2 9.7 %collective-permute-done.58 = f32[96,768]{1,0:T(8,128)S(1)} collective-permute-done((f32[96,768]{1,0:T(8,128)S(1)}, f32[96,768]{1,0:T(8,128)S(1)}, u32[]{:S(2)}, u32[]{:S(2)}) %collective-permute-start.58) | collective-permute-done | bytes 294944 | tf_op jit(solution)/shard_map/ppermute | solution.py:367
  767.6 11.3 %shard_map.320 = (bf16[768,768]{1,0:T(8,128)(2,1)S(1)}, bf16[768,768]{1,0:T(8,128)(2,1)S(1)}, bf16[768,768]{1,0:T(8,128)(2,1)S(1)}) custom-call(s32[3]{0:T(128)S(1)} %copy-done.5, f32[4,96,768]{2,1,0:T(8,128)S(1)} %pad_maximum_fusion.10.near_ref, f32[4,96,768]{2,1,0:T(8,128)S(1)} %collective-permute-done.60.far_ref), custom_call_target="tpu_custom_call" | custom-call | flops 7247757312 | bytes 7077888 | tf_op jit(solution)/shard_map/pallas_call | solution.py:194
  779.0 9.8 %shard_map.321 = (bf16[768,768]{1,0:T(8,128)(2,1)S(1)}, bf16[768,768]{1,0:T(8,128)(2,1)S(1)}, bf16[768,768]{1,0:T(8,128)(2,1)S(1)}) custom-call(bf16[768,768]{1,0:T(8,128)(2,1)S(1)} %get-tuple-element.61.g_hi, bf16[768,768]{1,0:T(8,128)(2,1)S(1)} %get-tuple-element.62.g_lo, bf16[768,768]{1,0:T(8,128)(2,1)S(1)} %get-tuple-element.63.q_ref), custom_call_target="tpu_custom_call" | custom-call | flops 7247757312 | bytes 7077888 | tf_op jit(solution)/shard_map/pallas_call | solution.py:194
  788.8 9.8 %shard_map.322 = (bf16[768,768]{1,0:T(8,128)(2,1)S(1)}, bf16[768,768]{1,0:T(8,128)(2,1)S(1)}, bf16[768,768]{1,0:T(8,128)(2,1)S(1)}) custom-call(bf16[768,768]{1,0:T(8,128)(2,1)S(1)} %get-tuple-element.64.g_hi, bf16[768,768]{1,0:T(8,128)(2,1)S(1)} %get-tuple-element.65.g_lo, bf16[768,768]{1,0:T(8,128)(2,1)S(1)} %get-tuple-element.66.q_ref), custom_call_target="tpu_custom_call" | custom-call | flops 7247757312 | bytes 7077888 | tf_op jit(solution)/shard_map/pallas_call | solution.py:194
  798.6 11.7 %shard_map.323 = (bf16[768,768]{1,0:T(8,128)(2,1)S(1)}, bf16[768,768]{1,0:T(8,128)(2,1)S(1)}, bf16[768,768]{1,0:T(8,128)(2,1)S(1)}) custom-call(bf16[768,768]{1,0:T(8,128)(2,1)S(1)} %get-tuple-element.67.g_hi, bf16[768,768]{1,0:T(8,128)(2,1)S(1)} %get-tuple-element.68.g_lo, bf16[768,768]{1,0:T(8,128)(2,1)S(1)} %get-tuple-element.69.q_ref), custom_call_target="tpu_custom_call" | custom-call | flops 9059696640 | bytes 7077888 | tf_op jit(solution)/shard_map/pallas_call | solution.py:194
  818.2 12.4 %shard_map.325 = (bf16[768,768]{1,0:T(8,128)(2,1)S(1)}, bf16[768,768]{1,0:T(8,128)(2,1)S(1)}, bf16[768,768]{1,0:T(8,128)(2,1)S(1)}) custom-call(s32[3]{0:T(128)S(1)} %copy-done.5, f32[4,96,768]{2,1,0:T(8,128)} %pad_maximum_fusion.9.near_ref, f32[4,96,768]{2,1,0:T(8,128)} %collective-permute-done.61.far_ref), custom_call_target="tpu_custom_call" | custom-call | flops 7247757312 | bytes 7077888 | tf_op jit(solution)/shard_map/pallas_call | solution.py:194
  840.3 9.8 %shard_map.326 = (bf16[768,768]{1,0:T(8,128)(2,1)S(1)}, bf16[768,768]{1,0:T(8,128)(2,1)S(1)}, bf16[768,768]{1,0:T(8,128)(2,1)S(1)}) custom-call(bf16[768,768]{1,0:T(8,128)(2,1)S(1)} %copy-done.10, bf16[768,768]{1,0:T(8,128)(2,1)S(1)} %copy-done.12, bf16[768,768]{1,0:T(8,128)(2,1)S(1)} %copy-done.14), custom_call_target="tpu_custom_call" | custom-call | flops 7247757312 | bytes 7077888 | tf_op jit(solution)/shard_map/pallas_call | solution.py:194
  850.1 9.8 %shard_map.327 = (bf16[768,768]{1,0:T(8,128)(2,1)S(1)}, bf16[768,768]{1,0:T(8,128)(2,1)S(1)}, bf16[768,768]{1,0:T(8,128)(2,1)S(1)}) custom-call(bf16[768,768]{1,0:T(8,128)(2,1)S(1)} %get-tuple-element.78.g_hi, bf16[768,768]{1,0:T(8,128)(2,1)S(1)} %get-tuple-element.79.g_lo, bf16[768,768]{1,0:T(8,128)(2,1)S(1)} %get-tuple-element.80.q_ref), custom_call_target="tpu_custom_call" | custom-call | flops 7247757312 | bytes 7077888 | tf_op jit(solution)/shard_map/pallas_call | solution.py:194
  859.9 11.7 %shard_map.328 = (bf16[768,768]{1,0:T(8,128)(2,1)S(1)}, bf16[768,768]{1,0:T(8,128)(2,1)S(1)}, bf16[768,768]{1,0:T(8,128)(2,1)S(1)}) custom-call(bf16[768,768]{1,0:T(8,128)(2,1)S(1)} %get-tuple-element.81.g_hi, bf16[768,768]{1,0:T(8,128)(2,1)S(1)} %get-tuple-element.82.g_lo, bf16[768,768]{1,0:T(8,128)(2,1)S(1)} %get-tuple-element.83.q_ref), custom_call_target="tpu_custom_call" | custom-call | flops 9059696640 | bytes 7077888 | tf_op jit(solution)/shard_map/pallas_call | solution.py:194
  899.2 26.3 %all-to-all-done.6 = bf16[4,192,1024]{2,1,0:T(8,128)(2,1)} async-done(((bf16[4,192,1024]{2,1,0:T(8,128)(2,1)}), bf16[4,192,1024]{2,1,0:T(8,128)(2,1)}, u32[]{:S(2)}, u32[]{:S(2)}) %all-to-all-start.6) | async-done | bytes 1572896 | tf_op jit(solution)/shard_map/all_to_all | solution.py:380
  (519 shorter events, 421.6 us)
Async XLA Ops:
  4.1 46.3 %collective-permute-start.6 = (s32[128,544]{1,0:T(8,128)}, s32[128,544]{1,0:T(8,128)}, u32[]{:S(2)}, u32[]{:S(2)}) collective-permute-start(s32[128,544]{1,0:T(8,128)} %pad_add_fusion.1), channel_id=1, source_target_pairs={{0,3},{1,2},{2,1},{3,0},{4,7},{5,6},{6,5},{7,4},{8,11},{9,10},{10,... | collective-permute-start | bytes 835592 | tf_op jit(solution)/shard_map/ppermute | solution.py:367
  9.1 41.3 %collective-permute-start.5 = (s32[128,544]{1,0:T(8,128)}, s32[128,544]{1,0:T(8,128)}, u32[]{:S(2)}, u32[]{:S(2)}) collective-permute-start(s32[128,544]{1,0:T(8,128)} %pad_add_fusion.1), channel_id=1, source_target_pairs={{0,2},{1,3},{2,0},{3,1},{4,6},{5,7},{6,4},{7,5},{8,10},{9,11},{10,... | collective-permute-start | bytes 835592 | tf_op jit(solution)/shard_map/ppermute | solution.py:367
  9.1 41.3 %collective-permute-start.4 = (s32[128,544]{1,0:T(8,128)}, s32[128,544]{1,0:T(8,128)}, u32[]{:S(2)}, u32[]{:S(2)}) collective-permute-start(s32[128,544]{1,0:T(8,128)} %pad_add_fusion.1), channel_id=1, source_target_pairs={{0,1},{1,0},{2,3},{3,2},{4,5},{5,4},{6,7},{7,6},{8,9},{9,8},{10,11... | collective-permute-start | bytes 835592 | tf_op jit(solution)/shard_map/ppermute | solution.py:367
  34.5 74.6 %all-to-all-start = ((bf16[192,4,1024]{2,0,1:T(8,128)(2,1)}), bf16[192,4,1024]{2,0,1:T(8,128)(2,1)}, u32[]{:S(2)}, u32[]{:S(2)}) async-start(bf16[192,4,1024]{2,0,1:T(8,128)(2,1)} %bitcast.194), calls=%async_computation | async-start | bytes 3145728 | tf_op jit(solution)/shard_map/all_to_all | solution.py:374
  55.6 119.1 %collective-permute-start.7 = (s32[512,544]{0,1:T(8,128)}, s32[512,544]{0,1:T(8,128)}, u32[]{:S(2)}, u32[]{:S(2)}) collective-permute-start(s32[512,544]{0,1:T(8,128)} %copy.98), channel_id=1, source_target_pairs={{0,4},{4,0},{1,5},{5,1},{2,6},{6,2},{3,7},{7,3},{8,12},{12,8},{9,1... | collective-permute-start | bytes 3342344 | tf_op jit(solution)/shard_map/ppermute | solution.py:367
  112.9 63.5 %collective-permute-start.12 = (bf16[784,512]{1,0:T(8,128)(2,1)}, bf16[784,512]{1,0:T(8,128)(2,1)}, u32[]{:S(2)}, u32[]{:S(2)}) collective-permute-start(bf16[784,512]{1,0:T(8,128)(2,1)} %get-tuple-element.145), channel_id=1, source_target_pairs={{0,8},{8,0},{16,24},{24,16},{1,9},{9,1},{17,25},{25,17},{2,10},{10... | collective-permute-start | bytes 2408456 | tf_op jit(solution)/shard_map/ppermute | solution.py:367
  115.7 101.5 %all-to-all-start.1 = ((bf16[4,1024,192]{1,2,0:T(8,128)(2,1)}), bf16[4,1024,192]{1,2,0:T(8,128)(2,1)S(1)}, u32[]{:S(2)}, u32[]{:S(2)}) async-start(bf16[4,1024,192]{1,2,0:T(8,128)(2,1)} %bitcast.181), calls=%async_computation.1 | async-start | bytes 3145728 | tf_op jit(solution)/shard_map/all_to_all | solution.py:377
  119.6 50.2 %collective-permute-start.9 = (bf16[128,768]{1,0:T(8,128)(2,1)S(1)}, bf16[128,768]{1,0:T(8,128)(2,1)S(1)}, u32[]{:S(2)}, u32[]{:S(2)}) collective-permute-start(bf16[128,768]{1,0:T(8,128)(2,1)S(1)} %get-tuple-element.197), channel_id=1, source_target_pairs={{0,2},{1,3},{2,0},{3,1},{4,6},{5,7},{6,4},{7,5},{8,10},{9,11},{10,... | collective-permute-start | bytes 589832 | tf_op jit(solution)/shard_map/ppermute | solution.py:367
  122.6 47.2 %collective-permute-start.10 = (bf16[128,768]{1,0:T(8,128)(2,1)S(1)}, bf16[128,768]{1,0:T(8,128)(2,1)S(1)}, u32[]{:S(2)}, u32[]{:S(2)}) collective-permute-start(bf16[128,768]{1,0:T(8,128)(2,1)S(1)} %get-tuple-element.197), channel_id=1, source_target_pairs={{0,3},{1,2},{2,1},{3,0},{4,7},{5,6},{6,5},{7,4},{8,11},{9,10},{10,... | collective-permute-start | bytes 589832 | tf_op jit(solution)/shard_map/ppermute | solution.py:367
  124.0 56.4 %collective-permute-start.14 = (bf16[784,512]{1,0:T(8,128)(2,1)}, bf16[784,512]{1,0:T(8,128)(2,1)}, u32[]{:S(2)}, u32[]{:S(2)}) collective-permute-start(bf16[784,512]{1,0:T(8,128)(2,1)} %get-tuple-element.143), channel_id=1, source_target_pairs={{0,16},{8,24},{16,0},{24,8},{1,17},{9,25},{17,1},{25,9},{2,18},{10... | collective-permute-start | bytes 2408456 | tf_op jit(solution)/shard_map/ppermute | solution.py:367
  171.7 41.1 %collective-permute-start.11 = (bf16[512,768]{1,0:T(8,128)(2,1)}, bf16[512,768]{1,0:T(8,128)(2,1)}, u32[]{:S(2)}, u32[]{:S(2)}) collective-permute-start(bf16[512,768]{1,0:T(8,128)(2,1)} %pad_maximum_fusion.13), channel_id=1, source_target_pairs={{0,4},{4,0},{1,5},{5,1},{2,6},{6,2},{3,7},{7,3},{8,12},{12,8},{9,1... | collective-permute-start | bytes 2359304 | tf_op jit(solution)/shard_map/ppermute | solution.py:367
  179.1 41.4 %collective-permute-start.13 = (bf16[784,1024]{1,0:T(8,128)(2,1)}, bf16[784,1024]{1,0:T(8,128)(2,1)}, u32[]{:S(2)}, u32[]{:S(2)}) collective-permute-start(bf16[784,1024]{1,0:T(8,128)(2,1)} %pad_maximum_fusion.3), channel_id=1, source_target_pairs={{0,16},{8,24},{16,0},{24,8},{1,17},{9,25},{17,1},{25,9},{2,18},{10... | collective-permute-start | bytes 4816904 | tf_op jit(solution)/shard_map/ppermute | solution.py:367
  183.2 41.1 %collective-permute-start.15 = (bf16[784,1024]{1,0:T(8,128)(2,1)}, bf16[784,1024]{1,0:T(8,128)(2,1)}, u32[]{:S(2)}, u32[]{:S(2)}) collective-permute-start(bf16[784,1024]{1,0:T(8,128)(2,1)} %pad_maximum_fusion.4), channel_id=1, source_target_pairs={{0,8},{8,0},{16,24},{24,16},{1,9},{9,1},{17,25},{25,17},{2,10},{10... | collective-permute-start | bytes 4816904 | tf_op jit(solution)/shard_map/ppermute | solution.py:367
  239.2 35.7 %collective-permute-start.17 = (bf16[1024,768]{0,1:T(8,128)(2,1)}, bf16[1024,768]{0,1:T(8,128)(2,1)}, u32[]{:S(2)}, u32[]{:S(2)}) collective-permute-start(bf16[1024,768]{0,1:T(8,128)(2,1)} %pad_maximum_fusion.5), channel_id=1, source_target_pairs={{0,16},{8,24},{16,0},{24,8},{1,17},{9,25},{17,1},{25,9},{2,18},{10... | collective-permute-start | bytes 4718600 | tf_op jit(solution)/shard_map/ppermute | solution.py:367
  242.0 36.6 %collective-permute-start.19 = (bf16[1024,768]{0,1:T(8,128)(2,1)}, bf16[1024,768]{0,1:T(8,128)(2,1)S(1)}, u32[]{:S(2)}, u32[]{:S(2)}) collective-permute-start(bf16[1024,768]{0,1:T(8,128)(2,1)} %pad_maximum_fusion.6), channel_id=1, source_target_pairs={{0,8},{8,0},{16,24},{24,16},{1,9},{9,1},{17,25},{25,17},{2,10},{10... | collective-permute-start | bytes 4718600 | tf_op jit(solution)/shard_map/ppermute | solution.py:367
  443.9 72.8 %collective-permute-start.32 = (bf16[784,1024]{1,0:T(8,128)(2,1)}, bf16[784,1024]{1,0:T(8,128)(2,1)}, u32[]{:S(2)}, u32[]{:S(2)}) collective-permute-start(bf16[784,1024]{1,0:T(8,128)(2,1)} %maximum_maximum_fusion.1), channel_id=1, source_target_pairs={{0,16},{8,24},{16,0},{24,8},{1,17},{9,25},{17,1},{25,9},{2,18},{10... | collective-permute-start | bytes 4816904 | tf_op jit(solution)/shard_map/ppermute | solution.py:367
  456.1 59.0 %collective-permute-start.46 = (bf16[1024,768]{1,0:T(8,128)(2,1)}, bf16[1024,768]{1,0:T(8,128)(2,1)}, u32[]{:S(2)}, u32[]{:S(2)}) collective-permute-start(bf16[1024,768]{1,0:T(8,128)(2,1)} %slice.537), channel_id=1, source_target_pairs={{0,16},{8,24},{16,0},{24,8},{1,17},{9,25},{17,1},{25,9},{2,18},{10... | collective-permute-start | bytes 4718600 | tf_op jit(solution)/shard_map/ppermute | solution.py:367
  458.1 72.2 %all-to-all-start.2 = ((bf16[4,1024,192]{1,2,0:T(8,128)(2,1)}), bf16[4,1024,192]{1,2,0:T(8,128)(2,1)S(1)}, u32[]{:S(2)}, u32[]{:S(2)}) async-start(bf16[4,1024,192]{1,2,0:T(8,128)(2,1)} %bitcast.180), calls=%async_computation.2 | async-start | bytes 3145728 | tf_op jit(solution)/shard_map/all_to_all | solution.py:377
  471.1 73.8 %collective-permute-start.48 = (bf16[1024,768]{1,0:T(8,128)(2,1)}, bf16[1024,768]{1,0:T(8,128)(2,1)}, u32[]{:S(2)}, u32[]{:S(2)}) collective-permute-start(bf16[1024,768]{1,0:T(8,128)(2,1)} %pad_maximum_fusion.8), channel_id=1, source_target_pairs={{0,8},{8,0},{16,24},{24,16},{1,9},{9,1},{17,25},{25,17},{2,10},{10... | collective-permute-start | bytes 4718600 | tf_op jit(solution)/shard_map/ppermute | solution.py:367
  521.5 72.0 %collective-permute-start.34 = (bf16[784,1024]{1,0:T(8,128)(2,1)}, bf16[784,1024]{1,0:T(8,128)(2,1)}, u32[]{:S(2)}, u32[]{:S(2)}) collective-permute-start(bf16[784,1024]{1,0:T(8,128)(2,1)} %maximum_maximum_fusion.2), channel_id=1, source_target_pairs={{0,8},{8,0},{16,24},{24,16},{1,9},{9,1},{17,25},{25,17},{2,10},{10... | collective-permute-start | bytes 4816904 | tf_op jit(solution)/shard_map/ppermute | solution.py:367
  525.5 51.3 %collective-permute-start.47 = (bf16[512,768]{1,0:T(8,128)(2,1)}, bf16[512,768]{1,0:T(8,128)(2,1)}, u32[]{:S(2)}, u32[]{:S(2)}) collective-permute-start(bf16[512,768]{1,0:T(8,128)(2,1)} %fusion.25), channel_id=1, source_target_pairs={{0,8},{8,0},{16,24},{24,16},{1,9},{9,1},{17,25},{25,17},{2,10},{10... | collective-permute-start | bytes 2359304 | tf_op jit(solution)/shard_map/ppermute | solution.py:367
  528.8 63.4 %collective-permute-start.33 = (bf16[784,512]{1,0:T(8,128)(2,1)}, bf16[784,512]{1,0:T(8,128)(2,1)}, u32[]{:S(2)}, u32[]{:S(2)}) collective-permute-start(bf16[784,512]{1,0:T(8,128)(2,1)} %maximum_maximum_fusion.3), channel_id=1, source_target_pairs={{0,8},{8,0},{16,24},{24,16},{1,9},{9,1},{17,25},{25,17},{2,10},{10... | collective-permute-start | bytes 2408456 | tf_op jit(solution)/shard_map/ppermute | solution.py:367
  534.3 90.3 %all-to-all-start.3 = ((bf16[192,4,1024]{2,0,1:T(8,128)(2,1)}), bf16[192,4,1024]{2,0,1:T(8,128)(2,1)}, u32[]{:S(2)}, u32[]{:S(2)}) async-start(bf16[192,4,1024]{2,0,1:T(8,128)(2,1)} %bitcast.179), calls=%async_computation.3 | async-start | bytes 3145728 | tf_op jit(solution)/shard_map/all_to_all | solution.py:374
  653.7 102.1 %all-to-all-start.4 = ((bf16[1024,4,192]{0,2,1:T(8,128)(2,1)}), bf16[1024,4,192]{0,2,1:T(8,128)(2,1)}, u32[]{:S(2)}, u32[]{:S(2)}) async-start(bf16[1024,4,192]{0,2,1:T(8,128)(2,1)} %bitcast.66), calls=%async_computation.4 | async-start | bytes 3145728 | tf_op jit(solution)/shard_map/all_to_all | solution.py:383
  680.8 42.7 %collective-permute-start.41 = (bf16[112,768]{1,0:T(8,128)(2,1)}, bf16[112,768]{1,0:T(8,128)(2,1)}, u32[]{:S(2)}, u32[]{:S(2)}) collective-permute-start(bf16[112,768]{1,0:T(8,128)(2,1)} %get-tuple-element.182), channel_id=1, source_target_pairs={{0,2},{1,3},{2,0},{3,1},{4,6},{5,7},{6,4},{7,5},{8,10},{9,11},{10,... | collective-permute-start | bytes 516104 | tf_op jit(solution)/shard_map/ppermute | solution.py:367
  681.2 43.3 %collective-permute-start.40 = (bf16[112,768]{1,0:T(8,128)(2,1)}, bf16[112,768]{1,0:T(8,128)(2,1)}, u32[]{:S(2)}, u32[]{:S(2)}) collective-permute-start(bf16[112,768]{1,0:T(8,128)(2,1)} %get-tuple-element.182), channel_id=1, source_target_pairs={{0,1},{1,0},{2,3},{3,2},{4,5},{5,4},{6,7},{7,6},{8,9},{9,8},{10,11... | collective-permute-start | bytes 516104 | tf_op jit(solution)/shard_map/ppermute | solution.py:367
  686.5 41.8 %collective-permute-start.56 = (bf16[112,768]{1,0:T(8,128)(2,1)S(1)}, bf16[112,768]{1,0:T(8,128)(2,1)S(1)}, u32[]{:S(2)}, u32[]{:S(2)}) collective-permute-start(bf16[112,768]{1,0:T(8,128)(2,1)S(1)} %get-tuple-element.181), channel_id=1, source_target_pairs={{0,3},{1,2},{2,1},{3,0},{4,7},{5,6},{6,5},{7,4},{8,11},{9,10},{10,... | collective-permute-start | bytes 516104 | tf_op jit(solution)/shard_map/ppermute | solution.py:367
  690.1 40.5 %collective-permute-start.55 = (bf16[112,768]{1,0:T(8,128)(2,1)S(1)}, bf16[112,768]{1,0:T(8,128)(2,1)S(1)}, u32[]{:S(2)}, u32[]{:S(2)}) collective-permute-start(bf16[112,768]{1,0:T(8,128)(2,1)S(1)} %get-tuple-element.181), channel_id=1, source_target_pairs={{0,2},{1,3},{2,0},{3,1},{4,6},{5,7},{6,4},{7,5},{8,10},{9,11},{10,... | collective-permute-start | bytes 516104 | tf_op jit(solution)/shard_map/ppermute | solution.py:367
  755.3 62.9 %collective-permute-start.61 = (f32[4,96,768]{2,1,0:T(8,128)}, f32[4,96,768]{2,1,0:T(8,128)}, u32[]{:S(2)}, u32[]{:S(2)}) collective-permute-start(f32[4,96,768]{2,1,0:T(8,128)} %pad_maximum_fusion.9.near_ref), channel_id=1, source_target_pairs={{0,4},{4,0},{1,5},{5,1},{2,6},{6,2},{3,7},{7,3},{8,12},{12,8},{9,1... | collective-permute-start | bytes 3538952 | tf_op jit(solution)/shard_map/ppermute | solution.py:367
  758.5 75.3 %all-to-all-start.5 = ((bf16[4,192,1024]{2,1,0:T(8,128)(2,1)}), bf16[4,192,1024]{2,1,0:T(8,128)(2,1)}, u32[]{:S(2)}, u32[]{:S(2)}) async-start(bf16[4,192,1024]{2,1,0:T(8,128)(2,1)} %bitcast.195), calls=%async_computation.5 | async-start | bytes 3145728 | tf_op jit(solution)/shard_map/all_to_all | solution.py:380
  833.8 49.6 %all-to-all-start.7 = ((bf16[1024,4,192]{0,2,1:T(8,128)(2,1)}), bf16[1024,4,192]{0,2,1:T(8,128)(2,1)}, u32[]{:S(2)}, u32[]{:S(2)}) async-start(bf16[1024,4,192]{0,2,1:T(8,128)(2,1)} %bitcast.208), calls=%async_computation.7 | async-start | bytes 3145728 | tf_op jit(solution)/shard_map/all_to_all | solution.py:383
  883.5 42.0 %all-to-all-start.6 = ((bf16[4,192,1024]{2,1,0:T(8,128)(2,1)}), bf16[4,192,1024]{2,1,0:T(8,128)(2,1)}, u32[]{:S(2)}, u32[]{:S(2)}) async-start(bf16[4,192,1024]{2,1,0:T(8,128)(2,1)} %bitcast.209), calls=%async_computation.6 | async-start | bytes 3145728 | tf_op jit(solution)/shard_map/all_to_all | solution.py:380
  (123 other events, 1610.5 us)

commit v4 on v3

--- a/solution.py
+++ b/solution.py
@@ -209,16 +209,16 @@
     return square_call(first_kernel, 3, [jnp.float32] + [bf16] * 6, 8, place, near, far)
 
 
-def series_finish(state):
+def series_next(step, state):
     bf16 = jnp.bfloat16
-    for step in range(1, NS_STEPS - 1):
-        kernel = functools.partial(middle_kernel, step)
-        state = square_call(kernel, 3, [bf16] * 4, 8 if step < 3 else 10, *state)
-    return square_call(last_kernel, 1, [bf16] * 2, 4, *state)[0]
+    if step == NS_STEPS - 1:
+        return square_call(last_kernel, 1, [bf16] * 2, 4, *state)
+    kernel = functools.partial(middle_kernel, step)
+    return square_call(kernel, 3, [bf16] * 4, 8 if step < 3 else 10, *state)
 
 
 def code_kernel(shifts, place_ref, ids_ref, dead_ref, out_ref, high, low, stage):
-    wide_shift, own_shift, top_count = shifts
+    wide_shift, own_shift, top_count, orders = shifts
     batch, groups = stage.shape[:2]
     rows, picks = ids_ref.shape
     bf16, f32 = jnp.bfloat16, jnp.float32
@@ -234,9 +234,17 @@
     )
     inner = jnp.bitwise_and(within, (1 << own_shift) - 1)
     offset = jnp.bitwise_xor(lax.shift_right_logical(owner, 1), chip)
+    half = lax.shift_right_logical(inner, half_shift)
+    spots = []
+    for order in orders:
+        spot = jnp.zeros_like(offset)
+        for index, bit in enumerate(order[:-1]):
+            spot = spot + jnp.where(jnp.bitwise_and(offset, bit) != 0, 1 << index, 0)
+        sent = jnp.where(jnp.bitwise_and(offset, order[-1]) != 0, latent_count // 4, 0)
+        spots.append(sent + lax.shift_left(spot, half_shift))
     column = (
-        lax.shift_right_logical(inner, half_shift) * (latent_count // 2)
-        + lax.shift_left(offset, half_shift)
+        half * (latent_count // 2)
+        + jnp.where(half == 0, spots[0], spots[1])
         + jnp.bitwise_and(inner, (1 << half_shift) - 1)
     )
     high[...] = jnp.where(mine, lax.shift_right_logical(column, 7), -1).astype(f32)
@@ -276,11 +284,11 @@
     lax.fori_loop(0, rows // batch, one_batch, 0)
 
 
-def kind_codes(place, ids, dead_here, wide_latents, own_latents, top_count):
+def kind_codes(place, ids, dead_here, wide_latents, own_latents, top_count, orders):
     row_total, pick_total = ids.shape
     latent_count = dead_here.shape[1]
     rows = min(128, row_total)
-    shifts = (wide_latents.bit_length() - 1, own_latents.bit_length() - 1, top_count)
+    shifts = (wide_latents.bit_length() - 1, own_latents.bit_length() - 1, top_count, orders)
     return pl.pallas_call(
         functools.partial(code_kernel, shifts),
         grid=(row_total // rows,),
@@ -303,6 +311,227 @@
             transcendentals=0,
         ),
     )(place, ids, dead_here)
+
+
+def pick_copy(step, count, sources, target):
+    for index, source in enumerate(sources):
+
+        @pl.when(step // count == index)
+        def _(source=source):
+            target[...] = source[...]
+
+
+def forward_kernel(count, x_ref, codes_ref, *refs):
+    encs, decs = refs[:4], refs[4:8]
+    top_ref, aux_ref, far_ref, near_ref = refs[8:12]
+    enc, dec, acc_top, acc_aux = refs[12:]
+    step = pl.program_id(0)
+    rows_all, width = x_ref.shape
+    block = min(1024, rows_all)
+    pick_copy(step, count, encs, enc)
+    pick_copy(step, count, decs, dec)
+
+    @pl.when(step == 0)
+    def _():
+        acc_top[...] = jnp.zeros_like(acc_top)
+        acc_aux[...] = jnp.zeros_like(acc_aux)
+
+    bias = enc[pl.ds(width, 16), :].astype(jnp.float32)[:1]
+
+    def one(index, carry):
+        rows = pl.ds(pl.multiple_of(index * block, block), block)
+        pre = (dot_f32(x_ref[rows, :], enc[pl.ds(0, width), :]) + bias).astype(jnp.bfloat16)
+        codes = codes_ref[rows, :]
+        zero = jnp.zeros_like(pre)
+        top = jnp.where(codes == 1.0, pre, zero)
+        aux = jnp.where(codes == 2.0, pre, zero)
+        top_ref[rows, :] = top
+        aux_ref[rows, :] = aux
+        acc_top[rows, :] += dot_f32(top, dec[...])
+        acc_aux[rows, :] += dot_f32(aux, dec[...])
+        return carry
+
+    lax.fori_loop(0, rows_all // block, one, 0)
+
+    @pl.when(step == pl.num_programs(0) - 1)
+    def _():
+        half = rows_all // 2
+        for first, acc in ((0, acc_top), (width, acc_aux)):
+            near_ref[:, first : first + width] = acc[pl.ds(0, half), :]
+            far_ref[:, first : first + width] = acc[pl.ds(half, half), :].astype(jnp.bfloat16)
+
+
+def part_specs(shape, axis, block, count, starts):
+    specs = []
+    for index, first in enumerate(starts):
+
+        def place(step, index=index, first=first):
+            spot = jnp.clip(step - index * count, 0, count - 1)
+            return (spot + first, 0) if axis == 0 else (0, spot + first)
+
+        size = (block, shape[1]) if axis == 0 else (shape[0], block)
+        specs.append(pl.BlockSpec(size, place))
+    return specs
+
+
+def forward(x, codes, encs, decs):
+    rows, width = x.shape
+    quarter = encs[0].shape[1]
+    block = min(512, quarter)
+    count = quarter // block
+    lanes = pl.BlockSpec((rows, block), lambda step: (0, step))
+    fixed = lambda shape: pl.BlockSpec(shape, lambda step: (0, 0))
+    bf16, f32 = jnp.bfloat16, jnp.float32
+    half_shape = (rows // 2, 2 * width)
+    return pl.pallas_call(
+        functools.partial(forward_kernel, count),
+        grid=(4 * count,),
+        out_shape=[
+            jax.ShapeDtypeStruct(codes.shape, bf16),
+            jax.ShapeDtypeStruct(codes.shape, bf16),
+            jax.ShapeDtypeStruct(half_shape, bf16),
+            jax.ShapeDtypeStruct(half_shape, f32),
+        ],
+        in_specs=[fixed(x.shape), lanes]
+        + part_specs(encs[0].shape, 1, block, count, (0, 0, 0, 0))
+        + part_specs(decs[0].shape, 0, block, count, (0, 0, 0, 0)),
+        out_specs=[lanes, lanes, fixed(half_shape), fixed(half_shape)],
+        scratch_shapes=[
+            pltpu.VMEM((encs[0].shape[0], block), bf16),
+            pltpu.VMEM((block, width), bf16),
+            pltpu.VMEM((rows, width), f32),
+            pltpu.VMEM((rows, width), f32),
+        ],
+        compiler_params=pltpu.CompilerParams(vmem_limit_bytes=58 * 2**20),
+        cost_estimate=pl.CostEstimate(
+            flops=6 * rows * width * codes.shape[1],
+            bytes_accessed=6 * rows * codes.shape[1],
+            transcendentals=0,
+        ),
+    )(x, codes, *encs, *decs)
+
+
+def store_part(count, refs, rows, value):
+    step = pl.program_id(0)
+    for index, ref in enumerate(refs):
+
+        @pl.when(step // count == index)
+        def _(ref=ref):
+            ref[rows, :] = value.astype(ref.dtype)
+
+
+def dec_grad_kernel(count, recon_ref, aux_back_ref, top_ref, aux_ref, *outs):
+    def one(index, carry):
+        rows = pl.ds(pl.multiple_of(index * 384, 384), 384)
+        value = dot_f32(recon_ref[rows, :], top_ref[...]) + dot_f32(
+            aux_back_ref[rows, :], aux_ref[...]
+        )
+        store_part(count, outs, rows, value)
+        return carry
+
+    lax.fori_loop(0, recon_ref.shape[0] // 384, one, 0)
+
+
+def dec_grads(back_t, top_acts, aux_acts, quarters, kind):
+    width = back_t.shape[0] // 2
+    rows, latents = top_acts.shape
+    quarter = latents // 4
+    block = min(512, quarter)
+    count = quarter // block
+
+    def lanes(step):
+        return (0, jnp.where(step < count, quarters[0], quarters[1] - 1) * count + step)
+
+    acts = pl.BlockSpec((rows, block), lanes)
+    shape = (width, quarter)
+    return pl.pallas_call(
+        functools.partial(dec_grad_kernel, count),
+        grid=(2 * count,),
+        out_shape=[jax.ShapeDtypeStruct(shape, kind)] * 2,
+        in_specs=[
+            pl.BlockSpec((width, rows), lambda step: (0, 0)),
+            pl.BlockSpec((width, rows), lambda step: (1, 0)),
+            acts,
+            acts,
+        ],
+        out_specs=part_specs(shape, 1, block, count, (0, 0)),
+        compiler_params=pltpu.CompilerParams(vmem_limit_bytes=58 * 2**20),
+        cost_estimate=pl.CostEstimate(
+            flops=8 * rows * width * quarter, bytes_accessed=8 * rows * quarter, transcendentals=0
+        ),
+    )(back_t, back_t, top_acts, aux_acts)
+
+
+def enc_grad_kernel(count, x_ref, back_ref, codes_ref, dec_a, dec_b, out_a, out_b, dec, grads):
+    step = pl.program_id(0)
+    pick_copy(step, count, (dec_a, dec_b), dec)
+    width = x_ref.shape[0]
+    block = min(1024, back_ref.shape[0])
+    to_latents = (((1,), (1,)), ((), ()))
+
+    def one(index, total):
+        rows = pl.ds(pl.multiple_of(index * block, block), block)
+        codes = codes_ref[rows, :].astype(jnp.float32)
+        top = lax.dot_general(
+            back_ref[rows, :width], dec[...], to_latents, preferred_element_type=jnp.float32
+        )
+        aux = lax.dot_general(
+            back_ref[rows, width:], dec[...], to_latents, preferred_element_type=jnp.float32
+        )
+        value = jnp.where(codes == 1.0, top, jnp.where(codes == 2.0, aux, 0.0))
+        value = value.astype(jnp.bfloat16)
+        grads[rows, :] = value
+        return total + jnp.sum(value.astype(jnp.float32), 0, keepdims=True)
+
+    total = lax.fori_loop(
+        0, back_ref.shape[0] // block, one, jnp.zeros((1, dec.shape[0]), jnp.float32)
+    )
+
+    def two(index, carry):
+        rows = pl.ds(pl.multiple_of(index * 384, 384), 384)
+        store_part(count, (out_a, out_b), rows, dot_f32(x_ref[rows, :], grads[...]))
+        return carry
+
+    lax.fori_loop(0, width // 384, two, 0)
+    lines = lax.broadcasted_iota(jnp.int32, (16, dec.shape[0]), 0)
+    if out_a.dtype == jnp.bfloat16:
+        high = total.astype(jnp.bfloat16).astype(jnp.float32)
+        lines = jnp.where(lines == 0, high, jnp.where(lines == 1, total - high, 0.0))
+    else:
+        lines = jnp.where(lines == 0, total, 0.0)
+    store_part(count, (out_a, out_b), pl.ds(width, 16), lines)
+
+
+def enc_grads(x_t, back, codes, decs, quarters, kind):
+    width, rows = x_t.shape
+    quarter = codes.shape[1] // 4
+    block = min(512, quarter)
+    count = quarter // block
+
+    def lanes(step):
+        return (0, jnp.where(step < count, quarters[0], quarters[1] - 1) * count + step)
+
+    shape = (width + 16, quarter)
+    return pl.pallas_call(
+        functools.partial(enc_grad_kernel, count),
+        grid=(2 * count,),
+        out_shape=[jax.ShapeDtypeStruct(shape, kind)] * 2,
+        in_specs=[
+            pl.BlockSpec(x_t.shape, lambda step: (0, 0)),
+            pl.BlockSpec(back.shape, lambda step: (0, 0)),
+            pl.BlockSpec((rows, block), lanes),
+        ]
+        + part_specs(decs[0].shape, 0, block, count, (0, 0)),
+        out_specs=part_specs(shape, 1, block, count, (0, 0)),
+        scratch_shapes=[
+            pltpu.VMEM((block, width), jnp.bfloat16),
+            pltpu.VMEM((rows, block), jnp.bfloat16),
+        ],
+        compiler_params=pltpu.CompilerParams(vmem_limit_bytes=58 * 2**20),
+        cost_estimate=pl.CostEstimate(
+            flops=12 * rows * width * quarter, bytes_accessed=8 * rows * quarter, transcendentals=0
+        ),
+    )(x_t, back, codes, *decs)
 
 
 def adam_update(param, grad, first, second):
@@ -385,50 +614,28 @@
     def gather_chips(own, axis):
         pieces = []
         for part, order in enumerate(orders):
-            first = lax.slice_in_dim(own, part * half_latents, (part + 1) * half_latents, axis=axis)
-            held = {0: first}
-            for bit in order:
-                offsets = sorted(held)
-                sent = [held[offset] for offset in offsets]
-                sent = sent[0] if len(sent) == 1 else jnp.concatenate(sent, axis)
-                got = jnp.split(swap(sent, "chip", bit), len(offsets), axis)
-                held.update({offset ^ bit: piece for offset, piece in zip(offsets, got)})
-            pieces += [held[offset] for offset in range(chips)]
-        return jnp.concatenate(pieces, axis)
-
-    def scatter_chips(value, axis, extra=None):
-        results, extras = [], []
-        for part, order in enumerate(orders):
-            base = part * chips * half_latents
-            held, added = {}, {}
-            for offset in range(chips):
-                start = base + offset * half_latents
-                held[offset] = lax.slice_in_dim(value, start, start + half_latents, axis=axis)
-                if extra is not None:
-                    added[offset] = lax.slice_in_dim(extra, start, start + half_latents, axis=0)
-            for bit in reversed(order):
-                keep = sorted(offset for offset in held if not offset & bit)
-                sent = jnp.concatenate([held[offset | bit].astype(bf16) for offset in keep], axis)
-                if extra is not None:
-                    vector = jnp.concatenate([added[offset | bit] for offset in keep])
-                    lines = jnp.stack(split_bf(vector))
-                    lines = jnp.concatenate([lines, jnp.zeros((14, lines.shape[1]), bf16)], 0)
-                    sent = jnp.concatenate([sent, lines], 0)
-                got = swap(sent, "chip", bit).astype(f32)
-                if extra is not None:
-                    vector = got[model_width] + got[model_width + 1]
-                    got = got[:model_width]
-                    added = {
-                        offset: added[offset] + piece
-                        for offset, piece in zip(keep, jnp.split(vector, len(keep)))
-                    }
-                got = jnp.split(got, len(keep), axis)
-                held = {offset: held[offset] + piece for offset, piece in zip(keep, got)}
-            results.append(held[0])
-            if extra is not None:
-                extras.append(added[0])
-        result = jnp.concatenate(results, axis)
-        return result if extra is None else (result, jnp.concatenate(extras))
+            held = lax.slice_in_dim(own, part * half_latents, (part + 1) * half_latents, axis=axis)
+            for bit in order[:-1]:
+                held = jnp.concatenate([held, swap(held, "chip", bit)], axis)
+            pieces += [held, swap(held, "chip", order[-1])]
+        return pieces
+
+    def scatter_chips(keeps, sents):
+        results, sums = [], []
+        for order, held, sent in zip(orders, keeps, sents):
+            held = held + swap(sent, "chip", order[-1]).astype(f32)
+            for bit in reversed(order[:-1]):
+                lower, upper = jnp.split(held, 2, 1)
+                sent = upper[:model_width].astype(bf16)
+                if held.shape[0] > model_width:
+                    lines = split_bf(upper[model_width] + upper[model_width + 1])
+                    spare = jnp.zeros((14, upper.shape[1]), bf16)
+                    sent = jnp.concatenate([sent, *(line[None] for line in lines), spare], 0)
+                held = lower + swap(sent, "chip", bit).astype(f32)
+            results.append(held[:model_width])
+            if held.shape[0] > model_width:
+                sums.append(held[model_width] + held[model_width + 1])
+        return jnp.concatenate(results, 1), jnp.concatenate(sums) if sums else None
 
     vocab_dev = token_table.shape[0]
     every_ids = lax.all_gather(token_ids, wide, axis=0, tiled=False).reshape(wide_count, row_count)
@@ -444,7 +651,8 @@
     looked = jnp.take(token_table, jnp.clip(local_ids, 0, vocab_dev - 1), axis=0)
     looked = jnp.where(inside[:, None], looked, jnp.zeros((), bf16))
     enc_own = rows_to_latents(enc_weight.astype(bf16))
-    near_picks = spread_narrow(jnp.concatenate([top_ids, aux_ids], 1))
+    picks = after(jnp.concatenate([top_ids, aux_ids], 1), every_ids)
+    near_picks = spread_narrow(picks)
     far_picks = swap(near_picks, "core", 1)
 
     looked = looked.reshape(chips, 2, row_count, model_width)
@@ -453,14 +661,12 @@
     for k in range(1, chips):
         embedded = embedded + swap(looked[k], "chip", k).astype(f32)
 
-    enc_own = after(enc_own, looked)
-    dec_own = cols_to_latents(after(dec_weight, enc_own).astype(bf16))
     bias_rows = jnp.concatenate(
         [enc_bias.astype(bf16)[None], jnp.zeros((15, own_latents), bf16)], 0
     )
-    enc_biased = gather_chips(jnp.concatenate([enc_own, bias_rows], 0), 1)
-    enc_full = enc_biased[:model_width]
-    bias_copy = enc_biased[model_width]
+    enc_biased = jnp.concatenate([enc_own, bias_rows], 0)
+    enc_parts = gather_chips(enc_biased, 1)
+    dec_own = cols_to_latents(after(dec_weight, enc_own).astype(bf16))
 
     dead_here = jnp.stack(
         [
@@ -472,48 +678,42 @@
             for offset in range(chips)
         ]
     )
-    dead_here = dead_here.reshape(chips, 2, half_latents).transpose(1, 0, 2)
-    dead_here = dead_here.reshape(1, latent_count)
-    sizes = (wide_latents, own_latents, top_ids.shape[1])
-    near_codes = kind_codes(place, near_picks, dead_here, *sizes)
+    places = [0]
+    dead_parts = []
+    for part, order in enumerate(orders):
+        places = [0]
+        for bit in order:
+            places = places + [spot ^ bit for spot in places]
+        for spot in places:
+            dead_parts.append(dead_here[spot, part * half_latents : (part + 1) * half_latents])
+    dead_here = jnp.concatenate(dead_parts)[None]
+    sizes = (wide_latents, own_latents, top_ids.shape[1], orders)
+    near_codes = kind_codes(place, after(near_picks, enc_biased), dead_here, *sizes)
 
     start = after(embedded, near_codes) + position_table[:row_count].astype(f32)
     ctx_length = lengths[0]
     inputs = frozen_block(start, ctx_length, ln_gains, frozen_bias, w_qkv, w_proj, w_fc, w_out)
     counted = (jnp.arange(row_count) < ctx_length).astype(f32)
-    dec_full = gather_chips(after(dec_own, inputs), 0)
+    dec_own = after(dec_own, inputs)
+    dec_parts = gather_chips(dec_own, 0)
+    near_inputs = spread_narrow(after(inputs, dec_own))
     far_codes = kind_codes(place, after(far_picks, inputs), dead_here, *sizes)
-
-    near_inputs = spread_narrow(inputs)
+    near_inputs = after(near_inputs, far_codes)
     far_inputs = swap(near_inputs, "core", 1)
-    zero_bf = jnp.zeros((), bf16)
-
-    def encode(tokens, codes):
-        encoder_in = (tokens.astype(f32) - decoder_bias).astype(bf16)
-        pre_acts = (
-            jnp.dot(encoder_in, enc_full, preferred_element_type=f32) + bias_copy.astype(f32)
-        ).astype(bf16)
-        top_acts = jnp.where(codes == 1.0, pre_acts, zero_bf)
-        return encoder_in, top_acts, jnp.where(codes == 2.0, pre_acts, zero_bf)
-
+    codes = jnp.concatenate([near_codes, far_codes], 0)
     all_inputs = jnp.concatenate([near_inputs, far_inputs], 0)
-    codes = jnp.concatenate([near_codes, far_codes], 0)
-    encoder_in, top_acts, aux_acts = encode(all_inputs, codes)
-
-    def rebuild(acts):
-        far = jnp.dot(acts[core_rows:], dec_full, preferred_element_type=f32).astype(bf16)
-        near = jnp.dot(acts[:core_rows], dec_full, preferred_element_type=f32)
-        total = near + swap(far, "core", 1).astype(f32)
-        rounded = total.astype(bf16)
-        result = total[:row_count]
-        for k in range(1, narrow_count):
-            part = rounded[k * row_count : (k + 1) * row_count]
-            result = result + swap(part, "narrow", k).astype(f32)
-        return result
-
+    encoder_in = (all_inputs.astype(f32) - decoder_bias).astype(bf16)
+    top_acts, aux_acts, far, near = forward(encoder_in, codes, enc_parts, dec_parts)
+    encoder_t = encoder_in.T
+    rebuilt = near + swap(far, "core", 1).astype(f32)
+    rounded = rebuilt.astype(bf16)
+    rebuilt = rebuilt[:row_count]
+    for k in range(1, narrow_count):
+        part = rounded[k * row_count : (k + 1) * row_count]
+        rebuilt = rebuilt + swap(part, "narrow", k).astype(f32)
     target = inputs.astype(f32)
-    reconstructed_input = rebuild(top_acts) + decoder_bias
-    auxiliary_reconstruction = rebuild(aux_acts)
+    reconstructed_input = rebuilt[:, :model_width] + decoder_bias
+    auxiliary_reconstruction = rebuilt[:, model_width:]
     recon_error = target - reconstructed_input
     aux_gap = auxiliary_reconstruction - recon_error
     token_loss = (
@@ -526,29 +726,23 @@
     back_rows = jnp.concatenate([back_recon, back_aux], 1).astype(bf16)
     near_back = spread_narrow(back_rows)
     shard_rows = jnp.concatenate([near_back, swap(near_back, "core", 1)], 0)
-    recon_part = shard_rows[:, :model_width]
-    aux_back = shard_rows[:, model_width:]
-
-    grad_dec = lax.dot_general(top_acts, recon_part, over_rows, preferred_element_type=f32)
-    grad_dec = grad_dec + lax.dot_general(
-        aux_acts, aux_back, over_rows, preferred_element_type=f32
-    )
-    grad_dec, recon_part, aux_back = lax.optimization_barrier((grad_dec, recon_part, aux_back))
-    dec_grad = scatter_chips(grad_dec, 0)
-    back_top = lax.dot_general(recon_part, dec_full, to_latents, preferred_element_type=f32)
-    back_side = lax.dot_general(aux_back, dec_full, to_latents, preferred_element_type=f32)
-    latent_grad = jnp.where(codes == 1.0, back_top, jnp.where(codes == 2.0, back_side, 0.0))
-    latent_grad = latent_grad.astype(bf16)
-    grad_enc = lax.dot_general(encoder_in, latent_grad, over_rows, preferred_element_type=f32)
-    column_sum = jnp.sum(latent_grad, 0, dtype=f32)
-    enc_grad, encb_grad = scatter_chips(grad_enc, 1, column_sum)
+    back_t = shard_rows.T
+    dec_sent = dec_grads(back_t, top_acts, aux_acts, (1, 3), bf16)
+    shard_rows, top_acts, dec_sent = lax.optimization_barrier((shard_rows, top_acts, dec_sent))
+    dec_keep = dec_grads(back_t, top_acts, aux_acts, (0, 2), f32)
+    shard_rows, dec_keep = lax.optimization_barrier((shard_rows, dec_keep))
+    enc_sent = enc_grads(encoder_t, shard_rows, codes, dec_parts[1::2], (1, 3), bf16)
+    shard_rows, enc_sent = lax.optimization_barrier((shard_rows, enc_sent))
+    enc_keep = enc_grads(encoder_t, shard_rows, codes, dec_parts[::2], (0, 2), f32)
+    dec_moment_own = rows_to_latents(after(dec_moment, back_rows).astype(bf16).T)
+    enc_moment_own = rows_to_latents(after(enc_moment, dec_moment_own).astype(bf16))
+    dec_grad, _ = scatter_chips(dec_keep, dec_sent)
+    enc_grad, encb_grad = scatter_chips(enc_keep, enc_sent)
     bias_term = jnp.sum(back_rows[:, :model_width], 0, dtype=f32) - jnp.dot(
         enc_own.astype(f32), encb_grad, precision=HIGH_PRECISION
     )
-    dec_moment_own = cols_to_latents(after(dec_moment, back_rows).astype(bf16))
-    enc_moment_own = rows_to_latents(after(enc_moment, dec_moment_own).astype(bf16))
-
-    def sum_gram(part, extra):
+
+    def sum_gram(part, vector, fill):
         half = model_width // 2
         rows = half // chips
         spare = jnp.zeros((14, model_width), bf16)
@@ -564,44 +758,70 @@
         def block_of(value, index, count):
             return lax.dynamic_slice_in_dim(value, index * count, count, 0)
 
-        vector = extra
-        got, more = unpack(swap(pack(block_of(part, 1 - core_pos, half), vector), "core", 1))
+        def exchange(sents, axis):
+            got = [swap(sent, axis, k + 1) for k, sent in enumerate(sents)]
+            return fill(sents, got)
+
+        sent = pack(block_of(part, 1 - core_pos, half), vector)
+        (got,) = exchange([sent], "core")
+        got, more = unpack(got)
         part, vector = block_of(part, core_pos, half) + got, vector + more
-        total, sent_vector = block_of(part, chip_pos, rows), vector
-        for k in range(1, chips):
-            sent = pack(block_of(part, chip_pos ^ k, rows), sent_vector)
-            got, more = unpack(swap(sent, "chip", k))
+        total = block_of(part, chip_pos, rows)
+        sents = [pack(block_of(part, chip_pos ^ k, rows), vector) for k in range(1, chips)]
+        for got in exchange(sents, "chip"):
+            got, more = unpack(got)
             total, vector = total + got, vector + more
-        sent = pack(total, vector)
-        for k in range(1, narrow_count):
-            got, more = unpack(swap(sent, "narrow", k))
+        for got in exchange([pack(total, vector)] * (narrow_count - 1), "narrow"):
+            got, more = unpack(got)
             total, vector = total + got, vector + more
-        near = jnp.stack([total] + [swap(total, "chip", k) for k in range(1, chips)])
-        return near, swap(near, "core", 1), vector
+        near = jnp.stack([total, *exchange([total] * (chips - 1), "chip")])
+        (far,) = exchange([near], "core")
+        return near, far, vector
 
     dec_own_next = (MOMENTUM * dec_moment_own.astype(f32) + dec_grad).astype(bf16)
+    dec_own_next, enc_keep = lax.optimization_barrier((dec_own_next, enc_keep))
     dec_near, dec_far, _ = sum_gram(
-        lax.dot_general(dec_own_next, dec_own_next, over_rows, preferred_element_type=f32),
+        lax.dot_general(dec_own_next, dec_own_next, to_latents, preferred_element_type=f32),
         jnp.zeros((model_width,), f32),
-    )
-    dec_state = series_start(place, dec_near, dec_far)
-    dec_rows_grad = latents_to_cols(after(dec_grad, enc_moment_own).astype(bf16))
+        lambda sents, got: got,
+    )
     enc_own_next = (MOMENTUM * enc_moment_own.astype(f32) + enc_grad).astype(bf16)
-    enc_near, enc_far, grad_decb = sum_gram(
-        lax.dot_general(enc_own_next, enc_own_next, to_latents, preferred_element_type=f32),
-        bias_term,
-    )
-    dec_factor = series_finish(dec_state)
-    dec_ortho = latents_to_cols(
-        jnp.dot(dec_own_next, dec_factor, preferred_element_type=f32).astype(bf16)
-    )
-    enc_rows_grad = latents_to_rows(after(enc_grad, dec_rows_grad).astype(bf16))
-    enc_state = series_start(place, after(enc_near, dec_factor, dec_rows_grad), enc_far)
-    enc_factor = series_finish(enc_state)
+    enc_gram = lax.dot_general(
+        enc_own_next, enc_own_next, to_latents, preferred_element_type=f32
+    )
+    enc_gram, dec_near = lax.optimization_barrier((enc_gram, dec_near))
+    progress = []
+
+    def dec_fill(sents, got):
+        step = len(progress)
+        if step == 0:
+            state = series_start(after(place, sents), dec_near, dec_far)
+        else:
+            state = series_next(step, after(progress[-1], sents))
+        got, state = lax.optimization_barrier((got, state))
+        progress.append(state)
+        return got
+
+    enc_near, enc_far, grad_decb = sum_gram(enc_gram, bias_term, dec_fill)
+    dec_factor = progress[-1][0]
+    dec_rows_grad = latents_to_rows(after(dec_grad, enc_gram).astype(bf16))
+    dec_ortho = latents_to_rows(
+        jnp.dot(
+            after(dec_factor, dec_rows_grad), dec_own_next, preferred_element_type=f32
+        ).astype(bf16)
+    )
+    state = series_start(place, after(enc_near, dec_factor, dec_rows_grad), enc_far)
+    for step in range(1, NS_STEPS - 1):
+        state = series_next(step, state)
+    state = after(state, dec_ortho)
+    enc_rows_grad = latents_to_rows(after(enc_grad, dec_ortho).astype(bf16))
+    enc_factor = series_next(NS_STEPS - 1, state)[0]
     enc_factor = after(enc_factor, enc_rows_grad)
     enc_ortho = latents_to_rows(
         jnp.dot(enc_factor, enc_own_next, preferred_element_type=f32).astype(bf16)
     )
+    dec_ortho = dec_ortho.T
+    dec_rows_grad = dec_rows_grad.T
     enc_next = MOMENTUM * enc_moment + enc_rows_grad.astype(f32)
     dec_next = MOMENTUM * dec_moment + dec_rows_grad.astype(f32)
     step_scale = MUON_RATE * 0.2 * math.sqrt(max(D, L))

time: 939 us -> 813 us (0.87)
  matrix products: 130 us -> 24.9 us
  Pallas kernels: 151 us -> 245 us
  starting transfers between devices: 154 us -> 114 us
  other arithmetic: 125 us -> 91.8 us
  local copies, waits for them, and re-layouts: 99.7 us -> 70.7 us
  waiting for transfers between devices: 262 us -> 245 us
    dot_general x12 -> x2, matrix products: 110 us -> 3.94 us  [the longest x1 2.53 us: local(): jnp.dot(after(dec_factor, dec_rows_grad), dec_own_next, preferred_element...]
    pallas_call x0 -> x5, Pallas kernels: none -> 93.9 us  [the longest x2 38.2 us: enc_grads(): pl.pallas_call(functools.partial(enc_grad_kernel, count), grid=(2 * count...]
    ppermute x62 -> x58, waiting for transfers between devices: 235 us -> 176 us  [swap(): lax.ppermute(value, axis, [(spot, spot ^ offset) for spot in range(count)])]
    ppermute x62 -> x58, starting transfers between devices: 98.2 us -> 68.1 us  [swap(): lax.ppermute(value, axis, [(spot, spot ^ offset) for spot in range(count)])]
    unnamed x194 -> x176, local copies, waits for them, and re-layouts: 38.5 us -> 18.8 us
    all_to_all x2 -> x1, waiting for transfers between devices: 0.01 us -> 19.4 us  [cols_to_latents(): lax.all_to_all(value, 'narrow', split_axis=0, concat_axis=1, tiled=True)]
    all_to_all x2 -> x0, starting transfers between devices: 15.6 us -> none  [latents_to_cols(): lax.all_to_all(value, 'narrow', split_axis=1, concat_axis=0, tiled=True)]
    all_to_all x2 -> x4, waiting for transfers between devices: 26.3 us -> 40.9 us  [latents_to_rows(): lax.all_to_all(value, 'narrow', split_axis=0, concat_axis=1, tiled=True)]
  transfers between devices with their start and end apart: 70 -> 66, of which waited for: 21 -> 24; matrix products, arithmetic and copies ran while one was open for 25% -> 18% of each run, Pallas kernels for 16% -> 27%
where the time goes in v4:
time: 813 us; the launch traced here: 804 us
  waiting for transfers between devices  245 us (30%)
  Pallas kernels  245 us (30%)
  starting transfers between devices  114 us (14%)
  other arithmetic  91.8 us (11%)
  local copies, waits for them, and re-layouts  70.7 us (9%)
  matrix products  24.9 us (3%)
  blocking collectives  8.74 us (1%)
    ppermute x58, waiting for transfers between devices, swap(): lax.ppermute(value, axis, [(spot, spot ^ offset) for spot in range(count)])  176 us
    pallas_call x10, Pallas kernels, square_call(): pl.pallas_call(kernel, out_shape=[square] * outs, in_specs=specs, out_spe...  96.4 us
    ppermute x58, starting transfers between devices, swap(): lax.ppermute(value, axis, [(spot, spot ^ offset) for spot in range(count)])  68.1 us
    pallas_call x2, Pallas kernels, kind_codes(): pl.pallas_call(functools.partial(code_kernel, shifts), grid=(row_total //...  55.1 us
    all_to_all x4, waiting for transfers between devices, latents_to_rows(): lax.all_to_all(value, 'narrow', split_axis=0, concat_axis=1, tiled=True)  40.9 us
    pallas_call x2, Pallas kernels, enc_grads(): pl.pallas_call(functools.partial(enc_grad_kernel, count), grid=(2 * count...  38.2 us
    pallas_call x1, Pallas kernels, forward(): pl.pallas_call(functools.partial(forward_kernel, count), grid=(4 * count,...  31 us
    pallas_call x2, Pallas kernels, dec_grads(): pl.pallas_call(functools.partial(dec_grad_kernel, count), grid=(2 * count...  24.7 us
  transfers between devices with their start and end apart: 66, of which 24 were waited for; matrix products, arithmetic and copies ran while one was open for 18% of the time, Pallas kernels for 27%

profile of v4, /device:TPU:0, one launch (start us, length us, event | category | flops | bytes accessed | tf_op | source)
XLA Modules:
  0.0 803.8 jit_solution(17128138740681505505)
XLA Ops:
  18.3 8.7 %all-gather.1 = s32[8,1,128]{2,1,0:T(1,128)S(1)} all-gather(s32[1,1,128]{2,1,0:T(1,128)S(1)} %bitcast.236), channel_id=2, replica_groups=mesh['chip'=4,'core'=2,'narrow'=4] {'chip','core'}, dimensions={0}, use_global_device_ids=true | all-gather | bytes 4608 | tf_op jit(solution)/shard_map/all_gather | solution.py:641
  27.2 10.6 %gather_fusion = bf16[1024,768]{1,0:T(8,128)(2,1)} fusion(bf16[6288,768]{1,0:T(8,128)(2,1)} %param.28, s32[1024]{0:T(1024)S(1)} %broadcast_clamp_fusion), kind=kCustom, calls=%fused_computation | custom fusion | bytes 3149824 | tf_op jit(solution)/shard_map/jit(_take)/gather | solution.py:651
  64.0 8.4 %all-to-all-done = bf16[192,4,1024]{2,0,1:T(8,128)(2,1)} async-done(((bf16[192,4,1024]{2,0,1:T(8,128)(2,1)}), bf16[192,4,1024]{2,0,1:T(8,128)(2,1)}, u32[]{:S(2)}, u32[]{:S(2)}) %all-to-all-start) | async-done | bytes 1572896 | tf_op jit(solution)/shard_map/all_to_all | solution.py:603
  75.4 27.6 %shard_map.318 = bf16[512,4096]{1,0:T(8,128)(2,1)S(1)} custom-call(s32[3]{0:T(128)S(1)} %pad_add_fusion.2.place_ref, s32[512,544]{1,0:T(8,128)S(1)} %copy-done.2, s32[1,4096]{1,0:T(1,128)S(1)} %bitcast.184), custom_call_target="tpu_custom_call" | custom-call | flops 10737418240 | bytes 4194304 | tf_op jit(solution)/shard_map/pallas_call | solution.py:292
  135.7 19.4 %all-to-all-done.1 = bf16[4,1024,192]{1,2,0:T(8,128)(2,1)S(1)} async-done(((bf16[4,1024,192]{1,2,0:T(8,128)(2,1)}), bf16[4,1024,192]{1,2,0:T(8,128)(2,1)S(1)}, u32[]{:S(2)}, u32[]{:S(2)}) %all-to-all-start.1) | async-done | bytes 1572896 | tf_op jit(solution)/shard_map/all_to_all | solution.py:606
  167.2 9.4 %collective-permute-done.16 = bf16[512,768]{1,0:T(8,128)(2,1)} collective-permute-done((bf16[512,768]{1,0:T(8,128)(2,1)S(1)}, bf16[512,768]{1,0:T(8,128)(2,1)}, u32[]{:S(2)}, u32[]{:S(2)}) %collective-permute-start.16) | collective-permute-done | bytes 786464 | tf_op jit(solution)/shard_map/ppermute | solution.py:596
  190.7 27.5 %shard_map.319 = bf16[512,4096]{1,0:T(8,128)(2,1)S(1)} custom-call(s32[3]{0:T(128)S(1)} %pad_add_fusion.2.place_ref, s32[512,544]{1,0:T(8,128)S(1)} %copy.117.ids_ref, s32[1,4096]{1,0:T(1,128)S(1)} %bitcast.185), custom_call_target="tpu_custom_call" | custom-call | flops 10737418240 | bytes 4194304 | tf_op jit(solution)/shard_map/pallas_call | solution.py:292
  229.7 14.2 %collective-permute-done.17.refs_5_.dec_a = bf16[1024,768]{1,0:T(8,128)(2,1)} collective-permute-done((bf16[1024,768]{1,0:T(8,128)(2,1)}, bf16[1024,768]{1,0:T(8,128)(2,1)}, u32[]{:S(2)}, u32[]{:S(2)}) %collective-permute-start.17) | collective-permute-done | bytes 1572896 | tf_op jit(solution)/shard_map/ppermute | solution.py:596
  244.0 31.0 %shard_map.320 = (bf16[1024,4096]{1,0:T(8,128)(2,1)}, bf16[1024,4096]{1,0:T(8,128)(2,1)}, bf16[512,1536]{1,0:T(8,128)(2,1)}, f32[512,1536]{1,0:T(8,128)}) custom-call(bf16[1024,768]{1,0:T(8,128)(2,1)} %subtract_convert_fusion.x_ref, bf16[1024,4096]{1,0:T(8,128)(2,1)} %pad_maximum_fusion.codes_ref, bf16[784,1024]{1,0:T(8,128)(2,1)} %pad_maximum_fusion.3.refs_0_, ...), custom_call_target="tpu_custom_call" | custom-call | flops 19327352832 | bytes 25165824 | tf_op jit(solution)/shard_map/pallas_call | solution.py:386
  285.7 13.4 %collective-permute-done.21 = bf16[128,1536]{1,0:T(8,128)(2,1)S(1)} collective-permute-done((bf16[128,1536]{1,0:T(8,128)(2,1)S(1)}, bf16[128,1536]{1,0:T(8,128)(2,1)S(1)}, u32[]{:S(2)}, u32[]{:S(2)}) %collective-permute-start.21) | collective-permute-done | bytes 393248 | tf_op jit(solution)/shard_map/ppermute | solution.py:596
  299.0 12.1 %collective-permute-done.22 = bf16[128,1536]{1,0:T(8,128)(2,1)S(1)} collective-permute-done((bf16[128,1536]{1,0:T(8,128)(2,1)S(1)}, bf16[128,1536]{1,0:T(8,128)(2,1)S(1)}, u32[]{:S(2)}, u32[]{:S(2)}) %collective-permute-start.22) | collective-permute-done | bytes 393248 | tf_op jit(solution)/shard_map/ppermute | solution.py:596
  323.3 13.1 %collective-permute-done.24 = bf16[128,1536]{1,0:T(8,128)(2,1)S(1)} collective-permute-done((bf16[128,1536]{1,0:T(8,128)(2,1)S(1)}, bf16[128,1536]{1,0:T(8,128)(2,1)S(1)}, u32[]{:S(2)}, u32[]{:S(2)}) %collective-permute-start.24) | collective-permute-done | bytes 393248 | tf_op jit(solution)/shard_map/ppermute | solution.py:596
  336.4 14.4 %collective-permute-done.25 = bf16[128,1536]{1,0:T(8,128)(2,1)S(1)} collective-permute-done((bf16[128,1536]{1,0:T(8,128)(2,1)S(1)}, bf16[128,1536]{1,0:T(8,128)(2,1)S(1)}, u32[]{:S(2)}, u32[]{:S(2)}) %collective-permute-start.25) | collective-permute-done | bytes 393248 | tf_op jit(solution)/shard_map/ppermute | solution.py:596
  357.1 8.5 %all-to-all-start.2 = ((bf16[192,4,1024]{2,0,1:T(8,128)(2,1)}), bf16[192,4,1024]{2,0,1:T(8,128)(2,1)}, u32[]{:S(2)}, u32[]{:S(2)}) async-start(bf16[192,4,1024]{2,0,1:T(8,128)(2,1)} %bitcast.178), calls=%async_computation.2 | async-start | bytes 3145728 | tf_op jit(solution)/shard_map/all_to_all | solution.py:603
  371.6 12.1 %shard_map.321 = (bf16[768,1024]{1,0:T(8,128)(2,1)}, bf16[768,1024]{1,0:T(8,128)(2,1)}) custom-call(bf16[1536,1024]{1,0:T(8,128)(2,1)} %copy.122.recon_ref.aux_back_ref, bf16[1536,1024]{1,0:T(8,128)(2,1)} %copy.122.recon_ref.aux_back_ref, bf16[1024,4096]{1,0:T(8,128)(2,1)} %get-tuple-element.132.top_ref, bf16[1024,4096]{1,0:T(8,128)(2,1)} %get-tuple-element.128.aux_ref), custom_call_target="tpu_custom_call" | custom-call | flops 6442450944 | bytes 8388608 | tf_op jit(solution)/shard_map/pallas_call | solution.py:447
  383.7 12.6 %shard_map.322 = (f32[768,1024]{1,0:T(8,128)}, f32[768,1024]{1,0:T(8,128)}) custom-call(bf16[1536,1024]{1,0:T(8,128)(2,1)} %copy.122.recon_ref.aux_back_ref, bf16[1536,1024]{1,0:T(8,128)(2,1)} %copy.122.recon_ref.aux_back_ref, bf16[1024,4096]{1,0:T(8,128)(2,1)} %get-tuple-element.132.top_ref, bf16[1024,4096]{1,0:T(8,128)(2,1)} %get-tuple-element.128.aux_ref), custom_call_target="tpu_custom_call" | custom-call | flops 6442450944 | bytes 8388608 | tf_op jit(solution)/shard_map/pallas_call | solution.py:447
  398.3 18.6 %shard_map.323 = (bf16[784,1024]{1,0:T(8,128)(2,1)}, bf16[784,1024]{1,0:T(8,128)(2,1)}) custom-call(bf16[768,1024]{1,0:T(8,128)(2,1)} %copy.127.x_ref, bf16[1024,1536]{1,0:T(8,128)(2,1)} %copy-done.37, bf16[1024,4096]{1,0:T(8,128)(2,1)} %pad_maximum_fusion.codes_ref, bf16[1024,768]{1,0:T(8,128)(2,1)} %collective-permute-done.17.refs_5_.dec_a, ...), custom_call_target="tpu_custom_call" | custom-call | flops 9663676416 | bytes 8388608 | tf_op jit(solution)/shard_map/pallas_call | solution.py:515
  418.9 19.6 %shard_map.324 = (f32[784,1024]{1,0:T(8,128)}, f32[784,1024]{1,0:T(8,128)}) custom-call(bf16[768,1024]{1,0:T(8,128)(2,1)} %copy.127.x_ref, bf16[1024,1536]{1,0:T(8,128)(2,1)} %copy-done.37, bf16[1024,4096]{1,0:T(8,128)(2,1)} %pad_maximum_fusion.codes_ref, bf16[1024,768]{1,0:T(8,128)(2,1)} %pad_maximum_fusion.5.refs_4_.dec_a, ...), custom_call_target="tpu_custom_call" | custom-call | flops 9663676416 | bytes 8388608 | tf_op jit(solution)/shard_map/pallas_call | solution.py:515
  445.1 23.1 %collective-permute-done.28 = bf16[784,1024]{1,0:T(8,128)(2,1)} collective-permute-done((bf16[784,1024]{1,0:T(8,128)(2,1)}, bf16[784,1024]{1,0:T(8,128)(2,1)}, u32[]{:S(2)}, u32[]{:S(2)}) %collective-permute-start.28) | collective-permute-done | bytes 1605664 | tf_op jit(solution)/shard_map/ppermute | solution.py:596
  474.0 12.5 %collective-permute-done.33 = bf16[768,512]{1,0:T(8,128)(2,1)S(1)} collective-permute-done((bf16[768,512]{1,0:T(8,128)(2,1)S(1)}, bf16[768,512]{1,0:T(8,128)(2,1)S(1)}, u32[]{:S(2)}, u32[]{:S(2)}) %collective-permute-start.33) | collective-permute-done | bytes 786464 | tf_op jit(solution)/shard_map/ppermute | solution.py:596
  509.4 14.0 %collective-permute-done.31 = bf16[784,512]{1,0:T(8,128)(2,1)S(1)} collective-permute-done((bf16[784,512]{1,0:T(8,128)(2,1)}, bf16[784,512]{1,0:T(8,128)(2,1)S(1)}, u32[]{:S(2)}, u32[]{:S(2)}) %collective-permute-start.31) | collective-permute-done | bytes 802848 | tf_op jit(solution)/shard_map/ppermute | solution.py:596
  539.8 8.4 %collective-permute-done.41 = bf16[112,768]{1,0:T(8,128)(2,1)S(1)} collective-permute-done((bf16[112,768]{1,0:T(8,128)(2,1)S(1)}, bf16[112,768]{1,0:T(8,128)(2,1)S(1)}, u32[]{:S(2)}, u32[]{:S(2)}) %collective-permute-start.41) | collective-permute-done | bytes 172064 | tf_op jit(solution)/shard_map/ppermute | solution.py:596
  581.6 11.3 %shard_map.325 = (bf16[768,768]{1,0:T(8,128)(2,1)S(1)}, bf16[768,768]{1,0:T(8,128)(2,1)S(1)}, bf16[768,768]{1,0:T(8,128)(2,1)S(1)}) custom-call(s32[3]{0:T(128)S(1)} %pad_add_fusion.2.place_ref, f32[4,96,768]{2,1,0:T(8,128)S(1)} %pad_maximum_fusion.8.near_ref, f32[4,96,768]{2,1,0:T(8,128)S(1)} %collective-permute-done.47.far_ref), custom_call_target="tpu_custom_call" | custom-call | flops 7247757312 | bytes 7077888 | tf_op jit(solution)/shard_map/pallas_call | solution.py:194
  598.4 9.8 %shard_map.326 = (bf16[768,768]{1,0:T(8,128)(2,1)S(1)}, bf16[768,768]{1,0:T(8,128)(2,1)S(1)}, bf16[768,768]{1,0:T(8,128)(2,1)S(1)}) custom-call(bf16[768,768]{1,0:T(8,128)(2,1)S(1)} %get-tuple-element.158.g_hi, bf16[768,768]{1,0:T(8,128)(2,1)S(1)} %get-tuple-element.159.g_lo, bf16[768,768]{1,0:T(8,128)(2,1)S(1)} %get-tuple-element.160.q_ref), custom_call_target="tpu_custom_call" | custom-call | flops 7247757312 | bytes 7077888 | tf_op jit(solution)/shard_map/pallas_call | solution.py:194
  613.2 9.8 %shard_map.327 = (bf16[768,768]{1,0:T(8,128)(2,1)S(1)}, bf16[768,768]{1,0:T(8,128)(2,1)S(1)}, bf16[768,768]{1,0:T(8,128)(2,1)S(1)}) custom-call(bf16[768,768]{1,0:T(8,128)(2,1)S(1)} %get-tuple-element.170.g_hi, bf16[768,768]{1,0:T(8,128)(2,1)S(1)} %get-tuple-element.171.g_lo, bf16[768,768]{1,0:T(8,128)(2,1)S(1)} %get-tuple-element.172.q_ref), custom_call_target="tpu_custom_call" | custom-call | flops 7247757312 | bytes 7077888 | tf_op jit(solution)/shard_map/pallas_call | solution.py:194
  634.6 11.9 %shard_map.328 = (bf16[768,768]{1,0:T(8,128)(2,1)S(1)}, bf16[768,768]{1,0:T(8,128)(2,1)S(1)}, bf16[768,768]{1,0:T(8,128)(2,1)S(1)}) custom-call(bf16[768,768]{1,0:T(8,128)(2,1)S(1)} %get-tuple-element.182.g_hi, bf16[768,768]{1,0:T(8,128)(2,1)S(1)} %get-tuple-element.183.g_lo, bf16[768,768]{1,0:T(8,128)(2,1)S(1)} %get-tuple-element.184.q_ref), custom_call_target="tpu_custom_call" | custom-call | flops 9059696640 | bytes 7077888 | tf_op jit(solution)/shard_map/pallas_call | solution.py:194
  674.0 12.4 %shard_map.330 = (bf16[768,768]{1,0:T(8,128)(2,1)S(1)}, bf16[768,768]{1,0:T(8,128)(2,1)S(1)}, bf16[768,768]{1,0:T(8,128)(2,1)S(1)}) custom-call(s32[3]{0:T(128)S(1)} %pad_add_fusion.2.place_ref, f32[4,96,768]{2,1,0:T(8,128)} %pad_maximum_fusion.9.near_ref, f32[4,96,768]{2,1,0:T(8,128)} %collective-permute-done.57.far_ref), custom_call_target="tpu_custom_call" | custom-call | flops 7247757312 | bytes 7077888 | tf_op jit(solution)/shard_map/pallas_call | solution.py:194
  688.6 14.3 %all-to-all-done.5 = bf16[4,192,1024]{2,1,0:T(8,128)(2,1)} async-done(((bf16[4,192,1024]{2,1,0:T(8,128)(2,1)}), bf16[4,192,1024]{2,1,0:T(8,128)(2,1)}, u32[]{:S(2)}, u32[]{:S(2)}) %all-to-all-start.5) | async-done | bytes 1572896 | tf_op jit(solution)/shard_map/all_to_all | solution.py:609
  711.6 9.8 %shard_map.331 = (bf16[768,768]{1,0:T(8,128)(2,1)S(1)}, bf16[768,768]{1,0:T(8,128)(2,1)S(1)}, bf16[768,768]{1,0:T(8,128)(2,1)S(1)}) custom-call(bf16[768,768]{1,0:T(8,128)(2,1)S(1)} %copy-done.13, bf16[768,768]{1,0:T(8,128)(2,1)S(1)} %copy-done.15, bf16[768,768]{1,0:T(8,128)(2,1)S(1)} %copy-done.17), custom_call_target="tpu_custom_call" | custom-call | flops 7247757312 | bytes 7077888 | tf_op jit(solution)/shard_map/pallas_call | solution.py:194
  721.4 9.8 %shard_map.332 = (bf16[768,768]{1,0:T(8,128)(2,1)S(1)}, bf16[768,768]{1,0:T(8,128)(2,1)S(1)}, bf16[768,768]{1,0:T(8,128)(2,1)S(1)}) custom-call(bf16[768,768]{1,0:T(8,128)(2,1)S(1)} %get-tuple-element.204.g_hi, bf16[768,768]{1,0:T(8,128)(2,1)S(1)} %get-tuple-element.205.g_lo, bf16[768,768]{1,0:T(8,128)(2,1)S(1)} %get-tuple-element.206.q_ref), custom_call_target="tpu_custom_call" | custom-call | flops 7247757312 | bytes 7077888 | tf_op jit(solution)/shard_map/pallas_call | solution.py:194
  731.2 11.7 %shard_map.333 = (bf16[768,768]{1,0:T(8,128)(2,1)S(1)}, bf16[768,768]{1,0:T(8,128)(2,1)S(1)}, bf16[768,768]{1,0:T(8,128)(2,1)S(1)}) custom-call(bf16[768,768]{1,0:T(8,128)(2,1)S(1)} %get-tuple-element.207.g_hi, bf16[768,768]{1,0:T(8,128)(2,1)S(1)} %get-tuple-element.208.g_lo, bf16[768,768]{1,0:T(8,128)(2,1)S(1)} %get-tuple-element.209.q_ref), custom_call_target="tpu_custom_call" | custom-call | flops 9059696640 | bytes 7077888 | tf_op jit(solution)/shard_map/pallas_call | solution.py:194
  769.9 26.6 %all-to-all-done.7 = bf16[4,192,1024]{2,1,0:T(8,128)(2,1)} async-done(((bf16[4,192,1024]{2,1,0:T(8,128)(2,1)}), bf16[4,192,1024]{2,1,0:T(8,128)(2,1)}, u32[]{:S(2)}, u32[]{:S(2)}) %all-to-all-start.7) | async-done | bytes 1572896 | tf_op jit(solution)/shard_map/all_to_all | solution.py:609
  (468 shorter events, 333.9 us)
Async XLA Ops:
  4.1 47.1 %collective-permute-start.4 = (s32[128,544]{1,0:T(8,128)}, s32[128,544]{1,0:T(8,128)}, u32[]{:S(2)}, u32[]{:S(2)}) collective-permute-start(s32[128,544]{1,0:T(8,128)} %pad_add_fusion.1), channel_id=1, source_target_pairs={{0,1},{1,0},{2,3},{3,2},{4,5},{5,4},{6,7},{7,6},{8,9},{9,8},{10,11... | collective-permute-start | bytes 835592 | tf_op jit(solution)/shard_map/ppermute | solution.py:596
  7.1 47.5 %collective-permute-start.5 = (s32[128,544]{1,0:T(8,128)}, s32[128,544]{1,0:T(8,128)}, u32[]{:S(2)}, u32[]{:S(2)}) collective-permute-start(s32[128,544]{1,0:T(8,128)} %pad_add_fusion.1), channel_id=1, source_target_pairs={{0,2},{1,3},{2,0},{3,1},{4,6},{5,7},{6,4},{7,5},{8,10},{9,11},{10,... | collective-permute-start | bytes 835592 | tf_op jit(solution)/shard_map/ppermute | solution.py:596
  9.7 44.9 %collective-permute-start.6 = (s32[128,544]{1,0:T(8,128)}, s32[128,544]{1,0:T(8,128)}, u32[]{:S(2)}, u32[]{:S(2)}) collective-permute-start(s32[128,544]{1,0:T(8,128)} %pad_add_fusion.1), channel_id=1, source_target_pairs={{0,3},{1,2},{2,1},{3,0},{4,7},{5,6},{6,5},{7,4},{8,11},{9,10},{10,... | collective-permute-start | bytes 835592 | tf_op jit(solution)/shard_map/ppermute | solution.py:596
  13.1 59.3 %all-to-all-start = ((bf16[192,4,1024]{2,0,1:T(8,128)(2,1)}), bf16[192,4,1024]{2,0,1:T(8,128)(2,1)}, u32[]{:S(2)}, u32[]{:S(2)}) async-start(bf16[192,4,1024]{2,0,1:T(8,128)(2,1)} %bitcast.189), calls=%async_computation | async-start | bytes 3145728 | tf_op jit(solution)/shard_map/all_to_all | solution.py:603
  59.7 99.3 %collective-permute-start.10 = (s32[512,544]{0,1:T(8,128)}, s32[512,544]{0,1:T(8,128)}, u32[]{:S(2)}, u32[]{:S(2)}) collective-permute-start(s32[512,544]{0,1:T(8,128)} %copy.116), channel_id=1, source_target_pairs={{0,4},{4,0},{1,5},{5,1},{2,6},{6,2},{3,7},{7,3},{8,12},{12,8},{9,1... | collective-permute-start | bytes 3342344 | tf_op jit(solution)/shard_map/ppermute | solution.py:596
  115.2 39.9 %all-to-all-start.1 = ((bf16[4,1024,192]{1,2,0:T(8,128)(2,1)}), bf16[4,1024,192]{1,2,0:T(8,128)(2,1)S(1)}, u32[]{:S(2)}, u32[]{:S(2)}) async-start(bf16[4,1024,192]{1,2,0:T(8,128)(2,1)} %bitcast.194), calls=%async_computation.1 | async-start | bytes 3145728 | tf_op jit(solution)/shard_map/all_to_all | solution.py:606
  120.5 40.2 %collective-permute-start.12 = (bf16[784,512]{1,0:T(8,128)(2,1)}, bf16[784,512]{1,0:T(8,128)(2,1)}, u32[]{:S(2)}, u32[]{:S(2)}) collective-permute-start(bf16[784,512]{1,0:T(8,128)(2,1)} %get-tuple-element.261), channel_id=1, source_target_pairs={{0,8},{8,0},{16,24},{24,16},{1,9},{9,1},{17,25},{25,17},{2,10},{10... | collective-permute-start | bytes 2408456 | tf_op jit(solution)/shard_map/ppermute | solution.py:596
  122.0 41.9 %collective-permute-start.14 = (bf16[784,512]{1,0:T(8,128)(2,1)}, bf16[784,512]{1,0:T(8,128)(2,1)}, u32[]{:S(2)}, u32[]{:S(2)}) collective-permute-start(bf16[784,512]{1,0:T(8,128)(2,1)} %get-tuple-element.260), channel_id=1, source_target_pairs={{0,16},{8,24},{16,0},{24,8},{1,17},{9,25},{17,1},{25,9},{2,18},{10... | collective-permute-start | bytes 2408456 | tf_op jit(solution)/shard_map/ppermute | solution.py:596
  163.4 66.3 %collective-permute-start.13 = (bf16[784,1024]{1,0:T(8,128)(2,1)}, bf16[784,1024]{1,0:T(8,128)(2,1)}, u32[]{:S(2)}, u32[]{:S(2)}) collective-permute-start(bf16[784,1024]{1,0:T(8,128)(2,1)} %pad_maximum_fusion.3.refs_0_), channel_id=1, source_target_pairs={{0,16},{8,24},{16,0},{24,8},{1,17},{9,25},{17,1},{25,9},{2,18},{10... | collective-permute-start | bytes 4816904 | tf_op jit(solution)/shard_map/ppermute | solution.py:596
  166.7 63.1 %collective-permute-start.15 = (bf16[784,1024]{1,0:T(8,128)(2,1)}, bf16[784,1024]{1,0:T(8,128)(2,1)}, u32[]{:S(2)}, u32[]{:S(2)}) collective-permute-start(bf16[784,1024]{1,0:T(8,128)(2,1)} %pad_maximum_fusion.4.refs_2_), channel_id=1, source_target_pairs={{0,8},{8,0},{16,24},{24,16},{1,9},{9,1},{17,25},{25,17},{2,10},{10... | collective-permute-start | bytes 4816904 | tf_op jit(solution)/shard_map/ppermute | solution.py:596
  179.0 41.2 %collective-permute-start.9 = (bf16[128,768]{1,0:T(8,128)(2,1)S(1)}, bf16[128,768]{1,0:T(8,128)(2,1)S(1)}, u32[]{:S(2)}, u32[]{:S(2)}) collective-permute-start(bf16[128,768]{1,0:T(8,128)(2,1)S(1)} %fusion.18), channel_id=1, source_target_pairs={{0,3},{1,2},{2,1},{3,0},{4,7},{5,6},{6,5},{7,4},{8,11},{9,10},{10,... | collective-permute-start | bytes 589832 | tf_op jit(solution)/shard_map/ppermute | solution.py:596
  182.8 61.1 %collective-permute-start.17 = (bf16[1024,768]{1,0:T(8,128)(2,1)}, bf16[1024,768]{1,0:T(8,128)(2,1)}, u32[]{:S(2)}, u32[]{:S(2)}) collective-permute-start(bf16[1024,768]{1,0:T(8,128)(2,1)} %pad_maximum_fusion.5.refs_4_.dec_a), channel_id=1, source_target_pairs={{0,16},{8,24},{16,0},{24,8},{1,17},{9,25},{17,1},{25,9},{2,18},{10... | collective-permute-start | bytes 4718600 | tf_op jit(solution)/shard_map/ppermute | solution.py:596
  189.2 54.8 %collective-permute-start.19 = (bf16[1024,768]{1,0:T(8,128)(2,1)}, bf16[1024,768]{1,0:T(8,128)(2,1)}, u32[]{:S(2)}, u32[]{:S(2)}) collective-permute-start(bf16[1024,768]{1,0:T(8,128)(2,1)} %pad_maximum_fusion.6.refs_6_.dec_b), channel_id=1, source_target_pairs={{0,8},{8,0},{16,24},{24,16},{1,9},{9,1},{17,25},{25,17},{2,10},{10... | collective-permute-start | bytes 4718600 | tf_op jit(solution)/shard_map/ppermute | solution.py:596
  281.3 29.8 %collective-permute-start.22 = (bf16[128,1536]{1,0:T(8,128)(2,1)S(1)}, bf16[128,1536]{1,0:T(8,128)(2,1)S(1)}, u32[]{:S(2)}, u32[]{:S(2)}) collective-permute-start(bf16[128,1536]{1,0:T(8,128)(2,1)S(1)} %get-tuple-element.264), channel_id=1, source_target_pairs={{0,2},{1,3},{2,0},{3,1},{4,6},{5,7},{6,4},{7,5},{8,10},{9,11},{10,... | collective-permute-start | bytes 1179656 | tf_op jit(solution)/shard_map/ppermute | solution.py:596
  281.8 29.3 %collective-permute-start.23 = (bf16[128,1536]{1,0:T(8,128)(2,1)S(1)}, bf16[128,1536]{1,0:T(8,128)(2,1)S(1)}, u32[]{:S(2)}, u32[]{:S(2)}) collective-permute-start(bf16[128,1536]{1,0:T(8,128)(2,1)S(1)} %get-tuple-element.263), channel_id=1, source_target_pairs={{0,3},{1,2},{2,1},{3,0},{4,7},{5,6},{6,5},{7,4},{8,11},{9,10},{10,... | collective-permute-start | bytes 1179656 | tf_op jit(solution)/shard_map/ppermute | solution.py:596
  312.8 23.6 %collective-permute-start.24 = (bf16[128,1536]{1,0:T(8,128)(2,1)S(1)}, bf16[128,1536]{1,0:T(8,128)(2,1)S(1)}, u32[]{:S(2)}, u32[]{:S(2)}) collective-permute-start(bf16[128,1536]{1,0:T(8,128)(2,1)S(1)} %get-tuple-element.279), channel_id=1, source_target_pairs={{0,1},{1,0},{2,3},{3,2},{4,5},{5,4},{6,7},{7,6},{8,9},{9,8},{10,11... | collective-permute-start | bytes 1179656 | tf_op jit(solution)/shard_map/ppermute | solution.py:596
  321.0 29.8 %collective-permute-start.25 = (bf16[128,1536]{1,0:T(8,128)(2,1)S(1)}, bf16[128,1536]{1,0:T(8,128)(2,1)S(1)}, u32[]{:S(2)}, u32[]{:S(2)}) collective-permute-start(bf16[128,1536]{1,0:T(8,128)(2,1)S(1)} %get-tuple-element.279), channel_id=1, source_target_pairs={{0,2},{1,3},{2,0},{3,1},{4,6},{5,7},{6,4},{7,5},{8,10},{9,11},{10,... | collective-permute-start | bytes 1179656 | tf_op jit(solution)/shard_map/ppermute | solution.py:596
  321.0 29.8 %collective-permute-start.26 = (bf16[128,1536]{1,0:T(8,128)(2,1)S(1)}, bf16[128,1536]{1,0:T(8,128)(2,1)S(1)}, u32[]{:S(2)}, u32[]{:S(2)}) collective-permute-start(bf16[128,1536]{1,0:T(8,128)(2,1)S(1)} %get-tuple-element.279), channel_id=1, source_target_pairs={{0,3},{1,2},{2,1},{3,0},{4,7},{5,6},{6,5},{7,4},{8,11},{9,10},{10,... | collective-permute-start | bytes 1179656 | tf_op jit(solution)/shard_map/ppermute | solution.py:596
  357.1 130.0 %all-to-all-start.2 = ((bf16[192,4,1024]{2,0,1:T(8,128)(2,1)}), bf16[192,4,1024]{2,0,1:T(8,128)(2,1)}, u32[]{:S(2)}, u32[]{:S(2)}) async-start(bf16[192,4,1024]{2,0,1:T(8,128)(2,1)} %bitcast.178), calls=%async_computation.2 | async-start | bytes 3145728 | tf_op jit(solution)/shard_map/all_to_all | solution.py:603
  396.2 42.3 %collective-permute-start.32 = (bf16[768,1024]{1,0:T(8,128)(2,1)}, bf16[768,1024]{1,0:T(8,128)(2,1)}, u32[]{:S(2)}, u32[]{:S(2)}) collective-permute-start(bf16[768,1024]{1,0:T(8,128)(2,1)} %get-tuple-element.144), channel_id=1, source_target_pairs={{0,16},{8,24},{16,0},{24,8},{1,17},{9,25},{17,1},{25,9},{2,18},{10... | collective-permute-start | bytes 4718600 | tf_op jit(solution)/shard_map/ppermute | solution.py:596
  397.8 43.6 %collective-permute-start.34 = (bf16[768,1024]{1,0:T(8,128)(2,1)}, bf16[768,1024]{1,0:T(8,128)(2,1)}, u32[]{:S(2)}, u32[]{:S(2)}) collective-permute-start(bf16[768,1024]{1,0:T(8,128)(2,1)} %get-tuple-element.146), channel_id=1, source_target_pairs={{0,8},{8,0},{16,24},{24,16},{1,9},{9,1},{17,25},{25,17},{2,10},{10... | collective-permute-start | bytes 4718600 | tf_op jit(solution)/shard_map/ppermute | solution.py:596
  416.9 51.3 %collective-permute-start.28 = (bf16[784,1024]{1,0:T(8,128)(2,1)}, bf16[784,1024]{1,0:T(8,128)(2,1)}, u32[]{:S(2)}, u32[]{:S(2)}) collective-permute-start(bf16[784,1024]{1,0:T(8,128)(2,1)} %get-tuple-element.140), channel_id=1, source_target_pairs={{0,16},{8,24},{16,0},{24,8},{1,17},{9,25},{17,1},{25,9},{2,18},{10... | collective-permute-start | bytes 4816904 | tf_op jit(solution)/shard_map/ppermute | solution.py:596
  417.4 52.9 %collective-permute-start.30 = (bf16[784,1024]{1,0:T(8,128)(2,1)}, bf16[784,1024]{1,0:T(8,128)(2,1)S(1)}, u32[]{:S(2)}, u32[]{:S(2)}) collective-permute-start(bf16[784,1024]{1,0:T(8,128)(2,1)} %get-tuple-element.142), channel_id=1, source_target_pairs={{0,8},{8,0},{16,24},{24,16},{1,9},{9,1},{17,25},{25,17},{2,10},{10... | collective-permute-start | bytes 4816904 | tf_op jit(solution)/shard_map/ppermute | solution.py:596
  440.7 45.8 %collective-permute-start.33 = (bf16[768,512]{1,0:T(8,128)(2,1)S(1)}, bf16[768,512]{1,0:T(8,128)(2,1)S(1)}, u32[]{:S(2)}, u32[]{:S(2)}) collective-permute-start(bf16[768,512]{1,0:T(8,128)(2,1)S(1)} %split.41), channel_id=1, source_target_pairs={{0,8},{8,0},{16,24},{24,16},{1,9},{9,1},{17,25},{25,17},{2,10},{10... | collective-permute-start | bytes 2359304 | tf_op jit(solution)/shard_map/ppermute | solution.py:596
  443.5 43.3 %collective-permute-start.35 = (bf16[768,512]{1,0:T(8,128)(2,1)S(1)}, bf16[768,512]{1,0:T(8,128)(2,1)S(1)}, u32[]{:S(2)}, u32[]{:S(2)}) collective-permute-start(bf16[768,512]{1,0:T(8,128)(2,1)S(1)} %split.40), channel_id=1, source_target_pairs={{0,16},{8,24},{16,0},{24,8},{1,17},{9,25},{17,1},{25,9},{2,18},{10... | collective-permute-start | bytes 2359304 | tf_op jit(solution)/shard_map/ppermute | solution.py:596
  473.5 29.3 %collective-permute-start.29 = (bf16[784,512]{1,0:T(8,128)(2,1)}, bf16[784,512]{1,0:T(8,128)(2,1)}, u32[]{:S(2)}, u32[]{:S(2)}) collective-permute-start(bf16[784,512]{1,0:T(8,128)(2,1)} %get-tuple-element.304), channel_id=1, source_target_pairs={{0,8},{8,0},{16,24},{24,16},{1,9},{9,1},{17,25},{25,17},{2,10},{10... | collective-permute-start | bytes 2408456 | tf_op jit(solution)/shard_map/ppermute | solution.py:596
  493.6 74.4 %all-to-all-start.3 = ((bf16[192,4,1024]{2,0,1:T(8,128)(2,1)}), bf16[192,4,1024]{2,0,1:T(8,128)(2,1)}, u32[]{:S(2)}, u32[]{:S(2)}) async-start(bf16[192,4,1024]{2,0,1:T(8,128)(2,1)} %bitcast.190), calls=%async_computation.3 | async-start | bytes 3145728 | tf_op jit(solution)/shard_map/all_to_all | solution.py:603
  498.8 24.6 %collective-permute-start.31 = (bf16[784,512]{1,0:T(8,128)(2,1)}, bf16[784,512]{1,0:T(8,128)(2,1)S(1)}, u32[]{:S(2)}, u32[]{:S(2)}) collective-permute-start(bf16[784,512]{1,0:T(8,128)(2,1)} %get-tuple-element.305), channel_id=1, source_target_pairs={{0,16},{8,24},{16,0},{24,8},{1,17},{9,25},{17,1},{25,9},{2,18},{10... | collective-permute-start | bytes 2408456 | tf_op jit(solution)/shard_map/ppermute | solution.py:596
  574.5 79.6 %all-to-all-start.4 = ((bf16[4,192,1024]{2,1,0:T(8,128)(2,1)}), bf16[4,192,1024]{2,1,0:T(8,128)(2,1)}, u32[]{:S(2)}, u32[]{:S(2)}) async-start(bf16[4,192,1024]{2,1,0:T(8,128)(2,1)} %bitcast.195), calls=%async_computation.4 | async-start | bytes 3145728 | tf_op jit(solution)/shard_map/all_to_all | solution.py:609
  659.6 43.3 %all-to-all-start.5 = ((bf16[4,192,1024]{2,1,0:T(8,128)(2,1)}), bf16[4,192,1024]{2,1,0:T(8,128)(2,1)}, u32[]{:S(2)}, u32[]{:S(2)}) async-start(bf16[4,192,1024]{2,1,0:T(8,128)(2,1)} %bitcast.70), calls=%async_computation.5 | async-start | bytes 3145728 | tf_op jit(solution)/shard_map/all_to_all | solution.py:609
  705.5 43.3 %all-to-all-start.6 = ((bf16[4,192,1024]{2,1,0:T(8,128)(2,1)}), bf16[4,192,1024]{2,1,0:T(8,128)(2,1)}, u32[]{:S(2)}, u32[]{:S(2)}) async-start(bf16[4,192,1024]{2,1,0:T(8,128)(2,1)} %bitcast.196), calls=%async_computation.6 | async-start | bytes 3145728 | tf_op jit(solution)/shard_map/all_to_all | solution.py:609
  754.3 42.2 %all-to-all-start.7 = ((bf16[4,192,1024]{2,1,0:T(8,128)(2,1)}), bf16[4,192,1024]{2,1,0:T(8,128)(2,1)}, u32[]{:S(2)}, u32[]{:S(2)}) async-start(bf16[4,192,1024]{2,1,0:T(8,128)(2,1)} %bitcast.208), calls=%async_computation.7 | async-start | bytes 3145728 | tf_op jit(solution)/shard_map/all_to_all | solution.py:609
  (113 other events, 1143.8 us)

commit v5 on v4

--- a/solution.py
+++ b/solution.py
@@ -199,7 +199,7 @@
         scratch_shapes=[pltpu.VMEM((size, size), kind) for kind in scratch],
         compiler_params=pltpu.CompilerParams(vmem_limit_bytes=40 * 2**20),
         cost_estimate=pl.CostEstimate(
-            flops=passes * 2 * size**3, bytes_accessed=12 * size * size, transcendentals=0
+            flops=passes * size**3 // 16, bytes_accessed=size * size // 2, transcendentals=0
         ),
     )(*operands)
 
@@ -284,21 +284,33 @@
     lax.fori_loop(0, rows // batch, one_batch, 0)
 
 
-def kind_codes(place, ids, dead_here, wide_latents, own_latents, top_count, orders):
+def kind_codes(place, ids, dead_here, sizes, part, parts, held=None):
+    wide_latents, own_latents, top_count, orders = sizes
     row_total, pick_total = ids.shape
     latent_count = dead_here.shape[1]
     rows = min(128, row_total)
+    first = part * (row_total // rows)
     shifts = (wide_latents.bit_length() - 1, own_latents.bit_length() - 1, top_count, orders)
+    kernel = functools.partial(code_kernel, shifts)
+    operands, specs, aliases = [place, ids, dead_here], [], {}
+    if held is not None:
+        operands, specs, aliases = operands + [held], [pl.BlockSpec(memory_space=pl.ANY)], {3: 0}
+
+    def body(place_ref, ids_ref, dead_ref, *refs):
+        kernel(place_ref, ids_ref, dead_ref, *refs[len(specs) :])
+
     return pl.pallas_call(
-        functools.partial(code_kernel, shifts),
+        body,
         grid=(row_total // rows,),
-        out_shape=jax.ShapeDtypeStruct((row_total, latent_count), jnp.bfloat16),
+        out_shape=jax.ShapeDtypeStruct((parts * row_total, latent_count), jnp.bfloat16),
         in_specs=[
             pl.BlockSpec(memory_space=pltpu.SMEM),
             pl.BlockSpec((rows, pick_total), lambda i: (i, 0)),
             pl.BlockSpec((1, latent_count), lambda i: (0, 0)),
-        ],
-        out_specs=pl.BlockSpec((rows, latent_count), lambda i: (i, 0)),
+        ]
+        + specs,
+        out_specs=pl.BlockSpec((rows, latent_count), lambda i: (i + first, 0)),
+        input_output_aliases=aliases,
         scratch_shapes=[
             pltpu.VMEM((rows, pick_total), jnp.float32),
             pltpu.VMEM((rows, pick_total), jnp.float32),
@@ -306,11 +318,11 @@
         ],
         compiler_params=pltpu.CompilerParams(vmem_limit_bytes=40 * 2**20),
         cost_estimate=pl.CostEstimate(
-            flops=40 * row_total * latent_count * 128,
-            bytes_accessed=2 * row_total * latent_count,
+            flops=row_total * latent_count,
+            bytes_accessed=row_total * pick_total,
             transcendentals=0,
         ),
-    )(place, ids, dead_here)
+    )(*operands)
 
 
 def pick_copy(step, count, sources, target):
@@ -337,6 +349,7 @@
         acc_aux[...] = jnp.zeros_like(acc_aux)
 
     bias = enc[pl.ds(width, 16), :].astype(jnp.float32)[:1]
+    to_features = (((1,), (1,)), ((), ()))
 
     def one(index, carry):
         rows = pl.ds(pl.multiple_of(index * block, block), block)
@@ -347,8 +360,12 @@
         aux = jnp.where(codes == 2.0, pre, zero)
         top_ref[rows, :] = top
         aux_ref[rows, :] = aux
-        acc_top[rows, :] += dot_f32(top, dec[...])
-        acc_aux[rows, :] += dot_f32(aux, dec[...])
+        acc_top[rows, :] += lax.dot_general(
+            top, dec[...], to_features, preferred_element_type=jnp.float32
+        )
+        acc_aux[rows, :] += lax.dot_general(
+            aux, dec[...], to_features, preferred_element_type=jnp.float32
+        )
         return carry
 
     lax.fori_loop(0, rows_all // block, one, 0)
@@ -394,17 +411,17 @@
         ],
         in_specs=[fixed(x.shape), lanes]
         + part_specs(encs[0].shape, 1, block, count, (0, 0, 0, 0))
-        + part_specs(decs[0].shape, 0, block, count, (0, 0, 0, 0)),
+        + part_specs(decs[0].shape, 1, block, count, (0, 0, 0, 0)),
         out_specs=[lanes, lanes, fixed(half_shape), fixed(half_shape)],
         scratch_shapes=[
-            pltpu.VMEM((encs[0].shape[0], block), bf16),
-            pltpu.VMEM((block, width), bf16),
+            pltpu.VMEM((width + 16, block), bf16),
+            pltpu.VMEM((width, block), bf16),
             pltpu.VMEM((rows, width), f32),
             pltpu.VMEM((rows, width), f32),
         ],
         compiler_params=pltpu.CompilerParams(vmem_limit_bytes=58 * 2**20),
         cost_estimate=pl.CostEstimate(
-            flops=6 * rows * width * codes.shape[1],
+            flops=2 * rows * width * codes.shape[1],
             bytes_accessed=6 * rows * codes.shape[1],
             transcendentals=0,
         ),
@@ -457,7 +474,7 @@
         out_specs=part_specs(shape, 1, block, count, (0, 0)),
         compiler_params=pltpu.CompilerParams(vmem_limit_bytes=58 * 2**20),
         cost_estimate=pl.CostEstimate(
-            flops=8 * rows * width * quarter, bytes_accessed=8 * rows * quarter, transcendentals=0
+            flops=rows * width * quarter // 8, bytes_accessed=rows * quarter // 4, transcendentals=0
         ),
     )(back_t, back_t, top_acts, aux_acts)
 
@@ -465,26 +482,21 @@
 def enc_grad_kernel(count, x_ref, back_ref, codes_ref, dec_a, dec_b, out_a, out_b, dec, grads):
     step = pl.program_id(0)
     pick_copy(step, count, (dec_a, dec_b), dec)
-    width = x_ref.shape[0]
+    width, latents = dec.shape
     block = min(1024, back_ref.shape[0])
-    to_latents = (((1,), (1,)), ((), ()))
 
     def one(index, total):
         rows = pl.ds(pl.multiple_of(index * block, block), block)
         codes = codes_ref[rows, :].astype(jnp.float32)
-        top = lax.dot_general(
-            back_ref[rows, :width], dec[...], to_latents, preferred_element_type=jnp.float32
-        )
-        aux = lax.dot_general(
-            back_ref[rows, width:], dec[...], to_latents, preferred_element_type=jnp.float32
-        )
+        top = dot_f32(back_ref[rows, :width], dec[...])
+        aux = dot_f32(back_ref[rows, width:], dec[...])
         value = jnp.where(codes == 1.0, top, jnp.where(codes == 2.0, aux, 0.0))
         value = value.astype(jnp.bfloat16)
         grads[rows, :] = value
         return total + jnp.sum(value.astype(jnp.float32), 0, keepdims=True)
 
     total = lax.fori_loop(
-        0, back_ref.shape[0] // block, one, jnp.zeros((1, dec.shape[0]), jnp.float32)
+        0, back_ref.shape[0] // block, one, jnp.zeros((1, latents), jnp.float32)
     )
 
     def two(index, carry):
@@ -493,7 +505,7 @@
         return carry
 
     lax.fori_loop(0, width // 384, two, 0)
-    lines = lax.broadcasted_iota(jnp.int32, (16, dec.shape[0]), 0)
+    lines = lax.broadcasted_iota(jnp.int32, (16, latents), 0)
     if out_a.dtype == jnp.bfloat16:
         high = total.astype(jnp.bfloat16).astype(jnp.float32)
         lines = jnp.where(lines == 0, high, jnp.where(lines == 1, total - high, 0.0))
@@ -502,7 +514,7 @@
     store_part(count, (out_a, out_b), pl.ds(width, 16), lines)
 
 
-def enc_grads(x_t, back, codes, decs, quarters, kind):
+def enc_grads(x_t, back, codes, parts, quarters, kind):
     width, rows = x_t.shape
     quarter = codes.shape[1] // 4
     block = min(512, quarter)
@@ -521,17 +533,61 @@
             pl.BlockSpec(back.shape, lambda step: (0, 0)),
             pl.BlockSpec((rows, block), lanes),
         ]
-        + part_specs(decs[0].shape, 0, block, count, (0, 0)),
+        + part_specs(parts[0].shape, 1, block, count, (0, 0)),
         out_specs=part_specs(shape, 1, block, count, (0, 0)),
         scratch_shapes=[
-            pltpu.VMEM((block, width), jnp.bfloat16),
+            pltpu.VMEM((width, block), jnp.bfloat16),
             pltpu.VMEM((rows, block), jnp.bfloat16),
         ],
         compiler_params=pltpu.CompilerParams(vmem_limit_bytes=58 * 2**20),
         cost_estimate=pl.CostEstimate(
-            flops=12 * rows * width * quarter, bytes_accessed=8 * rows * quarter, transcendentals=0
+            flops=rows * width * quarter // 8, bytes_accessed=rows * quarter // 4, transcendentals=0
         ),
-    )(x_t, back, codes, *decs)
+    )(x_t, back, codes, *parts)
+
+
+def finish_kernel(place_ref, factor_ref, momentum_ref, weight_ref, *outs):
+    new_ref, next_ref, copy_ref = outs
+    rows = factor_ref.shape[0]
+    f32 = jnp.float32
+    momentum = momentum_ref[0]
+    kept = momentum_ref[0, pl.ds(pl.multiple_of(place_ref[2] * rows, 16), rows), :].astype(f32)
+    ortho = dot_f32(factor_ref[...], momentum)
+    next_ref[...] = kept
+    step_scale = MUON_RATE * 0.2 * math.sqrt(max(D, L))
+    value = weight_ref[...] * (1.0 - MUON_RATE * DECAY) - step_scale * ortho
+    new_ref[...] = value
+    copy_ref[...] = value.astype(jnp.bfloat16)
+
+
+def finish(place, factor, momenta, weight):
+    count, width, block = momenta.shape
+    rows = weight.shape[0]
+    part = pl.BlockSpec((rows, block), lambda step, place: (0, step))
+    return pl.pallas_call(
+        finish_kernel,
+        grid_spec=pltpu.PrefetchScalarGridSpec(
+            num_scalar_prefetch=1,
+            grid=(count,),
+            in_specs=[
+                pl.BlockSpec((rows, width), lambda step, place: (place[2], 0)),
+                pl.BlockSpec((1, width, block), lambda step, place: (step, 0, 0)),
+                part,
+            ],
+            out_specs=[part] * 3,
+        ),
+        out_shape=[
+            jax.ShapeDtypeStruct(weight.shape, jnp.float32),
+            jax.ShapeDtypeStruct(weight.shape, jnp.float32),
+            jax.ShapeDtypeStruct(weight.shape, jnp.bfloat16),
+        ],
+        compiler_params=pltpu.CompilerParams(vmem_limit_bytes=58 * 2**20),
+        cost_estimate=pl.CostEstimate(
+            flops=2 * rows * width * block * count,
+            bytes_accessed=8 * rows * block * count,
+            transcendentals=0,
+        ),
+    )(place, factor, momenta, weight)
 
 
 def adam_update(param, grad, first, second):
@@ -588,8 +644,7 @@
     bits = [1 << bit for bit in range(chips.bit_length() - 1)]
     orders = (bits, bits[::-1])
 
-    def after(value, *others):
-        return lax.optimization_barrier((value, others))[0]
+    tie = lambda *values: lax.optimization_barrier(values)
 
     def swap(value, axis, offset):
         count = lax.axis_size(axis)
@@ -602,28 +657,25 @@
     def rows_to_latents(value):
         return lax.all_to_all(value, "narrow", split_axis=1, concat_axis=0, tiled=True)
 
-    def cols_to_latents(value):
-        return lax.all_to_all(value, "narrow", split_axis=0, concat_axis=1, tiled=True)
-
-    def latents_to_rows(value):
-        return lax.all_to_all(value, "narrow", split_axis=0, concat_axis=1, tiled=True)
-
-    def latents_to_cols(value):
-        return lax.all_to_all(value, "narrow", split_axis=1, concat_axis=0, tiled=True)
-
-    def gather_chips(own, axis):
-        pieces = []
+    def gather_start(own, axis):
+        halves = []
         for part, order in enumerate(orders):
             held = lax.slice_in_dim(own, part * half_latents, (part + 1) * half_latents, axis=axis)
             for bit in order[:-1]:
                 held = jnp.concatenate([held, swap(held, "chip", bit)], axis)
+            halves.append(held)
+        return halves
+
+    def gather_end(halves):
+        pieces = []
+        for held, order in zip(halves, orders):
             pieces += [held, swap(held, "chip", order[-1])]
         return pieces
 
-    def scatter_chips(keeps, sents):
+    def scatter_chips(keeps, gots):
         results, sums = [], []
-        for order, held, sent in zip(orders, keeps, sents):
-            held = held + swap(sent, "chip", order[-1]).astype(f32)
+        for order, held, got in zip(orders, keeps, gots):
+            held = held + got.astype(f32)
             for bit in reversed(order[:-1]):
                 lower, upper = jnp.split(held, 2, 1)
                 sent = upper[:model_width].astype(bf16)
@@ -650,8 +702,10 @@
     inside = (local_ids >= 0) & (local_ids < vocab_dev)
     looked = jnp.take(token_table, jnp.clip(local_ids, 0, vocab_dev - 1), axis=0)
     looked = jnp.where(inside[:, None], looked, jnp.zeros((), bf16))
+    dec_weight_t, dec_moment_t = dec_weight.T, dec_moment.T
+    rows_each = enc_weight.shape[0]
     enc_own = rows_to_latents(enc_weight.astype(bf16))
-    picks = after(jnp.concatenate([top_ids, aux_ids], 1), every_ids)
+    picks = jnp.concatenate([top_ids, aux_ids], 1)
     near_picks = spread_narrow(picks)
     far_picks = swap(near_picks, "core", 1)
 
@@ -664,9 +718,10 @@
     bias_rows = jnp.concatenate(
         [enc_bias.astype(bf16)[None], jnp.zeros((15, own_latents), bf16)], 0
     )
-    enc_biased = jnp.concatenate([enc_own, bias_rows], 0)
-    enc_parts = gather_chips(enc_biased, 1)
-    dec_own = cols_to_latents(after(dec_weight, enc_own).astype(bf16))
+    enc_own, embedded = tie(enc_own, embedded)
+    dec_cast, enc_own = tie(dec_weight_t.astype(bf16), enc_own)
+    dec_own = rows_to_latents(dec_cast)
+    enc_halves = gather_start(jnp.concatenate([enc_own, bias_rows], 0), 1)
 
     dead_here = jnp.stack(
         [
@@ -688,24 +743,37 @@
             dead_parts.append(dead_here[spot, part * half_latents : (part + 1) * half_latents])
     dead_here = jnp.concatenate(dead_parts)[None]
     sizes = (wide_latents, own_latents, top_ids.shape[1], orders)
-    near_codes = kind_codes(place, after(near_picks, enc_biased), dead_here, *sizes)
-
-    start = after(embedded, near_codes) + position_table[:row_count].astype(f32)
+    start = embedded + position_table[:row_count].astype(f32)
     ctx_length = lengths[0]
     inputs = frozen_block(start, ctx_length, ln_gains, frozen_bias, w_qkv, w_proj, w_fc, w_out)
     counted = (jnp.arange(row_count) < ctx_length).astype(f32)
-    dec_own = after(dec_own, inputs)
-    dec_parts = gather_chips(dec_own, 0)
-    near_inputs = spread_narrow(after(inputs, dec_own))
-    far_codes = kind_codes(place, after(far_picks, inputs), dead_here, *sizes)
-    near_inputs = after(near_inputs, far_codes)
-    far_inputs = swap(near_inputs, "core", 1)
-    codes = jnp.concatenate([near_codes, far_codes], 0)
+    dec_own, near_picks, inputs, enc_halves = tie(dec_own, near_picks, inputs, enc_halves)
+    enc_parts = gather_end(enc_halves)
+    got_inputs = [swap(inputs, "narrow", k) for k in range(1, narrow_count)]
+    dec_halves = gather_start(dec_own, 1)
+    moments = jnp.concatenate([enc_moment.astype(bf16), dec_moment_t.astype(bf16)], 0)
+    moments, dec_own = tie(moments, dec_own)
+    moments = rows_to_latents(moments)
+    near_codes = kind_codes(place, near_picks, dead_here, sizes, 0, 2)
+    enc_lasts = [enc_parts[1], enc_parts[3]]
+    dec_halves, got_inputs, near_codes, enc_lasts = tie(
+        dec_halves, got_inputs, near_codes, enc_lasts
+    )
+    enc_parts = [enc_parts[0], enc_lasts[0], enc_parts[2], enc_lasts[1]]
+    dec_parts = gather_end(dec_halves)
+    near_inputs = jnp.concatenate([inputs, *got_inputs], 0)
+    codes = kind_codes(place, far_picks, dead_here, sizes, 1, 2, near_codes)
+    far_inputs, codes = tie(swap(near_inputs, "core", 1), codes)
     all_inputs = jnp.concatenate([near_inputs, far_inputs], 0)
     encoder_in = (all_inputs.astype(f32) - decoder_bias).astype(bf16)
     top_acts, aux_acts, far, near = forward(encoder_in, codes, enc_parts, dec_parts)
+    far, moments = tie(far, moments)
+    moments = moments.reshape(narrow_count, 2, rows_each, own_latents)
+    enc_moment_own = moments[:, 0].reshape(model_width, own_latents)
+    dec_moment_own = moments[:, 1].reshape(model_width, own_latents)
     encoder_t = encoder_in.T
-    rebuilt = near + swap(far, "core", 1).astype(f32)
+    far_got, encoder_t = tie(swap(far, "core", 1), encoder_t)
+    rebuilt = near + far_got.astype(f32)
     rounded = rebuilt.astype(bf16)
     rebuilt = rebuilt[:row_count]
     for k in range(1, narrow_count):
@@ -728,20 +796,17 @@
     shard_rows = jnp.concatenate([near_back, swap(near_back, "core", 1)], 0)
     back_t = shard_rows.T
     dec_sent = dec_grads(back_t, top_acts, aux_acts, (1, 3), bf16)
-    shard_rows, top_acts, dec_sent = lax.optimization_barrier((shard_rows, top_acts, dec_sent))
+    back_t, dec_sent = tie(back_t, dec_sent)
     dec_keep = dec_grads(back_t, top_acts, aux_acts, (0, 2), f32)
-    shard_rows, dec_keep = lax.optimization_barrier((shard_rows, dec_keep))
+    shard_rows, dec_keep = tie(shard_rows, dec_keep)
     enc_sent = enc_grads(encoder_t, shard_rows, codes, dec_parts[1::2], (1, 3), bf16)
-    shard_rows, enc_sent = lax.optimization_barrier((shard_rows, enc_sent))
+    shard_rows, enc_sent = tie(shard_rows, enc_sent)
     enc_keep = enc_grads(encoder_t, shard_rows, codes, dec_parts[::2], (0, 2), f32)
-    dec_moment_own = rows_to_latents(after(dec_moment, back_rows).astype(bf16).T)
-    enc_moment_own = rows_to_latents(after(enc_moment, dec_moment_own).astype(bf16))
-    dec_grad, _ = scatter_chips(dec_keep, dec_sent)
-    enc_grad, encb_grad = scatter_chips(enc_keep, enc_sent)
-    bias_term = jnp.sum(back_rows[:, :model_width], 0, dtype=f32) - jnp.dot(
-        enc_own.astype(f32), encb_grad, precision=HIGH_PRECISION
-    )
-
+    dec_gots = [swap(sent, "chip", order[-1]) for order, sent in zip(orders, dec_sent)]
+    dec_gots, enc_sent = tie(dec_gots, enc_sent)
+    enc_gots = [swap(sent, "chip", order[-1]) for order, sent in zip(orders, enc_sent)]
+    dec_grad, _ = scatter_chips(dec_keep, dec_gots)
+    dec_grad, enc_keep = tie(dec_grad, enc_keep)
     def sum_gram(part, vector, fill):
         half = model_width // 2
         rows = half // chips
@@ -774,69 +839,75 @@
         for got in exchange([pack(total, vector)] * (narrow_count - 1), "narrow"):
             got, more = unpack(got)
             total, vector = total + got, vector + more
+        total = total.astype(bf16)
         near = jnp.stack([total, *exchange([total] * (chips - 1), "chip")])
         (far,) = exchange([near], "core")
         return near, far, vector
 
     dec_own_next = (MOMENTUM * dec_moment_own.astype(f32) + dec_grad).astype(bf16)
-    dec_own_next, enc_keep = lax.optimization_barrier((dec_own_next, enc_keep))
+    dec_momenta = lax.all_gather(dec_own_next, "narrow")
+    stages = []
+    enc_grad = encb_grad = None
+
+    def dec_note(sents, got):
+        nonlocal enc_grad, encb_grad
+        if not stages:
+            got, gots = tie(got, enc_gots)
+            enc_grad, encb_grad = scatter_chips(enc_keep, gots)
+        if len(stages) == 2:
+            got, enc_grad = tie(got, enc_grad)
+        stages.append(got)
+        return got
+
     dec_near, dec_far, _ = sum_gram(
         lax.dot_general(dec_own_next, dec_own_next, to_latents, preferred_element_type=f32),
         jnp.zeros((model_width,), f32),
-        lambda sents, got: got,
-    )
+        dec_note,
+    )
+    bias_term = jnp.sum(back_rows[:, :model_width], 0, dtype=f32) - jnp.dot(
+        enc_own.astype(f32),
+        encb_grad,
+        precision=HIGH_PRECISION,
+    )
+
     enc_own_next = (MOMENTUM * enc_moment_own.astype(f32) + enc_grad).astype(bf16)
     enc_gram = lax.dot_general(
         enc_own_next, enc_own_next, to_latents, preferred_element_type=f32
     )
     enc_gram, dec_near = lax.optimization_barrier((enc_gram, dec_near))
+    enc_momenta = lax.all_gather(enc_own_next, "narrow")
     progress = []
 
     def dec_fill(sents, got):
         step = len(progress)
         if step == 0:
-            state = series_start(after(place, sents), dec_near, dec_far)
+            early, _ = tie(dec_near, sents)
+            state = series_start(place, early, dec_far)
         else:
-            state = series_next(step, after(progress[-1], sents))
+            state = series_next(step, progress[-1])
         got, state = lax.optimization_barrier((got, state))
         progress.append(state)
         return got
 
     enc_near, enc_far, grad_decb = sum_gram(enc_gram, bias_term, dec_fill)
     dec_factor = progress[-1][0]
-    dec_rows_grad = latents_to_rows(after(dec_grad, enc_gram).astype(bf16))
-    dec_ortho = latents_to_rows(
-        jnp.dot(
-            after(dec_factor, dec_rows_grad), dec_own_next, preferred_element_type=f32
-        ).astype(bf16)
-    )
-    state = series_start(place, after(enc_near, dec_factor, dec_rows_grad), enc_far)
-    for step in range(1, NS_STEPS - 1):
+    dec_new, dec_next, dec_copy = finish(
+        place, dec_factor, dec_momenta, dec_weight_t
+    )
+    state = series_start(place, enc_near, enc_far)
+    for step in range(1, NS_STEPS):
         state = series_next(step, state)
-    state = after(state, dec_ortho)
-    enc_rows_grad = latents_to_rows(after(enc_grad, dec_ortho).astype(bf16))
-    enc_factor = series_next(NS_STEPS - 1, state)[0]
-    enc_factor = after(enc_factor, enc_rows_grad)
-    enc_ortho = latents_to_rows(
-        jnp.dot(enc_factor, enc_own_next, preferred_element_type=f32).astype(bf16)
-    )
-    dec_ortho = dec_ortho.T
-    dec_rows_grad = dec_rows_grad.T
-    enc_next = MOMENTUM * enc_moment + enc_rows_grad.astype(f32)
-    dec_next = MOMENTUM * dec_moment + dec_rows_grad.astype(f32)
-    step_scale = MUON_RATE * 0.2 * math.sqrt(max(D, L))
-    enc_new = enc_weight * (1.0 - MUON_RATE * DECAY) - step_scale * enc_ortho.astype(f32)
-    dec_new = dec_weight * (1.0 - MUON_RATE * DECAY) - step_scale * dec_ortho.astype(f32)
+    enc_new, enc_next, enc_copy = finish(place, state[0], enc_momenta, enc_weight)
     encb_new, encb_one, encb_two = adam_update(enc_bias, encb_grad, encb_first, encb_second)
     decb_new, decb_one, decb_two = adam_update(decoder_bias, grad_decb, decb_first, decb_second)
     return (
         token_loss,
         enc_new,
         enc_next,
-        enc_new.astype(bf16),
-        dec_new,
-        dec_next,
-        dec_new.astype(bf16),
+        enc_copy,
+        dec_new.T,
+        dec_next.T,
+        dec_copy.T,
         encb_new,
         encb_one,
         encb_two,

time: 813 us -> 792 us (0.974)
  other arithmetic: 91.8 us -> 62.8 us
  Pallas kernels: 245 us -> 262 us
  waiting for transfers between devices: 245 us -> 230 us
  between operations: 3.51 us -> 16.4 us
  matrix products: 24.9 us -> 16.2 us
    all_to_all x5 -> x0, waiting for transfers between devices: 60.3 us -> none  [the longest x4 40.9 us: latents_to_rows(): lax.all_to_all(value, 'narrow', split_axis=0, concat_axis=1, tiled=True)]
    all_to_all x5 -> x0, starting transfers between devices: 26.9 us -> none  [the longest x4 22.9 us: latents_to_rows(): lax.all_to_all(value, 'narrow', split_axis=0, concat_axis=1, tiled=True)]
    ppermute x58, starting transfers between devices: 68.1 us -> 92.9 us  [swap(): lax.ppermute(value, axis, [(spot, spot ^ offset) for spot in range(count)])]
    all_to_all x3, waiting for transfers between devices: 8.41 us -> 32.2 us  [rows_to_latents(): lax.all_to_all(value, 'narrow', split_axis=1, concat_axis=0, tiled=True)]
    pallas_call x2 -> x4, Pallas kernels: 55.1 us -> 72.4 us  [the longest x2 55.3 us: kind_codes(): pl.pallas_call(body, grid=(row_total // rows,), out_shape=jax.ShapeDtypeS...]
    all_gather x0 -> x2, waiting for transfers between devices: none -> 11.9 us  [the longest x1 11.9 us: local(): enc_momenta = lax.all_gather(enc_own_next, 'narrow')]
    unnamed x176 -> x146, local copies, waits for them, and re-layouts: 18.8 us -> 29.9 us
    ppermute x58, waiting for transfers between devices: 176 us -> 186 us  [swap(): lax.ppermute(value, axis, [(spot, spot ^ offset) for spot in range(count)])]
  transfers between devices with their start and end apart: 66 -> 63, of which waited for: 24 -> 24; matrix products, arithmetic and copies ran while one was open for 18% -> 13% of each run, Pallas kernels for 27% -> 31%
where the time goes in v5:
time: 792 us; the launch traced here: 782 us
  Pallas kernels  262 us (33%)
  waiting for transfers between devices  230 us (29%)
  starting transfers between devices  107 us (14%)
  local copies, waits for them, and re-layouts  77.8 us (10%)
  other arithmetic  62.8 us (8%)
  between operations  16.4 us (2%)
  matrix products  16.2 us (2%)
  blocking collectives  9.07 us (1%)
    ppermute x58, waiting for transfers between devices, swap(): lax.ppermute(value, axis, [(spot, spot ^ offset) for spot in range(count)])  186 us
    pallas_call x10, Pallas kernels, square_call(): pl.pallas_call(kernel, out_shape=[square] * outs, in_specs=specs, out_spe...  96.2 us
    ppermute x58, starting transfers between devices, swap(): lax.ppermute(value, axis, [(spot, spot ^ offset) for spot in range(count)])  92.9 us
    pallas_call x2, Pallas kernels, kind_codes(): pl.pallas_call(body, grid=(row_total // rows,), out_shape=jax.ShapeDtypeS...  55.3 us
    pallas_call x2, Pallas kernels, enc_grads(): pl.pallas_call(functools.partial(enc_grad_kernel, count), grid=(2 * count...  37.6 us
    all_to_all x3, waiting for transfers between devices, rows_to_latents(): lax.all_to_all(value, 'narrow', split_axis=1, concat_axis=0, tiled=True)  32.2 us
    pallas_call x1, Pallas kernels, forward(): pl.pallas_call(functools.partial(forward_kernel, count), grid=(4 * count,...  30.7 us
    unnamed x146, local copies, waits for them, and re-layouts  29.9 us
  transfers between devices with their start and end apart: 63, of which 24 were waited for; matrix products, arithmetic and copies ran while one was open for 13% of the time, Pallas kernels for 31%

profile of v5, /device:TPU:0, one launch (start us, length us, event | category | flops | bytes accessed | tf_op | source)
XLA Modules:
  0.0 781.6 jit_solution(68389840799471093)
XLA Ops:
  16.2 9.1 %all-gather.3 = s32[8,1,128]{2,1,0:T(1,128)S(1)} all-gather(s32[1,1,128]{2,1,0:T(1,128)} %bitcast.199), channel_id=2, replica_groups=mesh['chip'=4,'core'=2,'narrow'=4] {'chip','core'}, dimensions={0}, use_global_device_ids=true | all-gather | bytes 4608 | tf_op jit(solution)/shard_map/all_gather | solution.py:693
  25.5 10.6 %gather_fusion = bf16[1024,768]{1,0:T(8,128)(2,1)} fusion(bf16[6288,768]{1,0:T(8,128)(2,1)} %param.28, s32[1024]{0:T(1024)S(1)} %broadcast_clamp_fusion), kind=kCustom, calls=%fused_computation | custom fusion | bytes 3149824 | tf_op jit(solution)/shard_map/jit(_take)/gather | solution.py:703
  72.0 11.3 %all-to-all-done = bf16[192,4,1024]{2,0,1:T(8,128)(2,1)} async-done(((bf16[192,4,1024]{2,0,1:T(8,128)(2,1)}), bf16[192,4,1024]{2,0,1:T(8,128)(2,1)}, u32[]{:S(2)}, u32[]{:S(2)}) %all-to-all-start) | async-done | bytes 1572896 | tf_op jit(solution)/shard_map/all_to_all | solution.py:658
  116.7 20.8 %all-to-all-done.1 = bf16[192,4,1024]{2,0,1:T(8,128)(2,1)} async-done(((bf16[192,4,1024]{2,0,1:T(8,128)(2,1)}), bf16[192,4,1024]{2,0,1:T(8,128)(2,1)}, u32[]{:S(2)}, u32[]{:S(2)}) %all-to-all-start.1) | async-done | bytes 1572896 | tf_op jit(solution)/shard_map/all_to_all | solution.py:658
  155.0 44.4 %collective-permute-done.11 = bf16[128,768]{1,0:T(8,128)(2,1)S(1)} collective-permute-done((bf16[128,768]{1,0:T(8,128)(2,1)S(1)}, bf16[128,768]{1,0:T(8,128)(2,1)S(1)}, u32[]{:S(2)}, u32[]{:S(2)}) %collective-permute-start.11) | collective-permute-done | bytes 196640 | tf_op jit(solution)/shard_map/ppermute | solution.py:651
  199.5 27.8 %shard_map.318.refs_0_ = bf16[1024,4096]{1,0:T(8,128)(2,1)S(1)} custom-call(s32[3]{0:T(128)S(1)} %pad_add_fusion.2.place_ref, s32[512,544]{1,0:T(8,128)S(1)} %copy-done.5, s32[1,4096]{1,0:T(1,128)S(1)} %bitcast.157), custom_call_target="tpu_custom_call" | custom-call | flops 2097152 | bytes 278528 | tf_op jit(solution)/shard_map/pallas_call | solution.py:302
  240.3 8.9 %collective-permute-done.12 = bf16[128,768]{1,0:T(8,128)(2,1)S(1)} collective-permute-done((bf16[128,768]{1,0:T(8,128)(2,1)S(1)}, bf16[128,768]{1,0:T(8,128)(2,1)S(1)}, u32[]{:S(2)}, u32[]{:S(2)}) %collective-permute-start.12) | collective-permute-done | bytes 196640 | tf_op jit(solution)/shard_map/ppermute | solution.py:651
  257.4 27.5 %shard_map.319.codes_ref = bf16[1024,4096]{1,0:T(8,128)(2,1)S(1)} custom-call(s32[3]{0:T(128)S(1)} %pad_add_fusion.2.place_ref, s32[512,544]{1,0:T(8,128)S(1)} %copy.121.ids_ref, s32[1,4096]{1,0:T(1,128)S(1)} %bitcast.158, bf16[1024,4096]{1,0:T(8,128)(2,1)S(1)} %copy-done.3), custom_call_target="tpu_custom_call", output_to_operand_aliasing={{}: (3, {})} | custom-call | flops 2097152 | bytes 278528 | tf_op jit(solution)/shard_map/pallas_call | solution.py:302
  291.1 30.7 %shard_map.320 = (bf16[1024,4096]{1,0:T(8,128)(2,1)}, bf16[1024,4096]{1,0:T(8,128)(2,1)}, bf16[512,1536]{1,0:T(8,128)(2,1)}, f32[512,1536]{1,0:T(8,128)}) custom-call(bf16[1024,768]{1,0:T(8,128)(2,1)} %subtract_convert_fusion.x_ref, bf16[1024,4096]{1,0:T(8,128)(2,1)} %copy-done.4, bf16[784,1024]{1,0:T(8,128)(2,1)} %pad_maximum_fusion.3.refs_0_, ...), custom_call_target="tpu_custom_call" | custom-call | flops 6442450944 | bytes 25165824 | tf_op jit(solution)/shard_map/pallas_call | solution.py:403
  338.2 14.7 %collective-permute-done.21 = bf16[128,1536]{1,0:T(8,128)(2,1)S(1)} collective-permute-done((bf16[128,1536]{1,0:T(8,128)(2,1)S(1)}, bf16[128,1536]{1,0:T(8,128)(2,1)S(1)}, u32[]{:S(2)}, u32[]{:S(2)}) %collective-permute-start.21) | collective-permute-done | bytes 393248 | tf_op jit(solution)/shard_map/ppermute | solution.py:651
  352.9 12.6 %collective-permute-done.22 = bf16[128,1536]{1,0:T(8,128)(2,1)S(1)} collective-permute-done((bf16[128,1536]{1,0:T(8,128)(2,1)S(1)}, bf16[128,1536]{1,0:T(8,128)(2,1)S(1)}, u32[]{:S(2)}, u32[]{:S(2)}) %collective-permute-start.22) | collective-permute-done | bytes 393248 | tf_op jit(solution)/shard_map/ppermute | solution.py:651
  366.1 8.2 %collective-permute-start.24 = (bf16[128,1536]{1,0:T(8,128)(2,1)S(1)}, bf16[128,1536]{1,0:T(8,128)(2,1)S(1)}, u32[]{:S(2)}, u32[]{:S(2)}) collective-permute-start(bf16[128,1536]{1,0:T(8,128)(2,1)S(1)} %get-tuple-element.303), channel_id=1, source_target_pairs={{0,1},{1,0},{2,3},{3,2},{4,5},{5,4},{6,7},{7,6},{8,9},{9,8},{10,11... | collective-permute-start | bytes 1179656 | tf_op jit(solution)/shard_map/ppermute | solution.py:651
  376.7 13.0 %collective-permute-done.24 = bf16[128,1536]{1,0:T(8,128)(2,1)S(1)} collective-permute-done((bf16[128,1536]{1,0:T(8,128)(2,1)S(1)}, bf16[128,1536]{1,0:T(8,128)(2,1)S(1)}, u32[]{:S(2)}, u32[]{:S(2)}) %collective-permute-start.24) | collective-permute-done | bytes 393248 | tf_op jit(solution)/shard_map/ppermute | solution.py:651
  389.7 14.3 %collective-permute-done.25 = bf16[128,1536]{1,0:T(8,128)(2,1)S(1)} collective-permute-done((bf16[128,1536]{1,0:T(8,128)(2,1)S(1)}, bf16[128,1536]{1,0:T(8,128)(2,1)S(1)}, u32[]{:S(2)}, u32[]{:S(2)}) %collective-permute-start.25) | collective-permute-done | bytes 393248 | tf_op jit(solution)/shard_map/ppermute | solution.py:651
  411.1 12.6 %shard_map.321 = (bf16[768,1024]{1,0:T(8,128)(2,1)}, bf16[768,1024]{1,0:T(8,128)(2,1)}) custom-call(bf16[1536,1024]{1,0:T(8,128)(2,1)} %copy.124.recon_ref.aux_back_ref, bf16[1536,1024]{1,0:T(8,128)(2,1)} %copy.124.recon_ref.aux_back_ref, bf16[1024,4096]{1,0:T(8,128)(2,1)} %get-tuple-element.154.top_ref, bf16[1024,4096]{1,0:T(8,128)(2,1)} %get-tuple-element.155.aux_ref), custom_call_target="tpu_custom_call" | custom-call | flops 100663296 | bytes 262144 | tf_op jit(solution)/shard_map/pallas_call | solution.py:464
  431.0 12.6 %shard_map.322 = (f32[768,1024]{1,0:T(8,128)}, f32[768,1024]{1,0:T(8,128)}) custom-call(bf16[1536,1024]{1,0:T(8,128)(2,1)} %copy.126.recon_ref.aux_back_ref, bf16[1536,1024]{1,0:T(8,128)(2,1)} %copy.126.recon_ref.aux_back_ref, bf16[1024,4096]{1,0:T(8,128)(2,1)} %get-tuple-element.154.top_ref, bf16[1024,4096]{1,0:T(8,128)(2,1)} %get-tuple-element.155.aux_ref), custom_call_target="tpu_custom_call" | custom-call | flops 100663296 | bytes 262144 | tf_op jit(solution)/shard_map/pallas_call | solution.py:464
  443.6 18.5 %shard_map.323 = (bf16[784,1024]{1,0:T(8,128)(2,1)}, bf16[784,1024]{1,0:T(8,128)(2,1)}) custom-call(bf16[768,1024]{1,0:T(8,128)(2,1)} %copy.128.x_ref, bf16[1024,1536]{1,0:T(8,128)(2,1)} %copy-done.9, bf16[1024,4096]{1,0:T(8,128)(2,1)} %copy-done.4, bf16[768,1024]{1,0:T(8,128)(2,1)} %collective-permute-done.18.refs_5_.dec_a, ...), custom_call_target="tpu_custom_call" | custom-call | flops 100663296 | bytes 262144 | tf_op jit(solution)/shard_map/pallas_call | solution.py:527
  476.7 19.1 %shard_map.324 = (f32[784,1024]{1,0:T(8,128)}, f32[784,1024]{1,0:T(8,128)}) custom-call(bf16[768,1024]{1,0:T(8,128)(2,1)} %copy.128.x_ref, bf16[1024,1536]{1,0:T(8,128)(2,1)} %copy-done.9, bf16[1024,4096]{1,0:T(8,128)(2,1)} %copy-done.4, bf16[768,1024]{1,0:T(8,128)(2,1)} %pad_maximum_fusion.5.refs_4_.dec_a, bf16[768,1024]{1,0:T(8,128)(2,1)} %pad_maximum_fusion.6.refs_6_.dec_b), custom_call_target="tpu_custom_call" | custom-call | flops 100663296 | bytes 262144 | tf_op jit(solution)/shard_map/pallas_call | solution.py:527
  510.1 29.4 %collective-permute-done.33 = bf16[784,1024]{1,0:T(8,128)(2,1)S(1)} collective-permute-done((bf16[784,1024]{1,0:T(8,128)(2,1)}, bf16[784,1024]{1,0:T(8,128)(2,1)S(1)}, u32[]{:S(2)}, u32[]{:S(2)}) %collective-permute-start.33) | collective-permute-done | bytes 1605664 | tf_op jit(solution)/shard_map/ppermute | solution.py:651
  606.1 11.6 %shard_map.325 = (bf16[768,768]{1,0:T(8,128)(2,1)S(1)}, bf16[768,768]{1,0:T(8,128)(2,1)S(1)}, bf16[768,768]{1,0:T(8,128)(2,1)S(1)}) custom-call(s32[3]{0:T(128)S(1)} %pad_add_fusion.2.place_ref, bf16[4,96,768]{2,1,0:T(8,128)(2,1)S(1)} %pad_maximum_fusion.19.near_ref, bf16[4,96,768]{2,1,0:T(8,128)(2,1)S(1)} %collective-permute-done.47.far_ref), custom_call_target="tpu_custom_call" | custom-call | flops 226492416 | bytes 294912 | tf_op jit(solution)/shard_map/pallas_call | solution.py:194
  621.7 9.8 %shard_map.326 = (bf16[768,768]{1,0:T(8,128)(2,1)S(1)}, bf16[768,768]{1,0:T(8,128)(2,1)S(1)}, bf16[768,768]{1,0:T(8,128)(2,1)S(1)}) custom-call(bf16[768,768]{1,0:T(8,128)(2,1)S(1)} %get-tuple-element.195.g_hi, bf16[768,768]{1,0:T(8,128)(2,1)S(1)} %get-tuple-element.196.g_lo, bf16[768,768]{1,0:T(8,128)(2,1)S(1)} %get-tuple-element.197.q_ref), custom_call_target="tpu_custom_call" | custom-call | flops 226492416 | bytes 294912 | tf_op jit(solution)/shard_map/pallas_call | solution.py:194
  631.9 14.9 %collective-permute-start.51 = (bf16[112,768]{1,0:T(8,128)(2,1)S(1)}, bf16[112,768]{1,0:T(8,128)(2,1)S(1)}, u32[]{:S(2)}, u32[]{:S(2)}) collective-permute-start(bf16[112,768]{1,0:T(8,128)(2,1)S(1)} %pad_maximum_fusion.11), channel_id=1, source_target_pairs={{0,1},{1,0},{2,3},{3,2},{4,5},{5,4},{6,7},{7,6},{8,9},{9,8},{10,11... | collective-permute-start | bytes 516104 | tf_op jit(solution)/shard_map/ppermute | solution.py:651
  649.2 9.9 %shard_map.327 = (bf16[768,768]{1,0:T(8,128)(2,1)S(1)}, bf16[768,768]{1,0:T(8,128)(2,1)S(1)}, bf16[768,768]{1,0:T(8,128)(2,1)S(1)}) custom-call(bf16[768,768]{1,0:T(8,128)(2,1)S(1)} %get-tuple-element.204.g_hi, bf16[768,768]{1,0:T(8,128)(2,1)S(1)} %get-tuple-element.205.g_lo, bf16[768,768]{1,0:T(8,128)(2,1)S(1)} %get-tuple-element.206.q_ref), custom_call_target="tpu_custom_call" | custom-call | flops 226492416 | bytes 294912 | tf_op jit(solution)/shard_map/pallas_call | solution.py:194
  659.1 14.2 %collective-permute-done.52 = bf16[112,768]{1,0:T(8,128)(2,1)S(1)} collective-permute-done((bf16[112,768]{1,0:T(8,128)(2,1)S(1)}, bf16[112,768]{1,0:T(8,128)(2,1)S(1)}, u32[]{:S(2)}, u32[]{:S(2)}) %collective-permute-start.52) | collective-permute-done | bytes 172064 | tf_op jit(solution)/shard_map/ppermute | solution.py:651
  677.1 11.9 %shard_map.328 = (bf16[768,768]{1,0:T(8,128)(2,1)S(1)}, bf16[768,768]{1,0:T(8,128)(2,1)S(1)}, bf16[768,768]{1,0:T(8,128)(2,1)S(1)}) custom-call(bf16[768,768]{1,0:T(8,128)(2,1)S(1)} %get-tuple-element.213.g_hi, bf16[768,768]{1,0:T(8,128)(2,1)S(1)} %get-tuple-element.214.g_lo, bf16[768,768]{1,0:T(8,128)(2,1)S(1)} %get-tuple-element.215.q_ref), custom_call_target="tpu_custom_call" | custom-call | flops 283115520 | bytes 294912 | tf_op jit(solution)/shard_map/pallas_call | solution.py:194
  696.5 11.3 %shard_map.330 = (bf16[768,768]{1,0:T(8,128)(2,1)S(1)}, bf16[768,768]{1,0:T(8,128)(2,1)S(1)}, bf16[768,768]{1,0:T(8,128)(2,1)S(1)}) custom-call(s32[3]{0:T(128)S(1)} %pad_add_fusion.2.place_ref, bf16[4,96,768]{2,1,0:T(8,128)(2,1)S(1)} %pad_maximum_fusion.20.near_ref, bf16[4,96,768]{2,1,0:T(8,128)(2,1)S(1)} %collective-permute-done.57.far_ref), custom_call_target="tpu_custom_call" | custom-call | flops 226492416 | bytes 294912 | tf_op jit(solution)/shard_map/pallas_call | solution.py:194
  707.9 9.8 %shard_map.331 = (bf16[768,768]{1,0:T(8,128)(2,1)S(1)}, bf16[768,768]{1,0:T(8,128)(2,1)S(1)}, bf16[768,768]{1,0:T(8,128)(2,1)S(1)}) custom-call(bf16[768,768]{1,0:T(8,128)(2,1)S(1)} %get-tuple-element.226.g_hi, bf16[768,768]{1,0:T(8,128)(2,1)S(1)} %get-tuple-element.227.g_lo, bf16[768,768]{1,0:T(8,128)(2,1)S(1)} %get-tuple-element.228.q_ref), custom_call_target="tpu_custom_call" | custom-call | flops 226492416 | bytes 294912 | tf_op jit(solution)/shard_map/pallas_call | solution.py:194
  717.7 9.8 %shard_map.332 = (bf16[768,768]{1,0:T(8,128)(2,1)S(1)}, bf16[768,768]{1,0:T(8,128)(2,1)S(1)}, bf16[768,768]{1,0:T(8,128)(2,1)S(1)}) custom-call(bf16[768,768]{1,0:T(8,128)(2,1)S(1)} %get-tuple-element.229.g_hi, bf16[768,768]{1,0:T(8,128)(2,1)S(1)} %get-tuple-element.230.g_lo, bf16[768,768]{1,0:T(8,128)(2,1)S(1)} %get-tuple-element.231.q_ref), custom_call_target="tpu_custom_call" | custom-call | flops 226492416 | bytes 294912 | tf_op jit(solution)/shard_map/pallas_call | solution.py:194
  727.5 12.1 %shard_map.333 = (bf16[768,768]{1,0:T(8,128)(2,1)S(1)}, bf16[768,768]{1,0:T(8,128)(2,1)S(1)}, bf16[768,768]{1,0:T(8,128)(2,1)S(1)}) custom-call(bf16[768,768]{1,0:T(8,128)(2,1)S(1)} %get-tuple-element.232.g_hi, bf16[768,768]{1,0:T(8,128)(2,1)S(1)} %get-tuple-element.233.g_lo, bf16[768,768]{1,0:T(8,128)(2,1)S(1)} %get-tuple-element.234.q_ref), custom_call_target="tpu_custom_call" | custom-call | flops 283115520 | bytes 294912 | tf_op jit(solution)/shard_map/pallas_call | solution.py:194
  745.6 8.4 %shard_map.336 = (f32[192,4096]{1,0:T(8,128)}, f32[192,4096]{1,0:T(8,128)}, bf16[192,4096]{1,0:T(8,128)(2,1)}) custom-call(s32[3]{0:T(128)} %copy-done.8, bf16[768,768]{1,0:T(8,128)(2,1)} %copy-done.6, bf16[4,768,1024]{2,1,0:T(8,128)(2,1)} %bitcast.167, f32[192,4096]{1,0:T(8,128)} %bitcast.162), custom_call_target="tpu_custom_call" | custom-call | flops 1207959552 | bytes 6291456 | tf_op jit(solution)/shard_map/pallas_call | solution.py:567
  754.0 11.9 %all-gather.7.cloned.1.call-done = bf16[3072,1024]{1,0:T(8,128)(2,1)} async-done(((bf16[768,1024]{1,0:T(8,128)(2,1)}), bf16[3072,1024]{1,0:T(8,128)(2,1)}) %all-gather.7.cloned.1.call-update) | async-done | bytes 6291472 | tf_op jit(solution)/shard_map/all_gather | solution.py:878
  765.8 8.7 %shard_map.335 = (f32[192,4096]{1,0:T(8,128)}, f32[192,4096]{1,0:T(8,128)}, bf16[192,4096]{1,0:T(8,128)(2,1)}) custom-call(s32[3]{0:T(128)} %copy-done.8, bf16[768,768]{1,0:T(8,128)(2,1)} %copy-done.7, bf16[4,768,1024]{2,1,0:T(8,128)(2,1)} %bitcast.168, f32[192,4096]{1,0:T(8,128)} %weight_ref.1), custom_call_target="tpu_custom_call" | custom-call | flops 1207959552 | bytes 6291456 | tf_op jit(solution)/shard_map/pallas_call | solution.py:567
  (427 shorter events, 274.5 us)
Async XLA Ops:
  10.6 48.9 %collective-permute-start.4 = (s32[128,544]{1,0:T(8,128)}, s32[128,544]{1,0:T(8,128)}, u32[]{:S(2)}, u32[]{:S(2)}) collective-permute-start(s32[128,544]{1,0:T(8,128)} %pad_add_fusion.1), channel_id=1, source_target_pairs={{0,1},{1,0},{2,3},{3,2},{4,5},{5,4},{6,7},{7,6},{8,9},{9,8},{10,11... | collective-permute-start | bytes 835592 | tf_op jit(solution)/shard_map/ppermute | solution.py:651
  13.6 51.2 %collective-permute-start.5 = (s32[128,544]{1,0:T(8,128)}, s32[128,544]{1,0:T(8,128)}, u32[]{:S(2)}, u32[]{:S(2)}) collective-permute-start(s32[128,544]{1,0:T(8,128)} %pad_add_fusion.1), channel_id=1, source_target_pairs={{0,2},{1,3},{2,0},{3,1},{4,6},{5,7},{6,4},{7,5},{8,10},{9,11},{10,... | collective-permute-start | bytes 835592 | tf_op jit(solution)/shard_map/ppermute | solution.py:651
  16.2 48.6 %collective-permute-start.6 = (s32[128,544]{1,0:T(8,128)}, s32[128,544]{1,0:T(8,128)}, u32[]{:S(2)}, u32[]{:S(2)}) collective-permute-start(s32[128,544]{1,0:T(8,128)} %pad_add_fusion.1), channel_id=1, source_target_pairs={{0,3},{1,2},{2,1},{3,0},{4,7},{5,6},{6,5},{7,4},{8,11},{9,10},{10,... | collective-permute-start | bytes 835592 | tf_op jit(solution)/shard_map/ppermute | solution.py:651
  41.0 42.3 %all-to-all-start = ((bf16[192,4,1024]{2,0,1:T(8,128)(2,1)}), bf16[192,4,1024]{2,0,1:T(8,128)(2,1)}, u32[]{:S(2)}, u32[]{:S(2)}) async-start(bf16[192,4,1024]{2,0,1:T(8,128)(2,1)} %bitcast.164), calls=%async_computation | async-start | bytes 3145728 | tf_op jit(solution)/shard_map/all_to_all | solution.py:658
  86.4 24.5 %collective-permute-start.8 = (bf16[784,512]{1,0:T(8,128)(2,1)}, bf16[784,512]{1,0:T(8,128)(2,1)}, u32[]{:S(2)}, u32[]{:S(2)}) collective-permute-start(bf16[784,512]{1,0:T(8,128)(2,1)} %get-tuple-element.284), channel_id=1, source_target_pairs={{0,16},{8,24},{16,0},{24,8},{1,17},{9,25},{17,1},{25,9},{2,18},{10... | collective-permute-start | bytes 2408456 | tf_op jit(solution)/shard_map/ppermute | solution.py:651
  87.8 26.0 %collective-permute-start.7 = (bf16[784,512]{1,0:T(8,128)(2,1)}, bf16[784,512]{1,0:T(8,128)(2,1)}, u32[]{:S(2)}, u32[]{:S(2)}) collective-permute-start(bf16[784,512]{1,0:T(8,128)(2,1)} %get-tuple-element.285), channel_id=1, source_target_pairs={{0,8},{8,0},{16,24},{24,16},{1,9},{9,1},{17,25},{25,17},{2,10},{10... | collective-permute-start | bytes 2408456 | tf_op jit(solution)/shard_map/ppermute | solution.py:651
  97.1 40.4 %all-to-all-start.1 = ((bf16[192,4,1024]{2,0,1:T(8,128)(2,1)}), bf16[192,4,1024]{2,0,1:T(8,128)(2,1)}, u32[]{:S(2)}, u32[]{:S(2)}) async-start(bf16[192,4,1024]{2,0,1:T(8,128)(2,1)} %bitcast.152), calls=%async_computation.1 | async-start | bytes 3145728 | tf_op jit(solution)/shard_map/all_to_all | solution.py:658
  140.3 181.6 %all-to-all-start.2 = ((bf16[384,4,1024]{0,2,1:T(8,128)(2,1)}), bf16[384,4,1024]{0,2,1:T(8,128)(2,1)}, u32[]{:S(2)}, u32[]{:S(2)}) async-start(bf16[384,4,1024]{0,2,1:T(8,128)(2,1)} %bitcast.161), calls=%async_computation.2 | async-start | bytes 6291456 | tf_op jit(solution)/shard_map/all_to_all | solution.py:658
  145.0 600.7 %all-gather.9.cloned.1.call-start = ((), (), s32[]{:S(2)}) async-start(), calls=%async_computation.4 | async-start | bytes 7864320 | tf_op jit(solution)/shard_map/all_gather | solution.py:848
  145.8 103.5 %collective-permute-start.14 = (bf16[784,1024]{1,0:T(8,128)(2,1)}, bf16[784,1024]{1,0:T(8,128)(2,1)}, u32[]{:S(2)}, u32[]{:S(2)}) collective-permute-start(bf16[784,1024]{1,0:T(8,128)(2,1)} %pad_maximum_fusion.3.refs_0_), channel_id=1, source_target_pairs={{0,16},{8,24},{16,0},{24,8},{1,17},{9,25},{17,1},{25,9},{2,18},{10... | collective-permute-start | bytes 4816904 | tf_op jit(solution)/shard_map/ppermute | solution.py:651
  147.3 101.9 %collective-permute-start.15 = (bf16[784,1024]{1,0:T(8,128)(2,1)}, bf16[784,1024]{1,0:T(8,128)(2,1)}, u32[]{:S(2)}, u32[]{:S(2)}) collective-permute-start(bf16[784,1024]{1,0:T(8,128)(2,1)} %pad_maximum_fusion.4.refs_2_), channel_id=1, source_target_pairs={{0,8},{8,0},{16,24},{24,16},{1,9},{9,1},{17,25},{25,17},{2,10},{10... | collective-permute-start | bytes 4816904 | tf_op jit(solution)/shard_map/ppermute | solution.py:651
  149.6 81.1 %collective-permute-start.10 = (bf16[768,512]{1,0:T(8,128)(2,1)S(1)}, bf16[768,512]{1,0:T(8,128)(2,1)}, u32[]{:S(2)}, u32[]{:S(2)}) collective-permute-start(bf16[768,512]{1,0:T(8,128)(2,1)S(1)} %get-tuple-element.289), channel_id=1, source_target_pairs={{0,16},{8,24},{16,0},{24,8},{1,17},{9,25},{17,1},{25,9},{2,18},{10... | collective-permute-start | bytes 2359304 | tf_op jit(solution)/shard_map/ppermute | solution.py:651
  151.0 84.2 %collective-permute-start.9 = (bf16[768,512]{1,0:T(8,128)(2,1)S(1)}, bf16[768,512]{1,0:T(8,128)(2,1)}, u32[]{:S(2)}, u32[]{:S(2)}) collective-permute-start(bf16[768,512]{1,0:T(8,128)(2,1)S(1)} %get-tuple-element.290), channel_id=1, source_target_pairs={{0,8},{8,0},{16,24},{24,16},{1,9},{9,1},{17,25},{25,17},{2,10},{10... | collective-permute-start | bytes 2359304 | tf_op jit(solution)/shard_map/ppermute | solution.py:651
  151.6 47.8 %collective-permute-start.11 = (bf16[128,768]{1,0:T(8,128)(2,1)S(1)}, bf16[128,768]{1,0:T(8,128)(2,1)S(1)}, u32[]{:S(2)}, u32[]{:S(2)}) collective-permute-start(bf16[128,768]{1,0:T(8,128)(2,1)S(1)} %fusion.18), channel_id=1, source_target_pairs={{0,1},{1,0},{2,3},{3,2},{4,5},{5,4},{6,7},{7,6},{8,9},{9,8},{10,11... | collective-permute-start | bytes 589832 | tf_op jit(solution)/shard_map/ppermute | solution.py:651
  199.4 53.0 %collective-permute-start.17 = (s32[512,544]{0,1:T(8,128)}, s32[512,544]{0,1:T(8,128)}, u32[]{:S(2)}, u32[]{:S(2)}) collective-permute-start(s32[512,544]{0,1:T(8,128)} %copy.120), channel_id=1, source_target_pairs={{0,4},{4,0},{1,5},{5,1},{2,6},{6,2},{3,7},{7,3},{8,12},{12,8},{9,1... | collective-permute-start | bytes 3342344 | tf_op jit(solution)/shard_map/ppermute | solution.py:651
  249.2 41.8 %collective-permute-start.18 = (bf16[768,1024]{1,0:T(8,128)(2,1)}, bf16[768,1024]{1,0:T(8,128)(2,1)}, u32[]{:S(2)}, u32[]{:S(2)}) collective-permute-start(bf16[768,1024]{1,0:T(8,128)(2,1)} %pad_maximum_fusion.5.refs_4_.dec_a), channel_id=1, source_target_pairs={{0,16},{8,24},{16,0},{24,8},{1,17},{9,25},{17,1},{25,9},{2,18},{10... | collective-permute-start | bytes 4718600 | tf_op jit(solution)/shard_map/ppermute | solution.py:651
  250.8 40.3 %collective-permute-start.19 = (bf16[768,1024]{1,0:T(8,128)(2,1)}, bf16[768,1024]{1,0:T(8,128)(2,1)}, u32[]{:S(2)}, u32[]{:S(2)}) collective-permute-start(bf16[768,1024]{1,0:T(8,128)(2,1)} %pad_maximum_fusion.6.refs_6_.dec_b), channel_id=1, source_target_pairs={{0,8},{8,0},{16,24},{24,16},{1,9},{9,1},{17,25},{25,17},{2,10},{10... | collective-permute-start | bytes 4718600 | tf_op jit(solution)/shard_map/ppermute | solution.py:651
  252.4 36.0 %collective-permute-start.16 = (bf16[512,768]{1,0:T(8,128)(2,1)}, bf16[512,768]{1,0:T(8,128)(2,1)}, u32[]{:S(2)}, u32[]{:S(2)}) collective-permute-start(bf16[512,768]{1,0:T(8,128)(2,1)} %pad_maximum_fusion.10), channel_id=1, source_target_pairs={{0,4},{4,0},{1,5},{5,1},{2,6},{6,2},{3,7},{7,3},{8,12},{12,8},{9,1... | collective-permute-start | bytes 2359304 | tf_op jit(solution)/shard_map/ppermute | solution.py:651
  335.8 29.8 %collective-permute-start.22 = (bf16[128,1536]{1,0:T(8,128)(2,1)S(1)}, bf16[128,1536]{1,0:T(8,128)(2,1)S(1)}, u32[]{:S(2)}, u32[]{:S(2)}) collective-permute-start(bf16[128,1536]{1,0:T(8,128)(2,1)S(1)} %get-tuple-element.288), channel_id=1, source_target_pairs={{0,2},{1,3},{2,0},{3,1},{4,6},{5,7},{6,4},{7,5},{8,10},{9,11},{10,... | collective-permute-start | bytes 1179656 | tf_op jit(solution)/shard_map/ppermute | solution.py:651
  336.0 29.5 %collective-permute-start.23 = (bf16[128,1536]{1,0:T(8,128)(2,1)S(1)}, bf16[128,1536]{1,0:T(8,128)(2,1)S(1)}, u32[]{:S(2)}, u32[]{:S(2)}) collective-permute-start(bf16[128,1536]{1,0:T(8,128)(2,1)S(1)} %get-tuple-element.287), channel_id=1, source_target_pairs={{0,3},{1,2},{2,1},{3,0},{4,7},{5,6},{6,5},{7,4},{8,11},{9,10},{10,... | collective-permute-start | bytes 1179656 | tf_op jit(solution)/shard_map/ppermute | solution.py:651
  374.3 29.8 %collective-permute-start.25 = (bf16[128,1536]{1,0:T(8,128)(2,1)S(1)}, bf16[128,1536]{1,0:T(8,128)(2,1)S(1)}, u32[]{:S(2)}, u32[]{:S(2)}) collective-permute-start(bf16[128,1536]{1,0:T(8,128)(2,1)S(1)} %get-tuple-element.303), channel_id=1, source_target_pairs={{0,2},{1,3},{2,0},{3,1},{4,6},{5,7},{6,4},{7,5},{8,10},{9,11},{10,... | collective-permute-start | bytes 1179656 | tf_op jit(solution)/shard_map/ppermute | solution.py:651
  374.5 29.5 %collective-permute-start.26 = (bf16[128,1536]{1,0:T(8,128)(2,1)S(1)}, bf16[128,1536]{1,0:T(8,128)(2,1)S(1)}, u32[]{:S(2)}, u32[]{:S(2)}) collective-permute-start(bf16[128,1536]{1,0:T(8,128)(2,1)S(1)} %get-tuple-element.303), channel_id=1, source_target_pairs={{0,3},{1,2},{2,1},{3,0},{4,7},{5,6},{6,5},{7,4},{8,11},{9,10},{10,... | collective-permute-start | bytes 1179656 | tf_op jit(solution)/shard_map/ppermute | solution.py:651
  423.6 38.5 %collective-permute-start.28 = (bf16[768,1024]{1,0:T(8,128)(2,1)}, bf16[768,1024]{1,0:T(8,128)(2,1)}, u32[]{:S(2)}, u32[]{:S(2)}) collective-permute-start(bf16[768,1024]{1,0:T(8,128)(2,1)} %get-tuple-element.162), channel_id=1, source_target_pairs={{0,16},{8,24},{16,0},{24,8},{1,17},{9,25},{17,1},{25,9},{2,18},{10... | collective-permute-start | bytes 4718600 | tf_op jit(solution)/shard_map/ppermute | solution.py:651
  425.0 37.1 %collective-permute-start.29 = (bf16[768,1024]{1,0:T(8,128)(2,1)}, bf16[768,1024]{1,0:T(8,128)(2,1)}, u32[]{:S(2)}, u32[]{:S(2)}) collective-permute-start(bf16[768,1024]{1,0:T(8,128)(2,1)} %get-tuple-element.163), channel_id=1, source_target_pairs={{0,8},{8,0},{16,24},{24,16},{1,9},{9,1},{17,25},{25,17},{2,10},{10... | collective-permute-start | bytes 4718600 | tf_op jit(solution)/shard_map/ppermute | solution.py:651
  466.8 29.0 %collective-permute-start.30 = (bf16[768,512]{1,0:T(8,128)(2,1)S(1)}, bf16[768,512]{1,0:T(8,128)(2,1)S(1)}, u32[]{:S(2)}, u32[]{:S(2)}) collective-permute-start(bf16[768,512]{1,0:T(8,128)(2,1)S(1)} %split.41), channel_id=1, source_target_pairs={{0,8},{8,0},{16,24},{24,16},{1,9},{9,1},{17,25},{25,17},{2,10},{10... | collective-permute-start | bytes 2359304 | tf_op jit(solution)/shard_map/ppermute | solution.py:651
  472.4 23.8 %collective-permute-start.31 = (bf16[768,512]{1,0:T(8,128)(2,1)S(1)}, bf16[768,512]{1,0:T(8,128)(2,1)}, u32[]{:S(2)}, u32[]{:S(2)}) collective-permute-start(bf16[768,512]{1,0:T(8,128)(2,1)S(1)} %split.40), channel_id=1, source_target_pairs={{0,16},{8,24},{16,0},{24,8},{1,17},{9,25},{17,1},{25,9},{2,18},{10... | collective-permute-start | bytes 2359304 | tf_op jit(solution)/shard_map/ppermute | solution.py:651
  503.0 262.9 %all-gather.7.cloned.1.call-start = ((), (), s32[]{:S(2)}) async-start(), calls=%async_computation.3 | async-start | bytes 7864320 | tf_op jit(solution)/shard_map/all_gather | solution.py:878
  503.2 36.3 %collective-permute-start.33 = (bf16[784,1024]{1,0:T(8,128)(2,1)}, bf16[784,1024]{1,0:T(8,128)(2,1)S(1)}, u32[]{:S(2)}, u32[]{:S(2)}) collective-permute-start(bf16[784,1024]{1,0:T(8,128)(2,1)} %get-tuple-element.177), channel_id=1, source_target_pairs={{0,16},{8,24},{16,0},{24,8},{1,17},{9,25},{17,1},{25,9},{2,18},{10... | collective-permute-start | bytes 4816904 | tf_op jit(solution)/shard_map/ppermute | solution.py:651
  504.6 36.1 %collective-permute-start.34 = (bf16[784,1024]{1,0:T(8,128)(2,1)}, bf16[784,1024]{1,0:T(8,128)(2,1)}, u32[]{:S(2)}, u32[]{:S(2)}) collective-permute-start(bf16[784,1024]{1,0:T(8,128)(2,1)} %get-tuple-element.178), channel_id=1, source_target_pairs={{0,8},{8,0},{16,24},{24,16},{1,9},{9,1},{17,25},{25,17},{2,10},{10... | collective-permute-start | bytes 4816904 | tf_op jit(solution)/shard_map/ppermute | solution.py:651
  631.9 27.3 %collective-permute-start.51 = (bf16[112,768]{1,0:T(8,128)(2,1)S(1)}, bf16[112,768]{1,0:T(8,128)(2,1)S(1)}, u32[]{:S(2)}, u32[]{:S(2)}) collective-permute-start(bf16[112,768]{1,0:T(8,128)(2,1)S(1)} %pad_maximum_fusion.11), channel_id=1, source_target_pairs={{0,1},{1,0},{2,3},{3,2},{4,5},{5,4},{6,7},{7,6},{8,9},{9,8},{10,11... | collective-permute-start | bytes 516104 | tf_op jit(solution)/shard_map/ppermute | solution.py:651
  646.8 26.6 %collective-permute-start.52 = (bf16[112,768]{1,0:T(8,128)(2,1)S(1)}, bf16[112,768]{1,0:T(8,128)(2,1)S(1)}, u32[]{:S(2)}, u32[]{:S(2)}) collective-permute-start(bf16[112,768]{1,0:T(8,128)(2,1)S(1)} %pad_maximum_fusion.11), channel_id=1, source_target_pairs={{0,2},{1,3},{2,0},{3,1},{4,6},{5,7},{6,4},{7,5},{8,10},{9,11},{10,... | collective-permute-start | bytes 516104 | tf_op jit(solution)/shard_map/ppermute | solution.py:651
  646.8 26.6 %collective-permute-start.53 = (bf16[112,768]{1,0:T(8,128)(2,1)S(1)}, bf16[112,768]{1,0:T(8,128)(2,1)S(1)}, u32[]{:S(2)}, u32[]{:S(2)}) collective-permute-start(bf16[112,768]{1,0:T(8,128)(2,1)S(1)} %pad_maximum_fusion.11), channel_id=1, source_target_pairs={{0,3},{1,2},{2,1},{3,0},{4,7},{5,6},{6,5},{7,4},{8,11},{9,10},{10,... | collective-permute-start | bytes 516104 | tf_op jit(solution)/shard_map/ppermute | solution.py:651
  (94 other events, 1496.9 us)
Sparse Core Ops, SparseCore 0:
  503.1 133.5 all-gather.8
  638.9 126.9 all-gather.6

commit v6 on v5

--- a/solution.py
+++ b/solution.py
@@ -657,6 +657,9 @@
     def rows_to_latents(value):
         return lax.all_to_all(value, "narrow", split_axis=1, concat_axis=0, tiled=True)
 
+    def rows_of(value):
+        return lax.all_to_all(value, "narrow", split_axis=0, concat_axis=1, tiled=True)
+
     def gather_start(own, axis):
         halves = []
         for part, order in enumerate(orders):
@@ -747,30 +750,28 @@
     ctx_length = lengths[0]
     inputs = frozen_block(start, ctx_length, ln_gains, frozen_bias, w_qkv, w_proj, w_fc, w_out)
     counted = (jnp.arange(row_count) < ctx_length).astype(f32)
-    dec_own, near_picks, inputs, enc_halves = tie(dec_own, near_picks, inputs, enc_halves)
+    near_picks, inputs, enc_halves = tie(near_picks, inputs, enc_halves)
     enc_parts = gather_end(enc_halves)
     got_inputs = [swap(inputs, "narrow", k) for k in range(1, narrow_count)]
+    half_rows = core_rows // 2
+    codes = kind_codes(place, near_picks[:half_rows], dead_here, sizes, 0, 4)
+    dec_own, codes, got_inputs = tie(dec_own, codes, got_inputs)
     dec_halves = gather_start(dec_own, 1)
-    moments = jnp.concatenate([enc_moment.astype(bf16), dec_moment_t.astype(bf16)], 0)
-    moments, dec_own = tie(moments, dec_own)
-    moments = rows_to_latents(moments)
-    near_codes = kind_codes(place, near_picks, dead_here, sizes, 0, 2)
+    codes = kind_codes(place, near_picks[half_rows:], dead_here, sizes, 1, 4, codes)
     enc_lasts = [enc_parts[1], enc_parts[3]]
-    dec_halves, got_inputs, near_codes, enc_lasts = tie(
-        dec_halves, got_inputs, near_codes, enc_lasts
-    )
+    dec_halves, codes, enc_lasts = tie(dec_halves, codes, enc_lasts)
     enc_parts = [enc_parts[0], enc_lasts[0], enc_parts[2], enc_lasts[1]]
     dec_parts = gather_end(dec_halves)
+    moments = jnp.concatenate([enc_moment.astype(bf16), dec_moment_t.astype(bf16)], 0)
+    moments, got_inputs = tie(moments, got_inputs)
+    moments = rows_to_latents(moments)
     near_inputs = jnp.concatenate([inputs, *got_inputs], 0)
-    codes = kind_codes(place, far_picks, dead_here, sizes, 1, 2, near_codes)
+    codes = kind_codes(place, far_picks[:half_rows], dead_here, sizes, 2, 4, codes)
     far_inputs, codes = tie(swap(near_inputs, "core", 1), codes)
+    codes = kind_codes(place, far_picks[half_rows:], dead_here, sizes, 3, 4, codes)
     all_inputs = jnp.concatenate([near_inputs, far_inputs], 0)
     encoder_in = (all_inputs.astype(f32) - decoder_bias).astype(bf16)
     top_acts, aux_acts, far, near = forward(encoder_in, codes, enc_parts, dec_parts)
-    far, moments = tie(far, moments)
-    moments = moments.reshape(narrow_count, 2, rows_each, own_latents)
-    enc_moment_own = moments[:, 0].reshape(model_width, own_latents)
-    dec_moment_own = moments[:, 1].reshape(model_width, own_latents)
     encoder_t = encoder_in.T
     far_got, encoder_t = tie(swap(far, "core", 1), encoder_t)
     rebuilt = near + far_got.astype(f32)
@@ -792,11 +793,15 @@
     back_recon = 2.0 / model_width * counted[:, None] * (reconstructed_input - target)
     back_aux = 2.0 * AUX_COEF / model_width * counted[:, None] * aux_gap
     back_rows = jnp.concatenate([back_recon, back_aux], 1).astype(bf16)
+    back_rows, moments = tie(back_rows, moments)
     near_back = spread_narrow(back_rows)
     shard_rows = jnp.concatenate([near_back, swap(near_back, "core", 1)], 0)
     back_t = shard_rows.T
     dec_sent = dec_grads(back_t, top_acts, aux_acts, (1, 3), bf16)
-    back_t, dec_sent = tie(back_t, dec_sent)
+    moments = moments.reshape(narrow_count, 2, rows_each, own_latents)
+    enc_moment_own = moments[:, 0].reshape(model_width, own_latents)
+    dec_moment_own = moments[:, 1].reshape(model_width, own_latents)
+    top_acts, dec_sent = tie(top_acts, dec_sent)
     dec_keep = dec_grads(back_t, top_acts, aux_acts, (0, 2), f32)
     shard_rows, dec_keep = tie(shard_rows, dec_keep)
     enc_sent = enc_grads(encoder_t, shard_rows, codes, dec_parts[1::2], (1, 3), bf16)
@@ -806,7 +811,6 @@
     dec_gots, enc_sent = tie(dec_gots, enc_sent)
     enc_gots = [swap(sent, "chip", order[-1]) for order, sent in zip(orders, enc_sent)]
     dec_grad, _ = scatter_chips(dec_keep, dec_gots)
-    dec_grad, enc_keep = tie(dec_grad, enc_keep)
     def sum_gram(part, vector, fill):
         half = model_width // 2
         rows = half // chips
@@ -845,22 +849,26 @@
         return near, far, vector
 
     dec_own_next = (MOMENTUM * dec_moment_own.astype(f32) + dec_grad).astype(bf16)
-    dec_momenta = lax.all_gather(dec_own_next, "narrow")
+    dec_rows, dec_own_next = tie(dec_grad.astype(bf16), dec_own_next)
+    dec_rows = rows_of(dec_rows)
+    dec_gram = lax.dot_general(
+        dec_own_next, dec_own_next, to_latents, preferred_element_type=f32
+    )
+    dec_gram, enc_gots, enc_keep = tie(dec_gram, enc_gots, enc_keep)
     stages = []
     enc_grad = encb_grad = None
 
     def dec_note(sents, got):
-        nonlocal enc_grad, encb_grad
+        nonlocal enc_grad, encb_grad, dec_rows
         if not stages:
-            got, gots = tie(got, enc_gots)
-            enc_grad, encb_grad = scatter_chips(enc_keep, gots)
+            enc_grad, encb_grad = scatter_chips(enc_keep, enc_gots)
         if len(stages) == 2:
-            got, enc_grad = tie(got, enc_grad)
+            got, enc_grad, dec_rows = tie(got, enc_grad, dec_rows)
         stages.append(got)
         return got
 
     dec_near, dec_far, _ = sum_gram(
-        lax.dot_general(dec_own_next, dec_own_next, to_latents, preferred_element_type=f32),
+        dec_gram,
         jnp.zeros((model_width,), f32),
         dec_note,
     )
@@ -891,9 +899,13 @@
 
     enc_near, enc_far, grad_decb = sum_gram(enc_gram, bias_term, dec_fill)
     dec_factor = progress[-1][0]
-    dec_new, dec_next, dec_copy = finish(
-        place, dec_factor, dec_momenta, dec_weight_t
-    )
+    dec_ortho = rows_of(
+        jnp.dot(dec_factor, dec_own_next, preferred_element_type=f32).astype(bf16)
+    )
+    step_scale = MUON_RATE * 0.2 * math.sqrt(max(D, L))
+    dec_next = MOMENTUM * dec_moment_t + dec_rows.astype(f32)
+    dec_new = dec_weight_t * (1.0 - MUON_RATE * DECAY) - step_scale * dec_ortho.astype(f32)
+    dec_copy = dec_new.astype(bf16)
     state = series_start(place, enc_near, enc_far)
     for step in range(1, NS_STEPS):
         state = series_next(step, state)

time: 792 us -> 708 us (0.89)
  waiting for transfers between devices: 230 us -> 120 us
  other arithmetic: 62.8 us -> 79.5 us
  matrix products: 16.2 us -> 25 us
  Pallas kernels: 262 us -> 254 us
    ppermute x58, waiting for transfers between devices: 186 us -> 116 us  [swap(): lax.ppermute(value, axis, [(spot, spot ^ offset) for spot in range(count)])]
    all_to_all x3, waiting for transfers between devices: 32.2 us -> 3.37 us  [rows_to_latents(): lax.all_to_all(value, 'narrow', split_axis=1, concat_axis=0, tiled=True)]
    all_to_all x0 -> x2, starting transfers between devices: none -> 22.9 us  [rows_of(): lax.all_to_all(value, 'narrow', split_axis=0, concat_axis=1, tiled=True)]
    ppermute x58, starting transfers between devices: 92.9 us -> 75.1 us  [swap(): lax.ppermute(value, axis, [(spot, spot ^ offset) for spot in range(count)])]
    all_gather x1, waiting for transfers between devices: 11.9 us -> 0.01 us  [local(): enc_momenta = lax.all_gather(enc_own_next, 'narrow')]
    pallas_call x2 -> x1, Pallas kernels: 17.1 us -> 8.74 us  [finish(): pl.pallas_call(finish_kernel, grid_spec=pltpu.PrefetchScalarGridSpec(num_...]
    unnamed x146 -> x139, local copies, waits for them, and re-layouts: 29.9 us -> 31.8 us
    pallas_call x2 -> x4, Pallas kernels: 55.3 us -> 56.2 us  [kind_codes(): pl.pallas_call(body, grid=(row_total // rows,), out_shape=jax.ShapeDtypeS...]
  transfers between devices with their start and end apart: 63 -> 64, of which waited for: 24 -> 27; matrix products, arithmetic and copies ran while one was open for 13% -> 19% of each run, Pallas kernels for 31% -> 33%
where the time goes in v6:
time: 708 us; the launch traced here: 700 us
  Pallas kernels  254 us (36%)
  waiting for transfers between devices  120 us (17%)
  starting transfers between devices  113 us (16%)
  local copies, waits for them, and re-layouts  82.9 us (12%)
  other arithmetic  79.5 us (11%)
  matrix products  25 us (4%)
  between operations  16.6 us (2%)
  blocking collectives  8.74 us (1%)
    ppermute x58, waiting for transfers between devices, swap(): lax.ppermute(value, axis, [(spot, spot ^ offset) for spot in range(count)])  116 us
    pallas_call x10, Pallas kernels, square_call(): pl.pallas_call(kernel, out_shape=[square] * outs, in_specs=specs, out_spe...  96.1 us
    ppermute x58, starting transfers between devices, swap(): lax.ppermute(value, axis, [(spot, spot ^ offset) for spot in range(count)])  75.1 us
    pallas_call x4, Pallas kernels, kind_codes(): pl.pallas_call(body, grid=(row_total // rows,), out_shape=jax.ShapeDtypeS...  56.2 us
    pallas_call x2, Pallas kernels, enc_grads(): pl.pallas_call(functools.partial(enc_grad_kernel, count), grid=(2 * count...  37.5 us
    unnamed x139, local copies, waits for them, and re-layouts  31.8 us
    pallas_call x1, Pallas kernels, forward(): pl.pallas_call(functools.partial(forward_kernel, count), grid=(4 * count,...  30.8 us
    pallas_call x2, Pallas kernels, dec_grads(): pl.pallas_call(functools.partial(dec_grad_kernel, count), grid=(2 * count...  24.8 us
  transfers between devices with their start and end apart: 64, of which 27 were waited for; matrix products, arithmetic and copies ran while one was open for 19% of the time, Pallas kernels for 33%

profile of v6, /device:TPU:0, one launch (start us, length us, event | category | flops | bytes accessed | tf_op | source)
XLA Modules:
  0.0 699.9 jit_solution(11766077473626299487)
XLA Ops:
  24.8 8.7 %all-gather.2 = s32[8,1,128]{2,1,0:T(1,128)S(1)} all-gather(s32[1,1,128]{2,1,0:T(1,128)S(1)} %bitcast.224), channel_id=2, replica_groups=mesh['chip'=4,'core'=2,'narrow'=4] {'chip','core'}, dimensions={0}, use_global_device_ids=true | all-gather | bytes 4608 | tf_op jit(solution)/shard_map/all_gather | solution.py:696
  33.8 10.6 %gather_fusion = bf16[1024,768]{1,0:T(8,128)(2,1)} fusion(bf16[6288,768]{1,0:T(8,128)(2,1)} %param.28, s32[1024]{0:T(1024)S(1)} %broadcast_clamp_fusion), kind=kCustom, calls=%fused_computation | custom fusion | bytes 3149824 | tf_op jit(solution)/shard_map/jit(_take)/gather | solution.py:706
  102.2 6.3 fusion.21
  111.5 7.9 %collective-permute-done.8 = bf16[784,512]{1,0:T(8,128)(2,1)} collective-permute-done((bf16[784,512]{1,0:T(8,128)(2,1)S(1)}, bf16[784,512]{1,0:T(8,128)(2,1)}, u32[]{:S(2)}, u32[]{:S(2)}) %collective-permute-start.8) | collective-permute-done | bytes 802848 | tf_op jit(solution)/shard_map/ppermute | solution.py:651
  128.9 14.1 %shard_map.318.refs_0_ = bf16[1024,4096]{1,0:T(8,128)(2,1)S(1)} custom-call(s32[3]{0:T(128)S(1)} %copy-done.8, s32[256,544]{1,0:T(8,128)S(1)} %get-tuple-element.298.ids_ref, s32[1,4096]{1,0:T(1,128)S(1)} %bitcast.180), custom_call_target="tpu_custom_call" | custom-call | flops 1048576 | bytes 139264 | tf_op jit(solution)/shard_map/pallas_call | solution.py:302
  156.1 14.0 %shard_map.319.refs_0_ = bf16[1024,4096]{1,0:T(8,128)(2,1)S(1)} custom-call(s32[3]{0:T(128)S(1)} %copy-done.8, s32[256,544]{1,0:T(8,128)S(1)} %get-tuple-element.297.ids_ref, s32[1,4096]{1,0:T(1,128)S(1)} %bitcast.181, bf16[1024,4096]{1,0:T(8,128)(2,1)S(1)} %copy-done.3), custom_call_target="tpu_custom_call", output_to_operand_aliasing={{}: (3, {})} | custom-call | flops 1048576 | bytes 139264 | tf_op jit(solution)/shard_map/pallas_call | solution.py:302
  204.0 14.0 %shard_map.320.refs_0_ = bf16[1024,4096]{1,0:T(8,128)(2,1)S(1)} custom-call(s32[3]{0:T(128)S(1)} %copy-done.8, s32[256,544]{1,0:T(8,128)S(1)} %copy.145.ids_ref, s32[1,4096]{1,0:T(1,128)S(1)} %bitcast.182, bf16[1024,4096]{1,0:T(8,128)(2,1)S(1)} %copy-done.5), custom_call_target="tpu_custom_call", output_to_operand_aliasing={{}: (3, {})} | custom-call | flops 1048576 | bytes 139264 | tf_op jit(solution)/shard_map/pallas_call | solution.py:302
  218.0 14.0 %shard_map.321.codes_ref = bf16[1024,4096]{1,0:T(8,128)(2,1)S(1)} custom-call(s32[3]{0:T(128)S(1)} %copy-done.8, s32[256,544]{1,0:T(8,128)S(1)} %copy.146.ids_ref, s32[1,4096]{1,0:T(1,128)S(1)} %bitcast.183, bf16[1024,4096]{1,0:T(8,128)(2,1)S(1)} %shard_map.320.refs_0_), custom_call_target="tpu_custom_call", output_to_operand_aliasing={{}: (3, {})} | custom-call | flops 1048576 | bytes 139264 | tf_op jit(solution)/shard_map/pallas_call | solution.py:302
  238.1 30.8 %shard_map.322 = (bf16[1024,4096]{1,0:T(8,128)(2,1)}, bf16[1024,4096]{1,0:T(8,128)(2,1)}, bf16[512,1536]{1,0:T(8,128)(2,1)}, f32[512,1536]{1,0:T(8,128)}) custom-call(bf16[1024,768]{1,0:T(8,128)(2,1)} %subtract_convert_fusion.x_ref, bf16[1024,4096]{1,0:T(8,128)(2,1)} %copy-done.6, bf16[784,1024]{1,0:T(8,128)(2,1)} %pad_maximum_fusion.3.refs_0_, ...), custom_call_target="tpu_custom_call" | custom-call | flops 6442450944 | bytes 25165824 | tf_op jit(solution)/shard_map/pallas_call | solution.py:403
  277.9 9.5 %collective-permute-done.23 = bf16[128,1536]{1,0:T(8,128)(2,1)S(1)} collective-permute-done((bf16[128,1536]{1,0:T(8,128)(2,1)S(1)}, bf16[128,1536]{1,0:T(8,128)(2,1)S(1)}, u32[]{:S(2)}, u32[]{:S(2)}) %collective-permute-start.23) | collective-permute-done | bytes 393248 | tf_op jit(solution)/shard_map/ppermute | solution.py:651
  287.3 23.9 %collective-permute-done.22 = bf16[128,1536]{1,0:T(8,128)(2,1)S(1)} collective-permute-done((bf16[128,1536]{1,0:T(8,128)(2,1)S(1)}, bf16[128,1536]{1,0:T(8,128)(2,1)S(1)}, u32[]{:S(2)}, u32[]{:S(2)}) %collective-permute-start.22) | collective-permute-done | bytes 393248 | tf_op jit(solution)/shard_map/ppermute | solution.py:651
  321.0 13.7 %collective-permute-done.24 = bf16[128,1536]{1,0:T(8,128)(2,1)S(1)} collective-permute-done((bf16[128,1536]{1,0:T(8,128)(2,1)}, bf16[128,1536]{1,0:T(8,128)(2,1)S(1)}, u32[]{:S(2)}, u32[]{:S(2)}) %collective-permute-start.24) | collective-permute-done | bytes 393248 | tf_op jit(solution)/shard_map/ppermute | solution.py:651
  334.8 12.0 %collective-permute-done.25 = bf16[128,1536]{1,0:T(8,128)(2,1)S(1)} collective-permute-done((bf16[128,1536]{1,0:T(8,128)(2,1)}, bf16[128,1536]{1,0:T(8,128)(2,1)S(1)}, u32[]{:S(2)}, u32[]{:S(2)}) %collective-permute-start.25) | collective-permute-done | bytes 393248 | tf_op jit(solution)/shard_map/ppermute | solution.py:651
  357.2 12.0 %shard_map.323 = (bf16[768,1024]{1,0:T(8,128)(2,1)}, bf16[768,1024]{1,0:T(8,128)(2,1)}) custom-call(bf16[1536,1024]{1,0:T(8,128)(2,1)} %copy.138.recon_ref.aux_back_ref, bf16[1536,1024]{1,0:T(8,128)(2,1)} %copy.138.recon_ref.aux_back_ref, bf16[1024,4096]{1,0:T(8,128)(2,1)} %get-tuple-element.165.top_ref, bf16[1024,4096]{1,0:T(8,128)(2,1)} %get-tuple-element.162.aux_ref), custom_call_target="tpu_custom_call" | custom-call | flops 100663296 | bytes 262144 | tf_op jit(solution)/shard_map/pallas_call | solution.py:464
  374.2 12.7 %shard_map.324 = (f32[768,1024]{1,0:T(8,128)}, f32[768,1024]{1,0:T(8,128)}) custom-call(bf16[1536,1024]{1,0:T(8,128)(2,1)} %copy.138.recon_ref.aux_back_ref, bf16[1536,1024]{1,0:T(8,128)(2,1)} %copy.138.recon_ref.aux_back_ref, bf16[1024,4096]{1,0:T(8,128)(2,1)} %get-tuple-element.165.top_ref, bf16[1024,4096]{1,0:T(8,128)(2,1)} %get-tuple-element.162.aux_ref), custom_call_target="tpu_custom_call" | custom-call | flops 100663296 | bytes 262144 | tf_op jit(solution)/shard_map/pallas_call | solution.py:464
  387.0 18.5 %shard_map.325 = (bf16[784,1024]{1,0:T(8,128)(2,1)}, bf16[784,1024]{1,0:T(8,128)(2,1)}) custom-call(bf16[768,1024]{1,0:T(8,128)(2,1)} %copy.140.x_ref, bf16[1024,1536]{1,0:T(8,128)(2,1)} %constant_dynamic-update-slice_fusion.14.back_ref, bf16[1024,4096]{1,0:T(8,128)(2,1)} %copy-done.6, bf16[768,1024]{1,0:T(8,128)(2,1)} %collective-permute-done.18.refs_5_.dec_a, ...), custom_call_target="tpu_custom_call" | custom-call | flops 100663296 | bytes 262144 | tf_op jit(solution)/shard_map/pallas_call | solution.py:527
  422.1 19.0 %shard_map.326 = (f32[784,1024]{1,0:T(8,128)}, f32[784,1024]{1,0:T(8,128)}) custom-call(bf16[768,1024]{1,0:T(8,128)(2,1)} %copy.140.x_ref, bf16[1024,1536]{1,0:T(8,128)(2,1)} %constant_dynamic-update-slice_fusion.14.back_ref, bf16[1024,4096]{1,0:T(8,128)(2,1)} %copy-done.6, bf16[768,1024]{1,0:T(8,128)(2,1)} %pad_maximum_fusion.5.refs_4_.dec_a, ...), custom_call_target="tpu_custom_call" | custom-call | flops 100663296 | bytes 262144 | tf_op jit(solution)/shard_map/pallas_call | solution.py:527
  449.2 9.6 %all-to-all-start.3 = ((bf16[4,192,1024]{2,1,0:T(8,128)(2,1)}), bf16[4,192,1024]{2,1,0:T(8,128)(2,1)}, u32[]{:S(2)}, u32[]{:S(2)}) async-start(bf16[4,192,1024]{2,1,0:T(8,128)(2,1)} %bitcast.188), calls=%async_computation.3 | async-start | bytes 3145728 | tf_op jit(solution)/shard_map/all_to_all | solution.py:661
  486.7 7.4 %collective-permute-start.38 = (bf16[112,768]{1,0:T(8,128)(2,1)}, bf16[112,768]{1,0:T(8,128)(2,1)S(1)}, u32[]{:S(2)}, u32[]{:S(2)}) collective-permute-start(bf16[112,768]{1,0:T(8,128)(2,1)} %pad_maximum_fusion.15), channel_id=1, source_target_pairs={{0,1},{1,0},{2,3},{3,2},{4,5},{5,4},{6,7},{7,6},{8,9},{9,8},{10,11... | collective-permute-start | bytes 516104 | tf_op jit(solution)/shard_map/ppermute | solution.py:651
  496.5 5.6 collective-permute-done.42
  526.9 11.8 %shard_map.327 = (bf16[768,768]{1,0:T(8,128)(2,1)S(1)}, bf16[768,768]{1,0:T(8,128)(2,1)S(1)}, bf16[768,768]{1,0:T(8,128)(2,1)S(1)}) custom-call(s32[3]{0:T(128)S(1)} %copy-done.8, bf16[4,96,768]{2,1,0:T(8,128)(2,1)S(1)} %pad_maximum_fusion.19.near_ref, bf16[4,96,768]{2,1,0:T(8,128)(2,1)S(1)} %collective-permute-done.47.far_ref), custom_call_target="tpu_custom_call" | custom-call | flops 226492416 | bytes 294912 | tf_op jit(solution)/shard_map/pallas_call | solution.py:194
  542.6 9.8 %shard_map.328 = (bf16[768,768]{1,0:T(8,128)(2,1)S(1)}, bf16[768,768]{1,0:T(8,128)(2,1)S(1)}, bf16[768,768]{1,0:T(8,128)(2,1)S(1)}) custom-call(bf16[768,768]{1,0:T(8,128)(2,1)S(1)} %get-tuple-element.203.g_hi, bf16[768,768]{1,0:T(8,128)(2,1)S(1)} %get-tuple-element.204.g_lo, bf16[768,768]{1,0:T(8,128)(2,1)S(1)} %get-tuple-element.205.q_ref), custom_call_target="tpu_custom_call" | custom-call | flops 226492416 | bytes 294912 | tf_op jit(solution)/shard_map/pallas_call | solution.py:194
  552.8 6.8 collective-permute-start.51
  562.1 9.9 %shard_map.329 = (bf16[768,768]{1,0:T(8,128)(2,1)S(1)}, bf16[768,768]{1,0:T(8,128)(2,1)S(1)}, bf16[768,768]{1,0:T(8,128)(2,1)S(1)}) custom-call(bf16[768,768]{1,0:T(8,128)(2,1)S(1)} %get-tuple-element.212.g_hi, bf16[768,768]{1,0:T(8,128)(2,1)S(1)} %get-tuple-element.213.g_lo, bf16[768,768]{1,0:T(8,128)(2,1)S(1)} %get-tuple-element.214.q_ref), custom_call_target="tpu_custom_call" | custom-call | flops 226492416 | bytes 294912 | tf_op jit(solution)/shard_map/pallas_call | solution.py:194
  576.1 9.3 %collective-permute-done.52 = bf16[112,768]{1,0:T(8,128)(2,1)S(1)} collective-permute-done((bf16[112,768]{1,0:T(8,128)(2,1)S(1)}, bf16[112,768]{1,0:T(8,128)(2,1)S(1)}, u32[]{:S(2)}, u32[]{:S(2)}) %collective-permute-start.52) | collective-permute-done | bytes 172064 | tf_op jit(solution)/shard_map/ppermute | solution.py:651
  589.2 11.8 %shard_map.330 = (bf16[768,768]{1,0:T(8,128)(2,1)S(1)}, bf16[768,768]{1,0:T(8,128)(2,1)S(1)}, bf16[768,768]{1,0:T(8,128)(2,1)S(1)}) custom-call(bf16[768,768]{1,0:T(8,128)(2,1)S(1)} %get-tuple-element.221.g_hi, bf16[768,768]{1,0:T(8,128)(2,1)S(1)} %get-tuple-element.222.g_lo, bf16[768,768]{1,0:T(8,128)(2,1)S(1)} %get-tuple-element.223.q_ref), custom_call_target="tpu_custom_call" | custom-call | flops 283115520 | bytes 294912 | tf_op jit(solution)/shard_map/pallas_call | solution.py:194
  608.8 13.3 %all-to-all-start.4 = ((bf16[4,192,1024]{2,1,0:T(8,128)(2,1)}), bf16[4,192,1024]{2,1,0:T(8,128)(2,1)}, u32[]{:S(2)}, u32[]{:S(2)}) async-start(bf16[4,192,1024]{2,1,0:T(8,128)(2,1)} %bitcast.197), calls=%async_computation.4 | async-start | bytes 3145728 | tf_op jit(solution)/shard_map/all_to_all | solution.py:661
  628.3 11.3 %shard_map.332 = (bf16[768,768]{1,0:T(8,128)(2,1)S(1)}, bf16[768,768]{1,0:T(8,128)(2,1)S(1)}, bf16[768,768]{1,0:T(8,128)(2,1)S(1)}) custom-call(s32[3]{0:T(128)S(1)} %copy-done.8, bf16[4,96,768]{2,1,0:T(8,128)(2,1)S(1)} %pad_maximum_fusion.20.near_ref, bf16[4,96,768]{2,1,0:T(8,128)(2,1)S(1)} %collective-permute-done.57.far_ref), custom_call_target="tpu_custom_call" | custom-call | flops 226492416 | bytes 294912 | tf_op jit(solution)/shard_map/pallas_call | solution.py:194
  639.6 9.8 %shard_map.333 = (bf16[768,768]{1,0:T(8,128)(2,1)S(1)}, bf16[768,768]{1,0:T(8,128)(2,1)S(1)}, bf16[768,768]{1,0:T(8,128)(2,1)S(1)}) custom-call(bf16[768,768]{1,0:T(8,128)(2,1)S(1)} %get-tuple-element.234.g_hi, bf16[768,768]{1,0:T(8,128)(2,1)S(1)} %get-tuple-element.235.g_lo, bf16[768,768]{1,0:T(8,128)(2,1)S(1)} %get-tuple-element.236.q_ref), custom_call_target="tpu_custom_call" | custom-call | flops 226492416 | bytes 294912 | tf_op jit(solution)/shard_map/pallas_call | solution.py:194
  649.5 9.8 %shard_map.334 = (bf16[768,768]{1,0:T(8,128)(2,1)S(1)}, bf16[768,768]{1,0:T(8,128)(2,1)S(1)}, bf16[768,768]{1,0:T(8,128)(2,1)S(1)}) custom-call(bf16[768,768]{1,0:T(8,128)(2,1)S(1)} %get-tuple-element.237.g_hi, bf16[768,768]{1,0:T(8,128)(2,1)S(1)} %get-tuple-element.238.g_lo, bf16[768,768]{1,0:T(8,128)(2,1)S(1)} %get-tuple-element.239.q_ref), custom_call_target="tpu_custom_call" | custom-call | flops 226492416 | bytes 294912 | tf_op jit(solution)/shard_map/pallas_call | solution.py:194
  659.3 11.7 %shard_map.335 = (bf16[768,768]{1,0:T(8,128)(2,1)S(1)}, bf16[768,768]{1,0:T(8,128)(2,1)S(1)}, bf16[768,768]{1,0:T(8,128)(2,1)S(1)}) custom-call(bf16[768,768]{1,0:T(8,128)(2,1)S(1)} %get-tuple-element.240.g_hi, bf16[768,768]{1,0:T(8,128)(2,1)S(1)} %get-tuple-element.241.g_lo, bf16[768,768]{1,0:T(8,128)(2,1)S(1)} %get-tuple-element.242.q_ref), custom_call_target="tpu_custom_call" | custom-call | flops 283115520 | bytes 294912 | tf_op jit(solution)/shard_map/pallas_call | solution.py:194
  684.1 8.7 %shard_map.337 = (f32[192,4096]{1,0:T(8,128)}, f32[192,4096]{1,0:T(8,128)}, bf16[192,4096]{1,0:T(8,128)(2,1)}) custom-call(s32[3]{0:T(128)} %pad_add_fusion.2.place_ref, bf16[768,768]{1,0:T(8,128)(2,1)} %copy-done.7, bf16[4,768,1024]{2,1,0:T(8,128)(2,1)} %bitcast.191, f32[192,4096]{1,0:T(8,128)} %weight_ref.1), custom_call_target="tpu_custom_call" | custom-call | flops 1207959552 | bytes 6291456 | tf_op jit(solution)/shard_map/pallas_call | solution.py:567
  (428 shorter events, 294.8 us)
Async XLA Ops:
  10.6 52.0 %collective-permute-start.2 = (s32[128,544]{1,0:T(8,128)}, s32[128,544]{1,0:T(8,128)}, u32[]{:S(2)}, u32[]{:S(2)}) collective-permute-start(s32[128,544]{1,0:T(8,128)} %pad_add_fusion.1), channel_id=1, source_target_pairs={{0,3},{1,2},{2,1},{3,0},{4,7},{5,6},{6,5},{7,4},{8,11},{9,10},{10,... | collective-permute-start | bytes 835592 | tf_op jit(solution)/shard_map/ppermute | solution.py:651
  15.7 50.7 %collective-permute-start.1 = (s32[128,544]{1,0:T(8,128)}, s32[128,544]{1,0:T(8,128)}, u32[]{:S(2)}, u32[]{:S(2)}) collective-permute-start(s32[128,544]{1,0:T(8,128)} %pad_add_fusion.1), channel_id=1, source_target_pairs={{0,2},{1,3},{2,0},{3,1},{4,6},{5,7},{6,4},{7,5},{8,10},{9,11},{10,... | collective-permute-start | bytes 835592 | tf_op jit(solution)/shard_map/ppermute | solution.py:651
  15.7 50.7 %collective-permute-start = (s32[128,544]{1,0:T(8,128)}, s32[128,544]{1,0:T(8,128)}, u32[]{:S(2)}, u32[]{:S(2)}) collective-permute-start(s32[128,544]{1,0:T(8,128)} %pad_add_fusion.1), channel_id=1, source_target_pairs={{0,1},{1,0},{2,3},{3,2},{4,5},{5,4},{6,7},{7,6},{8,9},{9,8},{10,11... | collective-permute-start | bytes 835592 | tf_op jit(solution)/shard_map/ppermute | solution.py:651
  19.6 58.0 %all-to-all-start = ((bf16[192,4,1024]{2,0,1:T(8,128)(2,1)}), bf16[192,4,1024]{2,0,1:T(8,128)(2,1)}, u32[]{:S(2)}, u32[]{:S(2)}) async-start(bf16[192,4,1024]{2,0,1:T(8,128)(2,1)} %bitcast.187), calls=%async_computation | async-start | bytes 3145728 | tf_op jit(solution)/shard_map/all_to_all | solution.py:658
  92.4 54.5 %all-to-all-start.1 = ((bf16[192,4,1024]{2,0,1:T(8,128)(2,1)}), bf16[192,4,1024]{2,0,1:T(8,128)(2,1)}, u32[]{:S(2)}, u32[]{:S(2)}) async-start(bf16[192,4,1024]{2,0,1:T(8,128)(2,1)} %bitcast.175), calls=%async_computation.1 | async-start | bytes 3145728 | tf_op jit(solution)/shard_map/all_to_all | solution.py:658
  121.9 24.4 %collective-permute-start.9 = (bf16[128,768]{1,0:T(8,128)(2,1)}, bf16[128,768]{1,0:T(8,128)(2,1)S(1)}, u32[]{:S(2)}, u32[]{:S(2)}) collective-permute-start(bf16[128,768]{1,0:T(8,128)(2,1)} %fusion.21), channel_id=1, source_target_pairs={{0,1},{1,0},{2,3},{3,2},{4,5},{5,4},{6,7},{7,6},{8,9},{9,8},{10,11... | collective-permute-start | bytes 589832 | tf_op jit(solution)/shard_map/ppermute | solution.py:651
  126.3 55.2 %collective-permute-start.16 = (bf16[784,1024]{1,0:T(8,128)(2,1)}, bf16[784,1024]{1,0:T(8,128)(2,1)}, u32[]{:S(2)}, u32[]{:S(2)}) collective-permute-start(bf16[784,1024]{1,0:T(8,128)(2,1)} %pad_maximum_fusion.3.refs_0_), channel_id=1, source_target_pairs={{0,16},{8,24},{16,0},{24,8},{1,17},{9,25},{17,1},{25,9},{2,18},{10... | collective-permute-start | bytes 4816904 | tf_op jit(solution)/shard_map/ppermute | solution.py:651
  127.8 53.6 %collective-permute-start.17 = (bf16[784,1024]{1,0:T(8,128)(2,1)}, bf16[784,1024]{1,0:T(8,128)(2,1)}, u32[]{:S(2)}, u32[]{:S(2)}) collective-permute-start(bf16[784,1024]{1,0:T(8,128)(2,1)} %pad_maximum_fusion.4.refs_2_), channel_id=1, source_target_pairs={{0,8},{8,0},{16,24},{24,16},{1,9},{9,1},{17,25},{25,17},{2,10},{10... | collective-permute-start | bytes 4816904 | tf_op jit(solution)/shard_map/ppermute | solution.py:651
  146.3 40.9 %collective-permute-start.13 = (s32[512,544]{0,1:T(8,128)}, s32[512,544]{0,1:T(8,128)}, u32[]{:S(2)}, u32[]{:S(2)}) collective-permute-start(s32[512,544]{0,1:T(8,128)} %copy.131), channel_id=1, source_target_pairs={{0,4},{4,0},{1,5},{5,1},{2,6},{6,2},{3,7},{7,3},{8,12},{12,8},{9,1... | collective-permute-start | bytes 3342344 | tf_op jit(solution)/shard_map/ppermute | solution.py:651
  149.1 29.5 %collective-permute-start.14 = (bf16[768,512]{1,0:T(8,128)(2,1)S(1)}, bf16[768,512]{1,0:T(8,128)(2,1)S(1)}, u32[]{:S(2)}, u32[]{:S(2)}) collective-permute-start(bf16[768,512]{1,0:T(8,128)(2,1)S(1)} %get-tuple-element.296), channel_id=1, source_target_pairs={{0,8},{8,0},{16,24},{24,16},{1,9},{9,1},{17,25},{25,17},{2,10},{10... | collective-permute-start | bytes 2359304 | tf_op jit(solution)/shard_map/ppermute | solution.py:651
  150.2 29.8 %collective-permute-start.15 = (bf16[768,512]{1,0:T(8,128)(2,1)S(1)}, bf16[768,512]{1,0:T(8,128)(2,1)S(1)}, u32[]{:S(2)}, u32[]{:S(2)}) collective-permute-start(bf16[768,512]{1,0:T(8,128)(2,1)S(1)} %get-tuple-element.295), channel_id=1, source_target_pairs={{0,16},{8,24},{16,0},{24,8},{1,17},{9,25},{17,1},{25,9},{2,18},{10... | collective-permute-start | bytes 2359304 | tf_op jit(solution)/shard_map/ppermute | solution.py:651
  181.5 56.6 %collective-permute-start.18 = (bf16[768,1024]{1,0:T(8,128)(2,1)}, bf16[768,1024]{1,0:T(8,128)(2,1)}, u32[]{:S(2)}, u32[]{:S(2)}) collective-permute-start(bf16[768,1024]{1,0:T(8,128)(2,1)} %pad_maximum_fusion.5.refs_4_.dec_a), channel_id=1, source_target_pairs={{0,16},{8,24},{16,0},{24,8},{1,17},{9,25},{17,1},{25,9},{2,18},{10... | collective-permute-start | bytes 4718600 | tf_op jit(solution)/shard_map/ppermute | solution.py:651
  182.0 56.1 %collective-permute-start.19 = (bf16[768,1024]{1,0:T(8,128)(2,1)}, bf16[768,1024]{1,0:T(8,128)(2,1)}, u32[]{:S(2)}, u32[]{:S(2)}) collective-permute-start(bf16[768,1024]{1,0:T(8,128)(2,1)} %pad_maximum_fusion.6.refs_6_.dec_b), channel_id=1, source_target_pairs={{0,8},{8,0},{16,24},{24,16},{1,9},{9,1},{17,25},{25,17},{2,10},{10... | collective-permute-start | bytes 4718600 | tf_op jit(solution)/shard_map/ppermute | solution.py:651
  187.2 30.8 %collective-permute-start.12 = (bf16[512,768]{1,0:T(8,128)(2,1)}, bf16[512,768]{1,0:T(8,128)(2,1)}, u32[]{:S(2)}, u32[]{:S(2)}) collective-permute-start(bf16[512,768]{1,0:T(8,128)(2,1)} %pad_maximum_fusion.10), channel_id=1, source_target_pairs={{0,4},{4,0},{1,5},{5,1},{2,6},{6,2},{3,7},{7,3},{8,12},{12,8},{9,1... | collective-permute-start | bytes 2359304 | tf_op jit(solution)/shard_map/ppermute | solution.py:651
  194.5 118.9 %all-to-all-start.2 = ((bf16[384,4,1024]{0,2,1:T(8,128)(2,1)}), bf16[384,4,1024]{0,2,1:T(8,128)(2,1)}, u32[]{:S(2)}, u32[]{:S(2)}) async-start(bf16[384,4,1024]{0,2,1:T(8,128)(2,1)} %bitcast.184), calls=%async_computation.2 | async-start | bytes 6291456 | tf_op jit(solution)/shard_map/all_to_all | solution.py:658
  277.1 34.2 %collective-permute-start.22 = (bf16[128,1536]{1,0:T(8,128)(2,1)S(1)}, bf16[128,1536]{1,0:T(8,128)(2,1)S(1)}, u32[]{:S(2)}, u32[]{:S(2)}) collective-permute-start(bf16[128,1536]{1,0:T(8,128)(2,1)S(1)} %get-tuple-element.294), channel_id=1, source_target_pairs={{0,2},{1,3},{2,0},{3,1},{4,6},{5,7},{6,4},{7,5},{8,10},{9,11},{10,... | collective-permute-start | bytes 1179656 | tf_op jit(solution)/shard_map/ppermute | solution.py:651
  277.1 34.2 %collective-permute-start.21 = (bf16[128,1536]{1,0:T(8,128)(2,1)S(1)}, bf16[128,1536]{1,0:T(8,128)(2,1)S(1)}, u32[]{:S(2)}, u32[]{:S(2)}) collective-permute-start(bf16[128,1536]{1,0:T(8,128)(2,1)S(1)} %get-tuple-element.292), channel_id=1, source_target_pairs={{0,1},{1,0},{2,3},{3,2},{4,5},{5,4},{6,7},{7,6},{8,9},{9,8},{10,11... | collective-permute-start | bytes 1179656 | tf_op jit(solution)/shard_map/ppermute | solution.py:651
  316.7 30.1 %collective-permute-start.25 = (bf16[128,1536]{1,0:T(8,128)(2,1)}, bf16[128,1536]{1,0:T(8,128)(2,1)S(1)}, u32[]{:S(2)}, u32[]{:S(2)}) collective-permute-start(bf16[128,1536]{1,0:T(8,128)(2,1)} %pad_maximum_fusion.21), channel_id=1, source_target_pairs={{0,2},{1,3},{2,0},{3,1},{4,6},{5,7},{6,4},{7,5},{8,10},{9,11},{10,... | collective-permute-start | bytes 1179656 | tf_op jit(solution)/shard_map/ppermute | solution.py:651
  319.6 27.2 %collective-permute-start.26 = (bf16[128,1536]{1,0:T(8,128)(2,1)}, bf16[128,1536]{1,0:T(8,128)(2,1)S(1)}, u32[]{:S(2)}, u32[]{:S(2)}) collective-permute-start(bf16[128,1536]{1,0:T(8,128)(2,1)} %pad_maximum_fusion.21), channel_id=1, source_target_pairs={{0,3},{1,2},{2,1},{3,0},{4,7},{5,6},{6,5},{7,4},{8,11},{9,10},{10,... | collective-permute-start | bytes 1179656 | tf_op jit(solution)/shard_map/ppermute | solution.py:651
  369.3 36.8 %collective-permute-start.28 = (bf16[768,1024]{1,0:T(8,128)(2,1)}, bf16[768,1024]{1,0:T(8,128)(2,1)}, u32[]{:S(2)}, u32[]{:S(2)}) collective-permute-start(bf16[768,1024]{1,0:T(8,128)(2,1)} %get-tuple-element.169), channel_id=1, source_target_pairs={{0,16},{8,24},{16,0},{24,8},{1,17},{9,25},{17,1},{25,9},{2,18},{10... | collective-permute-start | bytes 4718600 | tf_op jit(solution)/shard_map/ppermute | solution.py:651
  370.8 36.5 %collective-permute-start.29 = (bf16[768,1024]{1,0:T(8,128)(2,1)}, bf16[768,1024]{1,0:T(8,128)(2,1)}, u32[]{:S(2)}, u32[]{:S(2)}) collective-permute-start(bf16[768,1024]{1,0:T(8,128)(2,1)} %get-tuple-element.170), channel_id=1, source_target_pairs={{0,8},{8,0},{16,24},{24,16},{1,9},{9,1},{17,25},{25,17},{2,10},{10... | collective-permute-start | bytes 4718600 | tf_op jit(solution)/shard_map/ppermute | solution.py:651
  410.5 30.6 %collective-permute-start.31 = (bf16[768,512]{1,0:T(8,128)(2,1)S(1)}, bf16[768,512]{1,0:T(8,128)(2,1)S(1)}, u32[]{:S(2)}, u32[]{:S(2)}) collective-permute-start(bf16[768,512]{1,0:T(8,128)(2,1)S(1)} %split.40), channel_id=1, source_target_pairs={{0,16},{8,24},{16,0},{24,8},{1,17},{9,25},{17,1},{25,9},{2,18},{10... | collective-permute-start | bytes 2359304 | tf_op jit(solution)/shard_map/ppermute | solution.py:651
  415.3 27.7 %collective-permute-start.30 = (bf16[768,512]{1,0:T(8,128)(2,1)S(1)}, bf16[768,512]{1,0:T(8,128)(2,1)}, u32[]{:S(2)}, u32[]{:S(2)}) collective-permute-start(bf16[768,512]{1,0:T(8,128)(2,1)S(1)} %split.41), channel_id=1, source_target_pairs={{0,8},{8,0},{16,24},{24,16},{1,9},{9,1},{17,25},{25,17},{2,10},{10... | collective-permute-start | bytes 2359304 | tf_op jit(solution)/shard_map/ppermute | solution.py:651
  419.6 43.9 %collective-permute-start.32 = (bf16[784,1024]{1,0:T(8,128)(2,1)}, bf16[784,1024]{1,0:T(8,128)(2,1)}, u32[]{:S(2)}, u32[]{:S(2)}) collective-permute-start(bf16[784,1024]{1,0:T(8,128)(2,1)} %get-tuple-element.181), channel_id=1, source_target_pairs={{0,16},{8,24},{16,0},{24,8},{1,17},{9,25},{17,1},{25,9},{2,18},{10... | collective-permute-start | bytes 4816904 | tf_op jit(solution)/shard_map/ppermute | solution.py:651
  420.8 47.5 %collective-permute-start.33 = (bf16[784,1024]{1,0:T(8,128)(2,1)}, bf16[784,1024]{1,0:T(8,128)(2,1)}, u32[]{:S(2)}, u32[]{:S(2)}) collective-permute-start(bf16[784,1024]{1,0:T(8,128)(2,1)} %get-tuple-element.182), channel_id=1, source_target_pairs={{0,8},{8,0},{16,24},{24,16},{1,9},{9,1},{17,25},{25,17},{2,10},{10... | collective-permute-start | bytes 4816904 | tf_op jit(solution)/shard_map/ppermute | solution.py:651
  449.2 55.2 %all-to-all-start.3 = ((bf16[4,192,1024]{2,1,0:T(8,128)(2,1)}), bf16[4,192,1024]{2,1,0:T(8,128)(2,1)}, u32[]{:S(2)}, u32[]{:S(2)}) async-start(bf16[4,192,1024]{2,1,0:T(8,128)(2,1)} %bitcast.188), calls=%async_computation.3 | async-start | bytes 3145728 | tf_op jit(solution)/shard_map/all_to_all | solution.py:661
  458.8 225.3 %all-gather.5.cloned.1.call-start = ((), (), s32[]{:S(2)}) async-start(), calls=%async_computation.5 | async-start | bytes 7864320 | tf_op jit(solution)/shard_map/all_gather | solution.py:886
  477.5 24.6 %collective-permute-start.42 = (bf16[784,512]{1,0:T(8,128)(2,1)S(1)}, bf16[784,512]{1,0:T(8,128)(2,1)S(1)}, u32[]{:S(2)}, u32[]{:S(2)}) collective-permute-start(bf16[784,512]{1,0:T(8,128)(2,1)S(1)} %get-tuple-element.336), channel_id=1, source_target_pairs={{0,16},{8,24},{16,0},{24,8},{1,17},{9,25},{17,1},{25,9},{2,18},{10... | collective-permute-start | bytes 2408456 | tf_op jit(solution)/shard_map/ppermute | solution.py:651
  478.4 24.1 %collective-permute-start.41 = (bf16[784,512]{1,0:T(8,128)(2,1)S(1)}, bf16[784,512]{1,0:T(8,128)(2,1)S(1)}, u32[]{:S(2)}, u32[]{:S(2)}) collective-permute-start(bf16[784,512]{1,0:T(8,128)(2,1)S(1)} %get-tuple-element.335), channel_id=1, source_target_pairs={{0,8},{8,0},{16,24},{24,16},{1,9},{9,1},{17,25},{25,17},{2,10},{10... | collective-permute-start | bytes 2408456 | tf_op jit(solution)/shard_map/ppermute | solution.py:651
  559.6 25.8 %collective-permute-start.52 = (bf16[112,768]{1,0:T(8,128)(2,1)S(1)}, bf16[112,768]{1,0:T(8,128)(2,1)S(1)}, u32[]{:S(2)}, u32[]{:S(2)}) collective-permute-start(bf16[112,768]{1,0:T(8,128)(2,1)S(1)} %pad_maximum_fusion.11), channel_id=1, source_target_pairs={{0,2},{1,3},{2,0},{3,1},{4,6},{5,7},{6,4},{7,5},{8,10},{9,11},{10,... | collective-permute-start | bytes 516104 | tf_op jit(solution)/shard_map/ppermute | solution.py:651
  560.6 24.8 %collective-permute-start.53 = (bf16[112,768]{1,0:T(8,128)(2,1)S(1)}, bf16[112,768]{1,0:T(8,128)(2,1)S(1)}, u32[]{:S(2)}, u32[]{:S(2)}) collective-permute-start(bf16[112,768]{1,0:T(8,128)(2,1)S(1)} %pad_maximum_fusion.11), channel_id=1, source_target_pairs={{0,3},{1,2},{2,1},{3,0},{4,7},{5,6},{6,5},{7,4},{8,11},{9,10},{10,... | collective-permute-start | bytes 516104 | tf_op jit(solution)/shard_map/ppermute | solution.py:651
  608.8 68.7 %all-to-all-start.4 = ((bf16[4,192,1024]{2,1,0:T(8,128)(2,1)}), bf16[4,192,1024]{2,1,0:T(8,128)(2,1)}, u32[]{:S(2)}, u32[]{:S(2)}) async-start(bf16[4,192,1024]{2,1,0:T(8,128)(2,1)} %bitcast.197), calls=%async_computation.4 | async-start | bytes 3145728 | tf_op jit(solution)/shard_map/all_to_all | solution.py:661
  (89 other events, 733.4 us)
Sparse Core Ops, SparseCore 0:
  512.1 160.7 all-gather.4

commit v7 on v6

--- a/solution.py
+++ b/solution.py
@@ -217,13 +217,13 @@
     return square_call(kernel, 3, [bf16] * 4, 8 if step < 3 else 10, *state)
 
 
-def code_kernel(shifts, place_ref, ids_ref, dead_ref, out_ref, high, low, stage):
+def code_kernel(shifts, place_ref, ids_ref, out_ref, high, low, stage):
     wide_shift, own_shift, top_count, orders = shifts
     batch, groups = stage.shape[:2]
     rows, picks = ids_ref.shape
     bf16, f32 = jnp.bfloat16, jnp.float32
     chip, core, narrow = place_ref[0], place_ref[1], place_ref[2]
-    latent_count = dead_ref.shape[1]
+    latent_count = out_ref.shape[1]
     half_shift = own_shift - 1
 
     ids = ids_ref[...]
@@ -276,41 +276,26 @@
             stage[token] = codes[:groups]
         for group in range(groups):
             lanes = slice(group * 128, (group + 1) * 128)
-            codes = stage[:, group, :]
-            live = (codes != 2.0) | (dead_ref[:, lanes] == 1)
-            out_ref[pl.ds(first, batch), lanes] = jnp.where(live, codes, 0.0).astype(bf16)
+            out_ref[pl.ds(first, batch), lanes] = stage[:, group, :].astype(bf16)
         return carry
 
     lax.fori_loop(0, rows // batch, one_batch, 0)
 
 
-def kind_codes(place, ids, dead_here, sizes, part, parts, held=None):
+def kind_codes(place, ids, latent_count, sizes):
     wide_latents, own_latents, top_count, orders = sizes
     row_total, pick_total = ids.shape
-    latent_count = dead_here.shape[1]
     rows = min(128, row_total)
-    first = part * (row_total // rows)
     shifts = (wide_latents.bit_length() - 1, own_latents.bit_length() - 1, top_count, orders)
-    kernel = functools.partial(code_kernel, shifts)
-    operands, specs, aliases = [place, ids, dead_here], [], {}
-    if held is not None:
-        operands, specs, aliases = operands + [held], [pl.BlockSpec(memory_space=pl.ANY)], {3: 0}
-
-    def body(place_ref, ids_ref, dead_ref, *refs):
-        kernel(place_ref, ids_ref, dead_ref, *refs[len(specs) :])
-
     return pl.pallas_call(
-        body,
+        functools.partial(code_kernel, shifts),
         grid=(row_total // rows,),
-        out_shape=jax.ShapeDtypeStruct((parts * row_total, latent_count), jnp.bfloat16),
+        out_shape=jax.ShapeDtypeStruct((row_total, latent_count), jnp.bfloat16),
         in_specs=[
             pl.BlockSpec(memory_space=pltpu.SMEM),
             pl.BlockSpec((rows, pick_total), lambda i: (i, 0)),
-            pl.BlockSpec((1, latent_count), lambda i: (0, 0)),
-        ]
-        + specs,
-        out_specs=pl.BlockSpec((rows, latent_count), lambda i: (i + first, 0)),
-        input_output_aliases=aliases,
+        ],
+        out_specs=pl.BlockSpec((rows, latent_count), lambda i: (i, 0)),
         scratch_shapes=[
             pltpu.VMEM((rows, pick_total), jnp.float32),
             pltpu.VMEM((rows, pick_total), jnp.float32),
@@ -322,7 +307,13 @@
             bytes_accessed=row_total * pick_total,
             transcendentals=0,
         ),
-    )(*operands)
+    )(place, ids)
+
+
+def join_rows(sources, target):
+    rows = sources[0].shape[0]
+    for index, source in enumerate(sources):
+        target[index * rows : (index + 1) * rows, :] = source[...]
 
 
 def pick_copy(step, count, sources, target):
@@ -333,10 +324,11 @@
             target[...] = source[...]
 
 
-def forward_kernel(count, x_ref, codes_ref, *refs):
-    encs, decs = refs[:4], refs[4:8]
-    top_ref, aux_ref, far_ref, near_ref = refs[8:12]
-    enc, dec, acc_top, acc_aux = refs[12:]
+def forward_kernel(count, x_ref, dead_ref, *refs):
+    code_parts, encs, decs = refs[:4], refs[4:8], refs[8:12]
+    top_ref, aux_ref, far_ref, near_ref = refs[12:16]
+    codes_ref, enc, dec, acc_top, acc_aux = refs[16:]
+    join_rows(code_parts, codes_ref)
     step = pl.program_id(0)
     rows_all, width = x_ref.shape
     block = min(1024, rows_all)
@@ -353,11 +345,11 @@
 
     def one(index, carry):
         rows = pl.ds(pl.multiple_of(index * block, block), block)
-        pre = (dot_f32(x_ref[rows, :], enc[pl.ds(0, width), :]) + bias).astype(jnp.bfloat16)
+        pre = dot_f32(x_ref[rows, :], enc[pl.ds(0, width), :]) + bias
         codes = codes_ref[rows, :]
-        zero = jnp.zeros_like(pre)
-        top = jnp.where(codes == 1.0, pre, zero)
-        aux = jnp.where(codes == 2.0, pre, zero)
+        zero = jnp.zeros(codes.shape, jnp.bfloat16)
+        top = jnp.where(codes == 1.0, pre.astype(jnp.bfloat16), zero)
+        aux = jnp.where(codes == 2.0, (pre * dead_ref[...]).astype(jnp.bfloat16), zero)
         top_ref[rows, :] = top
         aux_ref[rows, :] = aux
         acc_top[rows, :] += lax.dot_general(
@@ -391,8 +383,9 @@
     return specs
 
 
-def forward(x, codes, encs, decs):
+def forward(x, codes, dead, encs, decs):
     rows, width = x.shape
+    acts_shape = (rows, dead.shape[1])
     quarter = encs[0].shape[1]
     block = min(512, quarter)
     count = quarter // block
@@ -404,16 +397,18 @@
         functools.partial(forward_kernel, count),
         grid=(4 * count,),
         out_shape=[
-            jax.ShapeDtypeStruct(codes.shape, bf16),
-            jax.ShapeDtypeStruct(codes.shape, bf16),
+            jax.ShapeDtypeStruct(acts_shape, bf16),
+            jax.ShapeDtypeStruct(acts_shape, bf16),
             jax.ShapeDtypeStruct(half_shape, bf16),
             jax.ShapeDtypeStruct(half_shape, f32),
         ],
-        in_specs=[fixed(x.shape), lanes]
+        in_specs=[fixed(x.shape), pl.BlockSpec((1, block), lambda step: (0, step))]
+        + [pl.BlockSpec((rows // 4, block), lambda step: (0, step))] * 4
         + part_specs(encs[0].shape, 1, block, count, (0, 0, 0, 0))
         + part_specs(decs[0].shape, 1, block, count, (0, 0, 0, 0)),
         out_specs=[lanes, lanes, fixed(half_shape), fixed(half_shape)],
         scratch_shapes=[
+            pltpu.VMEM((rows, block), bf16),
             pltpu.VMEM((width + 16, block), bf16),
             pltpu.VMEM((width, block), bf16),
             pltpu.VMEM((rows, width), f32),
@@ -421,11 +416,11 @@
         ],
         compiler_params=pltpu.CompilerParams(vmem_limit_bytes=58 * 2**20),
         cost_estimate=pl.CostEstimate(
-            flops=2 * rows * width * codes.shape[1],
-            bytes_accessed=6 * rows * codes.shape[1],
+            flops=2 * rows * width * dead.shape[1],
+            bytes_accessed=6 * rows * dead.shape[1],
             transcendentals=0,
         ),
-    )(x, codes, *encs, *decs)
+    )(x, dead, *codes, *encs, *decs)
 
 
 def store_part(count, refs, rows, value):
@@ -437,20 +432,23 @@
             ref[rows, :] = value.astype(ref.dtype)
 
 
-def dec_grad_kernel(count, recon_ref, aux_back_ref, top_ref, aux_ref, *outs):
+def dec_grad_kernel(count, near_r, near_a, far_r, far_a, top_ref, aux_ref, *outs):
+    half = near_r.shape[1]
+
     def one(index, carry):
         rows = pl.ds(pl.multiple_of(index * 384, 384), 384)
-        value = dot_f32(recon_ref[rows, :], top_ref[...]) + dot_f32(
-            aux_back_ref[rows, :], aux_ref[...]
-        )
+        value = dot_f32(near_r[rows, :], top_ref[:half, :])
+        value = value + dot_f32(near_a[rows, :], aux_ref[:half, :])
+        value = value + dot_f32(far_r[rows, :], top_ref[half:, :])
+        value = value + dot_f32(far_a[rows, :], aux_ref[half:, :])
         store_part(count, outs, rows, value)
         return carry
 
-    lax.fori_loop(0, recon_ref.shape[0] // 384, one, 0)
-
-
-def dec_grads(back_t, top_acts, aux_acts, quarters, kind):
-    width = back_t.shape[0] // 2
+    lax.fori_loop(0, near_r.shape[0] // 384, one, 0)
+
+
+def dec_grads(near_t, far_t, top_acts, aux_acts, quarters, kind):
+    width = near_t.shape[0] // 2
     rows, latents = top_acts.shape
     quarter = latents // 4
     block = min(512, quarter)
@@ -466,8 +464,10 @@
         grid=(2 * count,),
         out_shape=[jax.ShapeDtypeStruct(shape, kind)] * 2,
         in_specs=[
-            pl.BlockSpec((width, rows), lambda step: (0, 0)),
-            pl.BlockSpec((width, rows), lambda step: (1, 0)),
+            pl.BlockSpec((width, rows // 2), lambda step: (0, 0)),
+            pl.BlockSpec((width, rows // 2), lambda step: (1, 0)),
+            pl.BlockSpec((width, rows // 2), lambda step: (0, 0)),
+            pl.BlockSpec((width, rows // 2), lambda step: (1, 0)),
             acts,
             acts,
         ],
@@ -476,28 +476,27 @@
         cost_estimate=pl.CostEstimate(
             flops=rows * width * quarter // 8, bytes_accessed=rows * quarter // 4, transcendentals=0
         ),
-    )(back_t, back_t, top_acts, aux_acts)
-
-
-def enc_grad_kernel(count, x_ref, back_ref, codes_ref, dec_a, dec_b, out_a, out_b, dec, grads):
+    )(near_t, near_t, far_t, far_t, top_acts, aux_acts)
+
+
+def enc_grad_kernel(count, x_ref, near_ref, far_ref, dead_ref, *refs):
+    code_parts, (dec_a, dec_b, out_a, out_b, dec, grads) = refs[:4], refs[4:]
     step = pl.program_id(0)
     pick_copy(step, count, (dec_a, dec_b), dec)
     width, latents = dec.shape
-    block = min(1024, back_ref.shape[0])
-
-    def one(index, total):
-        rows = pl.ds(pl.multiple_of(index * block, block), block)
-        codes = codes_ref[rows, :].astype(jnp.float32)
-        top = dot_f32(back_ref[rows, :width], dec[...])
-        aux = dot_f32(back_ref[rows, width:], dec[...])
-        value = jnp.where(codes == 1.0, top, jnp.where(codes == 2.0, aux, 0.0))
-        value = value.astype(jnp.bfloat16)
-        grads[rows, :] = value
-        return total + jnp.sum(value.astype(jnp.float32), 0, keepdims=True)
-
-    total = lax.fori_loop(
-        0, back_ref.shape[0] // block, one, jnp.zeros((1, latents), jnp.float32)
-    )
+    quarter = code_parts[0].shape[0]
+    total = jnp.zeros((1, latents), jnp.float32)
+    for index, back_ref in enumerate((near_ref, far_ref)):
+        top = dot_f32(back_ref[:, :width], dec[...])
+        aux = dot_f32(back_ref[:, width:], dec[...]) * dead_ref[...]
+        for part in range(2):
+            codes = code_parts[2 * index + part][...].astype(jnp.float32)
+            lines = slice(part * quarter, (part + 1) * quarter)
+            value = jnp.where(codes == 2.0, aux[lines], 0.0)
+            value = jnp.where(codes == 1.0, top[lines], value).astype(jnp.bfloat16)
+            first = (2 * index + part) * quarter
+            grads[first : first + quarter, :] = value
+            total = total + jnp.sum(value.astype(jnp.float32), 0, keepdims=True)
 
     def two(index, carry):
         rows = pl.ds(pl.multiple_of(index * 384, 384), 384)
@@ -514,9 +513,9 @@
     store_part(count, (out_a, out_b), pl.ds(width, 16), lines)
 
 
-def enc_grads(x_t, back, codes, parts, quarters, kind):
+def enc_grads(x_t, near, far, codes, dead, parts, quarters, kind):
     width, rows = x_t.shape
-    quarter = codes.shape[1] // 4
+    quarter = dead.shape[1] // 4
     block = min(512, quarter)
     count = quarter // block
 
@@ -530,9 +529,11 @@
         out_shape=[jax.ShapeDtypeStruct(shape, kind)] * 2,
         in_specs=[
             pl.BlockSpec(x_t.shape, lambda step: (0, 0)),
-            pl.BlockSpec(back.shape, lambda step: (0, 0)),
-            pl.BlockSpec((rows, block), lanes),
+            pl.BlockSpec(near.shape, lambda step: (0, 0)),
+            pl.BlockSpec(far.shape, lambda step: (0, 0)),
+            pl.BlockSpec((1, block), lanes),
         ]
+        + [pl.BlockSpec((rows // 4, block), lanes)] * 4
         + part_specs(parts[0].shape, 1, block, count, (0, 0)),
         out_specs=part_specs(shape, 1, block, count, (0, 0)),
         scratch_shapes=[
@@ -543,7 +544,7 @@
         cost_estimate=pl.CostEstimate(
             flops=rows * width * quarter // 8, bytes_accessed=rows * quarter // 4, transcendentals=0
         ),
-    )(x_t, back, codes, *parts)
+    )(x_t, near, far, dead, *codes, *parts)
 
 
 def finish_kernel(place_ref, factor_ref, momentum_ref, weight_ref, *outs):
@@ -744,8 +745,9 @@
             places = places + [spot ^ bit for spot in places]
         for spot in places:
             dead_parts.append(dead_here[spot, part * half_latents : (part + 1) * half_latents])
-    dead_here = jnp.concatenate(dead_parts)[None]
+    dead_here = jnp.concatenate(dead_parts)[None].astype(f32)
     sizes = (wide_latents, own_latents, top_ids.shape[1], orders)
+    near_picks, dead_here, embedded = tie(near_picks, dead_here, embedded)
     start = embedded + position_table[:row_count].astype(f32)
     ctx_length = lengths[0]
     inputs = frozen_block(start, ctx_length, ln_gains, frozen_bias, w_qkv, w_proj, w_fc, w_out)
@@ -754,24 +756,28 @@
     enc_parts = gather_end(enc_halves)
     got_inputs = [swap(inputs, "narrow", k) for k in range(1, narrow_count)]
     half_rows = core_rows // 2
-    codes = kind_codes(place, near_picks[:half_rows], dead_here, sizes, 0, 4)
-    dec_own, codes, got_inputs = tie(dec_own, codes, got_inputs)
+    codes = [kind_codes(place, near_picks[:half_rows], latent_count, sizes)]
+    enc_lasts = [enc_parts[1], enc_parts[3]]
+    dec_own, codes, got_inputs, enc_lasts = tie(dec_own, codes, got_inputs, enc_lasts)
+    near_picks, codes = tie(near_picks, codes)
     dec_halves = gather_start(dec_own, 1)
-    codes = kind_codes(place, near_picks[half_rows:], dead_here, sizes, 1, 4, codes)
-    enc_lasts = [enc_parts[1], enc_parts[3]]
-    dec_halves, codes, enc_lasts = tie(dec_halves, codes, enc_lasts)
+    codes = [*codes, kind_codes(place, near_picks[half_rows:], latent_count, sizes)]
+    dec_halves, codes = tie(dec_halves, codes)
     enc_parts = [enc_parts[0], enc_lasts[0], enc_parts[2], enc_lasts[1]]
     dec_parts = gather_end(dec_halves)
     moments = jnp.concatenate([enc_moment.astype(bf16), dec_moment_t.astype(bf16)], 0)
     moments, got_inputs = tie(moments, got_inputs)
     moments = rows_to_latents(moments)
     near_inputs = jnp.concatenate([inputs, *got_inputs], 0)
-    codes = kind_codes(place, far_picks[:half_rows], dead_here, sizes, 2, 4, codes)
+    far_picks, codes = tie(far_picks, codes)
+    codes = [*codes, kind_codes(place, far_picks[:half_rows], latent_count, sizes)]
     far_inputs, codes = tie(swap(near_inputs, "core", 1), codes)
-    codes = kind_codes(place, far_picks[half_rows:], dead_here, sizes, 3, 4, codes)
+    far_picks, codes = tie(far_picks, codes)
+    codes = [*codes, kind_codes(place, far_picks[half_rows:], latent_count, sizes)]
     all_inputs = jnp.concatenate([near_inputs, far_inputs], 0)
     encoder_in = (all_inputs.astype(f32) - decoder_bias).astype(bf16)
-    top_acts, aux_acts, far, near = forward(encoder_in, codes, enc_parts, dec_parts)
+    encoder_in, moments = tie(encoder_in, moments)
+    top_acts, aux_acts, far, near = forward(encoder_in, codes, dead_here, enc_parts, dec_parts)
     encoder_t = encoder_in.T
     far_got, encoder_t = tie(swap(far, "core", 1), encoder_t)
     rebuilt = near + far_got.astype(f32)
@@ -793,20 +799,24 @@
     back_recon = 2.0 / model_width * counted[:, None] * (reconstructed_input - target)
     back_aux = 2.0 * AUX_COEF / model_width * counted[:, None] * aux_gap
     back_rows = jnp.concatenate([back_recon, back_aux], 1).astype(bf16)
-    back_rows, moments = tie(back_rows, moments)
     near_back = spread_narrow(back_rows)
-    shard_rows = jnp.concatenate([near_back, swap(near_back, "core", 1)], 0)
-    back_t = shard_rows.T
-    dec_sent = dec_grads(back_t, top_acts, aux_acts, (1, 3), bf16)
+    far_back = swap(near_back, "core", 1)
+    near_t, far_back = tie(near_back.T, far_back)
+    far_t = far_back.T
+    dec_sent = dec_grads(near_t, far_t, top_acts, aux_acts, (1, 3), bf16)
     moments = moments.reshape(narrow_count, 2, rows_each, own_latents)
     enc_moment_own = moments[:, 0].reshape(model_width, own_latents)
     dec_moment_own = moments[:, 1].reshape(model_width, own_latents)
     top_acts, dec_sent = tie(top_acts, dec_sent)
-    dec_keep = dec_grads(back_t, top_acts, aux_acts, (0, 2), f32)
-    shard_rows, dec_keep = tie(shard_rows, dec_keep)
-    enc_sent = enc_grads(encoder_t, shard_rows, codes, dec_parts[1::2], (1, 3), bf16)
-    shard_rows, enc_sent = tie(shard_rows, enc_sent)
-    enc_keep = enc_grads(encoder_t, shard_rows, codes, dec_parts[::2], (0, 2), f32)
+    dec_keep = dec_grads(near_t, far_t, top_acts, aux_acts, (0, 2), f32)
+    far_back, dec_keep = tie(far_back, dec_keep)
+    enc_sent = enc_grads(
+        encoder_t, near_back, far_back, codes, dead_here, dec_parts[1::2], (1, 3), bf16
+    )
+    far_back, enc_sent = tie(far_back, enc_sent)
+    enc_keep = enc_grads(
+        encoder_t, near_back, far_back, codes, dead_here, dec_parts[::2], (0, 2), f32
+    )
     dec_gots = [swap(sent, "chip", order[-1]) for order, sent in zip(orders, dec_sent)]
     dec_gots, enc_sent = tie(dec_gots, enc_sent)
     enc_gots = [swap(sent, "chip", order[-1]) for order, sent in zip(orders, enc_sent)]

time: 708 us -> 710 us (level)
  waiting for transfers between devices: 120 us -> 150 us
  local copies, waits for them, and re-layouts: 82.9 us -> 67.5 us
  Pallas kernels: 254 us -> 245 us
    all_to_all x3, waiting for transfers between devices: 3.37 us -> 26.1 us  [rows_to_latents(): lax.all_to_all(value, 'narrow', split_axis=1, concat_axis=0, tiled=True)]
    unnamed x139 -> x159, local copies, waits for them, and re-layouts: 31.8 us -> 17.4 us
    pallas_call x4, Pallas kernels: 56.2 us -> 45.5 us  [kind_codes(): pl.pallas_call(functools.partial(code_kernel, shifts), grid=(row_total //...]
    ppermute x58, waiting for transfers between devices: 116 us -> 124 us  [swap(): lax.ppermute(value, axis, [(spot, spot ^ offset) for spot in range(count)])]
  transfers between devices with their start and end apart: 64 -> 64, of which waited for: 27 -> 26; matrix products, arithmetic and copies ran while one was open for 19% -> 17% of each run, Pallas kernels for 33% -> 27%
where the time goes in v7:
time: 710 us; the launch traced here: 702 us
  Pallas kernels  245 us (35%)
  waiting for transfers between devices  150 us (21%)
  starting transfers between devices  116 us (16%)
  other arithmetic  73.7 us (10%)
  local copies, waits for them, and re-layouts  67.5 us (10%)
  matrix products  24.5 us (3%)
  between operations  16.6 us (2%)
  blocking collectives  9.07 us (1%)
    ppermute x58, waiting for transfers between devices, swap(): lax.ppermute(value, axis, [(spot, spot ^ offset) for spot in range(count)])  124 us
    pallas_call x10, Pallas kernels, square_call(): pl.pallas_call(kernel, out_shape=[square] * outs, in_specs=specs, out_spe...  96.1 us
    ppermute x58, starting transfers between devices, swap(): lax.ppermute(value, axis, [(spot, spot ^ offset) for spot in range(count)])  78.7 us
    pallas_call x4, Pallas kernels, kind_codes(): pl.pallas_call(functools.partial(code_kernel, shifts), grid=(row_total //...  45.5 us
    pallas_call x2, Pallas kernels, enc_grads(): pl.pallas_call(functools.partial(enc_grad_kernel, count), grid=(2 * count...  38 us
    pallas_call x1, Pallas kernels, forward(): pl.pallas_call(functools.partial(forward_kernel, count), grid=(4 * count,...  31.8 us
    all_to_all x3, waiting for transfers between devices, rows_to_latents(): lax.all_to_all(value, 'narrow', split_axis=1, concat_axis=0, tiled=True)  26.1 us
    pallas_call x2, Pallas kernels, dec_grads(): pl.pallas_call(functools.partial(dec_grad_kernel, count), grid=(2 * count...  24.7 us
  transfers between devices with their start and end apart: 64, of which 26 were waited for; matrix products, arithmetic and copies ran while one was open for 17% of the time, Pallas kernels for 27%

profile of v7, /device:TPU:0, one launch (start us, length us, event | category | flops | bytes accessed | tf_op | source)
XLA Modules:
  0.0 702.1 jit_solution(15418382117966215636)
XLA Ops:
  16.2 9.1 %all-gather.2 = s32[8,1,128]{2,1,0:T(1,128)S(1)} all-gather(s32[1,1,128]{2,1,0:T(1,128)} %bitcast.209), channel_id=2, replica_groups=mesh['chip'=4,'core'=2,'narrow'=4] {'chip','core'}, dimensions={0}, use_global_device_ids=true | all-gather | bytes 4608 | tf_op jit(solution)/shard_map/all_gather | solution.py:697
  25.5 10.6 %gather_fusion = bf16[1024,768]{1,0:T(8,128)(2,1)} fusion(bf16[6288,768]{1,0:T(8,128)(2,1)} %param.28, s32[1024]{0:T(1024)S(1)} %broadcast_clamp_fusion), kind=kCustom, calls=%fused_computation | custom fusion | bytes 3149824 | tf_op jit(solution)/shard_map/jit(_take)/gather | solution.py:707
  66.6 16.7 %all-to-all-done = bf16[192,4,1024]{2,0,1:T(8,128)(2,1)} async-done(((bf16[192,4,1024]{2,0,1:T(8,128)(2,1)}), bf16[192,4,1024]{2,0,1:T(8,128)(2,1)}, u32[]{:S(2)}, u32[]{:S(2)}) %all-to-all-start) | async-done | bytes 1572896 | tf_op jit(solution)/shard_map/all_to_all | solution.py:659
  126.8 11.4 %shard_map.318.refs_0_ = bf16[256,4096]{1,0:T(8,128)(2,1)S(1)} custom-call(s32[3]{0:T(128)S(1)} %pad_add_fusion.2.place_ref, s32[256,544]{1,0:T(8,128)S(1)} %slice.323.ids_ref), custom_call_target="tpu_custom_call" | custom-call | flops 1048576 | bytes 139264 | tf_op jit(solution)/shard_map/pallas_call | solution.py:290
  139.5 16.8 %collective-permute-done.10 = bf16[128,768]{1,0:T(8,128)(2,1)S(1)} collective-permute-done((bf16[128,768]{1,0:T(8,128)(2,1)S(1)}, bf16[128,768]{1,0:T(8,128)(2,1)S(1)}, u32[]{:S(2)}, u32[]{:S(2)}) %collective-permute-start.10) | collective-permute-done | bytes 196640 | tf_op jit(solution)/shard_map/ppermute | solution.py:652
  169.9 11.4 %shard_map.319.refs_1_ = bf16[256,4096]{1,0:T(8,128)(2,1)S(1)} custom-call(s32[3]{0:T(128)S(1)} %pad_add_fusion.2.place_ref, s32[256,544]{1,0:T(8,128)S(1)} %slice.326.ids_ref), custom_call_target="tpu_custom_call" | custom-call | flops 1048576 | bytes 139264 | tf_op jit(solution)/shard_map/pallas_call | solution.py:290
  196.8 11.4 %shard_map.320.refs_2_ = bf16[256,4096]{1,0:T(8,128)(2,1)S(1)} custom-call(s32[3]{0:T(128)S(1)} %pad_add_fusion.2.place_ref, s32[256,544]{1,0:T(8,128)S(1)} %slice.410.ids_ref), custom_call_target="tpu_custom_call" | custom-call | flops 1048576 | bytes 139264 | tf_op jit(solution)/shard_map/pallas_call | solution.py:290
  211.2 11.4 %shard_map.321.refs_3_ = bf16[256,4096]{1,0:T(8,128)(2,1)S(1)} custom-call(s32[3]{0:T(128)S(1)} %pad_add_fusion.2.place_ref, s32[256,544]{1,0:T(8,128)S(1)} %slice.411.ids_ref), custom_call_target="tpu_custom_call" | custom-call | flops 1048576 | bytes 139264 | tf_op jit(solution)/shard_map/pallas_call | solution.py:290
  226.6 9.4 %all-to-all-done.2 = bf16[384,4,1024]{0,2,1:T(8,128)(2,1)} async-done(((bf16[384,4,1024]{0,2,1:T(8,128)(2,1)}), bf16[384,4,1024]{0,2,1:T(8,128)(2,1)}, u32[]{:S(2)}, u32[]{:S(2)}) %all-to-all-start.2) | async-done | bytes 3145760 | tf_op jit(solution)/shard_map/all_to_all | solution.py:659
  240.7 31.8 %shard_map.322 = (bf16[1024,4096]{1,0:T(8,128)(2,1)}, bf16[1024,4096]{1,0:T(8,128)(2,1)}, bf16[512,1536]{1,0:T(8,128)(2,1)}, f32[512,1536]{1,0:T(8,128)}) custom-call(bf16[1024,768]{1,0:T(8,128)(2,1)} %subtract_convert_fusion.x_ref, f32[1,4096]{1,0:T(1,128)} %convert_element_type.331.dead_ref, bf16[256,4096]{1,0:T(8,128)(2,1)} %copy-done.2, ...), custom_call_target="tpu_custom_call" | custom-call | flops 6442450944 | bytes 25165824 | tf_op jit(solution)/shard_map/pallas_call | solution.py:396
  283.2 14.7 %collective-permute-done.21 = bf16[128,1536]{1,0:T(8,128)(2,1)S(1)} collective-permute-done((bf16[128,1536]{1,0:T(8,128)(2,1)S(1)}, bf16[128,1536]{1,0:T(8,128)(2,1)S(1)}, u32[]{:S(2)}, u32[]{:S(2)}) %collective-permute-start.21) | collective-permute-done | bytes 393248 | tf_op jit(solution)/shard_map/ppermute | solution.py:652
  297.9 11.7 %collective-permute-done.22 = bf16[128,1536]{1,0:T(8,128)(2,1)S(1)} collective-permute-done((bf16[128,1536]{1,0:T(8,128)(2,1)S(1)}, bf16[128,1536]{1,0:T(8,128)(2,1)S(1)}, u32[]{:S(2)}, u32[]{:S(2)}) %collective-permute-start.22) | collective-permute-done | bytes 393248 | tf_op jit(solution)/shard_map/ppermute | solution.py:652
  310.1 8.3 %collective-permute-start.24 = (bf16[128,1536]{1,0:T(8,128)(2,1)S(1)}, bf16[128,1536]{1,0:T(8,128)(2,1)S(1)}, u32[]{:S(2)}, u32[]{:S(2)}) collective-permute-start(bf16[128,1536]{1,0:T(8,128)(2,1)S(1)} %pad_maximum_fusion.21), channel_id=1, source_target_pairs={{0,1},{1,0},{2,3},{3,2},{4,5},{5,4},{6,7},{7,6},{8,9},{9,8},{10,11... | collective-permute-start | bytes 1179656 | tf_op jit(solution)/shard_map/ppermute | solution.py:652
  320.8 13.5 %collective-permute-done.24 = bf16[128,1536]{1,0:T(8,128)(2,1)S(1)} collective-permute-done((bf16[128,1536]{1,0:T(8,128)(2,1)S(1)}, bf16[128,1536]{1,0:T(8,128)(2,1)S(1)}, u32[]{:S(2)}, u32[]{:S(2)}) %collective-permute-start.24) | collective-permute-done | bytes 393248 | tf_op jit(solution)/shard_map/ppermute | solution.py:652
  334.3 13.9 %collective-permute-done.25 = bf16[128,1536]{1,0:T(8,128)(2,1)S(1)} collective-permute-done((bf16[128,1536]{1,0:T(8,128)(2,1)S(1)}, bf16[128,1536]{1,0:T(8,128)(2,1)S(1)}, u32[]{:S(2)}, u32[]{:S(2)}) %collective-permute-start.25) | collective-permute-done | bytes 393248 | tf_op jit(solution)/shard_map/ppermute | solution.py:652
  356.5 12.2 %shard_map.323 = (bf16[768,1024]{1,0:T(8,128)(2,1)}, bf16[768,1024]{1,0:T(8,128)(2,1)}) custom-call(bf16[1536,512]{1,0:T(8,128)(2,1)} %copy.153.near_r.near_a, bf16[1536,512]{1,0:T(8,128)(2,1)} %copy.153.near_r.near_a, bf16[1536,512]{1,0:T(8,128)(2,1)} %copy.155.far_r.far_a, bf16[1536,512]{1,0:T(8,128)(2,1)} %copy.155.far_r.far_a, ...), custom_call_target="tpu_custom_call" | custom-call | flops 100663296 | bytes 262144 | tf_op jit(solution)/shard_map/pallas_call | solution.py:462
  372.4 12.5 %shard_map.324 = (f32[768,1024]{1,0:T(8,128)}, f32[768,1024]{1,0:T(8,128)}) custom-call(bf16[1536,512]{1,0:T(8,128)(2,1)} %copy.153.near_r.near_a, bf16[1536,512]{1,0:T(8,128)(2,1)} %copy.153.near_r.near_a, bf16[1536,512]{1,0:T(8,128)(2,1)} %copy.155.far_r.far_a, bf16[1536,512]{1,0:T(8,128)(2,1)} %copy.155.far_r.far_a, ...), custom_call_target="tpu_custom_call" | custom-call | flops 100663296 | bytes 262144 | tf_op jit(solution)/shard_map/pallas_call | solution.py:462
  384.9 18.7 %shard_map.325 = (bf16[784,1024]{1,0:T(8,128)(2,1)}, bf16[784,1024]{1,0:T(8,128)(2,1)}) custom-call(bf16[768,1024]{1,0:T(8,128)(2,1)} %copy.157.x_ref, bf16[512,1536]{1,0:T(8,128)(2,1)} %copy-done.8, bf16[512,1536]{1,0:T(8,128)(2,1)} %copy-done.9, f32[1,4096]{1,0:T(1,128)} %convert_element_type.331.dead_ref, bf16[256,4096]{1,0:T(8,128)(2,1)} %copy-done.2, ...), custom_call_target="tpu_custom_call" | custom-call | flops 100663296 | bytes 262144 | tf_op jit(solution)/shard_map/pallas_call | solution.py:526
  424.4 19.4 %shard_map.326 = (f32[784,1024]{1,0:T(8,128)}, f32[784,1024]{1,0:T(8,128)}) custom-call(bf16[768,1024]{1,0:T(8,128)(2,1)} %copy.157.x_ref, bf16[512,1536]{1,0:T(8,128)(2,1)} %copy-done.8, bf16[512,1536]{1,0:T(8,128)(2,1)} %copy-done.9, f32[1,4096]{1,0:T(1,128)} %convert_element_type.331.dead_ref, bf16[256,4096]{1,0:T(8,128)(2,1)} %copy-done.2, ...), custom_call_target="tpu_custom_call" | custom-call | flops 100663296 | bytes 262144 | tf_op jit(solution)/shard_map/pallas_call | solution.py:526
  452.2 9.3 %all-to-all-start.3 = ((bf16[4,192,1024]{2,1,0:T(8,128)(2,1)}), bf16[4,192,1024]{2,1,0:T(8,128)(2,1)}, u32[]{:S(2)}, u32[]{:S(2)}) async-start(bf16[4,192,1024]{2,1,0:T(8,128)(2,1)} %bitcast.177), calls=%async_computation.3 | async-start | bytes 3145728 | tf_op jit(solution)/shard_map/all_to_all | solution.py:662
  489.5 7.0 %collective-permute-start.38 = (bf16[112,768]{1,0:T(8,128)(2,1)}, bf16[112,768]{1,0:T(8,128)(2,1)S(1)}, u32[]{:S(2)}, u32[]{:S(2)}) collective-permute-start(bf16[112,768]{1,0:T(8,128)(2,1)} %pad_maximum_fusion.15), channel_id=1, source_target_pairs={{0,1},{1,0},{2,3},{3,2},{4,5},{5,4},{6,7},{7,6},{8,9},{9,8},{10,11... | collective-permute-start | bytes 516104 | tf_op jit(solution)/shard_map/ppermute | solution.py:652
  529.2 11.7 %shard_map.327 = (bf16[768,768]{1,0:T(8,128)(2,1)S(1)}, bf16[768,768]{1,0:T(8,128)(2,1)S(1)}, bf16[768,768]{1,0:T(8,128)(2,1)S(1)}) custom-call(s32[3]{0:T(128)S(1)} %pad_add_fusion.2.place_ref, bf16[4,96,768]{2,1,0:T(8,128)(2,1)S(1)} %pad_maximum_fusion.19.near_ref, bf16[4,96,768]{2,1,0:T(8,128)(2,1)S(1)} %collective-permute-done.47.far_ref), custom_call_target="tpu_custom_call" | custom-call | flops 226492416 | bytes 294912 | tf_op jit(solution)/shard_map/pallas_call | solution.py:194
  545.0 9.8 %shard_map.328 = (bf16[768,768]{1,0:T(8,128)(2,1)S(1)}, bf16[768,768]{1,0:T(8,128)(2,1)S(1)}, bf16[768,768]{1,0:T(8,128)(2,1)S(1)}) custom-call(bf16[768,768]{1,0:T(8,128)(2,1)S(1)} %get-tuple-element.237.g_hi, bf16[768,768]{1,0:T(8,128)(2,1)S(1)} %get-tuple-element.238.g_lo, bf16[768,768]{1,0:T(8,128)(2,1)S(1)} %get-tuple-element.239.q_ref), custom_call_target="tpu_custom_call" | custom-call | flops 226492416 | bytes 294912 | tf_op jit(solution)/shard_map/pallas_call | solution.py:194
  563.7 9.9 %shard_map.329 = (bf16[768,768]{1,0:T(8,128)(2,1)S(1)}, bf16[768,768]{1,0:T(8,128)(2,1)S(1)}, bf16[768,768]{1,0:T(8,128)(2,1)S(1)}) custom-call(bf16[768,768]{1,0:T(8,128)(2,1)S(1)} %get-tuple-element.246.g_hi, bf16[768,768]{1,0:T(8,128)(2,1)S(1)} %get-tuple-element.247.g_lo, bf16[768,768]{1,0:T(8,128)(2,1)S(1)} %get-tuple-element.248.q_ref), custom_call_target="tpu_custom_call" | custom-call | flops 226492416 | bytes 294912 | tf_op jit(solution)/shard_map/pallas_call | solution.py:194
  577.9 9.7 %collective-permute-done.52 = bf16[112,768]{1,0:T(8,128)(2,1)S(1)} collective-permute-done((bf16[112,768]{1,0:T(8,128)(2,1)S(1)}, bf16[112,768]{1,0:T(8,128)(2,1)S(1)}, u32[]{:S(2)}, u32[]{:S(2)}) %collective-permute-start.52) | collective-permute-done | bytes 172064 | tf_op jit(solution)/shard_map/ppermute | solution.py:652
  591.3 11.8 %shard_map.330 = (bf16[768,768]{1,0:T(8,128)(2,1)S(1)}, bf16[768,768]{1,0:T(8,128)(2,1)S(1)}, bf16[768,768]{1,0:T(8,128)(2,1)S(1)}) custom-call(bf16[768,768]{1,0:T(8,128)(2,1)S(1)} %get-tuple-element.255.g_hi, bf16[768,768]{1,0:T(8,128)(2,1)S(1)} %get-tuple-element.256.g_lo, bf16[768,768]{1,0:T(8,128)(2,1)S(1)} %get-tuple-element.257.q_ref), custom_call_target="tpu_custom_call" | custom-call | flops 283115520 | bytes 294912 | tf_op jit(solution)/shard_map/pallas_call | solution.py:194
  610.9 13.3 %all-to-all-start.4 = ((bf16[4,192,1024]{2,1,0:T(8,128)(2,1)}), bf16[4,192,1024]{2,1,0:T(8,128)(2,1)}, u32[]{:S(2)}, u32[]{:S(2)}) async-start(bf16[4,192,1024]{2,1,0:T(8,128)(2,1)} %bitcast.186), calls=%async_computation.4 | async-start | bytes 3145728 | tf_op jit(solution)/shard_map/all_to_all | solution.py:662
  630.4 11.3 %shard_map.332 = (bf16[768,768]{1,0:T(8,128)(2,1)S(1)}, bf16[768,768]{1,0:T(8,128)(2,1)S(1)}, bf16[768,768]{1,0:T(8,128)(2,1)S(1)}) custom-call(s32[3]{0:T(128)S(1)} %pad_add_fusion.2.place_ref, bf16[4,96,768]{2,1,0:T(8,128)(2,1)S(1)} %pad_maximum_fusion.20.near_ref, bf16[4,96,768]{2,1,0:T(8,128)(2,1)S(1)} %collective-permute-done.57.far_ref), custom_call_target="tpu_custom_call" | custom-call | flops 226492416 | bytes 294912 | tf_op jit(solution)/shard_map/pallas_call | solution.py:194
  641.7 9.8 %shard_map.333 = (bf16[768,768]{1,0:T(8,128)(2,1)S(1)}, bf16[768,768]{1,0:T(8,128)(2,1)S(1)}, bf16[768,768]{1,0:T(8,128)(2,1)S(1)}) custom-call(bf16[768,768]{1,0:T(8,128)(2,1)S(1)} %get-tuple-element.268.g_hi, bf16[768,768]{1,0:T(8,128)(2,1)S(1)} %get-tuple-element.269.g_lo, bf16[768,768]{1,0:T(8,128)(2,1)S(1)} %get-tuple-element.270.q_ref), custom_call_target="tpu_custom_call" | custom-call | flops 226492416 | bytes 294912 | tf_op jit(solution)/shard_map/pallas_call | solution.py:194
  651.5 9.8 %shard_map.334 = (bf16[768,768]{1,0:T(8,128)(2,1)S(1)}, bf16[768,768]{1,0:T(8,128)(2,1)S(1)}, bf16[768,768]{1,0:T(8,128)(2,1)S(1)}) custom-call(bf16[768,768]{1,0:T(8,128)(2,1)S(1)} %get-tuple-element.271.g_hi, bf16[768,768]{1,0:T(8,128)(2,1)S(1)} %get-tuple-element.272.g_lo, bf16[768,768]{1,0:T(8,128)(2,1)S(1)} %get-tuple-element.273.q_ref), custom_call_target="tpu_custom_call" | custom-call | flops 226492416 | bytes 294912 | tf_op jit(solution)/shard_map/pallas_call | solution.py:194
  661.4 11.7 %shard_map.335 = (bf16[768,768]{1,0:T(8,128)(2,1)S(1)}, bf16[768,768]{1,0:T(8,128)(2,1)S(1)}, bf16[768,768]{1,0:T(8,128)(2,1)S(1)}) custom-call(bf16[768,768]{1,0:T(8,128)(2,1)S(1)} %get-tuple-element.274.g_hi, bf16[768,768]{1,0:T(8,128)(2,1)S(1)} %get-tuple-element.275.g_lo, bf16[768,768]{1,0:T(8,128)(2,1)S(1)} %get-tuple-element.276.q_ref), custom_call_target="tpu_custom_call" | custom-call | flops 283115520 | bytes 294912 | tf_op jit(solution)/shard_map/pallas_call | solution.py:194
  686.2 8.7 %shard_map.337 = (f32[192,4096]{1,0:T(8,128)}, f32[192,4096]{1,0:T(8,128)}, bf16[192,4096]{1,0:T(8,128)(2,1)}) custom-call(s32[3]{0:T(128)} %copy-done.7, bf16[768,768]{1,0:T(8,128)(2,1)} %copy-done.6, bf16[4,768,1024]{2,1,0:T(8,128)(2,1)} %bitcast.180, f32[192,4096]{1,0:T(8,128)} %weight_ref.1), custom_call_target="tpu_custom_call" | custom-call | flops 1207959552 | bytes 6291456 | tf_op jit(solution)/shard_map/pallas_call | solution.py:568
  (447 shorter events, 287.1 us)
Async XLA Ops:
  10.6 45.0 %collective-permute-start = (s32[128,544]{1,0:T(8,128)}, s32[128,544]{1,0:T(8,128)}, u32[]{:S(2)}, u32[]{:S(2)}) collective-permute-start(s32[128,544]{1,0:T(8,128)} %pad_add_fusion.1), channel_id=1, source_target_pairs={{0,1},{1,0},{2,3},{3,2},{4,5},{5,4},{6,7},{7,6},{8,9},{9,8},{10,11... | collective-permute-start | bytes 835592 | tf_op jit(solution)/shard_map/ppermute | solution.py:652
  13.6 48.6 %collective-permute-start.1 = (s32[128,544]{1,0:T(8,128)}, s32[128,544]{1,0:T(8,128)}, u32[]{:S(2)}, u32[]{:S(2)}) collective-permute-start(s32[128,544]{1,0:T(8,128)} %pad_add_fusion.1), channel_id=1, source_target_pairs={{0,2},{1,3},{2,0},{3,1},{4,6},{5,7},{6,4},{7,5},{8,10},{9,11},{10,... | collective-permute-start | bytes 835592 | tf_op jit(solution)/shard_map/ppermute | solution.py:652
  16.2 46.1 %collective-permute-start.2 = (s32[128,544]{1,0:T(8,128)}, s32[128,544]{1,0:T(8,128)}, u32[]{:S(2)}, u32[]{:S(2)}) collective-permute-start(s32[128,544]{1,0:T(8,128)} %pad_add_fusion.1), channel_id=1, source_target_pairs={{0,3},{1,2},{2,1},{3,0},{4,7},{5,6},{6,5},{7,4},{8,11},{9,10},{10,... | collective-permute-start | bytes 835592 | tf_op jit(solution)/shard_map/ppermute | solution.py:652
  41.0 42.3 %all-to-all-start = ((bf16[192,4,1024]{2,0,1:T(8,128)(2,1)}), bf16[192,4,1024]{2,0,1:T(8,128)(2,1)}, u32[]{:S(2)}, u32[]{:S(2)}) async-start(bf16[192,4,1024]{2,0,1:T(8,128)(2,1)} %bitcast.175), calls=%async_computation | async-start | bytes 3145728 | tf_op jit(solution)/shard_map/all_to_all | solution.py:659
  102.0 54.3 %all-to-all-start.1 = ((bf16[192,4,1024]{2,0,1:T(8,128)(2,1)}), bf16[192,4,1024]{2,0,1:T(8,128)(2,1)}, u32[]{:S(2)}, u32[]{:S(2)}) async-start(bf16[192,4,1024]{2,0,1:T(8,128)(2,1)} %bitcast.167), calls=%async_computation.1 | async-start | bytes 3145728 | tf_op jit(solution)/shard_map/all_to_all | solution.py:659
  118.6 37.7 %collective-permute-start.12 = (bf16[784,1024]{1,0:T(8,128)(2,1)}, bf16[784,1024]{1,0:T(8,128)(2,1)}, u32[]{:S(2)}, u32[]{:S(2)}) collective-permute-start(bf16[784,1024]{1,0:T(8,128)(2,1)} %pad_maximum_fusion.3.refs_4_), channel_id=1, source_target_pairs={{0,16},{8,24},{16,0},{24,8},{1,17},{9,25},{17,1},{25,9},{2,18},{10... | collective-permute-start | bytes 4816904 | tf_op jit(solution)/shard_map/ppermute | solution.py:652
  120.0 36.4 %collective-permute-start.13 = (bf16[784,1024]{1,0:T(8,128)(2,1)}, bf16[784,1024]{1,0:T(8,128)(2,1)}, u32[]{:S(2)}, u32[]{:S(2)}) collective-permute-start(bf16[784,1024]{1,0:T(8,128)(2,1)} %pad_maximum_fusion.4.refs_6_), channel_id=1, source_target_pairs={{0,8},{8,0},{16,24},{24,16},{1,9},{9,1},{17,25},{25,17},{2,10},{10... | collective-permute-start | bytes 4816904 | tf_op jit(solution)/shard_map/ppermute | solution.py:652
  120.7 35.6 %collective-permute-start.10 = (bf16[128,768]{1,0:T(8,128)(2,1)S(1)}, bf16[128,768]{1,0:T(8,128)(2,1)S(1)}, u32[]{:S(2)}, u32[]{:S(2)}) collective-permute-start(bf16[128,768]{1,0:T(8,128)(2,1)S(1)} %fusion.21), channel_id=1, source_target_pairs={{0,2},{1,3},{2,0},{3,1},{4,6},{5,7},{6,4},{7,5},{8,10},{9,11},{10,... | collective-permute-start | bytes 589832 | tf_op jit(solution)/shard_map/ppermute | solution.py:652
  123.2 33.1 %collective-permute-start.11 = (bf16[128,768]{1,0:T(8,128)(2,1)S(1)}, bf16[128,768]{1,0:T(8,128)(2,1)S(1)}, u32[]{:S(2)}, u32[]{:S(2)}) collective-permute-start(bf16[128,768]{1,0:T(8,128)(2,1)S(1)} %fusion.21), channel_id=1, source_target_pairs={{0,3},{1,2},{2,1},{3,0},{4,7},{5,6},{6,5},{7,4},{8,11},{9,10},{10,... | collective-permute-start | bytes 589832 | tf_op jit(solution)/shard_map/ppermute | solution.py:652
  124.6 31.7 %collective-permute-start.9 = (bf16[128,768]{1,0:T(8,128)(2,1)S(1)}, bf16[128,768]{1,0:T(8,128)(2,1)S(1)}, u32[]{:S(2)}, u32[]{:S(2)}) collective-permute-start(bf16[128,768]{1,0:T(8,128)(2,1)S(1)} %fusion.21), channel_id=1, source_target_pairs={{0,1},{1,0},{2,3},{3,2},{4,5},{5,4},{6,7},{7,6},{8,9},{9,8},{10,11... | collective-permute-start | bytes 589832 | tf_op jit(solution)/shard_map/ppermute | solution.py:652
  161.2 74.9 %all-to-all-start.2 = ((bf16[384,4,1024]{0,2,1:T(8,128)(2,1)}), bf16[384,4,1024]{0,2,1:T(8,128)(2,1)}, u32[]{:S(2)}, u32[]{:S(2)}) async-start(bf16[384,4,1024]{0,2,1:T(8,128)(2,1)} %bitcast.39), calls=%async_computation.2 | async-start | bytes 6291456 | tf_op jit(solution)/shard_map/all_to_all | solution.py:659
  188.8 51.9 %collective-permute-start.18 = (bf16[768,1024]{1,0:T(8,128)(2,1)}, bf16[768,1024]{1,0:T(8,128)(2,1)}, u32[]{:S(2)}, u32[]{:S(2)}) collective-permute-start(bf16[768,1024]{1,0:T(8,128)(2,1)} %pad_maximum_fusion.5.refs_8_.refs_4_), channel_id=1, source_target_pairs={{0,16},{8,24},{16,0},{24,8},{1,17},{9,25},{17,1},{25,9},{2,18},{10... | collective-permute-start | bytes 4718600 | tf_op jit(solution)/shard_map/ppermute | solution.py:652
  190.3 50.4 %collective-permute-start.19 = (bf16[768,1024]{1,0:T(8,128)(2,1)}, bf16[768,1024]{1,0:T(8,128)(2,1)}, u32[]{:S(2)}, u32[]{:S(2)}) collective-permute-start(bf16[768,1024]{1,0:T(8,128)(2,1)} %pad_maximum_fusion.6.refs_10_.refs_5_), channel_id=1, source_target_pairs={{0,8},{8,0},{16,24},{24,16},{1,9},{9,1},{17,25},{25,17},{2,10},{10... | collective-permute-start | bytes 4718600 | tf_op jit(solution)/shard_map/ppermute | solution.py:652
  279.4 30.2 %collective-permute-start.22 = (bf16[128,1536]{1,0:T(8,128)(2,1)S(1)}, bf16[128,1536]{1,0:T(8,128)(2,1)S(1)}, u32[]{:S(2)}, u32[]{:S(2)}) collective-permute-start(bf16[128,1536]{1,0:T(8,128)(2,1)S(1)} %get-tuple-element.330), channel_id=1, source_target_pairs={{0,2},{1,3},{2,0},{3,1},{4,6},{5,7},{6,4},{7,5},{8,10},{9,11},{10,... | collective-permute-start | bytes 1179656 | tf_op jit(solution)/shard_map/ppermute | solution.py:652
  282.8 26.8 %collective-permute-start.23 = (bf16[128,1536]{1,0:T(8,128)(2,1)S(1)}, bf16[128,1536]{1,0:T(8,128)(2,1)S(1)}, u32[]{:S(2)}, u32[]{:S(2)}) collective-permute-start(bf16[128,1536]{1,0:T(8,128)(2,1)S(1)} %get-tuple-element.329), channel_id=1, source_target_pairs={{0,3},{1,2},{2,1},{3,0},{4,7},{5,6},{6,5},{7,4},{8,11},{9,10},{10,... | collective-permute-start | bytes 1179656 | tf_op jit(solution)/shard_map/ppermute | solution.py:652
  310.1 24.2 %collective-permute-start.24 = (bf16[128,1536]{1,0:T(8,128)(2,1)S(1)}, bf16[128,1536]{1,0:T(8,128)(2,1)S(1)}, u32[]{:S(2)}, u32[]{:S(2)}) collective-permute-start(bf16[128,1536]{1,0:T(8,128)(2,1)S(1)} %pad_maximum_fusion.21), channel_id=1, source_target_pairs={{0,1},{1,0},{2,3},{3,2},{4,5},{5,4},{6,7},{7,6},{8,9},{9,8},{10,11... | collective-permute-start | bytes 1179656 | tf_op jit(solution)/shard_map/ppermute | solution.py:652
  318.4 29.8 %collective-permute-start.25 = (bf16[128,1536]{1,0:T(8,128)(2,1)S(1)}, bf16[128,1536]{1,0:T(8,128)(2,1)S(1)}, u32[]{:S(2)}, u32[]{:S(2)}) collective-permute-start(bf16[128,1536]{1,0:T(8,128)(2,1)S(1)} %pad_maximum_fusion.21), channel_id=1, source_target_pairs={{0,2},{1,3},{2,0},{3,1},{4,6},{5,7},{6,4},{7,5},{8,10},{9,11},{10,... | collective-permute-start | bytes 1179656 | tf_op jit(solution)/shard_map/ppermute | solution.py:652
  319.4 28.8 %collective-permute-start.26 = (bf16[128,1536]{1,0:T(8,128)(2,1)S(1)}, bf16[128,1536]{1,0:T(8,128)(2,1)S(1)}, u32[]{:S(2)}, u32[]{:S(2)}) collective-permute-start(bf16[128,1536]{1,0:T(8,128)(2,1)S(1)} %pad_maximum_fusion.21), channel_id=1, source_target_pairs={{0,3},{1,2},{2,1},{3,0},{4,7},{5,6},{6,5},{7,4},{8,11},{9,10},{10,... | collective-permute-start | bytes 1179656 | tf_op jit(solution)/shard_map/ppermute | solution.py:652
  368.7 36.6 %collective-permute-start.28 = (bf16[768,1024]{1,0:T(8,128)(2,1)}, bf16[768,1024]{1,0:T(8,128)(2,1)S(1)}, u32[]{:S(2)}, u32[]{:S(2)}) collective-permute-start(bf16[768,1024]{1,0:T(8,128)(2,1)} %get-tuple-element.203), channel_id=1, source_target_pairs={{0,16},{8,24},{16,0},{24,8},{1,17},{9,25},{17,1},{25,9},{2,18},{10... | collective-permute-start | bytes 4718600 | tf_op jit(solution)/shard_map/ppermute | solution.py:652
  370.2 36.5 %collective-permute-start.29 = (bf16[768,1024]{1,0:T(8,128)(2,1)}, bf16[768,1024]{1,0:T(8,128)(2,1)}, u32[]{:S(2)}, u32[]{:S(2)}) collective-permute-start(bf16[768,1024]{1,0:T(8,128)(2,1)} %get-tuple-element.204), channel_id=1, source_target_pairs={{0,8},{8,0},{16,24},{24,16},{1,9},{9,1},{17,25},{25,17},{2,10},{10... | collective-permute-start | bytes 4718600 | tf_op jit(solution)/shard_map/ppermute | solution.py:652
  411.6 32.2 %collective-permute-start.30 = (bf16[768,512]{1,0:T(8,128)(2,1)}, bf16[768,512]{1,0:T(8,128)(2,1)}, u32[]{:S(2)}, u32[]{:S(2)}) collective-permute-start(bf16[768,512]{1,0:T(8,128)(2,1)} %split.41), channel_id=1, source_target_pairs={{0,8},{8,0},{16,24},{24,16},{1,9},{9,1},{17,25},{25,17},{2,10},{10... | collective-permute-start | bytes 2359304 | tf_op jit(solution)/shard_map/ppermute | solution.py:652
  417.9 28.0 %collective-permute-start.31 = (bf16[768,512]{1,0:T(8,128)(2,1)}, bf16[768,512]{1,0:T(8,128)(2,1)}, u32[]{:S(2)}, u32[]{:S(2)}) collective-permute-start(bf16[768,512]{1,0:T(8,128)(2,1)} %split.40), channel_id=1, source_target_pairs={{0,16},{8,24},{16,0},{24,8},{1,17},{9,25},{17,1},{25,9},{2,18},{10... | collective-permute-start | bytes 2359304 | tf_op jit(solution)/shard_map/ppermute | solution.py:652
  418.7 52.5 %collective-permute-start.32 = (bf16[784,1024]{1,0:T(8,128)(2,1)}, bf16[784,1024]{1,0:T(8,128)(2,1)}, u32[]{:S(2)}, u32[]{:S(2)}) collective-permute-start(bf16[784,1024]{1,0:T(8,128)(2,1)} %get-tuple-element.215), channel_id=1, source_target_pairs={{0,16},{8,24},{16,0},{24,8},{1,17},{9,25},{17,1},{25,9},{2,18},{10... | collective-permute-start | bytes 4816904 | tf_op jit(solution)/shard_map/ppermute | solution.py:652
  420.1 51.1 %collective-permute-start.33 = (bf16[784,1024]{1,0:T(8,128)(2,1)}, bf16[784,1024]{1,0:T(8,128)(2,1)}, u32[]{:S(2)}, u32[]{:S(2)}) collective-permute-start(bf16[784,1024]{1,0:T(8,128)(2,1)} %get-tuple-element.216), channel_id=1, source_target_pairs={{0,8},{8,0},{16,24},{24,16},{1,9},{9,1},{17,25},{25,17},{2,10},{10... | collective-permute-start | bytes 4816904 | tf_op jit(solution)/shard_map/ppermute | solution.py:652
  452.2 54.5 %all-to-all-start.3 = ((bf16[4,192,1024]{2,1,0:T(8,128)(2,1)}), bf16[4,192,1024]{2,1,0:T(8,128)(2,1)}, u32[]{:S(2)}, u32[]{:S(2)}) async-start(bf16[4,192,1024]{2,1,0:T(8,128)(2,1)} %bitcast.177), calls=%async_computation.3 | async-start | bytes 3145728 | tf_op jit(solution)/shard_map/all_to_all | solution.py:662
  461.4 224.8 %all-gather.5.cloned.1.call-start = ((), (), s32[]{:S(2)}) async-start(), calls=%async_computation.5 | async-start | bytes 7864320 | tf_op jit(solution)/shard_map/all_gather | solution.py:896
  480.4 23.9 %collective-permute-start.41 = (bf16[784,512]{1,0:T(8,128)(2,1)S(1)}, bf16[784,512]{1,0:T(8,128)(2,1)S(1)}, u32[]{:S(2)}, u32[]{:S(2)}) collective-permute-start(bf16[784,512]{1,0:T(8,128)(2,1)S(1)} %get-tuple-element.360), channel_id=1, source_target_pairs={{0,8},{8,0},{16,24},{24,16},{1,9},{9,1},{17,25},{25,17},{2,10},{10... | collective-permute-start | bytes 2408456 | tf_op jit(solution)/shard_map/ppermute | solution.py:652
  481.0 23.7 %collective-permute-start.42 = (bf16[784,512]{1,0:T(8,128)(2,1)S(1)}, bf16[784,512]{1,0:T(8,128)(2,1)S(1)}, u32[]{:S(2)}, u32[]{:S(2)}) collective-permute-start(bf16[784,512]{1,0:T(8,128)(2,1)S(1)} %get-tuple-element.361), channel_id=1, source_target_pairs={{0,16},{8,24},{16,0},{24,8},{1,17},{9,25},{17,1},{25,9},{2,18},{10... | collective-permute-start | bytes 2408456 | tf_op jit(solution)/shard_map/ppermute | solution.py:652
  555.2 22.7 %collective-permute-start.51 = (bf16[112,768]{1,0:T(8,128)(2,1)S(1)}, bf16[112,768]{1,0:T(8,128)(2,1)S(1)}, u32[]{:S(2)}, u32[]{:S(2)}) collective-permute-start(bf16[112,768]{1,0:T(8,128)(2,1)S(1)} %pad_maximum_fusion.11), channel_id=1, source_target_pairs={{0,1},{1,0},{2,3},{3,2},{4,5},{5,4},{6,7},{7,6},{8,9},{9,8},{10,11... | collective-permute-start | bytes 516104 | tf_op jit(solution)/shard_map/ppermute | solution.py:652
  561.2 26.3 %collective-permute-start.52 = (bf16[112,768]{1,0:T(8,128)(2,1)S(1)}, bf16[112,768]{1,0:T(8,128)(2,1)S(1)}, u32[]{:S(2)}, u32[]{:S(2)}) collective-permute-start(bf16[112,768]{1,0:T(8,128)(2,1)S(1)} %pad_maximum_fusion.11), channel_id=1, source_target_pairs={{0,2},{1,3},{2,0},{3,1},{4,6},{5,7},{6,4},{7,5},{8,10},{9,11},{10,... | collective-permute-start | bytes 516104 | tf_op jit(solution)/shard_map/ppermute | solution.py:652
  562.3 25.3 %collective-permute-start.53 = (bf16[112,768]{1,0:T(8,128)(2,1)S(1)}, bf16[112,768]{1,0:T(8,128)(2,1)S(1)}, u32[]{:S(2)}, u32[]{:S(2)}) collective-permute-start(bf16[112,768]{1,0:T(8,128)(2,1)S(1)} %pad_maximum_fusion.11), channel_id=1, source_target_pairs={{0,3},{1,2},{2,1},{3,0},{4,7},{5,6},{6,5},{7,4},{8,11},{9,10},{10,... | collective-permute-start | bytes 516104 | tf_op jit(solution)/shard_map/ppermute | solution.py:652
  610.9 68.8 %all-to-all-start.4 = ((bf16[4,192,1024]{2,1,0:T(8,128)(2,1)}), bf16[4,192,1024]{2,1,0:T(8,128)(2,1)}, u32[]{:S(2)}, u32[]{:S(2)}) async-start(bf16[4,192,1024]{2,1,0:T(8,128)(2,1)} %bitcast.186), calls=%async_computation.4 | async-start | bytes 3145728 | tf_op jit(solution)/shard_map/all_to_all | solution.py:662
  (102 other events, 1288.6 us)
Sparse Core Ops, SparseCore 0:
  514.0 161.0 all-gather.4

commit v8 on v7

--- a/solution.py
+++ b/solution.py
@@ -436,7 +436,7 @@
     half = near_r.shape[1]
 
     def one(index, carry):
-        rows = pl.ds(pl.multiple_of(index * 384, 384), 384)
+        rows = pl.ds(pl.multiple_of(index * 768, 768), 768)
         value = dot_f32(near_r[rows, :], top_ref[:half, :])
         value = value + dot_f32(near_a[rows, :], aux_ref[:half, :])
         value = value + dot_f32(far_r[rows, :], top_ref[half:, :])
@@ -444,7 +444,7 @@
         store_part(count, outs, rows, value)
         return carry
 
-    lax.fori_loop(0, near_r.shape[0] // 384, one, 0)
+    lax.fori_loop(0, near_r.shape[0] // 768, one, 0)
 
 
 def dec_grads(near_t, far_t, top_acts, aux_acts, quarters, kind):
@@ -499,11 +499,11 @@
             total = total + jnp.sum(value.astype(jnp.float32), 0, keepdims=True)
 
     def two(index, carry):
-        rows = pl.ds(pl.multiple_of(index * 384, 384), 384)
+        rows = pl.ds(pl.multiple_of(index * 768, 768), 768)
         store_part(count, (out_a, out_b), rows, dot_f32(x_ref[rows, :], grads[...]))
         return carry
 
-    lax.fori_loop(0, width // 384, two, 0)
+    lax.fori_loop(0, width // 768, two, 0)
     lines = lax.broadcasted_iota(jnp.int32, (16, latents), 0)
     if out_a.dtype == jnp.bfloat16:
         high = total.astype(jnp.bfloat16).astype(jnp.float32)
@@ -661,14 +661,18 @@
     def rows_of(value):
         return lax.all_to_all(value, "narrow", split_axis=0, concat_axis=1, tiled=True)
 
-    def gather_start(own, axis):
-        halves = []
+    def gather_start(own):
+        helds, gots = [], []
         for part, order in enumerate(orders):
-            held = lax.slice_in_dim(own, part * half_latents, (part + 1) * half_latents, axis=axis)
-            for bit in order[:-1]:
-                held = jnp.concatenate([held, swap(held, "chip", bit)], axis)
-            halves.append(held)
-        return halves
+            held = own[:, part * half_latents : (part + 1) * half_latents]
+            for bit in order[:-2]:
+                held = jnp.concatenate([held, swap(held, "chip", bit)], 1)
+            helds.append(held)
+            gots.append(swap(held, "chip", order[-2]))
+        return helds, gots
+
+    def gather_join(helds, gots):
+        return [jnp.concatenate(pair, 1) for pair in zip(helds, gots)]
 
     def gather_end(halves):
         pieces = []
@@ -725,7 +729,7 @@
     enc_own, embedded = tie(enc_own, embedded)
     dec_cast, enc_own = tie(dec_weight_t.astype(bf16), enc_own)
     dec_own = rows_to_latents(dec_cast)
-    enc_halves = gather_start(jnp.concatenate([enc_own, bias_rows], 0), 1)
+    enc_helds, enc_halves = gather_start(jnp.concatenate([enc_own, bias_rows], 0))
 
     dead_here = jnp.stack(
         [
@@ -747,24 +751,25 @@
             dead_parts.append(dead_here[spot, part * half_latents : (part + 1) * half_latents])
     dead_here = jnp.concatenate(dead_parts)[None].astype(f32)
     sizes = (wide_latents, own_latents, top_ids.shape[1], orders)
-    near_picks, dead_here, embedded = tie(near_picks, dead_here, embedded)
     start = embedded + position_table[:row_count].astype(f32)
     ctx_length = lengths[0]
     inputs = frozen_block(start, ctx_length, ln_gains, frozen_bias, w_qkv, w_proj, w_fc, w_out)
     counted = (jnp.arange(row_count) < ctx_length).astype(f32)
-    near_picks, inputs, enc_halves = tie(near_picks, inputs, enc_halves)
-    enc_parts = gather_end(enc_halves)
+    near_picks, inputs, enc_halves, dead_here, dec_own = tie(
+        near_picks, inputs, enc_halves, dead_here, dec_own
+    )
+    enc_parts = gather_end(gather_join(enc_helds, enc_halves))
     got_inputs = [swap(inputs, "narrow", k) for k in range(1, narrow_count)]
     half_rows = core_rows // 2
     codes = [kind_codes(place, near_picks[:half_rows], latent_count, sizes)]
     enc_lasts = [enc_parts[1], enc_parts[3]]
-    dec_own, codes, got_inputs, enc_lasts = tie(dec_own, codes, got_inputs, enc_lasts)
+    codes, got_inputs, enc_lasts = tie(codes, got_inputs, enc_lasts)
+    enc_parts = [enc_parts[0], enc_lasts[0], enc_parts[2], enc_lasts[1]]
     near_picks, codes = tie(near_picks, codes)
-    dec_halves = gather_start(dec_own, 1)
+    dec_helds, dec_halves = gather_start(dec_own)
     codes = [*codes, kind_codes(place, near_picks[half_rows:], latent_count, sizes)]
     dec_halves, codes = tie(dec_halves, codes)
-    enc_parts = [enc_parts[0], enc_lasts[0], enc_parts[2], enc_lasts[1]]
-    dec_parts = gather_end(dec_halves)
+    dec_parts = gather_end(gather_join(dec_helds, dec_halves))
     moments = jnp.concatenate([enc_moment.astype(bf16), dec_moment_t.astype(bf16)], 0)
     moments, got_inputs = tie(moments, got_inputs)
     moments = rows_to_latents(moments)
@@ -776,8 +781,8 @@
     codes = [*codes, kind_codes(place, far_picks[half_rows:], latent_count, sizes)]
     all_inputs = jnp.concatenate([near_inputs, far_inputs], 0)
     encoder_in = (all_inputs.astype(f32) - decoder_bias).astype(bf16)
-    encoder_in, moments = tie(encoder_in, moments)
     top_acts, aux_acts, far, near = forward(encoder_in, codes, dead_here, enc_parts, dec_parts)
+    far, moments = tie(far, moments)
     encoder_t = encoder_in.T
     far_got, encoder_t = tie(swap(far, "core", 1), encoder_t)
     rebuilt = near + far_got.astype(f32)

time: 710 us -> 716 us (level)
  waiting for transfers between devices: 150 us -> 158 us
    all_to_all x3, waiting for transfers between devices: 26.1 us -> 36.7 us  [rows_to_latents(): lax.all_to_all(value, 'narrow', split_axis=1, concat_axis=0, tiled=True)]
    unnamed x159 -> x147, local copies, waits for them, and re-layouts: 17.4 us -> 18.9 us
  transfers between devices with their start and end apart: 64 -> 64, of which waited for: 26 -> 26; matrix products, arithmetic and copies ran while one was open for 17% -> 18% of each run, Pallas kernels for 27% -> 31%
where the time goes in v8:
time: 716 us; the launch traced here: 710 us
  Pallas kernels  240 us (34%)
  waiting for transfers between devices  158 us (22%)
  starting transfers between devices  115 us (16%)
  other arithmetic  76.7 us (11%)
  local copies, waits for them, and re-layouts  73.4 us (10%)
  matrix products  21 us (3%)
  between operations  16.6 us (2%)
  blocking collectives  9.07 us (1%)
    ppermute x58, waiting for transfers between devices, swap(): lax.ppermute(value, axis, [(spot, spot ^ offset) for spot in range(count)])  121 us
    pallas_call x10, Pallas kernels, square_call(): pl.pallas_call(kernel, out_shape=[square] * outs, in_specs=specs, out_spe...  96.1 us
    ppermute x58, starting transfers between devices, swap(): lax.ppermute(value, axis, [(spot, spot ^ offset) for spot in range(count)])  78.4 us
    pallas_call x4, Pallas kernels, kind_codes(): pl.pallas_call(functools.partial(code_kernel, shifts), grid=(row_total //...  45.5 us
    all_to_all x3, waiting for transfers between devices, rows_to_latents(): lax.all_to_all(value, 'narrow', split_axis=1, concat_axis=0, tiled=True)  36.7 us
    pallas_call x2, Pallas kernels, enc_grads(): pl.pallas_call(functools.partial(enc_grad_kernel, count), grid=(2 * count...  34.6 us
    pallas_call x1, Pallas kernels, forward(): pl.pallas_call(functools.partial(forward_kernel, count), grid=(4 * count,...  31.4 us
    pallas_call x2, Pallas kernels, dec_grads(): pl.pallas_call(functools.partial(dec_grad_kernel, count), grid=(2 * count...  23.4 us
  transfers between devices with their start and end apart: 64, of which 26 were waited for; matrix products, arithmetic and copies ran while one was open for 18% of the time, Pallas kernels for 31%

profile of v8, /device:TPU:0, one launch (start us, length us, event | category | flops | bytes accessed | tf_op | source)
XLA Modules:
  0.0 709.6 jit_solution(16276844830488594326)
XLA Ops:
  16.2 9.1 %all-gather.2 = s32[8,1,128]{2,1,0:T(1,128)S(1)} all-gather(s32[1,1,128]{2,1,0:T(1,128)} %bitcast.210), channel_id=2, replica_groups=mesh['chip'=4,'core'=2,'narrow'=4] {'chip','core'}, dimensions={0}, use_global_device_ids=true | all-gather | bytes 4608 | tf_op jit(solution)/shard_map/all_gather | solution.py:701
  25.5 10.6 %gather_fusion = bf16[1024,768]{1,0:T(8,128)(2,1)} fusion(bf16[6288,768]{1,0:T(8,128)(2,1)} %param.28, s32[1024]{0:T(1024)S(1)} %broadcast_clamp_fusion), kind=kCustom, calls=%fused_computation | custom fusion | bytes 3149824 | tf_op jit(solution)/shard_map/jit(_take)/gather | solution.py:711
  66.7 16.7 %all-to-all-done = bf16[192,4,1024]{2,0,1:T(8,128)(2,1)} async-done(((bf16[192,4,1024]{2,0,1:T(8,128)(2,1)}), bf16[192,4,1024]{2,0,1:T(8,128)(2,1)}, u32[]{:S(2)}, u32[]{:S(2)}) %all-to-all-start) | async-done | bytes 1572896 | tf_op jit(solution)/shard_map/all_to_all | solution.py:659
  110.0 20.1 %all-to-all-done.1 = bf16[192,4,1024]{2,0,1:T(8,128)(2,1)} async-done(((bf16[192,4,1024]{2,0,1:T(8,128)(2,1)}), bf16[192,4,1024]{2,0,1:T(8,128)(2,1)}, u32[]{:S(2)}, u32[]{:S(2)}) %all-to-all-start.1) | async-done | bytes 1572896 | tf_op jit(solution)/shard_map/all_to_all | solution.py:659
  142.3 11.4 %shard_map.318.refs_0_ = bf16[256,4096]{1,0:T(8,128)(2,1)S(1)} custom-call(s32[3]{0:T(128)S(1)} %pad_add_fusion.2.place_ref, s32[256,544]{1,0:T(8,128)S(1)} %slice.323.ids_ref), custom_call_target="tpu_custom_call" | custom-call | flops 1048576 | bytes 139264 | tf_op jit(solution)/shard_map/pallas_call | solution.py:290
  155.1 12.7 %collective-permute-done.13.refs_7_ = bf16[784,1024]{1,0:T(8,128)(2,1)S(1)} collective-permute-done((bf16[784,1024]{1,0:T(8,128)(2,1)S(1)}, bf16[784,1024]{1,0:T(8,128)(2,1)S(1)}, u32[]{:S(2)}, u32[]{:S(2)}) %collective-permute-start.13) | collective-permute-done | bytes 1605664 | tf_op jit(solution)/shard_map/ppermute | solution.py:652
  186.8 11.4 %shard_map.319.refs_1_ = bf16[256,4096]{1,0:T(8,128)(2,1)S(1)} custom-call(s32[3]{0:T(128)S(1)} %pad_add_fusion.2.place_ref, s32[256,544]{1,0:T(8,128)S(1)} %slice.326.ids_ref), custom_call_target="tpu_custom_call" | custom-call | flops 1048576 | bytes 139264 | tf_op jit(solution)/shard_map/pallas_call | solution.py:290
  212.6 11.4 %shard_map.320.refs_2_ = bf16[256,4096]{1,0:T(8,128)(2,1)S(1)} custom-call(s32[3]{0:T(128)S(1)} %pad_add_fusion.2.place_ref, s32[256,544]{1,0:T(8,128)S(1)} %slice.410.ids_ref), custom_call_target="tpu_custom_call" | custom-call | flops 1048576 | bytes 139264 | tf_op jit(solution)/shard_map/pallas_call | solution.py:290
  229.1 11.4 %shard_map.321.refs_3_ = bf16[256,4096]{1,0:T(8,128)(2,1)S(1)} custom-call(s32[3]{0:T(128)S(1)} %pad_add_fusion.2.place_ref, s32[256,544]{1,0:T(8,128)S(1)} %slice.411.ids_ref), custom_call_target="tpu_custom_call" | custom-call | flops 1048576 | bytes 139264 | tf_op jit(solution)/shard_map/pallas_call | solution.py:290
  246.0 31.4 %shard_map.322 = (bf16[1024,4096]{1,0:T(8,128)(2,1)}, bf16[1024,4096]{1,0:T(8,128)(2,1)}, bf16[512,1536]{1,0:T(8,128)(2,1)}, f32[512,1536]{1,0:T(8,128)}) custom-call(bf16[1024,768]{1,0:T(8,128)(2,1)} %subtract_convert_fusion.x_ref, f32[1,4096]{1,0:T(1,128)} %convert_element_type.350.dead_ref, bf16[256,4096]{1,0:T(8,128)(2,1)} %copy-done.2, ...), custom_call_target="tpu_custom_call" | custom-call | flops 6442450944 | bytes 25165824 | tf_op jit(solution)/shard_map/pallas_call | solution.py:396
  291.5 14.7 %collective-permute-done.21 = bf16[128,1536]{1,0:T(8,128)(2,1)S(1)} collective-permute-done((bf16[128,1536]{1,0:T(8,128)(2,1)S(1)}, bf16[128,1536]{1,0:T(8,128)(2,1)S(1)}, u32[]{:S(2)}, u32[]{:S(2)}) %collective-permute-start.21) | collective-permute-done | bytes 393248 | tf_op jit(solution)/shard_map/ppermute | solution.py:652
  306.2 12.4 %collective-permute-done.22 = bf16[128,1536]{1,0:T(8,128)(2,1)S(1)} collective-permute-done((bf16[128,1536]{1,0:T(8,128)(2,1)S(1)}, bf16[128,1536]{1,0:T(8,128)(2,1)S(1)}, u32[]{:S(2)}, u32[]{:S(2)}) %collective-permute-start.22) | collective-permute-done | bytes 393248 | tf_op jit(solution)/shard_map/ppermute | solution.py:652
  319.1 8.1 %collective-permute-start.24 = (bf16[128,1536]{1,0:T(8,128)(2,1)S(1)}, bf16[128,1536]{1,0:T(8,128)(2,1)S(1)}, u32[]{:S(2)}, u32[]{:S(2)}) collective-permute-start(bf16[128,1536]{1,0:T(8,128)(2,1)S(1)} %pad_maximum_fusion.21), channel_id=1, source_target_pairs={{0,1},{1,0},{2,3},{3,2},{4,5},{5,4},{6,7},{7,6},{8,9},{9,8},{10,11... | collective-permute-start | bytes 1179656 | tf_op jit(solution)/shard_map/ppermute | solution.py:652
  329.6 13.2 %collective-permute-done.24 = bf16[128,1536]{1,0:T(8,128)(2,1)S(1)} collective-permute-done((bf16[128,1536]{1,0:T(8,128)(2,1)S(1)}, bf16[128,1536]{1,0:T(8,128)(2,1)S(1)}, u32[]{:S(2)}, u32[]{:S(2)}) %collective-permute-start.24) | collective-permute-done | bytes 393248 | tf_op jit(solution)/shard_map/ppermute | solution.py:652
  342.9 14.1 %collective-permute-done.25 = bf16[128,1536]{1,0:T(8,128)(2,1)S(1)} collective-permute-done((bf16[128,1536]{1,0:T(8,128)(2,1)S(1)}, bf16[128,1536]{1,0:T(8,128)(2,1)S(1)}, u32[]{:S(2)}, u32[]{:S(2)}) %collective-permute-start.25) | collective-permute-done | bytes 393248 | tf_op jit(solution)/shard_map/ppermute | solution.py:652
  365.4 11.5 %shard_map.323 = (bf16[768,1024]{1,0:T(8,128)(2,1)}, bf16[768,1024]{1,0:T(8,128)(2,1)}) custom-call(bf16[1536,512]{1,0:T(8,128)(2,1)} %copy.153.near_r.near_a, bf16[1536,512]{1,0:T(8,128)(2,1)} %copy.153.near_r.near_a, bf16[1536,512]{1,0:T(8,128)(2,1)} %copy.155.far_r.far_a, bf16[1536,512]{1,0:T(8,128)(2,1)} %copy.155.far_r.far_a, ...), custom_call_target="tpu_custom_call" | custom-call | flops 100663296 | bytes 262144 | tf_op jit(solution)/shard_map/pallas_call | solution.py:462
  380.2 12.0 %shard_map.324 = (f32[768,1024]{1,0:T(8,128)}, f32[768,1024]{1,0:T(8,128)}) custom-call(bf16[1536,512]{1,0:T(8,128)(2,1)} %copy.153.near_r.near_a, bf16[1536,512]{1,0:T(8,128)(2,1)} %copy.153.near_r.near_a, bf16[1536,512]{1,0:T(8,128)(2,1)} %copy.155.far_r.far_a, bf16[1536,512]{1,0:T(8,128)(2,1)} %copy.155.far_r.far_a, ...), custom_call_target="tpu_custom_call" | custom-call | flops 100663296 | bytes 262144 | tf_op jit(solution)/shard_map/pallas_call | solution.py:462
  392.2 16.9 %shard_map.325 = (bf16[784,1024]{1,0:T(8,128)(2,1)}, bf16[784,1024]{1,0:T(8,128)(2,1)}) custom-call(bf16[768,1024]{1,0:T(8,128)(2,1)} %copy.157.x_ref, bf16[512,1536]{1,0:T(8,128)(2,1)} %copy-done.8, bf16[512,1536]{1,0:T(8,128)(2,1)} %copy-done.9, f32[1,4096]{1,0:T(1,128)} %convert_element_type.350.dead_ref, bf16[256,4096]{1,0:T(8,128)(2,1)} %copy-done.2, ...), custom_call_target="tpu_custom_call" | custom-call | flops 100663296 | bytes 262144 | tf_op jit(solution)/shard_map/pallas_call | solution.py:526
  432.4 17.7 %shard_map.326 = (f32[784,1024]{1,0:T(8,128)}, f32[784,1024]{1,0:T(8,128)}) custom-call(bf16[768,1024]{1,0:T(8,128)(2,1)} %copy.157.x_ref, bf16[512,1536]{1,0:T(8,128)(2,1)} %copy-done.8, bf16[512,1536]{1,0:T(8,128)(2,1)} %copy-done.9, f32[1,4096]{1,0:T(1,128)} %convert_element_type.350.dead_ref, bf16[256,4096]{1,0:T(8,128)(2,1)} %copy-done.2, ...), custom_call_target="tpu_custom_call" | custom-call | flops 100663296 | bytes 262144 | tf_op jit(solution)/shard_map/pallas_call | solution.py:526
  458.5 9.0 %all-to-all-start.3 = ((bf16[4,192,1024]{2,1,0:T(8,128)(2,1)}), bf16[4,192,1024]{2,1,0:T(8,128)(2,1)}, u32[]{:S(2)}, u32[]{:S(2)}) async-start(bf16[4,192,1024]{2,1,0:T(8,128)(2,1)} %bitcast.178), calls=%async_computation.3 | async-start | bytes 3145728 | tf_op jit(solution)/shard_map/all_to_all | solution.py:662
  471.0 8.1 %collective-permute-done.32 = bf16[784,1024]{1,0:T(8,128)(2,1)} collective-permute-done((bf16[784,1024]{1,0:T(8,128)(2,1)}, bf16[784,1024]{1,0:T(8,128)(2,1)}, u32[]{:S(2)}, u32[]{:S(2)}) %collective-permute-start.32) | collective-permute-done | bytes 1605664 | tf_op jit(solution)/shard_map/ppermute | solution.py:652
  537.1 11.8 %shard_map.327 = (bf16[768,768]{1,0:T(8,128)(2,1)S(1)}, bf16[768,768]{1,0:T(8,128)(2,1)S(1)}, bf16[768,768]{1,0:T(8,128)(2,1)S(1)}) custom-call(s32[3]{0:T(128)S(1)} %pad_add_fusion.2.place_ref, bf16[4,96,768]{2,1,0:T(8,128)(2,1)S(1)} %pad_maximum_fusion.19.near_ref, bf16[4,96,768]{2,1,0:T(8,128)(2,1)S(1)} %collective-permute-done.47.far_ref), custom_call_target="tpu_custom_call" | custom-call | flops 226492416 | bytes 294912 | tf_op jit(solution)/shard_map/pallas_call | solution.py:194
  552.9 9.8 %shard_map.328 = (bf16[768,768]{1,0:T(8,128)(2,1)S(1)}, bf16[768,768]{1,0:T(8,128)(2,1)S(1)}, bf16[768,768]{1,0:T(8,128)(2,1)S(1)}) custom-call(bf16[768,768]{1,0:T(8,128)(2,1)S(1)} %get-tuple-element.233.g_hi, bf16[768,768]{1,0:T(8,128)(2,1)S(1)} %get-tuple-element.234.g_lo, bf16[768,768]{1,0:T(8,128)(2,1)S(1)} %get-tuple-element.235.q_ref), custom_call_target="tpu_custom_call" | custom-call | flops 226492416 | bytes 294912 | tf_op jit(solution)/shard_map/pallas_call | solution.py:194
  571.4 9.9 %shard_map.329 = (bf16[768,768]{1,0:T(8,128)(2,1)S(1)}, bf16[768,768]{1,0:T(8,128)(2,1)S(1)}, bf16[768,768]{1,0:T(8,128)(2,1)S(1)}) custom-call(bf16[768,768]{1,0:T(8,128)(2,1)S(1)} %get-tuple-element.242.g_hi, bf16[768,768]{1,0:T(8,128)(2,1)S(1)} %get-tuple-element.243.g_lo, bf16[768,768]{1,0:T(8,128)(2,1)S(1)} %get-tuple-element.244.q_ref), custom_call_target="tpu_custom_call" | custom-call | flops 226492416 | bytes 294912 | tf_op jit(solution)/shard_map/pallas_call | solution.py:194
  585.5 9.6 %collective-permute-done.52 = bf16[112,768]{1,0:T(8,128)(2,1)S(1)} collective-permute-done((bf16[112,768]{1,0:T(8,128)(2,1)S(1)}, bf16[112,768]{1,0:T(8,128)(2,1)S(1)}, u32[]{:S(2)}, u32[]{:S(2)}) %collective-permute-start.52) | collective-permute-done | bytes 172064 | tf_op jit(solution)/shard_map/ppermute | solution.py:652
  598.9 11.8 %shard_map.330 = (bf16[768,768]{1,0:T(8,128)(2,1)S(1)}, bf16[768,768]{1,0:T(8,128)(2,1)S(1)}, bf16[768,768]{1,0:T(8,128)(2,1)S(1)}) custom-call(bf16[768,768]{1,0:T(8,128)(2,1)S(1)} %get-tuple-element.251.g_hi, bf16[768,768]{1,0:T(8,128)(2,1)S(1)} %get-tuple-element.252.g_lo, bf16[768,768]{1,0:T(8,128)(2,1)S(1)} %get-tuple-element.253.q_ref), custom_call_target="tpu_custom_call" | custom-call | flops 283115520 | bytes 294912 | tf_op jit(solution)/shard_map/pallas_call | solution.py:194
  618.5 13.3 %all-to-all-start.4 = ((bf16[4,192,1024]{2,1,0:T(8,128)(2,1)}), bf16[4,192,1024]{2,1,0:T(8,128)(2,1)}, u32[]{:S(2)}, u32[]{:S(2)}) async-start(bf16[4,192,1024]{2,1,0:T(8,128)(2,1)} %bitcast.187), calls=%async_computation.4 | async-start | bytes 3145728 | tf_op jit(solution)/shard_map/all_to_all | solution.py:662
  638.0 11.3 %shard_map.332 = (bf16[768,768]{1,0:T(8,128)(2,1)S(1)}, bf16[768,768]{1,0:T(8,128)(2,1)S(1)}, bf16[768,768]{1,0:T(8,128)(2,1)S(1)}) custom-call(s32[3]{0:T(128)S(1)} %pad_add_fusion.2.place_ref, bf16[4,96,768]{2,1,0:T(8,128)(2,1)S(1)} %pad_maximum_fusion.20.near_ref, bf16[4,96,768]{2,1,0:T(8,128)(2,1)S(1)} %collective-permute-done.57.far_ref), custom_call_target="tpu_custom_call" | custom-call | flops 226492416 | bytes 294912 | tf_op jit(solution)/shard_map/pallas_call | solution.py:194
  649.3 9.8 %shard_map.333 = (bf16[768,768]{1,0:T(8,128)(2,1)S(1)}, bf16[768,768]{1,0:T(8,128)(2,1)S(1)}, bf16[768,768]{1,0:T(8,128)(2,1)S(1)}) custom-call(bf16[768,768]{1,0:T(8,128)(2,1)S(1)} %get-tuple-element.264.g_hi, bf16[768,768]{1,0:T(8,128)(2,1)S(1)} %get-tuple-element.265.g_lo, bf16[768,768]{1,0:T(8,128)(2,1)S(1)} %get-tuple-element.266.q_ref), custom_call_target="tpu_custom_call" | custom-call | flops 226492416 | bytes 294912 | tf_op jit(solution)/shard_map/pallas_call | solution.py:194
  659.1 9.8 %shard_map.334 = (bf16[768,768]{1,0:T(8,128)(2,1)S(1)}, bf16[768,768]{1,0:T(8,128)(2,1)S(1)}, bf16[768,768]{1,0:T(8,128)(2,1)S(1)}) custom-call(bf16[768,768]{1,0:T(8,128)(2,1)S(1)} %get-tuple-element.267.g_hi, bf16[768,768]{1,0:T(8,128)(2,1)S(1)} %get-tuple-element.268.g_lo, bf16[768,768]{1,0:T(8,128)(2,1)S(1)} %get-tuple-element.269.q_ref), custom_call_target="tpu_custom_call" | custom-call | flops 226492416 | bytes 294912 | tf_op jit(solution)/shard_map/pallas_call | solution.py:194
  669.0 11.7 %shard_map.335 = (bf16[768,768]{1,0:T(8,128)(2,1)S(1)}, bf16[768,768]{1,0:T(8,128)(2,1)S(1)}, bf16[768,768]{1,0:T(8,128)(2,1)S(1)}) custom-call(bf16[768,768]{1,0:T(8,128)(2,1)S(1)} %get-tuple-element.270.g_hi, bf16[768,768]{1,0:T(8,128)(2,1)S(1)} %get-tuple-element.271.g_lo, bf16[768,768]{1,0:T(8,128)(2,1)S(1)} %get-tuple-element.272.q_ref), custom_call_target="tpu_custom_call" | custom-call | flops 283115520 | bytes 294912 | tf_op jit(solution)/shard_map/pallas_call | solution.py:194
  693.8 8.7 %shard_map.337 = (f32[192,4096]{1,0:T(8,128)}, f32[192,4096]{1,0:T(8,128)}, bf16[192,4096]{1,0:T(8,128)(2,1)}) custom-call(s32[3]{0:T(128)} %copy-done.7, bf16[768,768]{1,0:T(8,128)(2,1)} %copy-done.6, bf16[4,768,1024]{2,1,0:T(8,128)(2,1)} %bitcast.181, f32[192,4096]{1,0:T(8,128)} %weight_ref.1), custom_call_target="tpu_custom_call" | custom-call | flops 1207959552 | bytes 6291456 | tf_op jit(solution)/shard_map/pallas_call | solution.py:568
  (436 shorter events, 291.7 us)
Async XLA Ops:
  10.6 45.1 %collective-permute-start = (s32[128,544]{1,0:T(8,128)}, s32[128,544]{1,0:T(8,128)}, u32[]{:S(2)}, u32[]{:S(2)}) collective-permute-start(s32[128,544]{1,0:T(8,128)} %pad_add_fusion.1), channel_id=1, source_target_pairs={{0,1},{1,0},{2,3},{3,2},{4,5},{5,4},{6,7},{7,6},{8,9},{9,8},{10,11... | collective-permute-start | bytes 835592 | tf_op jit(solution)/shard_map/ppermute | solution.py:652
  13.6 48.7 %collective-permute-start.1 = (s32[128,544]{1,0:T(8,128)}, s32[128,544]{1,0:T(8,128)}, u32[]{:S(2)}, u32[]{:S(2)}) collective-permute-start(s32[128,544]{1,0:T(8,128)} %pad_add_fusion.1), channel_id=1, source_target_pairs={{0,2},{1,3},{2,0},{3,1},{4,6},{5,7},{6,4},{7,5},{8,10},{9,11},{10,... | collective-permute-start | bytes 835592 | tf_op jit(solution)/shard_map/ppermute | solution.py:652
  16.2 46.1 %collective-permute-start.2 = (s32[128,544]{1,0:T(8,128)}, s32[128,544]{1,0:T(8,128)}, u32[]{:S(2)}, u32[]{:S(2)}) collective-permute-start(s32[128,544]{1,0:T(8,128)} %pad_add_fusion.1), channel_id=1, source_target_pairs={{0,3},{1,2},{2,1},{3,0},{4,7},{5,6},{6,5},{7,4},{8,11},{9,10},{10,... | collective-permute-start | bytes 835592 | tf_op jit(solution)/shard_map/ppermute | solution.py:652
  41.0 42.3 %all-to-all-start = ((bf16[192,4,1024]{2,0,1:T(8,128)(2,1)}), bf16[192,4,1024]{2,0,1:T(8,128)(2,1)}, u32[]{:S(2)}, u32[]{:S(2)}) async-start(bf16[192,4,1024]{2,0,1:T(8,128)(2,1)} %bitcast.176), calls=%async_computation | async-start | bytes 3145728 | tf_op jit(solution)/shard_map/all_to_all | solution.py:659
  86.4 23.7 %collective-permute-start.7 = (bf16[784,512]{1,0:T(8,128)(2,1)}, bf16[784,512]{1,0:T(8,128)(2,1)}, u32[]{:S(2)}, u32[]{:S(2)}) collective-permute-start(bf16[784,512]{1,0:T(8,128)(2,1)} %get-tuple-element.323), channel_id=1, source_target_pairs={{0,8},{8,0},{16,24},{24,16},{1,9},{9,1},{17,25},{25,17},{2,10},{10... | collective-permute-start | bytes 2408456 | tf_op jit(solution)/shard_map/ppermute | solution.py:652
  87.7 22.3 %collective-permute-start.8 = (bf16[784,512]{1,0:T(8,128)(2,1)}, bf16[784,512]{1,0:T(8,128)(2,1)}, u32[]{:S(2)}, u32[]{:S(2)}) collective-permute-start(bf16[784,512]{1,0:T(8,128)(2,1)} %get-tuple-element.322), channel_id=1, source_target_pairs={{0,16},{8,24},{16,0},{24,8},{1,17},{9,25},{17,1},{25,9},{2,18},{10... | collective-permute-start | bytes 2408456 | tf_op jit(solution)/shard_map/ppermute | solution.py:652
  89.6 40.5 %all-to-all-start.1 = ((bf16[192,4,1024]{2,0,1:T(8,128)(2,1)}), bf16[192,4,1024]{2,0,1:T(8,128)(2,1)}, u32[]{:S(2)}, u32[]{:S(2)}) async-start(bf16[192,4,1024]{2,0,1:T(8,128)(2,1)} %bitcast.177), calls=%async_computation.1 | async-start | bytes 3145728 | tf_op jit(solution)/shard_map/all_to_all | solution.py:659
  131.7 36.1 %collective-permute-start.13 = (bf16[784,1024]{1,0:T(8,128)(2,1)S(1)}, bf16[784,1024]{1,0:T(8,128)(2,1)S(1)}, u32[]{:S(2)}, u32[]{:S(2)}) collective-permute-start(bf16[784,1024]{1,0:T(8,128)(2,1)S(1)} %pad_maximum_fusion.4.refs_6_), channel_id=1, source_target_pairs={{0,8},{8,0},{16,24},{24,16},{1,9},{9,1},{17,25},{25,17},{2,10},{10... | collective-permute-start | bytes 4816904 | tf_op jit(solution)/shard_map/ppermute | solution.py:652
  134.9 36.2 %collective-permute-start.12 = (bf16[784,1024]{1,0:T(8,128)(2,1)S(1)}, bf16[784,1024]{1,0:T(8,128)(2,1)}, u32[]{:S(2)}, u32[]{:S(2)}) collective-permute-start(bf16[784,1024]{1,0:T(8,128)(2,1)S(1)} %pad_maximum_fusion.3.refs_4_), channel_id=1, source_target_pairs={{0,16},{8,24},{16,0},{24,8},{1,17},{9,25},{17,1},{25,9},{2,18},{10... | collective-permute-start | bytes 4816904 | tf_op jit(solution)/shard_map/ppermute | solution.py:652
  175.7 101.8 %all-to-all-start.2 = ((bf16[384,4,1024]{0,2,1:T(8,128)(2,1)}), bf16[384,4,1024]{0,2,1:T(8,128)(2,1)}, u32[]{:S(2)}, u32[]{:S(2)}) async-start(bf16[384,4,1024]{0,2,1:T(8,128)(2,1)} %bitcast.39), calls=%async_computation.2 | async-start | bytes 6291456 | tf_op jit(solution)/shard_map/all_to_all | solution.py:659
  186.8 24.1 %collective-permute-start.15 = (s32[512,544]{0,1:T(8,128)}, s32[512,544]{0,1:T(8,128)}, u32[]{:S(2)}, u32[]{:S(2)}) collective-permute-start(s32[512,544]{0,1:T(8,128)} %copy.144), channel_id=1, source_target_pairs={{0,4},{4,0},{1,5},{5,1},{2,6},{6,2},{3,7},{7,3},{8,12},{12,8},{9,1... | collective-permute-start | bytes 3342344 | tf_op jit(solution)/shard_map/ppermute | solution.py:652
  204.2 41.8 %collective-permute-start.19 = (bf16[768,1024]{1,0:T(8,128)(2,1)}, bf16[768,1024]{1,0:T(8,128)(2,1)}, u32[]{:S(2)}, u32[]{:S(2)}) collective-permute-start(bf16[768,1024]{1,0:T(8,128)(2,1)} %pad_maximum_fusion.6.refs_10_.refs_5_), channel_id=1, source_target_pairs={{0,8},{8,0},{16,24},{24,16},{1,9},{9,1},{17,25},{25,17},{2,10},{10... | collective-permute-start | bytes 4718600 | tf_op jit(solution)/shard_map/ppermute | solution.py:652
  208.3 37.7 %collective-permute-start.18 = (bf16[768,1024]{1,0:T(8,128)(2,1)}, bf16[768,1024]{1,0:T(8,128)(2,1)}, u32[]{:S(2)}, u32[]{:S(2)}) collective-permute-start(bf16[768,1024]{1,0:T(8,128)(2,1)} %pad_maximum_fusion.5.refs_8_.refs_4_), channel_id=1, source_target_pairs={{0,16},{8,24},{16,0},{24,8},{1,17},{9,25},{17,1},{25,9},{2,18},{10... | collective-permute-start | bytes 4718600 | tf_op jit(solution)/shard_map/ppermute | solution.py:652
  288.8 29.8 %collective-permute-start.22 = (bf16[128,1536]{1,0:T(8,128)(2,1)S(1)}, bf16[128,1536]{1,0:T(8,128)(2,1)S(1)}, u32[]{:S(2)}, u32[]{:S(2)}) collective-permute-start(bf16[128,1536]{1,0:T(8,128)(2,1)S(1)} %get-tuple-element.326), channel_id=1, source_target_pairs={{0,2},{1,3},{2,0},{3,1},{4,6},{5,7},{6,4},{7,5},{8,10},{9,11},{10,... | collective-permute-start | bytes 1179656 | tf_op jit(solution)/shard_map/ppermute | solution.py:652
  291.2 27.4 %collective-permute-start.23 = (bf16[128,1536]{1,0:T(8,128)(2,1)S(1)}, bf16[128,1536]{1,0:T(8,128)(2,1)S(1)}, u32[]{:S(2)}, u32[]{:S(2)}) collective-permute-start(bf16[128,1536]{1,0:T(8,128)(2,1)S(1)} %get-tuple-element.325), channel_id=1, source_target_pairs={{0,3},{1,2},{2,1},{3,0},{4,7},{5,6},{6,5},{7,4},{8,11},{9,10},{10,... | collective-permute-start | bytes 1179656 | tf_op jit(solution)/shard_map/ppermute | solution.py:652
  319.1 23.8 %collective-permute-start.24 = (bf16[128,1536]{1,0:T(8,128)(2,1)S(1)}, bf16[128,1536]{1,0:T(8,128)(2,1)S(1)}, u32[]{:S(2)}, u32[]{:S(2)}) collective-permute-start(bf16[128,1536]{1,0:T(8,128)(2,1)S(1)} %pad_maximum_fusion.21), channel_id=1, source_target_pairs={{0,1},{1,0},{2,3},{3,2},{4,5},{5,4},{6,7},{7,6},{8,9},{9,8},{10,11... | collective-permute-start | bytes 1179656 | tf_op jit(solution)/shard_map/ppermute | solution.py:652
  327.2 29.8 %collective-permute-start.25 = (bf16[128,1536]{1,0:T(8,128)(2,1)S(1)}, bf16[128,1536]{1,0:T(8,128)(2,1)S(1)}, u32[]{:S(2)}, u32[]{:S(2)}) collective-permute-start(bf16[128,1536]{1,0:T(8,128)(2,1)S(1)} %pad_maximum_fusion.21), channel_id=1, source_target_pairs={{0,2},{1,3},{2,0},{3,1},{4,6},{5,7},{6,4},{7,5},{8,10},{9,11},{10,... | collective-permute-start | bytes 1179656 | tf_op jit(solution)/shard_map/ppermute | solution.py:652
  328.2 28.8 %collective-permute-start.26 = (bf16[128,1536]{1,0:T(8,128)(2,1)S(1)}, bf16[128,1536]{1,0:T(8,128)(2,1)S(1)}, u32[]{:S(2)}, u32[]{:S(2)}) collective-permute-start(bf16[128,1536]{1,0:T(8,128)(2,1)S(1)} %pad_maximum_fusion.21), channel_id=1, source_target_pairs={{0,3},{1,2},{2,1},{3,0},{4,7},{5,6},{6,5},{7,4},{8,11},{9,10},{10,... | collective-permute-start | bytes 1179656 | tf_op jit(solution)/shard_map/ppermute | solution.py:652
  376.8 36.6 %collective-permute-start.28 = (bf16[768,1024]{1,0:T(8,128)(2,1)}, bf16[768,1024]{1,0:T(8,128)(2,1)S(1)}, u32[]{:S(2)}, u32[]{:S(2)}) collective-permute-start(bf16[768,1024]{1,0:T(8,128)(2,1)} %get-tuple-element.199), channel_id=1, source_target_pairs={{0,16},{8,24},{16,0},{24,8},{1,17},{9,25},{17,1},{25,9},{2,18},{10... | collective-permute-start | bytes 4718600 | tf_op jit(solution)/shard_map/ppermute | solution.py:652
  377.9 36.7 %collective-permute-start.29 = (bf16[768,1024]{1,0:T(8,128)(2,1)}, bf16[768,1024]{1,0:T(8,128)(2,1)}, u32[]{:S(2)}, u32[]{:S(2)}) collective-permute-start(bf16[768,1024]{1,0:T(8,128)(2,1)} %get-tuple-element.200), channel_id=1, source_target_pairs={{0,8},{8,0},{16,24},{24,16},{1,9},{9,1},{17,25},{25,17},{2,10},{10... | collective-permute-start | bytes 4718600 | tf_op jit(solution)/shard_map/ppermute | solution.py:652
  419.6 30.5 %collective-permute-start.30 = (bf16[768,512]{1,0:T(8,128)(2,1)}, bf16[768,512]{1,0:T(8,128)(2,1)}, u32[]{:S(2)}, u32[]{:S(2)}) collective-permute-start(bf16[768,512]{1,0:T(8,128)(2,1)} %split.41), channel_id=1, source_target_pairs={{0,8},{8,0},{16,24},{24,16},{1,9},{9,1},{17,25},{25,17},{2,10},{10... | collective-permute-start | bytes 2359304 | tf_op jit(solution)/shard_map/ppermute | solution.py:652
  425.8 26.3 %collective-permute-start.31 = (bf16[768,512]{1,0:T(8,128)(2,1)}, bf16[768,512]{1,0:T(8,128)(2,1)}, u32[]{:S(2)}, u32[]{:S(2)}) collective-permute-start(bf16[768,512]{1,0:T(8,128)(2,1)} %split.40), channel_id=1, source_target_pairs={{0,16},{8,24},{16,0},{24,8},{1,17},{9,25},{17,1},{25,9},{2,18},{10... | collective-permute-start | bytes 2359304 | tf_op jit(solution)/shard_map/ppermute | solution.py:652
  426.6 52.5 %collective-permute-start.32 = (bf16[784,1024]{1,0:T(8,128)(2,1)}, bf16[784,1024]{1,0:T(8,128)(2,1)}, u32[]{:S(2)}, u32[]{:S(2)}) collective-permute-start(bf16[784,1024]{1,0:T(8,128)(2,1)} %get-tuple-element.211), channel_id=1, source_target_pairs={{0,16},{8,24},{16,0},{24,8},{1,17},{9,25},{17,1},{25,9},{2,18},{10... | collective-permute-start | bytes 4816904 | tf_op jit(solution)/shard_map/ppermute | solution.py:652
  428.0 51.1 %collective-permute-start.33 = (bf16[784,1024]{1,0:T(8,128)(2,1)}, bf16[784,1024]{1,0:T(8,128)(2,1)}, u32[]{:S(2)}, u32[]{:S(2)}) collective-permute-start(bf16[784,1024]{1,0:T(8,128)(2,1)} %get-tuple-element.212), channel_id=1, source_target_pairs={{0,8},{8,0},{16,24},{24,16},{1,9},{9,1},{17,25},{25,17},{2,10},{10... | collective-permute-start | bytes 4816904 | tf_op jit(solution)/shard_map/ppermute | solution.py:652
  458.5 56.1 %all-to-all-start.3 = ((bf16[4,192,1024]{2,1,0:T(8,128)(2,1)}), bf16[4,192,1024]{2,1,0:T(8,128)(2,1)}, u32[]{:S(2)}, u32[]{:S(2)}) async-start(bf16[4,192,1024]{2,1,0:T(8,128)(2,1)} %bitcast.178), calls=%async_computation.3 | async-start | bytes 3145728 | tf_op jit(solution)/shard_map/all_to_all | solution.py:662
  467.5 226.2 %all-gather.5.cloned.1.call-start = ((), (), s32[]{:S(2)}) async-start(), calls=%async_computation.5 | async-start | bytes 7864320 | tf_op jit(solution)/shard_map/all_gather | solution.py:901
  488.4 23.9 %collective-permute-start.41 = (bf16[784,512]{1,0:T(8,128)(2,1)S(1)}, bf16[784,512]{1,0:T(8,128)(2,1)S(1)}, u32[]{:S(2)}, u32[]{:S(2)}) collective-permute-start(bf16[784,512]{1,0:T(8,128)(2,1)S(1)} %get-tuple-element.356), channel_id=1, source_target_pairs={{0,8},{8,0},{16,24},{24,16},{1,9},{9,1},{17,25},{25,17},{2,10},{10... | collective-permute-start | bytes 2408456 | tf_op jit(solution)/shard_map/ppermute | solution.py:652
  489.2 23.5 %collective-permute-start.42 = (bf16[784,512]{1,0:T(8,128)(2,1)S(1)}, bf16[784,512]{1,0:T(8,128)(2,1)S(1)}, u32[]{:S(2)}, u32[]{:S(2)}) collective-permute-start(bf16[784,512]{1,0:T(8,128)(2,1)S(1)} %get-tuple-element.357), channel_id=1, source_target_pairs={{0,16},{8,24},{16,0},{24,8},{1,17},{9,25},{17,1},{25,9},{2,18},{10... | collective-permute-start | bytes 2408456 | tf_op jit(solution)/shard_map/ppermute | solution.py:652
  563.0 22.5 %collective-permute-start.51 = (bf16[112,768]{1,0:T(8,128)(2,1)S(1)}, bf16[112,768]{1,0:T(8,128)(2,1)S(1)}, u32[]{:S(2)}, u32[]{:S(2)}) collective-permute-start(bf16[112,768]{1,0:T(8,128)(2,1)S(1)} %pad_maximum_fusion.11), channel_id=1, source_target_pairs={{0,1},{1,0},{2,3},{3,2},{4,5},{5,4},{6,7},{7,6},{8,9},{9,8},{10,11... | collective-permute-start | bytes 516104 | tf_op jit(solution)/shard_map/ppermute | solution.py:652
  568.9 26.2 %collective-permute-start.52 = (bf16[112,768]{1,0:T(8,128)(2,1)S(1)}, bf16[112,768]{1,0:T(8,128)(2,1)S(1)}, u32[]{:S(2)}, u32[]{:S(2)}) collective-permute-start(bf16[112,768]{1,0:T(8,128)(2,1)S(1)} %pad_maximum_fusion.11), channel_id=1, source_target_pairs={{0,2},{1,3},{2,0},{3,1},{4,6},{5,7},{6,4},{7,5},{8,10},{9,11},{10,... | collective-permute-start | bytes 516104 | tf_op jit(solution)/shard_map/ppermute | solution.py:652
  569.9 25.2 %collective-permute-start.53 = (bf16[112,768]{1,0:T(8,128)(2,1)S(1)}, bf16[112,768]{1,0:T(8,128)(2,1)S(1)}, u32[]{:S(2)}, u32[]{:S(2)}) collective-permute-start(bf16[112,768]{1,0:T(8,128)(2,1)S(1)} %pad_maximum_fusion.11), channel_id=1, source_target_pairs={{0,3},{1,2},{2,1},{3,0},{4,7},{5,6},{6,5},{7,4},{8,11},{9,10},{10,... | collective-permute-start | bytes 516104 | tf_op jit(solution)/shard_map/ppermute | solution.py:652
  618.5 68.7 %all-to-all-start.4 = ((bf16[4,192,1024]{2,1,0:T(8,128)(2,1)}), bf16[4,192,1024]{2,1,0:T(8,128)(2,1)}, u32[]{:S(2)}, u32[]{:S(2)}) async-start(bf16[4,192,1024]{2,1,0:T(8,128)(2,1)} %bitcast.187), calls=%async_computation.4 | async-start | bytes 3145728 | tf_op jit(solution)/shard_map/all_to_all | solution.py:662
  (96 other events, 1380.8 us)
Sparse Core Ops, SparseCore 0:
  521.7 160.9 all-gather.4

commit v9 on v8

--- a/solution.py
+++ b/solution.py
@@ -782,7 +782,6 @@
     all_inputs = jnp.concatenate([near_inputs, far_inputs], 0)
     encoder_in = (all_inputs.astype(f32) - decoder_bias).astype(bf16)
     top_acts, aux_acts, far, near = forward(encoder_in, codes, dead_here, enc_parts, dec_parts)
-    far, moments = tie(far, moments)
     encoder_t = encoder_in.T
     far_got, encoder_t = tie(swap(far, "core", 1), encoder_t)
     rebuilt = near + far_got.astype(f32)
@@ -804,6 +803,7 @@
     back_recon = 2.0 / model_width * counted[:, None] * (reconstructed_input - target)
     back_aux = 2.0 * AUX_COEF / model_width * counted[:, None] * aux_gap
     back_rows = jnp.concatenate([back_recon, back_aux], 1).astype(bf16)
+    back_rows, moments = tie(back_rows, moments)
     near_back = spread_narrow(back_rows)
     far_back = swap(near_back, "core", 1)
     near_t, far_back = tie(near_back.T, far_back)

time: 716 us -> 712 us (level)
    all_to_all x3, waiting for transfers between devices: 36.7 us -> 21.5 us  [rows_to_latents(): lax.all_to_all(value, 'narrow', split_axis=1, concat_axis=0, tiled=True)]
    ppermute x58, waiting for transfers between devices: 121 us -> 129 us  [swap(): lax.ppermute(value, axis, [(spot, spot ^ offset) for spot in range(count)])]
    unnamed x147 -> x156, local copies, waits for them, and re-layouts: 18.9 us -> 20.4 us
  transfers between devices with their start and end apart: 64 -> 64, of which waited for: 26 -> 30; matrix products, arithmetic and copies ran while one was open for 18% -> 19% of each run, Pallas kernels for 31% -> 31%
where the time goes in v9:
time: 712 us; the launch traced here: 705 us
  Pallas kernels  240 us (34%)
  waiting for transfers between devices  151 us (21%)
  starting transfers between devices  112 us (16%)
  other arithmetic  80.4 us (11%)
  local copies, waits for them, and re-layouts  72 us (10%)
  matrix products  24.8 us (3%)
  between operations  16.5 us (2%)
  blocking collectives  8.74 us (1%)
    ppermute x58, waiting for transfers between devices, swap(): lax.ppermute(value, axis, [(spot, spot ^ offset) for spot in range(count)])  129 us
    pallas_call x10, Pallas kernels, square_call(): pl.pallas_call(kernel, out_shape=[square] * outs, in_specs=specs, out_spe...  96.1 us
    ppermute x58, starting transfers between devices, swap(): lax.ppermute(value, axis, [(spot, spot ^ offset) for spot in range(count)])  74.7 us
    pallas_call x4, Pallas kernels, kind_codes(): pl.pallas_call(functools.partial(code_kernel, shifts), grid=(row_total //...  45.5 us
    pallas_call x2, Pallas kernels, enc_grads(): pl.pallas_call(functools.partial(enc_grad_kernel, count), grid=(2 * count...  34.4 us
    pallas_call x1, Pallas kernels, forward(): pl.pallas_call(functools.partial(forward_kernel, count), grid=(4 * count,...  31.4 us
    pallas_call x2, Pallas kernels, dec_grads(): pl.pallas_call(functools.partial(dec_grad_kernel, count), grid=(2 * count...  23.8 us
    all_to_all x2, starting transfers between devices, rows_of(): lax.all_to_all(value, 'narrow', split_axis=0, concat_axis=1, tiled=True)  22.8 us
  transfers between devices with their start and end apart: 64, of which 30 were waited for; matrix products, arithmetic and copies ran while one was open for 19% of the time, Pallas kernels for 31%

profile of v9, /device:TPU:0, one launch (start us, length us, event | category | flops | bytes accessed | tf_op | source)
XLA Modules:
  0.0 705.2 jit_solution(15170183850633683686)
XLA Ops:
  24.8 8.7 %all-gather.2 = s32[8,1,128]{2,1,0:T(1,128)S(1)} all-gather(s32[1,1,128]{2,1,0:T(1,128)S(1)} %bitcast.211), channel_id=2, replica_groups=mesh['chip'=4,'core'=2,'narrow'=4] {'chip','core'}, dimensions={0}, use_global_device_ids=true | all-gather | bytes 4608 | tf_op jit(solution)/shard_map/all_gather | solution.py:701
  33.8 10.6 %gather_fusion = bf16[1024,768]{1,0:T(8,128)(2,1)} fusion(bf16[6288,768]{1,0:T(8,128)(2,1)} %param.28, s32[1024]{0:T(1024)S(1)} %broadcast_clamp_fusion), kind=kCustom, calls=%fused_computation | custom fusion | bytes 3149824 | tf_op jit(solution)/shard_map/jit(_take)/gather | solution.py:711
  69.1 8.5 %all-to-all-done = bf16[192,4,1024]{2,0,1:T(8,128)(2,1)} async-done(((bf16[192,4,1024]{2,0,1:T(8,128)(2,1)}), bf16[192,4,1024]{2,0,1:T(8,128)(2,1)}, u32[]{:S(2)}, u32[]{:S(2)}) %all-to-all-start) | async-done | bytes 1572896 | tf_op jit(solution)/shard_map/all_to_all | solution.py:659
  114.9 13.0 %all-to-all-done.1 = bf16[192,4,1024]{2,0,1:T(8,128)(2,1)S(1)} async-done(((bf16[192,4,1024]{2,0,1:T(8,128)(2,1)}), bf16[192,4,1024]{2,0,1:T(8,128)(2,1)S(1)}, u32[]{:S(2)}, u32[]{:S(2)}) %all-to-all-start.1) | async-done | bytes 1572896 | tf_op jit(solution)/shard_map/all_to_all | solution.py:659
  146.2 7.3 %collective-permute-done.10 = bf16[128,768]{1,0:T(8,128)(2,1)S(1)} collective-permute-done((bf16[128,768]{1,0:T(8,128)(2,1)S(1)}, bf16[128,768]{1,0:T(8,128)(2,1)S(1)}, u32[]{:S(2)}, u32[]{:S(2)}) %collective-permute-start.10) | collective-permute-done | bytes 196640 | tf_op jit(solution)/shard_map/ppermute | solution.py:652
  159.9 11.4 %shard_map.318.refs_0_ = bf16[256,4096]{1,0:T(8,128)(2,1)S(1)} custom-call(s32[3]{0:T(128)S(1)} %pad_add_fusion.2.place_ref, s32[256,544]{1,0:T(8,128)S(1)} %slice.323.ids_ref), custom_call_target="tpu_custom_call" | custom-call | flops 1048576 | bytes 139264 | tf_op jit(solution)/shard_map/pallas_call | solution.py:290
  174.0 11.4 %shard_map.319.refs_1_ = bf16[256,4096]{1,0:T(8,128)(2,1)S(1)} custom-call(s32[3]{0:T(128)S(1)} %pad_add_fusion.2.place_ref, s32[256,544]{1,0:T(8,128)S(1)} %slice.326.ids_ref), custom_call_target="tpu_custom_call" | custom-call | flops 1048576 | bytes 139264 | tf_op jit(solution)/shard_map/pallas_call | solution.py:290
  212.1 11.4 %shard_map.320.refs_2_ = bf16[256,4096]{1,0:T(8,128)(2,1)S(1)} custom-call(s32[3]{0:T(128)S(1)} %pad_add_fusion.2.place_ref, s32[256,544]{1,0:T(8,128)S(1)} %slice.410.ids_ref), custom_call_target="tpu_custom_call" | custom-call | flops 1048576 | bytes 139264 | tf_op jit(solution)/shard_map/pallas_call | solution.py:290
  229.5 11.4 %shard_map.321.refs_3_ = bf16[256,4096]{1,0:T(8,128)(2,1)S(1)} custom-call(s32[3]{0:T(128)S(1)} %pad_add_fusion.2.place_ref, s32[256,544]{1,0:T(8,128)S(1)} %slice.411.ids_ref), custom_call_target="tpu_custom_call" | custom-call | flops 1048576 | bytes 139264 | tf_op jit(solution)/shard_map/pallas_call | solution.py:290
  246.4 31.4 %shard_map.322 = (bf16[1024,4096]{1,0:T(8,128)(2,1)}, bf16[1024,4096]{1,0:T(8,128)(2,1)}, bf16[512,1536]{1,0:T(8,128)(2,1)}, f32[512,1536]{1,0:T(8,128)}) custom-call(bf16[1024,768]{1,0:T(8,128)(2,1)} %subtract_convert_fusion.x_ref, f32[1,4096]{1,0:T(1,128)} %convert_element_type.350.dead_ref, bf16[256,4096]{1,0:T(8,128)(2,1)} %copy-done.2, ...), custom_call_target="tpu_custom_call" | custom-call | flops 6442450944 | bytes 25165824 | tf_op jit(solution)/shard_map/pallas_call | solution.py:396
  286.8 9.5 %collective-permute-done.23 = bf16[128,1536]{1,0:T(8,128)(2,1)S(1)} collective-permute-done((bf16[128,1536]{1,0:T(8,128)(2,1)S(1)}, bf16[128,1536]{1,0:T(8,128)(2,1)S(1)}, u32[]{:S(2)}, u32[]{:S(2)}) %collective-permute-start.23) | collective-permute-done | bytes 393248 | tf_op jit(solution)/shard_map/ppermute | solution.py:652
  296.3 23.9 %collective-permute-done.22 = bf16[128,1536]{1,0:T(8,128)(2,1)S(1)} collective-permute-done((bf16[128,1536]{1,0:T(8,128)(2,1)S(1)}, bf16[128,1536]{1,0:T(8,128)(2,1)S(1)}, u32[]{:S(2)}, u32[]{:S(2)}) %collective-permute-start.22) | collective-permute-done | bytes 393248 | tf_op jit(solution)/shard_map/ppermute | solution.py:652
  329.9 13.5 %collective-permute-done.24 = bf16[128,1536]{1,0:T(8,128)(2,1)S(1)} collective-permute-done((bf16[128,1536]{1,0:T(8,128)(2,1)S(1)}, bf16[128,1536]{1,0:T(8,128)(2,1)S(1)}, u32[]{:S(2)}, u32[]{:S(2)}) %collective-permute-start.24) | collective-permute-done | bytes 393248 | tf_op jit(solution)/shard_map/ppermute | solution.py:652
  343.5 11.8 %collective-permute-done.25 = bf16[128,1536]{1,0:T(8,128)(2,1)S(1)} collective-permute-done((bf16[128,1536]{1,0:T(8,128)(2,1)S(1)}, bf16[128,1536]{1,0:T(8,128)(2,1)S(1)}, u32[]{:S(2)}, u32[]{:S(2)}) %collective-permute-start.25) | collective-permute-done | bytes 393248 | tf_op jit(solution)/shard_map/ppermute | solution.py:652
  362.1 11.9 %shard_map.323 = (bf16[768,1024]{1,0:T(8,128)(2,1)}, bf16[768,1024]{1,0:T(8,128)(2,1)}) custom-call(bf16[1536,512]{1,0:T(8,128)(2,1)} %copy.153.near_r.near_a, bf16[1536,512]{1,0:T(8,128)(2,1)} %copy.153.near_r.near_a, bf16[1536,512]{1,0:T(8,128)(2,1)} %copy.155.far_r.far_a, bf16[1536,512]{1,0:T(8,128)(2,1)} %copy.155.far_r.far_a, ...), custom_call_target="tpu_custom_call" | custom-call | flops 100663296 | bytes 262144 | tf_op jit(solution)/shard_map/pallas_call | solution.py:462
  377.6 12.0 %shard_map.324 = (f32[768,1024]{1,0:T(8,128)}, f32[768,1024]{1,0:T(8,128)}) custom-call(bf16[1536,512]{1,0:T(8,128)(2,1)} %copy.153.near_r.near_a, bf16[1536,512]{1,0:T(8,128)(2,1)} %copy.153.near_r.near_a, bf16[1536,512]{1,0:T(8,128)(2,1)} %copy.155.far_r.far_a, bf16[1536,512]{1,0:T(8,128)(2,1)} %copy.155.far_r.far_a, ...), custom_call_target="tpu_custom_call" | custom-call | flops 100663296 | bytes 262144 | tf_op jit(solution)/shard_map/pallas_call | solution.py:462
  389.6 16.9 %shard_map.325 = (bf16[784,1024]{1,0:T(8,128)(2,1)}, bf16[784,1024]{1,0:T(8,128)(2,1)}) custom-call(bf16[768,1024]{1,0:T(8,128)(2,1)} %copy.157.x_ref, bf16[512,1536]{1,0:T(8,128)(2,1)} %copy-done.8, bf16[512,1536]{1,0:T(8,128)(2,1)} %copy-done.9, f32[1,4096]{1,0:T(1,128)} %convert_element_type.350.dead_ref, bf16[256,4096]{1,0:T(8,128)(2,1)} %copy-done.2, ...), custom_call_target="tpu_custom_call" | custom-call | flops 100663296 | bytes 262144 | tf_op jit(solution)/shard_map/pallas_call | solution.py:526
  427.0 17.5 %shard_map.326 = (f32[784,1024]{1,0:T(8,128)}, f32[784,1024]{1,0:T(8,128)}) custom-call(bf16[768,1024]{1,0:T(8,128)(2,1)} %copy.157.x_ref, bf16[512,1536]{1,0:T(8,128)(2,1)} %copy-done.8, bf16[512,1536]{1,0:T(8,128)(2,1)} %copy-done.9, f32[1,4096]{1,0:T(1,128)} %convert_element_type.350.dead_ref, bf16[256,4096]{1,0:T(8,128)(2,1)} %copy-done.2, ...), custom_call_target="tpu_custom_call" | custom-call | flops 100663296 | bytes 262144 | tf_op jit(solution)/shard_map/pallas_call | solution.py:526
  452.7 9.5 %all-to-all-start.3 = ((bf16[4,192,1024]{2,1,0:T(8,128)(2,1)}), bf16[4,192,1024]{2,1,0:T(8,128)(2,1)}, u32[]{:S(2)}, u32[]{:S(2)}) async-start(bf16[4,192,1024]{2,1,0:T(8,128)(2,1)} %bitcast.179), calls=%async_computation.3 | async-start | bytes 3145728 | tf_op jit(solution)/shard_map/all_to_all | solution.py:662
  492.0 7.4 %collective-permute-start.38 = (bf16[112,768]{1,0:T(8,128)(2,1)}, bf16[112,768]{1,0:T(8,128)(2,1)S(1)}, u32[]{:S(2)}, u32[]{:S(2)}) collective-permute-start(bf16[112,768]{1,0:T(8,128)(2,1)} %pad_maximum_fusion.14), channel_id=1, source_target_pairs={{0,1},{1,0},{2,3},{3,2},{4,5},{5,4},{6,7},{7,6},{8,9},{9,8},{10,11... | collective-permute-start | bytes 516104 | tf_op jit(solution)/shard_map/ppermute | solution.py:652
  532.1 11.6 %shard_map.327 = (bf16[768,768]{1,0:T(8,128)(2,1)S(1)}, bf16[768,768]{1,0:T(8,128)(2,1)S(1)}, bf16[768,768]{1,0:T(8,128)(2,1)S(1)}) custom-call(s32[3]{0:T(128)S(1)} %pad_add_fusion.2.place_ref, bf16[4,96,768]{2,1,0:T(8,128)(2,1)S(1)} %pad_maximum_fusion.18.near_ref, bf16[4,96,768]{2,1,0:T(8,128)(2,1)S(1)} %collective-permute-done.47.far_ref), custom_call_target="tpu_custom_call" | custom-call | flops 226492416 | bytes 294912 | tf_op jit(solution)/shard_map/pallas_call | solution.py:194
  547.7 9.8 %shard_map.328 = (bf16[768,768]{1,0:T(8,128)(2,1)S(1)}, bf16[768,768]{1,0:T(8,128)(2,1)S(1)}, bf16[768,768]{1,0:T(8,128)(2,1)S(1)}) custom-call(bf16[768,768]{1,0:T(8,128)(2,1)S(1)} %get-tuple-element.233.g_hi, bf16[768,768]{1,0:T(8,128)(2,1)S(1)} %get-tuple-element.234.g_lo, bf16[768,768]{1,0:T(8,128)(2,1)S(1)} %get-tuple-element.235.q_ref), custom_call_target="tpu_custom_call" | custom-call | flops 226492416 | bytes 294912 | tf_op jit(solution)/shard_map/pallas_call | solution.py:194
  557.8 7.1 %collective-permute-start.51 = (bf16[112,768]{1,0:T(8,128)(2,1)S(1)}, bf16[112,768]{1,0:T(8,128)(2,1)S(1)}, u32[]{:S(2)}, u32[]{:S(2)}) collective-permute-start(bf16[112,768]{1,0:T(8,128)(2,1)S(1)} %pad_maximum_fusion.10), channel_id=1, source_target_pairs={{0,1},{1,0},{2,3},{3,2},{4,5},{5,4},{6,7},{7,6},{8,9},{9,8},{10,11... | collective-permute-start | bytes 516104 | tf_op jit(solution)/shard_map/ppermute | solution.py:652
  567.4 9.9 %shard_map.329 = (bf16[768,768]{1,0:T(8,128)(2,1)S(1)}, bf16[768,768]{1,0:T(8,128)(2,1)S(1)}, bf16[768,768]{1,0:T(8,128)(2,1)S(1)}) custom-call(bf16[768,768]{1,0:T(8,128)(2,1)S(1)} %get-tuple-element.242.g_hi, bf16[768,768]{1,0:T(8,128)(2,1)S(1)} %get-tuple-element.243.g_lo, bf16[768,768]{1,0:T(8,128)(2,1)S(1)} %get-tuple-element.244.q_ref), custom_call_target="tpu_custom_call" | custom-call | flops 226492416 | bytes 294912 | tf_op jit(solution)/shard_map/pallas_call | solution.py:194
  581.4 9.3 %collective-permute-done.52 = bf16[112,768]{1,0:T(8,128)(2,1)S(1)} collective-permute-done((bf16[112,768]{1,0:T(8,128)(2,1)S(1)}, bf16[112,768]{1,0:T(8,128)(2,1)S(1)}, u32[]{:S(2)}, u32[]{:S(2)}) %collective-permute-start.52) | collective-permute-done | bytes 172064 | tf_op jit(solution)/shard_map/ppermute | solution.py:652
  594.5 12.1 %shard_map.330 = (bf16[768,768]{1,0:T(8,128)(2,1)S(1)}, bf16[768,768]{1,0:T(8,128)(2,1)S(1)}, bf16[768,768]{1,0:T(8,128)(2,1)S(1)}) custom-call(bf16[768,768]{1,0:T(8,128)(2,1)S(1)} %get-tuple-element.251.g_hi, bf16[768,768]{1,0:T(8,128)(2,1)S(1)} %get-tuple-element.252.g_lo, bf16[768,768]{1,0:T(8,128)(2,1)S(1)} %get-tuple-element.253.q_ref), custom_call_target="tpu_custom_call" | custom-call | flops 283115520 | bytes 294912 | tf_op jit(solution)/shard_map/pallas_call | solution.py:194
  614.4 13.3 %all-to-all-start.4 = ((bf16[4,192,1024]{2,1,0:T(8,128)(2,1)}), bf16[4,192,1024]{2,1,0:T(8,128)(2,1)}, u32[]{:S(2)}, u32[]{:S(2)}) async-start(bf16[4,192,1024]{2,1,0:T(8,128)(2,1)} %bitcast.188), calls=%async_computation.4 | async-start | bytes 3145728 | tf_op jit(solution)/shard_map/all_to_all | solution.py:662
  633.9 11.3 %shard_map.332 = (bf16[768,768]{1,0:T(8,128)(2,1)S(1)}, bf16[768,768]{1,0:T(8,128)(2,1)S(1)}, bf16[768,768]{1,0:T(8,128)(2,1)S(1)}) custom-call(s32[3]{0:T(128)S(1)} %pad_add_fusion.2.place_ref, bf16[4,96,768]{2,1,0:T(8,128)(2,1)S(1)} %pad_maximum_fusion.19.near_ref, bf16[4,96,768]{2,1,0:T(8,128)(2,1)S(1)} %collective-permute-done.57.far_ref), custom_call_target="tpu_custom_call" | custom-call | flops 226492416 | bytes 294912 | tf_op jit(solution)/shard_map/pallas_call | solution.py:194
  645.2 9.8 %shard_map.333 = (bf16[768,768]{1,0:T(8,128)(2,1)S(1)}, bf16[768,768]{1,0:T(8,128)(2,1)S(1)}, bf16[768,768]{1,0:T(8,128)(2,1)S(1)}) custom-call(bf16[768,768]{1,0:T(8,128)(2,1)S(1)} %get-tuple-element.264.g_hi, bf16[768,768]{1,0:T(8,128)(2,1)S(1)} %get-tuple-element.265.g_lo, bf16[768,768]{1,0:T(8,128)(2,1)S(1)} %get-tuple-element.266.q_ref), custom_call_target="tpu_custom_call" | custom-call | flops 226492416 | bytes 294912 | tf_op jit(solution)/shard_map/pallas_call | solution.py:194
  655.0 9.8 %shard_map.334 = (bf16[768,768]{1,0:T(8,128)(2,1)S(1)}, bf16[768,768]{1,0:T(8,128)(2,1)S(1)}, bf16[768,768]{1,0:T(8,128)(2,1)S(1)}) custom-call(bf16[768,768]{1,0:T(8,128)(2,1)S(1)} %get-tuple-element.267.g_hi, bf16[768,768]{1,0:T(8,128)(2,1)S(1)} %get-tuple-element.268.g_lo, bf16[768,768]{1,0:T(8,128)(2,1)S(1)} %get-tuple-element.269.q_ref), custom_call_target="tpu_custom_call" | custom-call | flops 226492416 | bytes 294912 | tf_op jit(solution)/shard_map/pallas_call | solution.py:194
  664.8 11.7 %shard_map.335 = (bf16[768,768]{1,0:T(8,128)(2,1)S(1)}, bf16[768,768]{1,0:T(8,128)(2,1)S(1)}, bf16[768,768]{1,0:T(8,128)(2,1)S(1)}) custom-call(bf16[768,768]{1,0:T(8,128)(2,1)S(1)} %get-tuple-element.270.g_hi, bf16[768,768]{1,0:T(8,128)(2,1)S(1)} %get-tuple-element.271.g_lo, bf16[768,768]{1,0:T(8,128)(2,1)S(1)} %get-tuple-element.272.q_ref), custom_call_target="tpu_custom_call" | custom-call | flops 283115520 | bytes 294912 | tf_op jit(solution)/shard_map/pallas_call | solution.py:194
  689.4 8.7 %shard_map.337 = (f32[192,4096]{1,0:T(8,128)}, f32[192,4096]{1,0:T(8,128)}, bf16[192,4096]{1,0:T(8,128)(2,1)}) custom-call(s32[3]{0:T(128)} %copy-done.7, bf16[768,768]{1,0:T(8,128)(2,1)} %copy-done.6, bf16[4,768,1024]{2,1,0:T(8,128)(2,1)} %bitcast.182, f32[192,4096]{1,0:T(8,128)} %weight_ref.1), custom_call_target="tpu_custom_call" | custom-call | flops 1207959552 | bytes 6291456 | tf_op jit(solution)/shard_map/pallas_call | solution.py:568
  (445 shorter events, 305.3 us)
Async XLA Ops:
  10.6 48.5 %collective-permute-start.2 = (s32[128,544]{1,0:T(8,128)}, s32[128,544]{1,0:T(8,128)}, u32[]{:S(2)}, u32[]{:S(2)}) collective-permute-start(s32[128,544]{1,0:T(8,128)} %pad_add_fusion.1), channel_id=1, source_target_pairs={{0,3},{1,2},{2,1},{3,0},{4,7},{5,6},{6,5},{7,4},{8,11},{9,10},{10,... | collective-permute-start | bytes 835592 | tf_op jit(solution)/shard_map/ppermute | solution.py:652
  15.7 47.6 %collective-permute-start.1 = (s32[128,544]{1,0:T(8,128)}, s32[128,544]{1,0:T(8,128)}, u32[]{:S(2)}, u32[]{:S(2)}) collective-permute-start(s32[128,544]{1,0:T(8,128)} %pad_add_fusion.1), channel_id=1, source_target_pairs={{0,2},{1,3},{2,0},{3,1},{4,6},{5,7},{6,4},{7,5},{8,10},{9,11},{10,... | collective-permute-start | bytes 835592 | tf_op jit(solution)/shard_map/ppermute | solution.py:652
  15.7 47.6 %collective-permute-start = (s32[128,544]{1,0:T(8,128)}, s32[128,544]{1,0:T(8,128)}, u32[]{:S(2)}, u32[]{:S(2)}) collective-permute-start(s32[128,544]{1,0:T(8,128)} %pad_add_fusion.1), channel_id=1, source_target_pairs={{0,1},{1,0},{2,3},{3,2},{4,5},{5,4},{6,7},{7,6},{8,9},{9,8},{10,11... | collective-permute-start | bytes 835592 | tf_op jit(solution)/shard_map/ppermute | solution.py:652
  19.6 58.0 %all-to-all-start = ((bf16[192,4,1024]{2,0,1:T(8,128)(2,1)}), bf16[192,4,1024]{2,0,1:T(8,128)(2,1)}, u32[]{:S(2)}, u32[]{:S(2)}) async-start(bf16[192,4,1024]{2,0,1:T(8,128)(2,1)} %bitcast.177), calls=%async_computation | async-start | bytes 3145728 | tf_op jit(solution)/shard_map/all_to_all | solution.py:659
  87.5 40.4 %all-to-all-start.1 = ((bf16[192,4,1024]{2,0,1:T(8,128)(2,1)}), bf16[192,4,1024]{2,0,1:T(8,128)(2,1)S(1)}, u32[]{:S(2)}, u32[]{:S(2)}) async-start(bf16[192,4,1024]{2,0,1:T(8,128)(2,1)} %bitcast.167), calls=%async_computation.1 | async-start | bytes 3145728 | tf_op jit(solution)/shard_map/all_to_all | solution.py:659
  131.2 41.4 %collective-permute-start.12 = (bf16[784,1024]{1,0:T(8,128)(2,1)}, bf16[784,1024]{1,0:T(8,128)(2,1)}, u32[]{:S(2)}, u32[]{:S(2)}) collective-permute-start(bf16[784,1024]{1,0:T(8,128)(2,1)} %pad_maximum_fusion.3.refs_4_), channel_id=1, source_target_pairs={{0,16},{8,24},{16,0},{24,8},{1,17},{9,25},{17,1},{25,9},{2,18},{10... | collective-permute-start | bytes 4816904 | tf_op jit(solution)/shard_map/ppermute | solution.py:652
  135.6 38.3 %collective-permute-start.13 = (bf16[784,1024]{1,0:T(8,128)(2,1)}, bf16[784,1024]{1,0:T(8,128)(2,1)}, u32[]{:S(2)}, u32[]{:S(2)}) collective-permute-start(bf16[784,1024]{1,0:T(8,128)(2,1)} %pad_maximum_fusion.4.refs_6_), channel_id=1, source_target_pairs={{0,8},{8,0},{16,24},{24,16},{1,9},{9,1},{17,25},{25,17},{2,10},{10... | collective-permute-start | bytes 4816904 | tf_op jit(solution)/shard_map/ppermute | solution.py:652
  139.1 33.5 %collective-permute-start.11 = (bf16[128,768]{1,0:T(8,128)(2,1)S(1)}, bf16[128,768]{1,0:T(8,128)(2,1)}, u32[]{:S(2)}, u32[]{:S(2)}) collective-permute-start(bf16[128,768]{1,0:T(8,128)(2,1)S(1)} %fusion.21), channel_id=1, source_target_pairs={{0,3},{1,2},{2,1},{3,0},{4,7},{5,6},{6,5},{7,4},{8,11},{9,10},{10,... | collective-permute-start | bytes 589832 | tf_op jit(solution)/shard_map/ppermute | solution.py:652
  145.7 42.8 %collective-permute-start.16 = (bf16[768,512]{1,0:T(8,128)(2,1)}, bf16[768,512]{1,0:T(8,128)(2,1)}, u32[]{:S(2)}, u32[]{:S(2)}) collective-permute-start(bf16[768,512]{1,0:T(8,128)(2,1)} %get-tuple-element.326), channel_id=1, source_target_pairs={{0,8},{8,0},{16,24},{24,16},{1,9},{9,1},{17,25},{25,17},{2,10},{10... | collective-permute-start | bytes 2359304 | tf_op jit(solution)/shard_map/ppermute | solution.py:652
  154.3 34.2 %collective-permute-start.17 = (bf16[768,512]{1,0:T(8,128)(2,1)}, bf16[768,512]{1,0:T(8,128)(2,1)}, u32[]{:S(2)}, u32[]{:S(2)}) collective-permute-start(bf16[768,512]{1,0:T(8,128)(2,1)} %get-tuple-element.325), channel_id=1, source_target_pairs={{0,16},{8,24},{16,0},{24,8},{1,17},{9,25},{17,1},{25,9},{2,18},{10... | collective-permute-start | bytes 2359304 | tf_op jit(solution)/shard_map/ppermute | solution.py:652
  172.6 28.3 %collective-permute-start.15 = (s32[512,544]{0,1:T(8,128)S(1)}, s32[512,544]{0,1:T(8,128)}, u32[]{:S(2)}, u32[]{:S(2)}) collective-permute-start(s32[512,544]{0,1:T(8,128)S(1)} %copy-done.43), channel_id=1, source_target_pairs={{0,4},{4,0},{1,5},{5,1},{2,6},{6,2},{3,7},{7,3},{8,12},{12,8},{9,1... | collective-permute-start | bytes 3342344 | tf_op jit(solution)/shard_map/ppermute | solution.py:652
  191.2 55.2 %collective-permute-start.18 = (bf16[768,1024]{1,0:T(8,128)(2,1)}, bf16[768,1024]{1,0:T(8,128)(2,1)}, u32[]{:S(2)}, u32[]{:S(2)}) collective-permute-start(bf16[768,1024]{1,0:T(8,128)(2,1)} %pad_maximum_fusion.5.refs_8_.refs_4_), channel_id=1, source_target_pairs={{0,16},{8,24},{16,0},{24,8},{1,17},{9,25},{17,1},{25,9},{2,18},{10... | collective-permute-start | bytes 4718600 | tf_op jit(solution)/shard_map/ppermute | solution.py:652
  194.8 51.6 %collective-permute-start.19 = (bf16[768,1024]{1,0:T(8,128)(2,1)}, bf16[768,1024]{1,0:T(8,128)(2,1)}, u32[]{:S(2)}, u32[]{:S(2)}) collective-permute-start(bf16[768,1024]{1,0:T(8,128)(2,1)} %pad_maximum_fusion.6.refs_10_.refs_5_), channel_id=1, source_target_pairs={{0,8},{8,0},{16,24},{24,16},{1,9},{9,1},{17,25},{25,17},{2,10},{10... | collective-permute-start | bytes 4718600 | tf_op jit(solution)/shard_map/ppermute | solution.py:652
  200.2 27.6 %collective-permute-start.14 = (bf16[512,768]{1,0:T(8,128)(2,1)}, bf16[512,768]{1,0:T(8,128)(2,1)}, u32[]{:S(2)}, u32[]{:S(2)}) collective-permute-start(bf16[512,768]{1,0:T(8,128)(2,1)} %pad_maximum_fusion.9), channel_id=1, source_target_pairs={{0,4},{4,0},{1,5},{5,1},{2,6},{6,2},{3,7},{7,3},{8,12},{12,8},{9,1... | collective-permute-start | bytes 2359304 | tf_op jit(solution)/shard_map/ppermute | solution.py:652
  207.2 113.5 %all-to-all-start.2 = ((bf16[384,4,1024]{0,2,1:T(8,128)(2,1)}), bf16[384,4,1024]{0,2,1:T(8,128)(2,1)}, u32[]{:S(2)}, u32[]{:S(2)}) async-start(bf16[384,4,1024]{0,2,1:T(8,128)(2,1)} %bitcast.174), calls=%async_computation.2 | async-start | bytes 6291456 | tf_op jit(solution)/shard_map/all_to_all | solution.py:659
  286.1 34.2 %collective-permute-start.22 = (bf16[128,1536]{1,0:T(8,128)(2,1)S(1)}, bf16[128,1536]{1,0:T(8,128)(2,1)S(1)}, u32[]{:S(2)}, u32[]{:S(2)}) collective-permute-start(bf16[128,1536]{1,0:T(8,128)(2,1)S(1)} %get-tuple-element.324), channel_id=1, source_target_pairs={{0,2},{1,3},{2,0},{3,1},{4,6},{5,7},{6,4},{7,5},{8,10},{9,11},{10,... | collective-permute-start | bytes 1179656 | tf_op jit(solution)/shard_map/ppermute | solution.py:652
  286.1 34.2 %collective-permute-start.21 = (bf16[128,1536]{1,0:T(8,128)(2,1)S(1)}, bf16[128,1536]{1,0:T(8,128)(2,1)S(1)}, u32[]{:S(2)}, u32[]{:S(2)}) collective-permute-start(bf16[128,1536]{1,0:T(8,128)(2,1)S(1)} %get-tuple-element.322), channel_id=1, source_target_pairs={{0,1},{1,0},{2,3},{3,2},{4,5},{5,4},{6,7},{7,6},{8,9},{9,8},{10,11... | collective-permute-start | bytes 1179656 | tf_op jit(solution)/shard_map/ppermute | solution.py:652
  325.5 29.8 %collective-permute-start.25 = (bf16[128,1536]{1,0:T(8,128)(2,1)S(1)}, bf16[128,1536]{1,0:T(8,128)(2,1)S(1)}, u32[]{:S(2)}, u32[]{:S(2)}) collective-permute-start(bf16[128,1536]{1,0:T(8,128)(2,1)S(1)} %pad_maximum_fusion.20), channel_id=1, source_target_pairs={{0,2},{1,3},{2,0},{3,1},{4,6},{5,7},{6,4},{7,5},{8,10},{9,11},{10,... | collective-permute-start | bytes 1179656 | tf_op jit(solution)/shard_map/ppermute | solution.py:652
  328.4 26.9 %collective-permute-start.26 = (bf16[128,1536]{1,0:T(8,128)(2,1)S(1)}, bf16[128,1536]{1,0:T(8,128)(2,1)S(1)}, u32[]{:S(2)}, u32[]{:S(2)}) collective-permute-start(bf16[128,1536]{1,0:T(8,128)(2,1)S(1)} %pad_maximum_fusion.20), channel_id=1, source_target_pairs={{0,3},{1,2},{2,1},{3,0},{4,7},{5,6},{6,5},{7,4},{8,11},{9,10},{10,... | collective-permute-start | bytes 1179656 | tf_op jit(solution)/shard_map/ppermute | solution.py:652
  374.0 36.7 %collective-permute-start.28 = (bf16[768,1024]{1,0:T(8,128)(2,1)}, bf16[768,1024]{1,0:T(8,128)(2,1)S(1)}, u32[]{:S(2)}, u32[]{:S(2)}) collective-permute-start(bf16[768,1024]{1,0:T(8,128)(2,1)} %get-tuple-element.199), channel_id=1, source_target_pairs={{0,16},{8,24},{16,0},{24,8},{1,17},{9,25},{17,1},{25,9},{2,18},{10... | collective-permute-start | bytes 4718600 | tf_op jit(solution)/shard_map/ppermute | solution.py:652
  375.3 36.6 %collective-permute-start.29 = (bf16[768,1024]{1,0:T(8,128)(2,1)}, bf16[768,1024]{1,0:T(8,128)(2,1)}, u32[]{:S(2)}, u32[]{:S(2)}) collective-permute-start(bf16[768,1024]{1,0:T(8,128)(2,1)} %get-tuple-element.200), channel_id=1, source_target_pairs={{0,8},{8,0},{16,24},{24,16},{1,9},{9,1},{17,25},{25,17},{2,10},{10... | collective-permute-start | bytes 4718600 | tf_op jit(solution)/shard_map/ppermute | solution.py:652
  416.6 28.0 %collective-permute-start.31 = (bf16[768,512]{1,0:T(8,128)(2,1)S(1)}, bf16[768,512]{1,0:T(8,128)(2,1)S(1)}, u32[]{:S(2)}, u32[]{:S(2)}) collective-permute-start(bf16[768,512]{1,0:T(8,128)(2,1)S(1)} %split.40), channel_id=1, source_target_pairs={{0,16},{8,24},{16,0},{24,8},{1,17},{9,25},{17,1},{25,9},{2,18},{10... | collective-permute-start | bytes 2359304 | tf_op jit(solution)/shard_map/ppermute | solution.py:652
  420.4 26.0 %collective-permute-start.30 = (bf16[768,512]{1,0:T(8,128)(2,1)S(1)}, bf16[768,512]{1,0:T(8,128)(2,1)}, u32[]{:S(2)}, u32[]{:S(2)}) collective-permute-start(bf16[768,512]{1,0:T(8,128)(2,1)S(1)} %split.41), channel_id=1, source_target_pairs={{0,8},{8,0},{16,24},{24,16},{1,9},{9,1},{17,25},{25,17},{2,10},{10... | collective-permute-start | bytes 2359304 | tf_op jit(solution)/shard_map/ppermute | solution.py:652
  424.6 45.4 %collective-permute-start.32 = (bf16[784,1024]{1,0:T(8,128)(2,1)}, bf16[784,1024]{1,0:T(8,128)(2,1)}, u32[]{:S(2)}, u32[]{:S(2)}) collective-permute-start(bf16[784,1024]{1,0:T(8,128)(2,1)} %get-tuple-element.211), channel_id=1, source_target_pairs={{0,16},{8,24},{16,0},{24,8},{1,17},{9,25},{17,1},{25,9},{2,18},{10... | collective-permute-start | bytes 4816904 | tf_op jit(solution)/shard_map/ppermute | solution.py:652
  425.5 48.0 %collective-permute-start.33 = (bf16[784,1024]{1,0:T(8,128)(2,1)}, bf16[784,1024]{1,0:T(8,128)(2,1)}, u32[]{:S(2)}, u32[]{:S(2)}) collective-permute-start(bf16[784,1024]{1,0:T(8,128)(2,1)} %get-tuple-element.212), channel_id=1, source_target_pairs={{0,8},{8,0},{16,24},{24,16},{1,9},{9,1},{17,25},{25,17},{2,10},{10... | collective-permute-start | bytes 4816904 | tf_op jit(solution)/shard_map/ppermute | solution.py:652
  452.7 57.1 %all-to-all-start.3 = ((bf16[4,192,1024]{2,1,0:T(8,128)(2,1)}), bf16[4,192,1024]{2,1,0:T(8,128)(2,1)}, u32[]{:S(2)}, u32[]{:S(2)}) async-start(bf16[4,192,1024]{2,1,0:T(8,128)(2,1)} %bitcast.179), calls=%async_computation.3 | async-start | bytes 3145728 | tf_op jit(solution)/shard_map/all_to_all | solution.py:662
  462.2 227.2 %all-gather.5.cloned.1.call-start = ((), (), s32[]{:S(2)}) async-start(), calls=%async_computation.5 | async-start | bytes 7864320 | tf_op jit(solution)/shard_map/all_gather | solution.py:901
  482.8 24.7 %collective-permute-start.42 = (bf16[784,512]{1,0:T(8,128)(2,1)S(1)}, bf16[784,512]{1,0:T(8,128)(2,1)S(1)}, u32[]{:S(2)}, u32[]{:S(2)}) collective-permute-start(bf16[784,512]{1,0:T(8,128)(2,1)S(1)} %get-tuple-element.354), channel_id=1, source_target_pairs={{0,16},{8,24},{16,0},{24,8},{1,17},{9,25},{17,1},{25,9},{2,18},{10... | collective-permute-start | bytes 2408456 | tf_op jit(solution)/shard_map/ppermute | solution.py:652
  484.0 23.9 %collective-permute-start.41 = (bf16[784,512]{1,0:T(8,128)(2,1)S(1)}, bf16[784,512]{1,0:T(8,128)(2,1)S(1)}, u32[]{:S(2)}, u32[]{:S(2)}) collective-permute-start(bf16[784,512]{1,0:T(8,128)(2,1)S(1)} %get-tuple-element.353), channel_id=1, source_target_pairs={{0,8},{8,0},{16,24},{24,16},{1,9},{9,1},{17,25},{25,17},{2,10},{10... | collective-permute-start | bytes 2408456 | tf_op jit(solution)/shard_map/ppermute | solution.py:652
  564.9 25.8 %collective-permute-start.52 = (bf16[112,768]{1,0:T(8,128)(2,1)S(1)}, bf16[112,768]{1,0:T(8,128)(2,1)S(1)}, u32[]{:S(2)}, u32[]{:S(2)}) collective-permute-start(bf16[112,768]{1,0:T(8,128)(2,1)S(1)} %pad_maximum_fusion.10), channel_id=1, source_target_pairs={{0,2},{1,3},{2,0},{3,1},{4,6},{5,7},{6,4},{7,5},{8,10},{9,11},{10,... | collective-permute-start | bytes 516104 | tf_op jit(solution)/shard_map/ppermute | solution.py:652
  565.9 24.9 %collective-permute-start.53 = (bf16[112,768]{1,0:T(8,128)(2,1)S(1)}, bf16[112,768]{1,0:T(8,128)(2,1)S(1)}, u32[]{:S(2)}, u32[]{:S(2)}) collective-permute-start(bf16[112,768]{1,0:T(8,128)(2,1)S(1)} %pad_maximum_fusion.10), channel_id=1, source_target_pairs={{0,3},{1,2},{2,1},{3,0},{4,7},{5,6},{6,5},{7,4},{8,11},{9,10},{10,... | collective-permute-start | bytes 516104 | tf_op jit(solution)/shard_map/ppermute | solution.py:652
  614.4 68.5 %all-to-all-start.4 = ((bf16[4,192,1024]{2,1,0:T(8,128)(2,1)}), bf16[4,192,1024]{2,1,0:T(8,128)(2,1)}, u32[]{:S(2)}, u32[]{:S(2)}) async-start(bf16[4,192,1024]{2,1,0:T(8,128)(2,1)} %bitcast.188), calls=%async_computation.4 | async-start | bytes 3145728 | tf_op jit(solution)/shard_map/all_to_all | solution.py:662
  (99 other events, 1249.0 us)
Sparse Core Ops, SparseCore 0:
  517.4 160.8 all-gather.4

commit v10 on v7

--- a/solution.py
+++ b/solution.py
@@ -776,7 +776,6 @@
     codes = [*codes, kind_codes(place, far_picks[half_rows:], latent_count, sizes)]
     all_inputs = jnp.concatenate([near_inputs, far_inputs], 0)
     encoder_in = (all_inputs.astype(f32) - decoder_bias).astype(bf16)
-    encoder_in, moments = tie(encoder_in, moments)
     top_acts, aux_acts, far, near = forward(encoder_in, codes, dead_here, enc_parts, dec_parts)
     encoder_t = encoder_in.T
     far_got, encoder_t = tie(swap(far, "core", 1), encoder_t)
@@ -799,6 +798,7 @@
     back_recon = 2.0 / model_width * counted[:, None] * (reconstructed_input - target)
     back_aux = 2.0 * AUX_COEF / model_width * counted[:, None] * aux_gap
     back_rows = jnp.concatenate([back_recon, back_aux], 1).astype(bf16)
+    back_rows, moments = tie(back_rows, moments)
     near_back = spread_narrow(back_rows)
     far_back = swap(near_back, "core", 1)
     near_t, far_back = tie(near_back.T, far_back)

time: 710 us -> 692 us (0.975)
  waiting for transfers between devices: 150 us -> 134 us
    all_to_all x3, waiting for transfers between devices: 26.1 us -> 8.52 us  [rows_to_latents(): lax.all_to_all(value, 'narrow', split_axis=1, concat_axis=0, tiled=True)]
    unnamed x159 -> x168, local copies, waits for them, and re-layouts: 17.4 us -> 19.1 us
  transfers between devices with their start and end apart: 64 -> 64, of which waited for: 26 -> 26; matrix products, arithmetic and copies ran while one was open for 17% -> 17% of each run, Pallas kernels for 27% -> 33%
where the time goes in v10:
time: 692 us; the launch traced here: 683 us
  Pallas kernels  244 us (35%)
  waiting for transfers between devices  134 us (19%)
  starting transfers between devices  115 us (17%)
  other arithmetic  74.6 us (11%)
  local copies, waits for them, and re-layouts  68.7 us (10%)
  matrix products  21 us (3%)
  between operations  16.6 us (2%)
  blocking collectives  8.74 us (1%)
    ppermute x58, waiting for transfers between devices, swap(): lax.ppermute(value, axis, [(spot, spot ^ offset) for spot in range(count)])  125 us
    pallas_call x10, Pallas kernels, square_call(): pl.pallas_call(kernel, out_shape=[square] * outs, in_specs=specs, out_spe...  96.1 us
    ppermute x58, starting transfers between devices, swap(): lax.ppermute(value, axis, [(spot, spot ^ offset) for spot in range(count)])  77.2 us
    pallas_call x4, Pallas kernels, kind_codes(): pl.pallas_call(functools.partial(code_kernel, shifts), grid=(row_total //...  45.5 us
    pallas_call x2, Pallas kernels, enc_grads(): pl.pallas_call(functools.partial(enc_grad_kernel, count), grid=(2 * count...  38 us
    pallas_call x1, Pallas kernels, forward(): pl.pallas_call(functools.partial(forward_kernel, count), grid=(4 * count,...  31.4 us
    pallas_call x2, Pallas kernels, dec_grads(): pl.pallas_call(functools.partial(dec_grad_kernel, count), grid=(2 * count...  24.6 us
    all_to_all x2, starting transfers between devices, rows_of(): lax.all_to_all(value, 'narrow', split_axis=0, concat_axis=1, tiled=True)  22.7 us
  transfers between devices with their start and end apart: 64, of which 26 were waited for; matrix products, arithmetic and copies ran while one was open for 17% of the time, Pallas kernels for 33%

profile of v10, /device:TPU:0, one launch (start us, length us, event | category | flops | bytes accessed | tf_op | source)
XLA Modules:
  0.0 683.3 jit_solution(6662693516921132253)
XLA Ops:
  24.8 8.7 %all-gather.2 = s32[8,1,128]{2,1,0:T(1,128)S(1)} all-gather(s32[1,1,128]{2,1,0:T(1,128)S(1)} %bitcast.209), channel_id=2, replica_groups=mesh['chip'=4,'core'=2,'narrow'=4] {'chip','core'}, dimensions={0}, use_global_device_ids=true | all-gather | bytes 4608 | tf_op jit(solution)/shard_map/all_gather | solution.py:697
  33.8 10.6 %gather_fusion = bf16[1024,768]{1,0:T(8,128)(2,1)} fusion(bf16[6288,768]{1,0:T(8,128)(2,1)} %param.28, s32[1024]{0:T(1024)S(1)} %broadcast_clamp_fusion), kind=kCustom, calls=%fused_computation | custom fusion | bytes 3149824 | tf_op jit(solution)/shard_map/jit(_take)/gather | solution.py:707
  69.1 8.5 %all-to-all-done = bf16[192,4,1024]{2,0,1:T(8,128)(2,1)} async-done(((bf16[192,4,1024]{2,0,1:T(8,128)(2,1)}), bf16[192,4,1024]{2,0,1:T(8,128)(2,1)}, u32[]{:S(2)}, u32[]{:S(2)}) %all-to-all-start) | async-done | bytes 1572896 | tf_op jit(solution)/shard_map/all_to_all | solution.py:659
  100.2 5.6 fusion.21
  124.3 11.4 %shard_map.318.refs_0_ = bf16[256,4096]{1,0:T(8,128)(2,1)S(1)} custom-call(s32[3]{0:T(128)S(1)} %pad_add_fusion.2.place_ref, s32[256,544]{1,0:T(8,128)S(1)} %slice.323.ids_ref), custom_call_target="tpu_custom_call" | custom-call | flops 1048576 | bytes 139264 | tf_op jit(solution)/shard_map/pallas_call | solution.py:290
  137.0 12.8 %collective-permute-done.10 = bf16[128,768]{1,0:T(8,128)(2,1)S(1)} collective-permute-done((bf16[128,768]{1,0:T(8,128)(2,1)S(1)}, bf16[128,768]{1,0:T(8,128)(2,1)S(1)}, u32[]{:S(2)}, u32[]{:S(2)}) %collective-permute-start.10) | collective-permute-done | bytes 196640 | tf_op jit(solution)/shard_map/ppermute | solution.py:652
  161.3 11.4 %shard_map.319.refs_1_ = bf16[256,4096]{1,0:T(8,128)(2,1)S(1)} custom-call(s32[3]{0:T(128)S(1)} %pad_add_fusion.2.place_ref, s32[256,544]{1,0:T(8,128)S(1)} %slice.326.ids_ref), custom_call_target="tpu_custom_call" | custom-call | flops 1048576 | bytes 139264 | tf_op jit(solution)/shard_map/pallas_call | solution.py:290
  194.8 11.4 %shard_map.320.refs_2_ = bf16[256,4096]{1,0:T(8,128)(2,1)S(1)} custom-call(s32[3]{0:T(128)S(1)} %pad_add_fusion.2.place_ref, s32[256,544]{1,0:T(8,128)S(1)} %slice.410.ids_ref), custom_call_target="tpu_custom_call" | custom-call | flops 1048576 | bytes 139264 | tf_op jit(solution)/shard_map/pallas_call | solution.py:290
  209.2 11.4 %shard_map.321.refs_3_ = bf16[256,4096]{1,0:T(8,128)(2,1)S(1)} custom-call(s32[3]{0:T(128)S(1)} %pad_add_fusion.2.place_ref, s32[256,544]{1,0:T(8,128)S(1)} %slice.411.ids_ref), custom_call_target="tpu_custom_call" | custom-call | flops 1048576 | bytes 139264 | tf_op jit(solution)/shard_map/pallas_call | solution.py:290
  223.8 31.4 %shard_map.322 = (bf16[1024,4096]{1,0:T(8,128)(2,1)}, bf16[1024,4096]{1,0:T(8,128)(2,1)}, bf16[512,1536]{1,0:T(8,128)(2,1)}, f32[512,1536]{1,0:T(8,128)}) custom-call(bf16[1024,768]{1,0:T(8,128)(2,1)} %subtract_convert_fusion.x_ref, f32[1,4096]{1,0:T(1,128)} %convert_element_type.331.dead_ref, bf16[256,4096]{1,0:T(8,128)(2,1)} %copy-done.2, ...), custom_call_target="tpu_custom_call" | custom-call | flops 6442450944 | bytes 25165824 | tf_op jit(solution)/shard_map/pallas_call | solution.py:396
  264.2 9.5 %collective-permute-done.23 = bf16[128,1536]{1,0:T(8,128)(2,1)S(1)} collective-permute-done((bf16[128,1536]{1,0:T(8,128)(2,1)S(1)}, bf16[128,1536]{1,0:T(8,128)(2,1)S(1)}, u32[]{:S(2)}, u32[]{:S(2)}) %collective-permute-start.23) | collective-permute-done | bytes 393248 | tf_op jit(solution)/shard_map/ppermute | solution.py:652
  273.7 24.0 %collective-permute-done.22 = bf16[128,1536]{1,0:T(8,128)(2,1)S(1)} collective-permute-done((bf16[128,1536]{1,0:T(8,128)(2,1)S(1)}, bf16[128,1536]{1,0:T(8,128)(2,1)S(1)}, u32[]{:S(2)}, u32[]{:S(2)}) %collective-permute-start.22) | collective-permute-done | bytes 393248 | tf_op jit(solution)/shard_map/ppermute | solution.py:652
  307.4 13.6 %collective-permute-done.24 = bf16[128,1536]{1,0:T(8,128)(2,1)S(1)} collective-permute-done((bf16[128,1536]{1,0:T(8,128)(2,1)S(1)}, bf16[128,1536]{1,0:T(8,128)(2,1)S(1)}, u32[]{:S(2)}, u32[]{:S(2)}) %collective-permute-start.24) | collective-permute-done | bytes 393248 | tf_op jit(solution)/shard_map/ppermute | solution.py:652
  321.1 11.8 %collective-permute-done.25 = bf16[128,1536]{1,0:T(8,128)(2,1)S(1)} collective-permute-done((bf16[128,1536]{1,0:T(8,128)(2,1)S(1)}, bf16[128,1536]{1,0:T(8,128)(2,1)S(1)}, u32[]{:S(2)}, u32[]{:S(2)}) %collective-permute-start.25) | collective-permute-done | bytes 393248 | tf_op jit(solution)/shard_map/ppermute | solution.py:652
  339.6 12.1 %shard_map.323 = (bf16[768,1024]{1,0:T(8,128)(2,1)}, bf16[768,1024]{1,0:T(8,128)(2,1)}) custom-call(bf16[1536,512]{1,0:T(8,128)(2,1)} %copy.153.near_r.near_a, bf16[1536,512]{1,0:T(8,128)(2,1)} %copy.153.near_r.near_a, bf16[1536,512]{1,0:T(8,128)(2,1)} %copy.155.far_r.far_a, bf16[1536,512]{1,0:T(8,128)(2,1)} %copy.155.far_r.far_a, ...), custom_call_target="tpu_custom_call" | custom-call | flops 100663296 | bytes 262144 | tf_op jit(solution)/shard_map/pallas_call | solution.py:462
  356.1 12.5 %shard_map.324 = (f32[768,1024]{1,0:T(8,128)}, f32[768,1024]{1,0:T(8,128)}) custom-call(bf16[1536,512]{1,0:T(8,128)(2,1)} %copy.153.near_r.near_a, bf16[1536,512]{1,0:T(8,128)(2,1)} %copy.153.near_r.near_a, bf16[1536,512]{1,0:T(8,128)(2,1)} %copy.155.far_r.far_a, bf16[1536,512]{1,0:T(8,128)(2,1)} %copy.155.far_r.far_a, ...), custom_call_target="tpu_custom_call" | custom-call | flops 100663296 | bytes 262144 | tf_op jit(solution)/shard_map/pallas_call | solution.py:462
  368.6 18.7 %shard_map.325 = (bf16[784,1024]{1,0:T(8,128)(2,1)}, bf16[784,1024]{1,0:T(8,128)(2,1)}) custom-call(bf16[768,1024]{1,0:T(8,128)(2,1)} %copy.157.x_ref, bf16[512,1536]{1,0:T(8,128)(2,1)} %copy-done.8, bf16[512,1536]{1,0:T(8,128)(2,1)} %copy-done.9, f32[1,4096]{1,0:T(1,128)} %convert_element_type.331.dead_ref, bf16[256,4096]{1,0:T(8,128)(2,1)} %copy-done.2, ...), custom_call_target="tpu_custom_call" | custom-call | flops 100663296 | bytes 262144 | tf_op jit(solution)/shard_map/pallas_call | solution.py:526
  404.6 19.3 %shard_map.326 = (f32[784,1024]{1,0:T(8,128)}, f32[784,1024]{1,0:T(8,128)}) custom-call(bf16[768,1024]{1,0:T(8,128)(2,1)} %copy.157.x_ref, bf16[512,1536]{1,0:T(8,128)(2,1)} %copy-done.8, bf16[512,1536]{1,0:T(8,128)(2,1)} %copy-done.9, f32[1,4096]{1,0:T(1,128)} %convert_element_type.331.dead_ref, bf16[256,4096]{1,0:T(8,128)(2,1)} %copy-done.2, ...), custom_call_target="tpu_custom_call" | custom-call | flops 100663296 | bytes 262144 | tf_op jit(solution)/shard_map/pallas_call | solution.py:526
  432.0 9.5 %all-to-all-start.3 = ((bf16[4,192,1024]{2,1,0:T(8,128)(2,1)}), bf16[4,192,1024]{2,1,0:T(8,128)(2,1)}, u32[]{:S(2)}, u32[]{:S(2)}) async-start(bf16[4,192,1024]{2,1,0:T(8,128)(2,1)} %bitcast.177), calls=%async_computation.3 | async-start | bytes 3145728 | tf_op jit(solution)/shard_map/all_to_all | solution.py:662
  469.6 7.8 %collective-permute-start.38 = (bf16[112,768]{1,0:T(8,128)(2,1)}, bf16[112,768]{1,0:T(8,128)(2,1)S(1)}, u32[]{:S(2)}, u32[]{:S(2)}) collective-permute-start(bf16[112,768]{1,0:T(8,128)(2,1)} %pad_maximum_fusion.14), channel_id=1, source_target_pairs={{0,1},{1,0},{2,3},{3,2},{4,5},{5,4},{6,7},{7,6},{8,9},{9,8},{10,11... | collective-permute-start | bytes 516104 | tf_op jit(solution)/shard_map/ppermute | solution.py:652
  510.1 11.8 %shard_map.327 = (bf16[768,768]{1,0:T(8,128)(2,1)S(1)}, bf16[768,768]{1,0:T(8,128)(2,1)S(1)}, bf16[768,768]{1,0:T(8,128)(2,1)S(1)}) custom-call(s32[3]{0:T(128)S(1)} %pad_add_fusion.2.place_ref, bf16[4,96,768]{2,1,0:T(8,128)(2,1)S(1)} %pad_maximum_fusion.18.near_ref, bf16[4,96,768]{2,1,0:T(8,128)(2,1)S(1)} %collective-permute-done.47.far_ref), custom_call_target="tpu_custom_call" | custom-call | flops 226492416 | bytes 294912 | tf_op jit(solution)/shard_map/pallas_call | solution.py:194
  525.9 9.8 %shard_map.328 = (bf16[768,768]{1,0:T(8,128)(2,1)S(1)}, bf16[768,768]{1,0:T(8,128)(2,1)S(1)}, bf16[768,768]{1,0:T(8,128)(2,1)S(1)}) custom-call(bf16[768,768]{1,0:T(8,128)(2,1)S(1)} %get-tuple-element.237.g_hi, bf16[768,768]{1,0:T(8,128)(2,1)S(1)} %get-tuple-element.238.g_lo, bf16[768,768]{1,0:T(8,128)(2,1)S(1)} %get-tuple-element.239.q_ref), custom_call_target="tpu_custom_call" | custom-call | flops 226492416 | bytes 294912 | tf_op jit(solution)/shard_map/pallas_call | solution.py:194
  536.0 7.1 %collective-permute-start.51 = (bf16[112,768]{1,0:T(8,128)(2,1)S(1)}, bf16[112,768]{1,0:T(8,128)(2,1)S(1)}, u32[]{:S(2)}, u32[]{:S(2)}) collective-permute-start(bf16[112,768]{1,0:T(8,128)(2,1)S(1)} %pad_maximum_fusion.10), channel_id=1, source_target_pairs={{0,1},{1,0},{2,3},{3,2},{4,5},{5,4},{6,7},{7,6},{8,9},{9,8},{10,11... | collective-permute-start | bytes 516104 | tf_op jit(solution)/shard_map/ppermute | solution.py:652
  545.6 9.9 %shard_map.329 = (bf16[768,768]{1,0:T(8,128)(2,1)S(1)}, bf16[768,768]{1,0:T(8,128)(2,1)S(1)}, bf16[768,768]{1,0:T(8,128)(2,1)S(1)}) custom-call(bf16[768,768]{1,0:T(8,128)(2,1)S(1)} %get-tuple-element.246.g_hi, bf16[768,768]{1,0:T(8,128)(2,1)S(1)} %get-tuple-element.247.g_lo, bf16[768,768]{1,0:T(8,128)(2,1)S(1)} %get-tuple-element.248.q_ref), custom_call_target="tpu_custom_call" | custom-call | flops 226492416 | bytes 294912 | tf_op jit(solution)/shard_map/pallas_call | solution.py:194
  559.3 9.8 %collective-permute-done.52 = bf16[112,768]{1,0:T(8,128)(2,1)S(1)} collective-permute-done((bf16[112,768]{1,0:T(8,128)(2,1)S(1)}, bf16[112,768]{1,0:T(8,128)(2,1)S(1)}, u32[]{:S(2)}, u32[]{:S(2)}) %collective-permute-start.52) | collective-permute-done | bytes 172064 | tf_op jit(solution)/shard_map/ppermute | solution.py:652
  572.8 11.8 %shard_map.330 = (bf16[768,768]{1,0:T(8,128)(2,1)S(1)}, bf16[768,768]{1,0:T(8,128)(2,1)S(1)}, bf16[768,768]{1,0:T(8,128)(2,1)S(1)}) custom-call(bf16[768,768]{1,0:T(8,128)(2,1)S(1)} %get-tuple-element.255.g_hi, bf16[768,768]{1,0:T(8,128)(2,1)S(1)} %get-tuple-element.256.g_lo, bf16[768,768]{1,0:T(8,128)(2,1)S(1)} %get-tuple-element.257.q_ref), custom_call_target="tpu_custom_call" | custom-call | flops 283115520 | bytes 294912 | tf_op jit(solution)/shard_map/pallas_call | solution.py:194
  592.5 13.3 %all-to-all-start.4 = ((bf16[4,192,1024]{2,1,0:T(8,128)(2,1)}), bf16[4,192,1024]{2,1,0:T(8,128)(2,1)}, u32[]{:S(2)}, u32[]{:S(2)}) async-start(bf16[4,192,1024]{2,1,0:T(8,128)(2,1)} %bitcast.186), calls=%async_computation.4 | async-start | bytes 3145728 | tf_op jit(solution)/shard_map/all_to_all | solution.py:662
  611.9 11.3 %shard_map.332 = (bf16[768,768]{1,0:T(8,128)(2,1)S(1)}, bf16[768,768]{1,0:T(8,128)(2,1)S(1)}, bf16[768,768]{1,0:T(8,128)(2,1)S(1)}) custom-call(s32[3]{0:T(128)S(1)} %pad_add_fusion.2.place_ref, bf16[4,96,768]{2,1,0:T(8,128)(2,1)S(1)} %pad_maximum_fusion.19.near_ref, bf16[4,96,768]{2,1,0:T(8,128)(2,1)S(1)} %collective-permute-done.57.far_ref), custom_call_target="tpu_custom_call" | custom-call | flops 226492416 | bytes 294912 | tf_op jit(solution)/shard_map/pallas_call | solution.py:194
  623.3 9.8 %shard_map.333 = (bf16[768,768]{1,0:T(8,128)(2,1)S(1)}, bf16[768,768]{1,0:T(8,128)(2,1)S(1)}, bf16[768,768]{1,0:T(8,128)(2,1)S(1)}) custom-call(bf16[768,768]{1,0:T(8,128)(2,1)S(1)} %get-tuple-element.268.g_hi, bf16[768,768]{1,0:T(8,128)(2,1)S(1)} %get-tuple-element.269.g_lo, bf16[768,768]{1,0:T(8,128)(2,1)S(1)} %get-tuple-element.270.q_ref), custom_call_target="tpu_custom_call" | custom-call | flops 226492416 | bytes 294912 | tf_op jit(solution)/shard_map/pallas_call | solution.py:194
  633.1 9.8 %shard_map.334 = (bf16[768,768]{1,0:T(8,128)(2,1)S(1)}, bf16[768,768]{1,0:T(8,128)(2,1)S(1)}, bf16[768,768]{1,0:T(8,128)(2,1)S(1)}) custom-call(bf16[768,768]{1,0:T(8,128)(2,1)S(1)} %get-tuple-element.271.g_hi, bf16[768,768]{1,0:T(8,128)(2,1)S(1)} %get-tuple-element.272.g_lo, bf16[768,768]{1,0:T(8,128)(2,1)S(1)} %get-tuple-element.273.q_ref), custom_call_target="tpu_custom_call" | custom-call | flops 226492416 | bytes 294912 | tf_op jit(solution)/shard_map/pallas_call | solution.py:194
  642.9 11.7 %shard_map.335 = (bf16[768,768]{1,0:T(8,128)(2,1)S(1)}, bf16[768,768]{1,0:T(8,128)(2,1)S(1)}, bf16[768,768]{1,0:T(8,128)(2,1)S(1)}) custom-call(bf16[768,768]{1,0:T(8,128)(2,1)S(1)} %get-tuple-element.274.g_hi, bf16[768,768]{1,0:T(8,128)(2,1)S(1)} %get-tuple-element.275.g_lo, bf16[768,768]{1,0:T(8,128)(2,1)S(1)} %get-tuple-element.276.q_ref), custom_call_target="tpu_custom_call" | custom-call | flops 283115520 | bytes 294912 | tf_op jit(solution)/shard_map/pallas_call | solution.py:194
  667.5 8.7 %shard_map.337 = (f32[192,4096]{1,0:T(8,128)}, f32[192,4096]{1,0:T(8,128)}, bf16[192,4096]{1,0:T(8,128)(2,1)}) custom-call(s32[3]{0:T(128)} %copy-done.7, bf16[768,768]{1,0:T(8,128)(2,1)} %copy-done.6, bf16[4,768,1024]{2,1,0:T(8,128)(2,1)} %bitcast.180, f32[192,4096]{1,0:T(8,128)} %weight_ref.1), custom_call_target="tpu_custom_call" | custom-call | flops 1207959552 | bytes 6291456 | tf_op jit(solution)/shard_map/pallas_call | solution.py:568
  (457 shorter events, 280.0 us)
Async XLA Ops:
  10.6 48.4 %collective-permute-start.2 = (s32[128,544]{1,0:T(8,128)}, s32[128,544]{1,0:T(8,128)}, u32[]{:S(2)}, u32[]{:S(2)}) collective-permute-start(s32[128,544]{1,0:T(8,128)} %pad_add_fusion.1), channel_id=1, source_target_pairs={{0,3},{1,2},{2,1},{3,0},{4,7},{5,6},{6,5},{7,4},{8,11},{9,10},{10,... | collective-permute-start | bytes 835592 | tf_op jit(solution)/shard_map/ppermute | solution.py:652
  15.7 47.6 %collective-permute-start.1 = (s32[128,544]{1,0:T(8,128)}, s32[128,544]{1,0:T(8,128)}, u32[]{:S(2)}, u32[]{:S(2)}) collective-permute-start(s32[128,544]{1,0:T(8,128)} %pad_add_fusion.1), channel_id=1, source_target_pairs={{0,2},{1,3},{2,0},{3,1},{4,6},{5,7},{6,4},{7,5},{8,10},{9,11},{10,... | collective-permute-start | bytes 835592 | tf_op jit(solution)/shard_map/ppermute | solution.py:652
  15.7 47.6 %collective-permute-start = (s32[128,544]{1,0:T(8,128)}, s32[128,544]{1,0:T(8,128)}, u32[]{:S(2)}, u32[]{:S(2)}) collective-permute-start(s32[128,544]{1,0:T(8,128)} %pad_add_fusion.1), channel_id=1, source_target_pairs={{0,1},{1,0},{2,3},{3,2},{4,5},{5,4},{6,7},{7,6},{8,9},{9,8},{10,11... | collective-permute-start | bytes 835592 | tf_op jit(solution)/shard_map/ppermute | solution.py:652
  19.6 58.0 %all-to-all-start = ((bf16[192,4,1024]{2,0,1:T(8,128)(2,1)}), bf16[192,4,1024]{2,0,1:T(8,128)(2,1)}, u32[]{:S(2)}, u32[]{:S(2)}) async-start(bf16[192,4,1024]{2,0,1:T(8,128)(2,1)} %bitcast.176), calls=%async_computation | async-start | bytes 3145728 | tf_op jit(solution)/shard_map/all_to_all | solution.py:659
  95.4 54.4 %all-to-all-start.1 = ((bf16[192,4,1024]{2,0,1:T(8,128)(2,1)}), bf16[192,4,1024]{2,0,1:T(8,128)(2,1)}, u32[]{:S(2)}, u32[]{:S(2)}) async-start(bf16[192,4,1024]{2,0,1:T(8,128)(2,1)} %bitcast.167), calls=%async_computation.1 | async-start | bytes 3145728 | tf_op jit(solution)/shard_map/all_to_all | solution.py:659
  115.4 35.6 %collective-permute-start.12 = (bf16[784,1024]{1,0:T(8,128)(2,1)}, bf16[784,1024]{1,0:T(8,128)(2,1)}, u32[]{:S(2)}, u32[]{:S(2)}) collective-permute-start(bf16[784,1024]{1,0:T(8,128)(2,1)} %pad_maximum_fusion.3.refs_4_), channel_id=1, source_target_pairs={{0,16},{8,24},{16,0},{24,8},{1,17},{9,25},{17,1},{25,9},{2,18},{10... | collective-permute-start | bytes 4816904 | tf_op jit(solution)/shard_map/ppermute | solution.py:652
  116.9 35.4 %collective-permute-start.13 = (bf16[784,1024]{1,0:T(8,128)(2,1)}, bf16[784,1024]{1,0:T(8,128)(2,1)}, u32[]{:S(2)}, u32[]{:S(2)}) collective-permute-start(bf16[784,1024]{1,0:T(8,128)(2,1)} %pad_maximum_fusion.4.refs_6_), channel_id=1, source_target_pairs={{0,8},{8,0},{16,24},{24,16},{1,9},{9,1},{17,25},{25,17},{2,10},{10... | collective-permute-start | bytes 4816904 | tf_op jit(solution)/shard_map/ppermute | solution.py:652
  118.4 31.4 %collective-permute-start.10 = (bf16[128,768]{1,0:T(8,128)(2,1)S(1)}, bf16[128,768]{1,0:T(8,128)(2,1)S(1)}, u32[]{:S(2)}, u32[]{:S(2)}) collective-permute-start(bf16[128,768]{1,0:T(8,128)(2,1)S(1)} %fusion.21), channel_id=1, source_target_pairs={{0,2},{1,3},{2,0},{3,1},{4,6},{5,7},{6,4},{7,5},{8,10},{9,11},{10,... | collective-permute-start | bytes 589832 | tf_op jit(solution)/shard_map/ppermute | solution.py:652
  121.3 28.5 %collective-permute-start.11 = (bf16[128,768]{1,0:T(8,128)(2,1)S(1)}, bf16[128,768]{1,0:T(8,128)(2,1)S(1)}, u32[]{:S(2)}, u32[]{:S(2)}) collective-permute-start(bf16[128,768]{1,0:T(8,128)(2,1)S(1)} %fusion.21), channel_id=1, source_target_pairs={{0,3},{1,2},{2,1},{3,0},{4,7},{5,6},{6,5},{7,4},{8,11},{9,10},{10,... | collective-permute-start | bytes 589832 | tf_op jit(solution)/shard_map/ppermute | solution.py:652
  161.3 31.8 %collective-permute-start.15 = (s32[512,544]{0,1:T(8,128)}, s32[512,544]{0,1:T(8,128)}, u32[]{:S(2)}, u32[]{:S(2)}) collective-permute-start(s32[512,544]{0,1:T(8,128)} %copy.144), channel_id=1, source_target_pairs={{0,4},{4,0},{1,5},{5,1},{2,6},{6,2},{3,7},{7,3},{8,12},{12,8},{9,1... | collective-permute-start | bytes 3342344 | tf_op jit(solution)/shard_map/ppermute | solution.py:652
  179.1 44.8 %collective-permute-start.18 = (bf16[768,1024]{1,0:T(8,128)(2,1)}, bf16[768,1024]{1,0:T(8,128)(2,1)}, u32[]{:S(2)}, u32[]{:S(2)}) collective-permute-start(bf16[768,1024]{1,0:T(8,128)(2,1)} %pad_maximum_fusion.5.refs_8_.refs_4_), channel_id=1, source_target_pairs={{0,16},{8,24},{16,0},{24,8},{1,17},{9,25},{17,1},{25,9},{2,18},{10... | collective-permute-start | bytes 4718600 | tf_op jit(solution)/shard_map/ppermute | solution.py:652
  180.6 43.2 %collective-permute-start.19 = (bf16[768,1024]{1,0:T(8,128)(2,1)}, bf16[768,1024]{1,0:T(8,128)(2,1)}, u32[]{:S(2)}, u32[]{:S(2)}) collective-permute-start(bf16[768,1024]{1,0:T(8,128)(2,1)} %pad_maximum_fusion.6.refs_10_.refs_5_), channel_id=1, source_target_pairs={{0,8},{8,0},{16,24},{24,16},{1,9},{9,1},{17,25},{25,17},{2,10},{10... | collective-permute-start | bytes 4718600 | tf_op jit(solution)/shard_map/ppermute | solution.py:652
  182.3 25.2 %collective-permute-start.14 = (bf16[512,768]{1,0:T(8,128)(2,1)}, bf16[512,768]{1,0:T(8,128)(2,1)}, u32[]{:S(2)}, u32[]{:S(2)}) collective-permute-start(bf16[512,768]{1,0:T(8,128)(2,1)} %pad_maximum_fusion.9), channel_id=1, source_target_pairs={{0,4},{4,0},{1,5},{5,1},{2,6},{6,2},{3,7},{7,3},{8,12},{12,8},{9,1... | collective-permute-start | bytes 2359304 | tf_op jit(solution)/shard_map/ppermute | solution.py:652
  185.7 112.5 %all-to-all-start.2 = ((bf16[384,4,1024]{0,2,1:T(8,128)(2,1)}), bf16[384,4,1024]{0,2,1:T(8,128)(2,1)}, u32[]{:S(2)}, u32[]{:S(2)}) async-start(bf16[384,4,1024]{0,2,1:T(8,128)(2,1)} %bitcast.40), calls=%async_computation.2 | async-start | bytes 6291456 | tf_op jit(solution)/shard_map/all_to_all | solution.py:659
  263.5 34.3 %collective-permute-start.22 = (bf16[128,1536]{1,0:T(8,128)(2,1)S(1)}, bf16[128,1536]{1,0:T(8,128)(2,1)S(1)}, u32[]{:S(2)}, u32[]{:S(2)}) collective-permute-start(bf16[128,1536]{1,0:T(8,128)(2,1)S(1)} %get-tuple-element.328), channel_id=1, source_target_pairs={{0,2},{1,3},{2,0},{3,1},{4,6},{5,7},{6,4},{7,5},{8,10},{9,11},{10,... | collective-permute-start | bytes 1179656 | tf_op jit(solution)/shard_map/ppermute | solution.py:652
  263.5 34.3 %collective-permute-start.21 = (bf16[128,1536]{1,0:T(8,128)(2,1)S(1)}, bf16[128,1536]{1,0:T(8,128)(2,1)S(1)}, u32[]{:S(2)}, u32[]{:S(2)}) collective-permute-start(bf16[128,1536]{1,0:T(8,128)(2,1)S(1)} %get-tuple-element.326), channel_id=1, source_target_pairs={{0,1},{1,0},{2,3},{3,2},{4,5},{5,4},{6,7},{7,6},{8,9},{9,8},{10,11... | collective-permute-start | bytes 1179656 | tf_op jit(solution)/shard_map/ppermute | solution.py:652
  303.0 29.8 %collective-permute-start.25 = (bf16[128,1536]{1,0:T(8,128)(2,1)S(1)}, bf16[128,1536]{1,0:T(8,128)(2,1)S(1)}, u32[]{:S(2)}, u32[]{:S(2)}) collective-permute-start(bf16[128,1536]{1,0:T(8,128)(2,1)S(1)} %pad_maximum_fusion.20), channel_id=1, source_target_pairs={{0,2},{1,3},{2,0},{3,1},{4,6},{5,7},{6,4},{7,5},{8,10},{9,11},{10,... | collective-permute-start | bytes 1179656 | tf_op jit(solution)/shard_map/ppermute | solution.py:652
  305.9 27.0 %collective-permute-start.26 = (bf16[128,1536]{1,0:T(8,128)(2,1)S(1)}, bf16[128,1536]{1,0:T(8,128)(2,1)S(1)}, u32[]{:S(2)}, u32[]{:S(2)}) collective-permute-start(bf16[128,1536]{1,0:T(8,128)(2,1)S(1)} %pad_maximum_fusion.20), channel_id=1, source_target_pairs={{0,3},{1,2},{2,1},{3,0},{4,7},{5,6},{6,5},{7,4},{8,11},{9,10},{10,... | collective-permute-start | bytes 1179656 | tf_op jit(solution)/shard_map/ppermute | solution.py:652
  351.7 36.6 %collective-permute-start.28 = (bf16[768,1024]{1,0:T(8,128)(2,1)}, bf16[768,1024]{1,0:T(8,128)(2,1)S(1)}, u32[]{:S(2)}, u32[]{:S(2)}) collective-permute-start(bf16[768,1024]{1,0:T(8,128)(2,1)} %get-tuple-element.203), channel_id=1, source_target_pairs={{0,16},{8,24},{16,0},{24,8},{1,17},{9,25},{17,1},{25,9},{2,18},{10... | collective-permute-start | bytes 4718600 | tf_op jit(solution)/shard_map/ppermute | solution.py:652
  352.8 36.7 %collective-permute-start.29 = (bf16[768,1024]{1,0:T(8,128)(2,1)}, bf16[768,1024]{1,0:T(8,128)(2,1)}, u32[]{:S(2)}, u32[]{:S(2)}) collective-permute-start(bf16[768,1024]{1,0:T(8,128)(2,1)} %get-tuple-element.204), channel_id=1, source_target_pairs={{0,8},{8,0},{16,24},{24,16},{1,9},{9,1},{17,25},{25,17},{2,10},{10... | collective-permute-start | bytes 4718600 | tf_op jit(solution)/shard_map/ppermute | solution.py:652
  394.3 29.6 %collective-permute-start.31 = (bf16[768,512]{1,0:T(8,128)(2,1)S(1)}, bf16[768,512]{1,0:T(8,128)(2,1)S(1)}, u32[]{:S(2)}, u32[]{:S(2)}) collective-permute-start(bf16[768,512]{1,0:T(8,128)(2,1)S(1)} %split.40), channel_id=1, source_target_pairs={{0,16},{8,24},{16,0},{24,8},{1,17},{9,25},{17,1},{25,9},{2,18},{10... | collective-permute-start | bytes 2359304 | tf_op jit(solution)/shard_map/ppermute | solution.py:652
  397.9 27.9 %collective-permute-start.30 = (bf16[768,512]{1,0:T(8,128)(2,1)S(1)}, bf16[768,512]{1,0:T(8,128)(2,1)}, u32[]{:S(2)}, u32[]{:S(2)}) collective-permute-start(bf16[768,512]{1,0:T(8,128)(2,1)S(1)} %split.41), channel_id=1, source_target_pairs={{0,8},{8,0},{16,24},{24,16},{1,9},{9,1},{17,25},{25,17},{2,10},{10... | collective-permute-start | bytes 2359304 | tf_op jit(solution)/shard_map/ppermute | solution.py:652
  402.9 44.7 %collective-permute-start.32 = (bf16[784,1024]{1,0:T(8,128)(2,1)}, bf16[784,1024]{1,0:T(8,128)(2,1)}, u32[]{:S(2)}, u32[]{:S(2)}) collective-permute-start(bf16[784,1024]{1,0:T(8,128)(2,1)} %get-tuple-element.215), channel_id=1, source_target_pairs={{0,16},{8,24},{16,0},{24,8},{1,17},{9,25},{17,1},{25,9},{2,18},{10... | collective-permute-start | bytes 4816904 | tf_op jit(solution)/shard_map/ppermute | solution.py:652
  403.9 47.3 %collective-permute-start.33 = (bf16[784,1024]{1,0:T(8,128)(2,1)}, bf16[784,1024]{1,0:T(8,128)(2,1)}, u32[]{:S(2)}, u32[]{:S(2)}) collective-permute-start(bf16[784,1024]{1,0:T(8,128)(2,1)} %get-tuple-element.216), channel_id=1, source_target_pairs={{0,8},{8,0},{16,24},{24,16},{1,9},{9,1},{17,25},{25,17},{2,10},{10... | collective-permute-start | bytes 4816904 | tf_op jit(solution)/shard_map/ppermute | solution.py:652
  432.0 55.4 %all-to-all-start.3 = ((bf16[4,192,1024]{2,1,0:T(8,128)(2,1)}), bf16[4,192,1024]{2,1,0:T(8,128)(2,1)}, u32[]{:S(2)}, u32[]{:S(2)}) async-start(bf16[4,192,1024]{2,1,0:T(8,128)(2,1)} %bitcast.177), calls=%async_computation.3 | async-start | bytes 3145728 | tf_op jit(solution)/shard_map/all_to_all | solution.py:662
  441.5 226.0 %all-gather.5.cloned.1.call-start = ((), (), s32[]{:S(2)}) async-start(), calls=%async_computation.5 | async-start | bytes 7864320 | tf_op jit(solution)/shard_map/all_gather | solution.py:896
  460.4 24.7 %collective-permute-start.42 = (bf16[784,512]{1,0:T(8,128)(2,1)S(1)}, bf16[784,512]{1,0:T(8,128)(2,1)S(1)}, u32[]{:S(2)}, u32[]{:S(2)}) collective-permute-start(bf16[784,512]{1,0:T(8,128)(2,1)S(1)} %get-tuple-element.358), channel_id=1, source_target_pairs={{0,16},{8,24},{16,0},{24,8},{1,17},{9,25},{17,1},{25,9},{2,18},{10... | collective-permute-start | bytes 2408456 | tf_op jit(solution)/shard_map/ppermute | solution.py:652
  461.6 24.0 %collective-permute-start.41 = (bf16[784,512]{1,0:T(8,128)(2,1)S(1)}, bf16[784,512]{1,0:T(8,128)(2,1)S(1)}, u32[]{:S(2)}, u32[]{:S(2)}) collective-permute-start(bf16[784,512]{1,0:T(8,128)(2,1)S(1)} %get-tuple-element.357), channel_id=1, source_target_pairs={{0,8},{8,0},{16,24},{24,16},{1,9},{9,1},{17,25},{25,17},{2,10},{10... | collective-permute-start | bytes 2408456 | tf_op jit(solution)/shard_map/ppermute | solution.py:652
  536.0 23.2 %collective-permute-start.51 = (bf16[112,768]{1,0:T(8,128)(2,1)S(1)}, bf16[112,768]{1,0:T(8,128)(2,1)S(1)}, u32[]{:S(2)}, u32[]{:S(2)}) collective-permute-start(bf16[112,768]{1,0:T(8,128)(2,1)S(1)} %pad_maximum_fusion.10), channel_id=1, source_target_pairs={{0,1},{1,0},{2,3},{3,2},{4,5},{5,4},{6,7},{7,6},{8,9},{9,8},{10,11... | collective-permute-start | bytes 516104 | tf_op jit(solution)/shard_map/ppermute | solution.py:652
  543.1 26.0 %collective-permute-start.52 = (bf16[112,768]{1,0:T(8,128)(2,1)S(1)}, bf16[112,768]{1,0:T(8,128)(2,1)S(1)}, u32[]{:S(2)}, u32[]{:S(2)}) collective-permute-start(bf16[112,768]{1,0:T(8,128)(2,1)S(1)} %pad_maximum_fusion.10), channel_id=1, source_target_pairs={{0,2},{1,3},{2,0},{3,1},{4,6},{5,7},{6,4},{7,5},{8,10},{9,11},{10,... | collective-permute-start | bytes 516104 | tf_op jit(solution)/shard_map/ppermute | solution.py:652
  543.7 25.4 %collective-permute-start.53 = (bf16[112,768]{1,0:T(8,128)(2,1)S(1)}, bf16[112,768]{1,0:T(8,128)(2,1)S(1)}, u32[]{:S(2)}, u32[]{:S(2)}) collective-permute-start(bf16[112,768]{1,0:T(8,128)(2,1)S(1)} %pad_maximum_fusion.10), channel_id=1, source_target_pairs={{0,3},{1,2},{2,1},{3,0},{4,7},{5,6},{6,5},{7,4},{8,11},{9,10},{10,... | collective-permute-start | bytes 516104 | tf_op jit(solution)/shard_map/ppermute | solution.py:652
  592.5 68.5 %all-to-all-start.4 = ((bf16[4,192,1024]{2,1,0:T(8,128)(2,1)}), bf16[4,192,1024]{2,1,0:T(8,128)(2,1)}, u32[]{:S(2)}, u32[]{:S(2)}) async-start(bf16[4,192,1024]{2,1,0:T(8,128)(2,1)} %bitcast.186), calls=%async_computation.4 | async-start | bytes 3145728 | tf_op jit(solution)/shard_map/all_to_all | solution.py:662
  (105 other events, 1281.9 us)
Sparse Core Ops, SparseCore 0:
  495.4 160.9 all-gather.4
